TPU v7x, 32 devices: a whole 2x2x4 slice. The times are simulated.
32 devices in a mesh: dp: 8 (over z, core), block: 4 (over y, x).
Axes of the slice: x: 2, y: 2, z: 4, core: 2. Of those that a mesh axis runs over, the one named last changes fastest.
Arguments:
- tokens: bfloat16 [2, 512, 16384], P(None, 'block', 'dp'), may hold values from -6 to 6
- cotangent: float32 [2, 512, 16384], P(None, 'block', 'dp'), may hold values from -6 to 6
- item_lengths: int32 [2, 16], P(None, 'dp'), may hold values from 0 to 2048, as said below
- item_offsets: int32 [2, 16], P(None, 'dp'), may hold values from 0 to 2048
- norm_gain: float32 [2, 512], P(None, 'block'), may hold values from 0.5 to 1.5
- lambda_log: float32 [2, 384], P(None, 'block'), may hold values from -3 to 1
- lambda_imag: float32 [2, 384], P(None, 'block'), may hold values from -50 to 50
- log_step: float32 [2, 384], P(None, 'block'), may hold values from -6.9 to -2.3
- input_map: bfloat16 [2, 2, 384, 512], P(None, None, 'block'), may hold values from -0.25 to 0.25
- output_map: bfloat16 [2, 4, 384, 512], P(None, None, 'block'), may hold values from -0.75 to 0.75
- skip_weight: float32 [2, 512], P(None, 'block'), may hold values from -4 to 4
Outputs:
- output: float32 [2, 512, 16384], P(None, 'block', 'dp')
- input_grad: float32 [2, 512, 16384], P(None, 'block', 'dp')
- grad_norm_gain: float32 [2, 512], P(None, 'block')
- grad_lambda_log: float32 [2, 384], P(None, 'block')
- grad_lambda_imag: float32 [2, 384], P(None, 'block')
- grad_log_step: float32 [2, 384], P(None, 'block')
- grad_input_map: float32 [2, 2, 384, 512], P(None, None, 'block')
- grad_output_map: float32 [2, 4, 384, 512], P(None, None, 'block')
- grad_skip_weight: float32 [2, 512], P(None, 'block')
Inputs may be any that keep to these rules, and one draw needn't show every extreme that they name: `item_lengths`: each run of 2048 slots holds its 2 items in order, without correlation, between them and around them padding slots. An item of length 0 has offset 2048. In every micro-batch one run holds a single item that fills all its slots.
All inputs are finite; a program needn't handle non-finite values.
Results may differ from a plain program's by a relative error of at most 0.039.
Values may be sent and summed in bfloat16 or wider, within the bound.
No kernel may reach another device: no remote copies, remote signals or barrier semaphores. Data moves between devices by JAX's collectives and lax.ppermute only.
A program may use at most 384 MiB of HBM per device.

v0:
```python
from functools import partial
from typing import NamedTuple

import jax
import jax.numpy as jnp
from jax import lax
from jax.experimental import pallas as pl
from jax.experimental.pallas import tpu as pltpu
from jax.sharding import PartitionSpec as P

EPSILON = 1e-05
SEGS = 16
LANES = 128
BF = jnp.bfloat16
F32 = jnp.float32
GELU_C = 0.7978845608028654
GELU_A = 0.044715


class Sizes(NamedTuple):
    blocks: int
    chunks: int
    toks: int
    run: int
    steps: int
    width: int
    states: int
    items: int


def nt(a, b):
    return lax.dot_general(a, b, (((1,), (1,)), ((), ())), preferred_element_type=F32)


def nn(a, b):
    return lax.dot_general(a, b, (((1,), (0,)), ((), ())), preferred_element_type=F32)


def tn(a, b):
    return lax.dot_general(a, b, (((0,), (0,)), ((), ())), preferred_element_type=F32)


def cmul(ar, ai, br, bi):
    return ar * br - ai * bi, ar * bi + ai * br


def rows_of(step):
    return pl.ds(pl.multiple_of(step * SEGS, SEGS), SEGS)


def widen(mask, count):
    return jnp.concatenate([mask] * count, axis=1)


def item_of(sz, meta, index):
    begin = meta[2 + sz.items + index]
    return begin, begin + meta[2 + index]


def fill_masks(sz, meta, live, ahead, behind):
    base = meta[1] * sz.toks
    seg = lax.broadcasted_iota(jnp.int32, (SEGS, LANES), 0)

    def body(step, carry):
        pos = base + seg * sz.steps + step
        inside = jnp.zeros((SEGS, LANES), F32)
        onward = jnp.zeros((SEGS, LANES), F32)
        onward_next = jnp.zeros((SEGS, LANES), F32)
        for index in range(sz.items):
            begin, end = item_of(sz, meta, index)
            inside = jnp.where((pos >= begin) & (pos < end), 1.0, inside)
            onward = jnp.where((pos > begin) & (pos < end), 1.0, onward)
            onward_next = jnp.where((pos >= begin) & (pos + 1 < end), 1.0, onward_next)
        onward_next = jnp.where(pos + 1 < sz.run, onward_next, 0.0)
        if live is not None:
            live[rows_of(step), :] = inside
        ahead[rows_of(step), :] = onward
        behind[rows_of(step), :] = onward_next
        return carry

    lax.fori_loop(0, sz.steps, body, 0, unroll=4)


def through(sz, meta, first, length):
    ahead = behind = False
    for index in range(sz.items):
        begin, end = item_of(sz, meta, index)
        ahead = ahead | ((begin < first) & (end >= first + length))
        behind = behind | ((begin <= first) & (end > first + length))
    behind = behind & (first + length < sz.run)
    return ahead, behind


def power(pair, count):
    while count > 1:
        pair = cmul(*pair, *pair)
        count //= 2
    return pair


def column_blocks(sz, decay):
    out = []
    for q in range(sz.states // LANES):
        cols = slice(q * LANES, (q + 1) * LANES)
        out.append((decay[0:1, cols], decay[1:2, cols]))
    return out


def spread(pairs):
    return [tuple(jnp.broadcast_to(v, (SEGS, LANES)) for v in pair) for pair in pairs]


def chain_ends(sz, decay, ahead, behind, source, ahead_col, behind_col, ends):
    nq = sz.states // LANES
    d = spread(column_blocks(sz, decay))
    zero = jnp.zeros((SEGS, LANES), F32)

    def body(step, held):
        up, down = rows_of(step), rows_of(sz.steps - 1 - step)
        on_up, on_down = ahead[up, :], behind[down, :]
        new = []
        for q in range(nq):
            for side, (rows, on, col) in enumerate(((up, on_up, ahead_col), (down, on_down, behind_col))):
                re, im = held[2 * q + side]
                re, im = cmul(*d[q], re * on, im * on)
                re += source[rows, col + q * LANES : col + (q + 1) * LANES]
                im += source[rows, col + sz.states + q * LANES : col + sz.states + (q + 1) * LANES]
                new.append((re, im))
        return tuple(new)

    held = lax.fori_loop(0, sz.steps, body, tuple((zero, zero) for _ in range(2 * nq)), unroll=4)
    for q in range(nq):
        cols = slice(q * LANES, (q + 1) * LANES)
        for side in range(2):
            ends[2 * side, :, cols] = held[2 * q + side][0]
            ends[2 * side + 1, :, cols] = held[2 * q + side][1]


def enter_states(sz, meta, decay, ends, start, enter):
    pair = (decay[0:1, :], decay[1:2, :])
    jump = power(pair, sz.steps)
    base = meta[1] * sz.toks
    state = list(start)
    for count in range(SEGS):
        for side, seg in ((0, count), (1, SEGS - 1 - count)):
            re, im = state[side]
            enter[2 * side, seg : seg + 1, :] = re
            enter[2 * side + 1, seg : seg + 1, :] = im
            passes = through(sz, meta, base + seg * sz.steps, sz.steps)[side]
            gain = jnp.where(passes, 1.0, 0.0).astype(F32)
            re, im = cmul(jump[0] * gain, jump[1] * gain, re, im)
            state[side] = (
                re + ends[2 * side, seg : seg + 1, :],
                im + ends[2 * side + 1, seg : seg + 1, :],
            )
    return state


def send_ends(sz, meta, decay, ends, enter, send):
    zero = jnp.zeros((1, sz.states), F32)
    ahead, behind = enter_states(sz, meta, decay, ends, ((zero, zero), (zero, zero)), enter)
    me = meta[1]
    for dist in range(1, sz.chunks):
        up = (me ^ dist) > me
        for part in range(2):
            send[dist - 1, part : part + 1, :] = jnp.where(up, ahead[part], behind[part])


def received(sz, meta, decay, recv):
    me = meta[1]
    zero = jnp.zeros((1, sz.states), F32)
    pair = (decay[0:1, :], decay[1:2, :])
    jump = power(pair, sz.toks) if sz.chunks > 2 else None
    sides = []
    for side in range(2):
        re, im = zero, zero
        order = range(sz.chunks) if side == 0 else range(sz.chunks - 1, -1, -1)
        for other in order:
            use = (other < me) if side == 0 else (other > me)
            slot = jnp.maximum((me ^ other) - 1, 0)
            got = recv[slot]
            new_re, new_im = got[0:1, :], got[1:2, :]
            if sz.chunks > 2:
                passes = through(sz, meta, other * sz.toks, sz.toks)[side]
                gain = jnp.where(passes, 1.0, 0.0).astype(F32)
                moved = cmul(jump[0] * gain, jump[1] * gain, re, im)
                new_re, new_im = new_re + moved[0], new_im + moved[1]
            re, im = jnp.where(use, new_re, re), jnp.where(use, new_im, im)
        sides.append((re, im))
    return sides


def load_enter(sz, enter):
    held = []
    for q in range(sz.states // LANES):
        cols = slice(q * LANES, (q + 1) * LANES)
        for side in range(2):
            held.append((enter[2 * side, :, cols], enter[2 * side + 1, :, cols]))
    return tuple(held)


def chain_states(sz, decay, ahead, behind, source, enter, states):
    nq = sz.states // LANES
    n = sz.states
    d = spread(column_blocks(sz, decay))

    def body(step, held):
        up, down = rows_of(step), rows_of(sz.steps - 1 - step)
        on_up, on_down = ahead[up, :], behind[down, :]
        new = []
        for q in range(nq):
            for side, (rows, on) in enumerate(((up, on_up), (down, on_down))):
                re, im = held[2 * q + side]
                re, im = cmul(*d[q], re * on, im * on)
                lo = q * LANES
                re += source[rows, lo : lo + LANES]
                im += source[rows, n + lo : n + lo + LANES]
                at = 2 * side * n + lo
                states[rows, at : at + LANES] = re.astype(BF)
                states[rows, at + n : at + n + LANES] = (-im).astype(BF)
                new.append((re, im))
        return tuple(new)

    lax.fori_loop(0, sz.steps, body, load_enter(sz, enter), unroll=4)


def adjoint_chains(sz, decay, ahead, behind, source, enter, states, half, grad_driven, grad_decay):
    nq = sz.states // LANES
    n = sz.states
    d = spread(column_blocks(sz, decay))
    zero = jnp.zeros((SEGS, LANES), F32)

    def make(second):
        def body(step, carry):
            held, sums = carry
            up, down = rows_of(step), rows_of(sz.steps - 1 - step)
            on_up, on_down = ahead[up, :], behind[down, :]
            new, total = [], []
            for q in range(nq):
                lo = q * LANES
                acc_re, acc_im = sums[q]
                for side, (rows, on, src, st) in enumerate(((up, on_up, 2 * n, 2 * n), (down, on_down, 0, 0))):
                    re, im = held[2 * q + side]
                    re, im = re * on, im * on
                    s_re = states[rows, st + lo : st + lo + LANES].astype(F32)
                    s_im = states[rows, st + n + lo : st + n + lo + LANES].astype(F32)
                    acc_re += re * s_re + im * s_im
                    acc_im += re * s_im - im * s_re
                    re, im = cmul(*d[q], re, im)
                    re += source[rows, src + lo : src + lo + LANES]
                    im += source[rows, src + n + lo : src + n + lo + LANES]
                    new.append((re, im))
                    if second:
                        out_re = re + half[rows, lo : lo + LANES]
                        out_im = im + half[rows, n + lo : n + lo + LANES]
                        grad_driven[rows, lo : lo + LANES] = out_re.astype(BF)
                        grad_driven[rows, n + lo : n + lo + LANES] = (-out_im).astype(BF)
                    else:
                        half[rows, lo : lo + LANES] = re
                        half[rows, n + lo : n + lo + LANES] = im
                total.append((acc_re, acc_im))
            return tuple(new), tuple(total)

        return body

    carry = (load_enter(sz, enter), tuple((zero, zero) for _ in range(nq)))
    carry = lax.fori_loop(0, sz.steps // 2, make(False), carry, unroll=2)
    carry = lax.fori_loop(sz.steps // 2, sz.steps, make(True), carry, unroll=2)
    for q in range(nq):
        cols = slice(q * LANES, (q + 1) * LANES)
        grad_decay[0:1, cols] = jnp.sum(carry[1][q][0], axis=0, keepdims=True)
        grad_decay[1:2, cols] = jnp.sum(carry[1][q][1], axis=0, keepdims=True)


ROWS = 64


def over_rows(sz, body, init=0):
    def step(index, carry):
        return body(pl.ds(pl.multiple_of(index * ROWS, ROWS), ROWS), carry)

    return lax.fori_loop(0, sz.toks // ROWS, step, init)


def norm_rows(sz, hidden, gain, live, normed):
    def body(rows, carry):
        u = hidden[rows, :].astype(F32)
        scale = lax.rsqrt(jnp.mean(u * u, axis=1, keepdims=True) + EPSILON)
        v = u * scale * gain[...]
        normed[rows, :] = (v * widen(live[rows, :], sz.width // LANES)).astype(BF)
        return carry

    over_rows(sz, body)


def matmul_nt(a, b, out, tile=256):
    for lo in range(0, b.shape[0], tile):
        out[:, lo : lo + tile] = nt(a[...], b[lo : lo + tile, :]).astype(out.dtype)


def matmul_nn(a, b, out, tile=256):
    for lo in range(0, b.shape[1], tile):
        out[:, lo : lo + tile] = nn(a[...], b[:, lo : lo + tile]).astype(out.dtype)


def matmul_tn(a, b, out, tile=256):
    for lo in range(0, a.shape[1], tile):
        out[lo : lo + tile, :] = tn(a[:, lo : lo + tile], b[...]).astype(out.dtype)


def finish_rows(sz, mixed, skip, normed, live, hidden, slope, result):
    def body(rows, carry):
        pre = 2.0 * mixed[rows, :] + skip[...] * normed[rows, :].astype(F32)
        square = pre * pre
        th = jnp.tanh(pre * (GELU_C + (GELU_C * GELU_A) * square))
        on = widen(live[rows, :], sz.width // LANES)
        part = 0.5 * (1.0 + th)
        deriv = part + 0.5 * pre * (1.0 - th * th) * (GELU_C + (3.0 * GELU_C * GELU_A) * square)
        slope[rows, :] = (on * deriv).astype(slope.dtype)
        result[rows, :] = (hidden[rows, :].astype(F32) + on * (pre * part)).astype(result.dtype)
        return carry

    over_rows(sz, body)


def layer_open(sz, meta, hidden, gain, w_in, decay, live, ahead, behind, normed, driven, ends, enter, send):
    norm_rows(sz, hidden, gain, live, normed)
    matmul_nt(normed, w_in, driven)
    chain_ends(sz, decay, ahead, behind, driven, 0, 0, ends)
    send_ends(sz, meta, decay, ends, enter, send)


def layer_close(sz, meta, recv, decay, ends, driven, normed, hidden, w_out, skip, live, ahead, behind, enter, mixed, states, slope, result):
    enter_states(sz, meta, decay, ends, received(sz, meta, decay, recv), enter)
    chain_states(sz, decay, ahead, behind, driven, enter, states)
    matmul_nn(states, w_out, mixed)
    finish_rows(sz, mixed, skip, normed, live, hidden, slope, result)


def back_open(sz, meta, upstream, slope, normed, w_out, decay, ahead, behind, twice, grad_states, grad_skip, ends, enter, send):
    def body(rows, total):
        e = upstream[rows, :] * slope[rows, :].astype(F32)
        low = e.astype(BF)
        twice[rows, :] = low + low
        part = e * normed[rows, :].astype(F32)
        return total + jnp.sum(part.reshape(ROWS // 8, 8, sz.width), axis=0)

    total = over_rows(sz, body, jnp.zeros((8, sz.width), F32))
    grad_skip[...] = jnp.sum(total, axis=0, keepdims=True)
    matmul_nt(twice, w_out, grad_states)
    chain_ends(sz, decay, ahead, behind, grad_states, 2 * sz.states, 0, ends)
    send_ends(sz, meta, decay, ends, enter, send)


def back_close(sz, meta, recv, decay, ends, grad_states, states, upstream, slope, skip, hidden, gain, w_in, ahead, behind,
               enter, half, grad_normed, grad_driven, grad_decay, grad_gain, result):
    enter_states(sz, meta, decay, ends, received(sz, meta, decay, recv), enter)
    adjoint_chains(sz, decay, ahead, behind, grad_states, enter, states, half, grad_driven, grad_decay)
    matmul_nn(grad_driven, w_in, grad_normed)

    def body(rows, total):
        u = hidden[rows, :].astype(F32)
        r = upstream[rows, :]
        gn = grad_normed[rows, :] + r * slope[rows, :].astype(F32) * skip[...]
        scale = lax.rsqrt(jnp.mean(u * u, axis=1, keepdims=True) + EPSILON)
        part = gn * u * scale
        dn = gn * gain[...]
        inner = jnp.sum(dn * u, axis=1, keepdims=True) * (1.0 / sz.width)
        result[rows, :] = (r + scale * dn - u * (scale * scale * scale * inner)).astype(result.dtype)
        return total + jnp.sum(part.reshape(ROWS // 8, 8, sz.width), axis=0)

    total = over_rows(sz, body, jnp.zeros((8, sz.width), F32))
    grad_gain[...] = jnp.sum(total, axis=0, keepdims=True)


def place_pieces(sz, meta, pieces, stacked):
    part = sz.width // sz.blocks
    for dist, piece in enumerate(pieces):
        owner = meta[0] ^ dist
        stacked[pl.ds(pl.multiple_of(owner * part, part), part), :] = piece[...]


def cut_pieces(sz, meta, rows, perm, stacked, pieces):
    part = sz.width // sz.blocks
    matmul_tn(rows, perm, stacked)
    for dist, piece in enumerate(pieces):
        owner = meta[0] ^ dist
        piece[...] = stacked[pl.ds(pl.multiple_of(owner * part, part), part), :]


def enter_kernel(sz, meta, gain, w_in, decay, perm, *refs):
    pieces, refs = refs[: sz.blocks], refs[sz.blocks :]
    hidden, normed, driven, ends, send, stacked, live, ahead, behind, enter = refs
    place_pieces(sz, meta, pieces, stacked)
    matmul_nt(perm, stacked, hidden)
    fill_masks(sz, meta, live, ahead, behind)
    layer_open(sz, meta, hidden, gain, w_in, decay, live, ahead, behind, normed, driven, ends, enter, send)


def middle_kernel(sz, meta, recv, decay, ends, driven, normed, hidden, w_out, skip, gain_b, w_in_b, decay_b,
                  states, slope, hidden_b, normed_b, driven_b, ends_b, send_b, live, ahead, behind, enter, mixed):
    fill_masks(sz, meta, live, ahead, behind)
    layer_close(sz, meta, recv, decay, ends, driven, normed, hidden, w_out, skip, live, ahead, behind, enter, mixed, states, slope, hidden_b)
    layer_open(sz, meta, hidden_b, gain_b, w_in_b, decay_b, live, ahead, behind, normed_b, driven_b, ends_b, enter, send_b)


def leave_kernel(sz, meta, recv, decay, ends, driven, normed, hidden, w_out, skip, perm, states, slope, *refs):
    pieces, refs = refs[: sz.blocks], refs[sz.blocks :]
    live, ahead, behind, enter, mixed, last, stacked = refs
    fill_masks(sz, meta, live, ahead, behind)
    layer_close(sz, meta, recv, decay, ends, driven, normed, hidden, w_out, skip, live, ahead, behind, enter, mixed, states, slope, last)
    cut_pieces(sz, meta, last, perm, stacked, pieces)


def turn_kernel(sz, meta, slope, normed, w_out, decay, perm, *refs):
    pieces, refs = refs[: sz.blocks], refs[sz.blocks :]
    upstream, twice, grad_states, grad_skip, ends, send, stacked, ahead, behind, enter = refs
    place_pieces(sz, meta, pieces, stacked)
    matmul_nt(perm, stacked, upstream)
    fill_masks(sz, meta, None, ahead, behind)
    back_open(sz, meta, upstream, slope, normed, w_out, decay, ahead, behind, twice, grad_states, grad_skip, ends, enter, send)


def back_middle_kernel(sz, meta, recv, decay, ends, grad_states, states, upstream, slope, skip, hidden, gain, w_in,
                       slope_b, normed_b, w_out_b, decay_b,
                       grad_driven, grad_decay, grad_gain, upstream_b, twice_b, grad_states_b, grad_skip_b, ends_b, send_b,
                       ahead, behind, enter, half, grad_normed):
    fill_masks(sz, meta, None, ahead, behind)
    back_close(sz, meta, recv, decay, ends, grad_states, states, upstream, slope, skip, hidden, gain, w_in, ahead, behind,
               enter, half, grad_normed, grad_driven, grad_decay, grad_gain, upstream_b)
    back_open(sz, meta, upstream_b, slope_b, normed_b, w_out_b, decay_b, ahead, behind, twice_b, grad_states_b, grad_skip_b, ends_b, enter, send_b)


def back_leave_kernel(sz, meta, recv, decay, ends, grad_states, states, upstream, slope, skip, hidden, gain, w_in, perm,
                      grad_driven, grad_decay, grad_gain, *refs):
    pieces, refs = refs[: sz.blocks], refs[sz.blocks :]
    ahead, behind, enter, half, grad_normed, last, stacked = refs
    fill_masks(sz, meta, None, ahead, behind)
    back_close(sz, meta, recv, decay, ends, grad_states, states, upstream, slope, skip, hidden, gain, w_in, ahead, behind,
               enter, half, grad_normed, grad_driven, grad_decay, grad_gain, last)
    cut_pieces(sz, meta, last, perm, stacked, pieces)


def weight_kernel(left, right, out):
    matmul_tn(left, right, out)


VMEM = pl.BlockSpec(memory_space=pltpu.VMEM)
SMEM = pl.BlockSpec(memory_space=pltpu.SMEM)


def call(name, body, meta, args, outs, scratch, flops, limit=20):
    has_meta = meta is not None
    out_shape = [jax.ShapeDtypeStruct(shape, dtype) for shape, dtype in outs]
    moved = sum(a.size * a.dtype.itemsize for a in args) + sum(o.size * o.dtype.itemsize for o in out_shape)
    return pl.pallas_call(
        body,
        out_shape=out_shape,
        in_specs=[SMEM] * has_meta + [VMEM] * len(args),
        out_specs=[VMEM] * len(outs),
        scratch_shapes=[pltpu.VMEM(shape, dtype) for shape, dtype in scratch],
        compiler_params=pltpu.CompilerParams(vmem_limit_bytes=limit << 20),
        cost_estimate=pl.CostEstimate(flops=flops, bytes_accessed=moved, transcendentals=0),
        name=name,
    )(*([meta] if has_meta else []), *args)


def discretize(lambda_log, lambda_imag, log_step, input_map):
    step_size = jnp.exp(log_step)
    lambda_real = -jnp.exp(lambda_log)
    modulus = jnp.exp(lambda_real * step_size)
    decay_real = modulus * jnp.cos(lambda_imag * step_size)
    decay_imag = modulus * jnp.sin(lambda_imag * step_size)
    denominator = lambda_real * lambda_real + lambda_imag * lambda_imag
    scale_real = ((decay_real - 1.0) * lambda_real + decay_imag * lambda_imag) / denominator
    scale_imag = (decay_imag * lambda_real - (decay_real - 1.0) * lambda_imag) / denominator
    scale_real, scale_imag = scale_real[:, None], scale_imag[:, None]
    drive_real = scale_real * input_map[0] - scale_imag * input_map[1]
    drive_imag = scale_real * input_map[1] + scale_imag * input_map[0]
    return decay_real, decay_imag, jnp.stack([drive_real, drive_imag])


def on_device(tokens, cotangent, item_lengths, item_offsets, norm_gain, lambda_log, lambda_imag, log_step, input_map, output_map, skip_weight):
    micro, part, run = tokens.shape
    layers = norm_gain.shape[0]
    blocks = lax.axis_size("block")
    chunks = blocks // micro
    toks = run // chunks
    own = lambda_log.shape[1]
    width, states = part * blocks, own * blocks
    sz = Sizes(blocks, chunks, toks, run, toks // SEGS, width, states, item_lengths.shape[1])
    me = lax.axis_index("block")
    mine, chunk = me // chunks, me % chunks

    def swap(x, dist):
        return lax.ppermute(x, "block", [(i, i ^ dist) for i in range(blocks)])

    def to_chunks(x):
        out = []
        for dist in range(blocks):
            to = me ^ dist
            piece = lax.dynamic_slice(x, (to // chunks, 0, (to % chunks) * toks), (1, part, toks))[0].astype(BF)
            out.append(swap(piece, dist) if dist else piece)
        return out

    def from_chunks(pieces):
        out = jnp.zeros((micro, part, run), F32)
        for dist, piece in enumerate(pieces):
            got = swap(piece, dist) if dist else piece
            owner = me ^ dist
            out = lax.dynamic_update_slice(out, got.astype(F32)[None], (owner // chunks, 0, (owner % chunks) * toks))
        return out

    def exchange(send):
        return jnp.stack([swap(send[dist - 1], dist) for dist in range(1, chunks)])

    meta = jnp.concatenate([
        jnp.stack([me, chunk]).astype(jnp.int32),
        lax.dynamic_index_in_dim(item_lengths, mine, 0, keepdims=False),
        lax.dynamic_index_in_dim(item_offsets, mine, 0, keepdims=False),
    ])
    row = jnp.arange(toks, dtype=jnp.int32)[:, None]
    col = jnp.arange(toks, dtype=jnp.int32)[None, :]
    perm = ((row % SEGS) * sz.steps + row // SEGS == col).astype(BF)

    token_pieces = to_chunks(tokens)
    discrete, pulls = [], []
    for layer in range(layers):
        values, pull = jax.vjp(discretize, lambda_log[layer], lambda_imag[layer], log_step[layer], input_map[layer].astype(F32))
        discrete.append(values)
        pulls.append(pull)
    small = jnp.concatenate(
        [norm_gain, skip_weight, jnp.stack([v[0] for v in discrete]), jnp.stack([v[1] for v in discrete])], axis=1
    )
    small = lax.all_gather(small, "block", axis=0)
    joined = lambda lo, n: jnp.swapaxes(small[:, :, lo : lo + n], 0, 1).reshape(layers, blocks * n)
    gains = joined(0, part)
    skips = joined(part, part)
    decays = jnp.stack([joined(2 * part, own), joined(2 * part + own, own)], axis=1)
    w_in = [lax.all_gather(v[2].astype(BF), "block", axis=1, tiled=True).reshape(2 * states, width) for v in discrete]
    w_out = [lax.all_gather(output_map[l], "block", axis=1, tiled=True).reshape(4 * states, width) for l in range(layers)]
    gain = [gains[l : l + 1] for l in range(layers)]
    skip = [skips[l : l + 1] for l in range(layers)]
    decay = [decays[l] for l in range(layers)]

    mask = ((toks, LANES), F32)
    enter = ((4, SEGS, states), F32)
    stacked = ((width, toks), BF)
    rows_f, rows_b = ((toks, width), F32), ((toks, width), BF)
    drv = ((toks, 2 * states), F32)
    sts = ((toks, 4 * states), BF)
    gst = ((toks, 4 * states), F32)
    snd = ((chunks - 1, 2, states), F32)
    line, gdec = ((1, width), F32), ((2, states), F32)
    piece_out = [((part, toks), BF)] * blocks
    unit = 2 * toks * width * states

    hidden_a, normed_a, driven_a, ends_a, send_a = call(
        "enter", partial(enter_kernel, sz), meta, [gain[0], w_in[0], decay[0], perm, *token_pieces],
        [rows_b, rows_b, drv, enter, snd], [stacked, mask, mask, mask, enter], 4 * unit)
    cot_pieces = to_chunks(cotangent)
    recv = exchange(send_a)
    states_a, slope_a, hidden_b, normed_b, driven_b, ends_b, send_b = call(
        "middle", partial(middle_kernel, sz), meta,
        [recv, decay[0], ends_a, driven_a, normed_a, hidden_a, w_out[0], skip[0], gain[1], w_in[1], decay[1]],
        [sts, rows_b, rows_f, rows_b, drv, enter, snd], [mask, mask, mask, enter, rows_f], 8 * unit)
    recv = exchange(send_b)
    states_b, slope_b, *out_pieces = call(
        "leave", partial(leave_kernel, sz), meta, [recv, decay[1], ends_b, driven_b, normed_b, hidden_b, w_out[1], skip[1], perm],
        [sts, rows_b, *piece_out], [mask, mask, mask, enter, rows_f, rows_b, stacked], 7 * unit)
    output = from_chunks(out_pieces)

    up_b, twice_b, gstates_b, gskip_b, ends, send = call(
        "turn", partial(turn_kernel, sz), meta, [slope_b, normed_b, w_out[1], decay[1], perm, *cot_pieces],
        [rows_f, rows_b, gst, line, enter, snd], [stacked, mask, mask, enter], 7 * unit)
    recv = exchange(send)
    (gout_b,) = call("grad_out_b", weight_kernel, None, [states_b, twice_b], [((4 * states, width), BF)], [], 4 * unit)
    gdriven_b, gdecay_b, ggain_b, up_a, twice_a, gstates_a, gskip_a, ends, send = call(
        "back_middle", partial(back_middle_kernel, sz), meta,
        [recv, decay[1], ends, gstates_b, states_b, up_b, slope_b, skip[1], hidden_b, gain[1], w_in[1], slope_a, normed_a, w_out[0], decay[0]],
        [((toks, 2 * states), BF), gdec, line, rows_f, rows_b, gst, line, enter, snd], [mask, mask, enter, drv, rows_f], 10 * unit)
    recv = exchange(send)
    (gin_b,) = call("grad_in_b", weight_kernel, None, [gdriven_b, normed_b], [((2 * states, width), BF)], [], 2 * unit)
    (gout_a,) = call("grad_out_a", weight_kernel, None, [states_a, twice_a], [((4 * states, width), BF)], [], 4 * unit)
    gdriven_a, gdecay_a, ggain_a, *grad_pieces = call(
        "back_leave", partial(back_leave_kernel, sz), meta,
        [recv, decay[0], ends, gstates_a, states_a, up_a, slope_a, skip[0], hidden_a, gain[0], w_in[0], perm],
        [((toks, 2 * states), BF), gdec, line, *piece_out], [mask, mask, enter, drv, rows_f, rows_b, stacked], 6 * unit)
    input_grad = from_chunks(grad_pieces)
    (gin_a,) = call("grad_in_a", weight_kernel, None, [gdriven_a, normed_a], [((2 * states, width), BF)], [], 2 * unit)

    def reduce_weights(gin, gout):
        whole = jnp.concatenate([gin.reshape(2, states, width), gout.reshape(4, states, width)])
        shard = lax.psum_scatter(whole, "block", scatter_dimension=1, tiled=True)
        return lax.psum(shard, "dp").astype(F32)

    big = jnp.stack([reduce_weights(gin_a, gout_a), reduce_weights(gin_b, gout_b)])
    tiny = jnp.concatenate([
        jnp.concatenate([ggain_a, ggain_b]), jnp.concatenate([gskip_a, gskip_b]),
        jnp.stack([gdecay_a, gdecay_b]).reshape(layers, 2 * states)], axis=1)
    tiny = lax.psum(tiny, ("dp", "block"))
    cut = lambda lo, n: lax.dynamic_slice_in_dim(tiny, lo + me * n, n, 1)
    grad_gain, grad_skip = cut(0, part), cut(width, part)
    gdr, gdi = cut(2 * width, own), cut(2 * width + states, own)
    pulled = [pulls[l]((gdr[l], gdi[l], big[l, :2])) for l in range(layers)]
    grad_log, grad_imag, grad_step, grad_in = (jnp.stack([p[i] for p in pulled]) for i in range(4))
    return output, input_grad, grad_gain, grad_log, grad_imag, grad_step, grad_in, big[:, 2:], grad_skip


def solution(mesh):
    half = P(None, "block")
    maps = P(None, None, "block", None)
    acts = P(None, "block", "dp")
    items = P(None, "dp")
    return jax.shard_map(
        on_device,
        mesh=mesh,
        in_specs=(acts, acts, items, items, half, half, half, half, maps, maps, half),
        out_specs=(acts, acts, half, half, half, half, maps, maps, half),
        check_vma=False,
    )
```

profile of v0, /device:TPU:0, one launch (start us, length us, event | category | flops | bytes accessed | tf_op | source)
XLA Modules:
  0.0 314.1 jit_solution(3280226197489240508)
XLA Ops:
  7.3 2.1 fusion.71
  10.6 2.9 collective-permute-start
  13.5 1.5 collective-permute-start.1
  15.5 16.7 %all-gather.3 = f32[4,2,448]{2,1,0:T(2,128)S(1)} all-gather(f32[1,2,448]{2,1,0:T(2,128)S(1)} %maximum_bitcast_fusion), channel_id=2, replica_groups=mesh['dp'=8,'block'=4] {'block'}, dimensions={0}, use_global_device_ids=true | all-gather | bytes 17920 | tf_op jit(solution)/shard_map/all_gather | solution.py:535
  33.0 17.7 %all_gather.20 = bf16[2,384,512]{2,1,0:T(8,128)(2,1)S(1)} all-gather(bf16[2,96,512]{2,1,0:T(8,128)(2,1)S(1)} %pad_maximum_fusion.4), channel_id=1, replica_groups=mesh['dp'=8,'block'=4] {'block'}, dimensions={1}, use_global_device_ids=true | all-gather | bytes 983040 | tf_op jit(solution)/shard_map/all_gather | solution.py:540
  51.2 6.9 %enter.1 = (bf16[1024,512]{1,0:T(8,128)(2,1)S(1)}, bf16[1024,512]{1,0:T(8,128)(2,1)S(1)}, f32[1024,768]{1,0:T(8,128)S(1)}, f32[4,16,384]{2,1,0:T(8,128)S(1)}, f32[1,2,384]{2,1,0:T(2,128)S(1)}) custom-call(s32[6]{0:T(128)S(1)} %pad_add_fusion.meta, f32[1,512]{1,0:T(1,128)S(1)} %get-tuple-element.151.gain, bf16[768,512]{1,0:T(8,128)(2,1)S(1)} %bitcast.368, ...), custom_call_target="tpu_custom_call" | custom-call | flops 1610612736 | bytes 9281536 | tf_op jit(solution)/shard_map/enter/pallas_call | solution.py:456
  60.1 1.6 copy-done.47
  62.6 12.2 %all_gather.22 = bf16[2,384,512]{2,1,0:T(8,128)(2,1)} all-gather(bf16[2,96,512]{2,1,0:T(8,128)(2,1)S(1)} %pad_maximum_fusion.5), channel_id=1, replica_groups=mesh['dp'=8,'block'=4] {'block'}, dimensions={1}, use_global_device_ids=true | all-gather | bytes 983040 | tf_op jit(solution)/shard_map/all_gather | solution.py:540
  79.8 1.9 copy-done.48
  81.7 10.9 %middle.1 = (bf16[1024,1536]{1,0:T(8,128)(2,1)S(1)}, bf16[1024,512]{1,0:T(8,128)(2,1)S(1)}, f32[1024,512]{1,0:T(8,128)S(1)}, bf16[1024,512]{1,0:T(8,128)(2,1)S(1...) custom-call(s32[6]{0:T(128)S(1)} %pad_add_fusion.meta, ...), custom_call_target="tpu_custom_call" | custom-call | flops 3221225472 | bytes 18300928 | tf_op jit(solution)/shard_map/middle/pallas_call | solution.py:456
  92.7 1.7 copy-done.10
  96.7 1.6 copy-done.45
  101.7 1.5 collective-permute-start.8
  103.7 1.6 copy-done.14
  107.9 1.9 copy-done.46
  110.7 7.7 %leave.1 = (bf16[1024,1536]{1,0:T(8,128)(2,1)S(1)}, bf16[1024,512]{1,0:T(8,128)(2,1)S(1)}, bf16[128,1024]{1,0:T(8,128)(2,1)S(1)}, bf16[128,1024]{1,0:T(8,128)(2,...) custom-call(s32[6]{0:T(128)S(1)} %pad_add_fusion.meta, f32[1,2,384]{2,1,0:T(2,128)S(1)} %bitcast.386, ...), custom_call_target="tpu_custom_call" | custom-call | flops 2818572288 | bytes 15310848 | tf_op jit(solution)/shard_map/leave/pallas_call | solution.py:456
  118.5 6.7 %turn.1 = (f32[1024,512]{1,0:T(8,128)S(1)}, bf16[1024,512]{1,0:T(8,128)(2,1)S(1)}, f32[1024,1536]{1,0:T(8,128)S(1)}, f32[1,512]{1,0:T(1,128)S(1)}, f32[4,16,384]{2,1,0:T(8,128)S(1)}, /*index=5*/f32[1,2,384]{2,1,0:T(2,128)S(1)}) custom-call(s32[6]{0:T(128)S(1)} %pad_add_fusion.meta, bf16[1024,512]{1,0:T(8,128)(2,1)S(1)} %get-tuple-element.63.slope, ...), custom_call_target="tpu_custom_call" | custom-call | flops 2818572288 | bytes 16359424 | tf_op jit(solution)/shard_map/turn/pallas_call | solution.py:456
  126.6 1.8 grad_out_b.1
  129.2 10.9 %back_middle.1 = (bf16[1024,768]{1,0:T(8,128)(2,1)S(1)}, f32[2,384]{1,0:T(2,128)S(1)}, f32[1,512]{1,0:T(1,128)S(1)}, f32[1024,512]{1,0:T(8,128)S(1)}, bf16[1024,...) custom-call(s32[6]{0:T(128)S(1)} %pad_add_fusion.meta, ...), custom_call_target="tpu_custom_call" | custom-call | flops 4026531840 | bytes 30366720 | tf_op jit(solution)/shard_map/back_middle/pallas_call | solution.py:456
  140.1 2.6 copy-done
  145.0 1.7 pad_maximum_fusion.1
  147.9 1.9 copy-done.11
  151.1 1.8 grad_out_a.1
  153.5 2.8 copy-done.1
  156.3 1.6 copy-done.17
  157.9 8.3 %back_leave.1 = (bf16[1024,768]{1,0:T(8,128)(2,1)S(1)}, f32[2,384]{1,0:T(2,128)S(1)}, f32[1,512]{1,0:T(1,128)S(1)}, bf16[128,1024]{1,0:T(8,128)(2,1)S(1)}, bf16[...) custom-call(s32[6]{0:T(128)S(1)} %pad_add_fusion.meta, ...), custom_call_target="tpu_custom_call" | custom-call | flops 2415919104 | bytes 19250176 | tf_op jit(solution)/shard_map/back_leave/pallas_call | solution.py:456
  167.3 1.6 pad_maximum_fusion
  176.3 1.6 broadcast.270.clone.1
  178.7 45.0 %psum.21 = f32[2,1792]{1,0:T(2,128)S(1)} all-reduce(f32[2,1792]{1,0:T(2,128)S(1)} %maximum_maximum_fusion), channel_id=1, replica_groups=mesh['dp'=8,'block'=4] {'dp','block'}, use_global_device_ids=true, to_apply=%region_0.1 | all-reduce | flops 3584 | bytes 28672 | tf_op jit(solution)/shard_map/psum | solution.py:601
  224.3 2.4 collective-permute-start.15
  229.2 9.7 %reduce-scatter.3.cloned.1.call-done = bf16[6,96,512]{2,1,0:T(8,128)(2,1)} async-done(((bf16[6,384,512]{2,1,0:T(8,128)(2,1)}), bf16[6,96,512]{2,1,0:T(8,128)(2,1)}) %reduce-scatter.3.cloned.1.call-update) | async-done | bytes 589840 | tf_op jit(solution)/shard_map/reduce_scatter | solution.py:594
  241.5 59.3 %all-reduce.11.cloned.1.call-done = (bf16[1,6,96,512]{3,2,1,0:T(8,128)(2,1)}, bf16[1,6,96,512]{3,2,1,0:T(8,128)(2,1)}) async-done(((bf16[1,6,96,512]{3,2,1,0:T(8,128)(2,1)}, bf16[1,6,96,512]{3,2,1,0:T(8,128)(2,1)}), (bf16[1,6,96,512]{3,2,1,0:T(8,128)(2,1)}, bf16[1,6,96,512]{3,2,1,0:T(8,128)(2,1)})) %all-reduce.11.cloned.1.call-update) | async-done | bytes 1179664 | tf_op jit(solution)/shard_map/psum | solution.py:595
  (259 shorter events, 48.9 us)
Async XLA Ops:
  7.2 25.2 %copy-start.59 = (bf16[2,2,96,512]{3,2,1,0:T(8,128)(2,1)S(1)}, bf16[2,2,96,512]{3,2,1,0:T(8,128)(2,1)}, u32[]{:S(2)}) copy-start(bf16[2,2,96,512]{3,2,1,0:T(8,128)(2,1)} %param.19) | copy-start | bytes 1179652
  7.3 67.6 %all-gather.7.cloned.1.call-start = ((), (), s32[]{:S(2)}) async-start(), calls=%async_computation.4 | async-start | bytes 1966080 | tf_op jit(solution)/shard_map/all_gather | solution.py:541
  9.5 23.1 %copy-start.84 = (s32[2,2]{1,0:T(2,128)S(1)}, s32[2,2]{1,0:T(2,128)}, u32[]{:S(2)}) copy-start(s32[2,2]{1,0:T(2,128)} %param.13) | copy-start | bytes 52
  9.5 23.1 %copy-start.85 = (s32[2,2]{1,0:T(2,128)S(1)}, s32[2,2]{1,0:T(2,128)}, u32[]{:S(2)}) copy-start(s32[2,2]{1,0:T(2,128)} %param.14) | copy-start | bytes 52
  9.5 94.2 %all-gather.9.cloned.1.call-start = ((), (), s32[]{:S(2)}) async-start(), calls=%async_computation.5 | async-start | bytes 1966080 | tf_op jit(solution)/shard_map/all_gather | solution.py:541
  10.6 40.6 %collective-permute-start = (bf16[128,1024]{1,0:T(8,128)(2,1)}, bf16[128,1024]{1,0:T(8,128)(2,1)S(1)}, u32[]{:S(2)}, u32[]{:S(2)}) collective-permute-start(bf16[128,1024]{1,0:T(8,128)(2,1)} %get-tuple-element.126), channel_id=1, source_target_pairs={{0,1},{1,0},{2,3},{3,2},{4,5},{5,4},{6,7},{7,6},{8,9},{9,8},{10,11... | collective-permute-start | bytes 786440 | tf_op jit(solution)/shard_map/ppermute | solution.py:496
  13.5 37.7 %collective-permute-start.1 = (bf16[128,1024]{1,0:T(8,128)(2,1)}, bf16[128,1024]{1,0:T(8,128)(2,1)S(1)}, u32[]{:S(2)}, u32[]{:S(2)}) collective-permute-start(bf16[128,1024]{1,0:T(8,128)(2,1)} %get-tuple-element.128), channel_id=1, source_target_pairs={{0,2},{1,3},{2,0},{3,1},{4,6},{5,7},{6,4},{7,5},{8,10},{9,11},{10,... | collective-permute-start | bytes 786440 | tf_op jit(solution)/shard_map/ppermute | solution.py:496
  15.1 36.2 %collective-permute-start.2 = (bf16[128,1024]{1,0:T(8,128)(2,1)}, bf16[128,1024]{1,0:T(8,128)(2,1)S(1)}, u32[]{:S(2)}, u32[]{:S(2)}) collective-permute-start(bf16[128,1024]{1,0:T(8,128)(2,1)} %get-tuple-element.125), channel_id=1, source_target_pairs={{0,3},{1,2},{2,1},{3,0},{4,7},{5,6},{6,5},{7,4},{8,11},{9,10},{10,... | collective-permute-start | bytes 786440 | tf_op jit(solution)/shard_map/ppermute | solution.py:496
  15.1 214.1 %reduce-scatter.5.cloned.1.call-start = ((), (), s32[]{:S(2)}) async-start(), calls=%async_computation.3 | async-start | bytes 2949120 | tf_op jit(solution)/shard_map/reduce_scatter | solution.py:594
  15.3 35.3 %copy-start.74 = (f32[96]{0:T(128)}, f32[96]{0:T(128)S(1)}, u32[]{:S(2)}) copy-start(f32[96]{0:T(128)S(1)} %get-tuple-element.152) | copy-start | bytes 1156
  15.4 35.3 %copy-start.76 = (f32[96]{0:T(128)}, f32[96]{0:T(128)S(1)}, u32[]{:S(2)}) copy-start(f32[96]{0:T(128)S(1)} %get-tuple-element.154) | copy-start | bytes 1156
  15.4 35.3 %copy-start.78 = (f32[96]{0:T(128)}, f32[96]{0:T(128)S(1)}, u32[]{:S(2)}) copy-start(f32[96]{0:T(128)S(1)} %get-tuple-element.153) | copy-start | bytes 1156
  15.4 35.3 %copy-start.80 = (f32[96]{0:T(128)}, f32[96]{0:T(128)S(1)}, u32[]{:S(2)}) copy-start(f32[96]{0:T(128)S(1)} %get-tuple-element.155) | copy-start | bytes 1156
  32.6 18.2 %copy-start.51 = (f32[1,2,96,512]{3,2,1,0:T(8,128)}, f32[1,2,96,512]{3,2,1,0:T(8,128)S(1)}, u32[]{:S(2)}) copy-start(f32[1,2,96,512]{3,2,1,0:T(8,128)S(1)} %get-tuple-element.135) | copy-start | bytes 1179652
  61.8 13.1 %collective-permute-start.3 = (f32[2,384]{1,0:T(2,128)S(1)}, f32[2,384]{1,0:T(2,128)S(1)}, u32[]{:S(2)}, u32[]{:S(2)}) collective-permute-start(f32[2,384]{1,0:T(2,128)S(1)} %bitcast.389), channel_id=1, source_target_pairs={{0,1},{1,0},{2,3},{3,2},{4,5},{5,4},{6,7},{7,6},{8,9},{9,8},{10,11... | collective-permute-start | bytes 9224 | tf_op jit(solution)/shard_map/ppermute | solution.py:496
  98.3 5.3 %collective-permute-start.4 = (f32[2,384]{1,0:T(2,128)S(1)}, f32[2,384]{1,0:T(2,128)S(1)}, u32[]{:S(2)}, u32[]{:S(2)}) collective-permute-start(f32[2,384]{1,0:T(2,128)S(1)} %bitcast.385), channel_id=1, source_target_pairs={{0,1},{1,0},{2,3},{3,2},{4,5},{5,4},{6,7},{7,6},{8,9},{9,8},{10,11... | collective-permute-start | bytes 9224 | tf_op jit(solution)/shard_map/ppermute | solution.py:496
  100.2 18.2 %collective-permute-start.10 = (bf16[128,1024]{1,0:T(8,128)(2,1)}, bf16[128,1024]{1,0:T(8,128)(2,1)}, u32[]{:S(2)}, u32[]{:S(2)}) collective-permute-start(bf16[128,1024]{1,0:T(8,128)(2,1)} %get-tuple-element.109), channel_id=1, source_target_pairs={{0,3},{1,2},{2,1},{3,0},{4,7},{5,6},{6,5},{7,4},{8,11},{9,10},{10,... | collective-permute-start | bytes 786440 | tf_op jit(solution)/shard_map/ppermute | solution.py:496
  101.7 16.8 %collective-permute-start.8 = (bf16[128,1024]{1,0:T(8,128)(2,1)}, bf16[128,1024]{1,0:T(8,128)(2,1)}, u32[]{:S(2)}, u32[]{:S(2)}) collective-permute-start(bf16[128,1024]{1,0:T(8,128)(2,1)} %get-tuple-element.110), channel_id=1, source_target_pairs={{0,1},{1,0},{2,3},{3,2},{4,5},{5,4},{6,7},{7,6},{8,9},{9,8},{10,11... | collective-permute-start | bytes 786440 | tf_op jit(solution)/shard_map/ppermute | solution.py:496
  103.1 15.3 %collective-permute-start.9 = (bf16[128,1024]{1,0:T(8,128)(2,1)}, bf16[128,1024]{1,0:T(8,128)(2,1)}, u32[]{:S(2)}, u32[]{:S(2)}) collective-permute-start(bf16[128,1024]{1,0:T(8,128)(2,1)} %get-tuple-element.112), channel_id=1, source_target_pairs={{0,2},{1,3},{2,0},{3,1},{4,6},{5,7},{6,4},{7,5},{8,10},{9,11},{10,... | collective-permute-start | bytes 786440 | tf_op jit(solution)/shard_map/ppermute | solution.py:496
  125.3 3.7 %collective-permute-start.11 = (f32[2,384]{1,0:T(2,128)S(1)}, f32[2,384]{1,0:T(2,128)S(1)}, u32[]{:S(2)}, u32[]{:S(2)}) collective-permute-start(f32[2,384]{1,0:T(2,128)S(1)} %bitcast.388), channel_id=1, source_target_pairs={{0,1},{1,0},{2,3},{3,2},{4,5},{5,4},{6,7},{7,6},{8,9},{9,8},{10,11... | collective-permute-start | bytes 9224 | tf_op jit(solution)/shard_map/ppermute | solution.py:496
  146.8 92.1 %reduce-scatter.3.cloned.1.call-start = ((), (), s32[]{:S(2)}) async-start(), calls=%async_computation.2 | async-start | bytes 2949120 | tf_op jit(solution)/shard_map/reduce_scatter | solution.py:594
  146.8 6.1 %collective-permute-start.12 = (f32[2,384]{1,0:T(2,128)S(1)}, f32[2,384]{1,0:T(2,128)S(1)}, u32[]{:S(2)}, u32[]{:S(2)}) collective-permute-start(f32[2,384]{1,0:T(2,128)S(1)} %bitcast.384), channel_id=1, source_target_pairs={{0,1},{1,0},{2,3},{3,2},{4,5},{5,4},{6,7},{7,6},{8,9},{9,8},{10,11... | collective-permute-start | bytes 9224 | tf_op jit(solution)/shard_map/ppermute | solution.py:496
  168.9 131.9 %all-reduce.11.cloned.1.call-start = ((), (), s32[]{:S(2)}) async-start(), calls=%async_computation.6 | async-start | bytes 2359296 | tf_op jit(solution)/shard_map/psum | solution.py:595
  169.8 54.5 %collective-permute-start.5 = (bf16[128,1024]{1,0:T(8,128)(2,1)S(1)}, bf16[128,1024]{1,0:T(8,128)(2,1)S(1)}, u32[]{:S(2)}, u32[]{:S(2)}) collective-permute-start(bf16[128,1024]{1,0:T(8,128)(2,1)S(1)} %copy-done.38), channel_id=1, source_target_pairs={{0,1},{1,0},{2,3},{3,2},{4,5},{5,4},{6,7},{7,6},{8,9},{9,8},{10,11... | collective-permute-start | bytes 786440 | tf_op jit(solution)/shard_map/ppermute | solution.py:496
  171.1 56.4 %collective-permute-start.6 = (bf16[128,1024]{1,0:T(8,128)(2,1)S(1)}, bf16[128,1024]{1,0:T(8,128)(2,1)S(1)}, u32[]{:S(2)}, u32[]{:S(2)}) collective-permute-start(bf16[128,1024]{1,0:T(8,128)(2,1)S(1)} %copy-done.36), channel_id=1, source_target_pairs={{0,2},{1,3},{2,0},{3,1},{4,6},{5,7},{6,4},{7,5},{8,10},{9,11},{10,... | collective-permute-start | bytes 786440 | tf_op jit(solution)/shard_map/ppermute | solution.py:496
  172.4 56.0 %collective-permute-start.7 = (bf16[128,1024]{1,0:T(8,128)(2,1)S(1)}, bf16[128,1024]{1,0:T(8,128)(2,1)S(1)}, u32[]{:S(2)}, u32[]{:S(2)}) collective-permute-start(bf16[128,1024]{1,0:T(8,128)(2,1)S(1)} %copy-done.34), channel_id=1, source_target_pairs={{0,3},{1,2},{2,1},{3,0},{4,7},{5,6},{6,5},{7,4},{8,11},{9,10},{10,... | collective-permute-start | bytes 786440 | tf_op jit(solution)/shard_map/ppermute | solution.py:496
  173.5 50.8 %copy-start.40 = (bf16[128,1024]{1,0:T(8,128)(2,1)S(1)}, bf16[128,1024]{1,0:T(8,128)(2,1)}, u32[]{:S(2)}) copy-start(bf16[128,1024]{1,0:T(8,128)(2,1)} %copy-done.39) | copy-start | bytes 786436
  173.6 65.3 %collective-permute-start.13 = (bf16[128,1024]{1,0:T(8,128)(2,1)S(1)}, bf16[128,1024]{1,0:T(8,128)(2,1)S(1)}, u32[]{:S(2)}, u32[]{:S(2)}) collective-permute-start(bf16[128,1024]{1,0:T(8,128)(2,1)S(1)} %copy-done.44), channel_id=1, source_target_pairs={{0,1},{1,0},{2,3},{3,2},{4,5},{5,4},{6,7},{7,6},{8,9},{9,8},{10,11... | collective-permute-start | bytes 786440 | tf_op jit(solution)/shard_map/ppermute | solution.py:496
  175.1 64.7 %collective-permute-start.14 = (bf16[128,1024]{1,0:T(8,128)(2,1)S(1)}, bf16[128,1024]{1,0:T(8,128)(2,1)S(1)}, u32[]{:S(2)}, u32[]{:S(2)}) collective-permute-start(bf16[128,1024]{1,0:T(8,128)(2,1)S(1)} %copy-done.42), channel_id=1, source_target_pairs={{0,2},{1,3},{2,0},{3,1},{4,6},{5,7},{6,4},{7,5},{8,10},{9,11},{10,... | collective-permute-start | bytes 786440 | tf_op jit(solution)/shard_map/ppermute | solution.py:496
  224.3 16.3 %collective-permute-start.15 = (bf16[128,1024]{1,0:T(8,128)(2,1)S(1)}, bf16[128,1024]{1,0:T(8,128)(2,1)S(1)}, u32[]{:S(2)}, u32[]{:S(2)}) collective-permute-start(bf16[128,1024]{1,0:T(8,128)(2,1)S(1)} %copy-done.40), channel_id=1, source_target_pairs={{0,3},{1,2},{2,1},{3,0},{4,7},{5,6},{6,5},{7,4},{8,11},{9,10},{10,... | collective-permute-start | bytes 786440 | tf_op jit(solution)/shard_map/ppermute | solution.py:496
  240.6 61.6 %copy-start.79 = (f32[96]{0:T(128)S(1)}, f32[96]{0:T(128)}, u32[]{:S(2)}) copy-start(f32[96]{0:T(128)} %copy-done.78) | copy-start | bytes 1156
  240.6 61.6 %copy-start.81 = (f32[96]{0:T(128)S(1)}, f32[96]{0:T(128)}, u32[]{:S(2)}) copy-start(f32[96]{0:T(128)} %copy-done.80) | copy-start | bytes 1156
  (75 other events, 316.8 us)
Sparse Core Ops, SparseCore 0:
  10.5 40.6 all-gather.6
  53.1 31.8 all-gather.8
  146.9 46.3 reduce-scatter.4
  196.2 42.6 reduce-scatter.2
  241.2 59.6 all-reduce.10
where the time goes:
time: 315 us; the launch traced here: 314 us
  blocking collectives  91.6 us (29%)
  waiting for transfers between devices  69.6 us (22%)
  Pallas kernels  57.1 us (18%)
  local copies, waits for them, and re-layouts  43.5 us (14%)
  starting transfers between devices  20.7 us (7%)
  other arithmetic  16.6 us (5%)
  between operations  15 us (5%)
    psum x1, waiting for transfers between devices, reduce_weights(): return lax.psum(shard, 'dp').astype(F32)  59.3 us
    pallas_call x10, Pallas kernels, call(): pl.pallas_call(body, out_shape=out_shape, in_specs=[SMEM] * has_meta + [V...  57.1 us
    psum x1, blocking collectives, on_device(): tiny = lax.psum(tiny, ('dp', 'block'))  45 us
    unnamed x174, local copies, waits for them, and re-layouts  36.6 us
    all_gather x2, blocking collectives, on_device(): lax.all_gather(v[2].astype(BF), 'block', axis=1, tiled=True)  29.9 us
    ppermute x16, starting transfers between devices, swap(): return lax.ppermute(x, 'block', [(i, i ^ dist) for i in range(blocks)])  20.5 us
    all_gather x1, blocking collectives, on_device(): small = lax.all_gather(small, 'block', axis=0)  16.7 us
    reduce_scatter x2, waiting for transfers between devices, reduce_weights(): shard = lax.psum_scatter(whole, 'block', scatter_dimension=1, tiled=True)  9.68 us
  transfers between devices with their start and end apart: 21, of which 3 were waited for; matrix products, arithmetic and copies ran while one was open for 4% of the time, Pallas kernels for 12%

commit v1 on v0

--- a/solution.py
+++ b/solution.py
@@ -6,7 +6,7 @@
 from jax import lax
 from jax.experimental import pallas as pl
 from jax.experimental.pallas import tpu as pltpu
-from jax.sharding import PartitionSpec as P
+from jax.sharding import Mesh, PartitionSpec as P
 
 EPSILON = 1e-05
 SEGS = 16
@@ -15,6 +15,7 @@
 F32 = jnp.float32
 GELU_C = 0.7978845608028654
 GELU_A = 0.044715
+COST = 400_000_000
 
 
 class Sizes(NamedTuple):
@@ -28,6 +29,18 @@
     items: int
 
 
+def place_of(sz, table):
+    me, core = lax.axis_index("block"), lax.axis_index("core")
+    q = lax.div(me, 2) * 2 + core
+    mine, chunk = lax.div(q, sz.chunks), lax.rem(q, sz.chunks)
+    out = [me, chunk, core, lax.axis_index("plane"), q]
+    if table is not None:
+        side = lax.rem(me, 2) ^ core
+        for which in range(2):
+            out += [table[side, which, mine, index] for index in range(sz.items)]
+    return out
+
+
 def nt(a, b):
     return lax.dot_general(a, b, (((1,), (1,)), ((), ())), preferred_element_type=F32)
 
@@ -40,6 +53,10 @@
     return lax.dot_general(a, b, (((0,), (0,)), ((), ())), preferred_element_type=F32)
 
 
+def after(*values):
+    return lax.optimization_barrier(values)
+
+
 def cmul(ar, ai, br, bi):
     return ar * br - ai * bi, ar * bi + ai * br
 
@@ -53,8 +70,8 @@
 
 
 def item_of(sz, meta, index):
-    begin = meta[2 + sz.items + index]
-    return begin, begin + meta[2 + index]
+    begin = meta[5 + sz.items + index]
+    return begin, begin + meta[5 + index]
 
 
 def fill_masks(sz, meta, live, ahead, behind):
@@ -373,99 +390,51 @@
     grad_gain[...] = jnp.sum(total, axis=0, keepdims=True)
 
 
+def gain_of(params, layer):
+    return params[layer : layer + 1, :]
+
+
+def skip_of(params, layer):
+    return params[2 + layer : 3 + layer, :]
+
+
+def decay_of(sz, params, layer):
+    return params[4 + 2 * layer : 6 + 2 * layer, 0 : sz.states]
+
+
 def place_pieces(sz, meta, pieces, stacked):
     part = sz.width // sz.blocks
     for dist, piece in enumerate(pieces):
-        owner = meta[0] ^ dist
-        stacked[pl.ds(pl.multiple_of(owner * part, part), part), :] = piece[...]
+        owner = meta[4] ^ dist
+        stacked[pl.ds(pl.multiple_of(owner * part, part), part), :] = piece[0:part, :]
 
 
 def cut_pieces(sz, meta, rows, perm, stacked, pieces):
     part = sz.width // sz.blocks
     matmul_tn(rows, perm, stacked)
     for dist, piece in enumerate(pieces):
-        owner = meta[0] ^ dist
+        owner = meta[4] ^ dist
         piece[...] = stacked[pl.ds(pl.multiple_of(owner * part, part), part), :]
 
 
-def enter_kernel(sz, meta, gain, w_in, decay, perm, *refs):
-    pieces, refs = refs[: sz.blocks], refs[sz.blocks :]
-    hidden, normed, driven, ends, send, stacked, live, ahead, behind, enter = refs
-    place_pieces(sz, meta, pieces, stacked)
-    matmul_nt(perm, stacked, hidden)
-    fill_masks(sz, meta, live, ahead, behind)
-    layer_open(sz, meta, hidden, gain, w_in, decay, live, ahead, behind, normed, driven, ends, enter, send)
-
-
-def middle_kernel(sz, meta, recv, decay, ends, driven, normed, hidden, w_out, skip, gain_b, w_in_b, decay_b,
-                  states, slope, hidden_b, normed_b, driven_b, ends_b, send_b, live, ahead, behind, enter, mixed):
-    fill_masks(sz, meta, live, ahead, behind)
-    layer_close(sz, meta, recv, decay, ends, driven, normed, hidden, w_out, skip, live, ahead, behind, enter, mixed, states, slope, hidden_b)
-    layer_open(sz, meta, hidden_b, gain_b, w_in_b, decay_b, live, ahead, behind, normed_b, driven_b, ends_b, enter, send_b)
-
-
-def leave_kernel(sz, meta, recv, decay, ends, driven, normed, hidden, w_out, skip, perm, states, slope, *refs):
-    pieces, refs = refs[: sz.blocks], refs[sz.blocks :]
-    live, ahead, behind, enter, mixed, last, stacked = refs
-    fill_masks(sz, meta, live, ahead, behind)
-    layer_close(sz, meta, recv, decay, ends, driven, normed, hidden, w_out, skip, live, ahead, behind, enter, mixed, states, slope, last)
-    cut_pieces(sz, meta, last, perm, stacked, pieces)
-
-
-def turn_kernel(sz, meta, slope, normed, w_out, decay, perm, *refs):
-    pieces, refs = refs[: sz.blocks], refs[sz.blocks :]
-    upstream, twice, grad_states, grad_skip, ends, send, stacked, ahead, behind, enter = refs
-    place_pieces(sz, meta, pieces, stacked)
-    matmul_nt(perm, stacked, upstream)
-    fill_masks(sz, meta, None, ahead, behind)
-    back_open(sz, meta, upstream, slope, normed, w_out, decay, ahead, behind, twice, grad_states, grad_skip, ends, enter, send)
-
-
-def back_middle_kernel(sz, meta, recv, decay, ends, grad_states, states, upstream, slope, skip, hidden, gain, w_in,
-                       slope_b, normed_b, w_out_b, decay_b,
-                       grad_driven, grad_decay, grad_gain, upstream_b, twice_b, grad_states_b, grad_skip_b, ends_b, send_b,
-                       ahead, behind, enter, half, grad_normed):
-    fill_masks(sz, meta, None, ahead, behind)
-    back_close(sz, meta, recv, decay, ends, grad_states, states, upstream, slope, skip, hidden, gain, w_in, ahead, behind,
-               enter, half, grad_normed, grad_driven, grad_decay, grad_gain, upstream_b)
-    back_open(sz, meta, upstream_b, slope_b, normed_b, w_out_b, decay_b, ahead, behind, twice_b, grad_states_b, grad_skip_b, ends_b, enter, send_b)
-
-
-def back_leave_kernel(sz, meta, recv, decay, ends, grad_states, states, upstream, slope, skip, hidden, gain, w_in, perm,
-                      grad_driven, grad_decay, grad_gain, *refs):
-    pieces, refs = refs[: sz.blocks], refs[sz.blocks :]
-    ahead, behind, enter, half, grad_normed, last, stacked = refs
-    fill_masks(sz, meta, None, ahead, behind)
-    back_close(sz, meta, recv, decay, ends, grad_states, states, upstream, slope, skip, hidden, gain, w_in, ahead, behind,
-               enter, half, grad_normed, grad_driven, grad_decay, grad_gain, last)
-    cut_pieces(sz, meta, last, perm, stacked, pieces)
-
-
-def weight_kernel(left, right, out):
-    matmul_tn(left, right, out)
-
-
-VMEM = pl.BlockSpec(memory_space=pltpu.VMEM)
-SMEM = pl.BlockSpec(memory_space=pltpu.SMEM)
-
-
-def call(name, body, meta, args, outs, scratch, flops, limit=20):
-    has_meta = meta is not None
-    out_shape = [jax.ShapeDtypeStruct(shape, dtype) for shape, dtype in outs]
-    moved = sum(a.size * a.dtype.itemsize for a in args) + sum(o.size * o.dtype.itemsize for o in out_shape)
-    return pl.pallas_call(
-        body,
-        out_shape=out_shape,
-        in_specs=[SMEM] * has_meta + [VMEM] * len(args),
-        out_specs=[VMEM] * len(outs),
-        scratch_shapes=[pltpu.VMEM(shape, dtype) for shape, dtype in scratch],
-        compiler_params=pltpu.CompilerParams(vmem_limit_bytes=limit << 20),
-        cost_estimate=pl.CostEstimate(flops=flops, bytes_accessed=moved, transcendentals=0),
-        name=name,
-    )(*([meta] if has_meta else []), *args)
-
-
-def discretize(lambda_log, lambda_imag, log_step, input_map):
+def cut_kernel(sz, meta, whole, *refs):
+    outs, wide, sems = refs[: sz.blocks], refs[-2], refs[-1]
+    straight = whole.dtype == BF
+    copies = []
+    for dist in range(sz.blocks):
+        to = meta[0] ^ dist
+        cols = pl.ds(pl.multiple_of(lax.rem(to, sz.chunks) * sz.toks, LANES), sz.toks)
+        source = whole.at[lax.div(to, sz.chunks), :, cols]
+        copy = pltpu.make_async_copy(source, outs[dist] if straight else wide.at[dist], sems.at[dist])
+        copy.start()
+        copies.append(copy)
+    for dist, copy in enumerate(copies):
+        copy.wait()
+        if not straight:
+            outs[dist][...] = wide[dist].astype(BF)
+
+
+def discretize(lambda_log, lambda_imag, log_step):
     step_size = jnp.exp(log_step)
     lambda_real = -jnp.exp(lambda_log)
     modulus = jnp.exp(lambda_real * step_size)
@@ -474,74 +443,464 @@
     denominator = lambda_real * lambda_real + lambda_imag * lambda_imag
     scale_real = ((decay_real - 1.0) * lambda_real + decay_imag * lambda_imag) / denominator
     scale_imag = (decay_imag * lambda_real - (decay_real - 1.0) * lambda_imag) / denominator
-    scale_real, scale_imag = scale_real[:, None], scale_imag[:, None]
-    drive_real = scale_real * input_map[0] - scale_imag * input_map[1]
-    drive_imag = scale_real * input_map[1] + scale_imag * input_map[0]
-    return decay_real, decay_imag, jnp.stack([drive_real, drive_imag])
+    return decay_real, decay_imag, scale_real, scale_imag
+
+
+def first_rows(sz):
+    part, own = sz.width // sz.blocks, sz.states // sz.blocks
+    return part, part + own * sz.width // sz.toks
+
+
+def half_map_parts(sz):
+    top, end = first_rows(sz)
+    rows = end - top
+    for index in range(sz.toks // sz.width):
+        yield slice(index * rows, (index + 1) * rows), slice(top, end), slice(index * sz.width, (index + 1) * sz.width)
+
+
+def split3(x):
+    hi = x.astype(BF).astype(F32)
+    mid = (x - hi).astype(BF).astype(F32)
+    return hi, mid, x - hi - mid
+
+
+def prepare_kernel(sz, meta, tokens, *refs):
+    inputs, refs = refs[:7], refs[7:]
+    outs, refs = refs[: sz.blocks], refs[sz.blocks :]
+    drive_b, half_b, half_c = refs[:3]
+    held, small, lines, drive_a, sems = refs[3:10], refs[10], refs[11], refs[12], refs[13]
+    top, end = first_rows(sz)
+    own, part = sz.states // sz.blocks, sz.width // sz.blocks
+    loads, copies = [], []
+    for index, (source, target) in enumerate(zip(inputs, held)):
+        loads.append(pltpu.make_async_copy(source, target, sems.at[index]))
+    for dist in range(sz.blocks):
+        to = meta[0] ^ dist
+        cols = pl.ds(pl.multiple_of(lax.rem(to, sz.chunks) * sz.toks, LANES), sz.toks)
+        source = tokens.at[lax.div(to, sz.chunks), :, cols]
+        copies.append(pltpu.make_async_copy(source, outs[dist].at[0:top, :], sems.at[len(inputs) + dist]))
+    for copy in copies + loads:
+        copy.start()
+    for copy in loads[:6]:
+        copy.wait()
+    gain, skip, lambda_log, lambda_imag, log_step, input_map, output_map = held
+    dr, di, sr, si = discretize(lambda_log[...], lambda_imag[...], log_step[...])
+    small[...] = jnp.zeros_like(small)
+    lines[...] = jnp.zeros_like(lines)
+    small[0:2, 0:part] = gain[...]
+    small[2:4, 0:part] = skip[...]
+    for layer in range(2):
+        small[4 + 2 * layer : 5 + 2 * layer, 0:own] = dr[layer : layer + 1]
+        small[5 + 2 * layer : 6 + 2 * layer, 0:own] = di[layer : layer + 1]
+    lines[0:2, 0:own] = sr
+    lines[2:4, 0:own] = si
+    cols = lines[...].T
+    for layer in range(2):
+        qr, qi = cols[0:own, layer : layer + 1], cols[0:own, 2 + layer : 3 + layer]
+        br, bi = input_map[layer, 0].astype(F32), input_map[layer, 1].astype(F32)
+        for index, value in enumerate((qr * br - qi * bi, qr * bi + qi * br)):
+            (drive_a, drive_b)[layer][index] = value.astype(BF)
+    rows = jnp.concatenate([*split3(small[...]), jnp.zeros((8, sz.toks - 3 * LANES), F32)], axis=1)
+    rows = jnp.concatenate([rows, jnp.zeros((8, sz.toks), F32)], axis=0).astype(BF)
+    for dist, out in enumerate(outs):
+        half = lax.rem(meta[0] ^ dist, 2)
+        for from_rows, to_rows, lanes in half_map_parts(sz):
+            out[to_rows, lanes] = drive_a[half, from_rows, :]
+        out[end:, :] = rows
+    loads[6].wait()
+    core = meta[2]
+    for index in range(2):
+        half_b[index] = output_map[0, 2 * core + index]
+        half_c[index] = output_map[1, 2 * core + index]
+    half_b[2] = drive_b[core]
+    for copy in copies:
+        copy.wait()
+
+
+def params_of(sz, piece):
+    rows = piece[piece.shape[0] - 16 :, 0 : 3 * LANES].astype(F32)[0:8]
+    return rows[:, 0:LANES] + rows[:, LANES : 2 * LANES] + rows[:, 2 * LANES :]
+
+
+def join_kernel(sz, meta, *refs):
+    pieces, maps, params = refs[: sz.blocks], refs[-2], refs[-1]
+    own = sz.states // sz.blocks
+    collect_params(sz, meta, [params_of(sz, piece) for piece in pieces], params)
+    for dist, piece in enumerate(pieces):
+        base = (meta[4] ^ dist) * own
+        for to_rows, from_rows, lanes in half_map_parts(sz):
+            rows = pl.ds(pl.multiple_of(base + to_rows.start, 16), to_rows.stop - to_rows.start)
+            maps[rows, :] = piece[from_rows, lanes]
+
+
+def collect_params(sz, meta, smalls, params):
+    own = sz.states // sz.blocks
+    part = sz.width // sz.blocks
+    lane = lax.broadcasted_iota(jnp.int32, (8, LANES), 1)
+    row = lax.broadcasted_iota(jnp.int32, (8, LANES), 0)
+    pad = jnp.zeros((8, sz.width - LANES), F32)
+    total = jnp.zeros((8, sz.width), F32)
+    for block in range(sz.blocks):
+        piece = smalls[0]
+        for dist in range(1, sz.blocks):
+            piece = jnp.where((meta[4] ^ dist) == block, smalls[dist], piece)
+        for first, count, size in ((0, 4, part), (4, 4, own)):
+            mine = jnp.where((row >= first) & (row < first + count) & (lane < size), piece, 0.0)
+            wide = jnp.concatenate([mine, pad], axis=1)
+            total += pltpu.roll(wide, block * size, 1) if block else wide
+    params[...] = total
+
+
+def place_maps(sz, meta, own_maps, mine, other, skip, out):
+    own = sz.states // sz.blocks
+    count = own_maps.shape[0] // 2
+
+    def put(index, owner, value):
+        out[pl.ds(pl.multiple_of(index * sz.states + owner * own, own), own), :] = value
+
+    for index in range(2 * count):
+        put(index, meta[0], own_maps[index])
+    for side, pieces in ((meta[2], mine), (1 - meta[2], other)):
+        for dist, piece in enumerate(pieces):
+            for index in range(count):
+                put(side * count + index, meta[0] ^ (dist + 1), piece[skip + index])
+
+
+def enter_kernel(sz, meta, perm, params, maps, other, *refs):
+    pieces, refs = refs[: sz.blocks], refs[sz.blocks :]
+    w_in, hidden, normed, driven, ends, send, stacked, live, ahead, behind, enter = refs
+    gain, decay = gain_of(params, 0), decay_of(sz, params, 0)
+    place_pieces(sz, meta, pieces, stacked)
+    matmul_nt(perm, stacked, hidden)
+    for side, half in ((meta[2], maps), (1 - meta[2], other)):
+        w_in[pl.ds(pl.multiple_of(side * sz.states, sz.states), sz.states), :] = half[...]
+    fill_masks(sz, meta, live, ahead, behind)
+    layer_open(sz, meta, hidden, gain, w_in, decay, live, ahead, behind, normed, driven, ends, enter, send)
+
+
+def middle_kernel(sz, meta, recv, params, ends, driven, normed, hidden, own_out, own_in, *refs):
+    decay, skip, gain_b, decay_b = decay_of(sz, params, 0), skip_of(params, 0), gain_of(params, 1), decay_of(sz, params, 1)
+    far = sz.blocks - 1
+    mine, other, refs = refs[:far], refs[far : 2 * far], refs[2 * far :]
+    w_out, w_in_b, states, slope, hidden_b, normed_b, driven_b, ends_b, send_b, live, ahead, behind, enter, mixed = refs
+    place_maps(sz, meta, own_out, mine, other, 0, w_out)
+    place_maps(sz, meta, own_in, mine, other, 2, w_in_b)
+    fill_masks(sz, meta, live, ahead, behind)
+    layer_close(sz, meta, recv, decay, ends, driven, normed, hidden, w_out, skip, live, ahead, behind, enter, mixed, states, slope, hidden_b)
+    layer_open(sz, meta, hidden_b, gain_b, w_in_b, decay_b, live, ahead, behind, normed_b, driven_b, ends_b, enter, send_b)
+
+
+def leave_kernel(sz, meta, recv, params, ends, driven, normed, hidden, perm, own_out, *refs):
+    decay, skip = decay_of(sz, params, 1), skip_of(params, 1)
+    far = sz.blocks - 1
+    mine, other, refs = refs[:far], refs[far : 2 * far], refs[2 * far :]
+    w_out, states, slope, refs = *refs[:3], refs[3:]
+    place_maps(sz, meta, own_out, mine, other, 0, w_out)
+    pieces, refs = refs[: sz.blocks], refs[sz.blocks :]
+    live, ahead, behind, enter, mixed, last, stacked = refs
+    fill_masks(sz, meta, live, ahead, behind)
+    layer_close(sz, meta, recv, decay, ends, driven, normed, hidden, w_out, skip, live, ahead, behind, enter, mixed, states, slope, last)
+    cut_pieces(sz, meta, last, perm, stacked, pieces)
+
+
+def turn_kernel(sz, meta, slope, normed, w_out, params, perm, *refs):
+    decay = decay_of(sz, params, 1)
+    pieces, refs = refs[: sz.blocks], refs[sz.blocks :]
+    upstream, twice, grad_states, grad_skip, ends, send, stacked, ahead, behind, enter = refs
+    place_pieces(sz, meta, pieces, stacked)
+    matmul_nt(perm, stacked, upstream)
+    fill_masks(sz, meta, None, ahead, behind)
+    back_open(sz, meta, upstream, slope, normed, w_out, decay, ahead, behind, twice, grad_states, grad_skip, ends, enter, send)
+
+
+def back_middle_kernel(sz, meta, recv, params, ends, grad_states, states, upstream, slope, hidden, w_in,
+                       slope_b, normed_b, w_out_b,
+                       grad_driven, grad_decay, grad_gain, upstream_b, twice_b, grad_states_b, grad_skip_b, ends_b, send_b,
+                       ahead, behind, enter, half, grad_normed):
+    decay, skip, gain, decay_b = decay_of(sz, params, 1), skip_of(params, 1), gain_of(params, 1), decay_of(sz, params, 0)
+    fill_masks(sz, meta, None, ahead, behind)
+    back_close(sz, meta, recv, decay, ends, grad_states, states, upstream, slope, skip, hidden, gain, w_in, ahead, behind,
+               enter, half, grad_normed, grad_driven, grad_decay, grad_gain, upstream_b)
+    back_open(sz, meta, upstream_b, slope_b, normed_b, w_out_b, decay_b, ahead, behind, twice_b, grad_states_b, grad_skip_b, ends_b, enter, send_b)
+
+
+def back_leave_kernel(sz, meta, recv, params, ends, grad_states, states, upstream, slope, hidden, w_in, perm,
+                      gain_b, skip_a, skip_b, decay_b, *refs):
+    done, refs = refs[: sz.blocks], refs[sz.blocks :]
+    grad_driven, tiny, refs = refs[0], refs[1], refs[2:]
+    decay, skip, gain = decay_of(sz, params, 0), skip_of(params, 0), gain_of(params, 0)
+    pieces, refs = refs[: sz.blocks], refs[sz.blocks :]
+    ahead, behind, enter, half, grad_normed, last, stacked, grad_decay, grad_gain = refs
+    fill_masks(sz, meta, None, ahead, behind)
+    back_close(sz, meta, recv, decay, ends, grad_states, states, upstream, slope, skip, hidden, gain, w_in, ahead, behind,
+               enter, half, grad_normed, grad_driven, grad_decay, grad_gain, last)
+    tiny[...] = jnp.zeros_like(tiny)
+    for row, line in enumerate((grad_gain, gain_b, skip_a, skip_b)):
+        tiny[row : row + 1, :] = line[...]
+    tiny[4:6, 0 : sz.states] = grad_decay[...]
+    tiny[6:8, 0 : sz.states] = decay_b[...]
+    part = sz.width // sz.blocks
+    for piece, first in zip(pieces, done):
+        piece[0:part, :] = first[...]
+    cut_pieces(sz, meta, last, perm, stacked, [piece.at[part : 2 * part, :] for piece in pieces])
+
+
+def weight_kernel(counts, sz, meta, *refs):
+    for half, out in ((1 - meta[2], refs[-2]), (meta[2], refs[-1])):
+        at = 0
+        for index, count in enumerate(counts):
+            left, right = refs[2 * index], refs[2 * index + 1]
+            for group in range(count):
+                cols = pl.ds(pl.multiple_of((half * count + group) * sz.states, LANES), sz.states)
+                out[at : at + sz.states, :] = tn(left[:, cols], right[...]).astype(out.dtype)
+                at += sz.states
+
+
+def fold_core_kernel(count, sz, meta, keep, got, *pieces):
+    own = sz.states // sz.blocks
+    part = sz.width // sz.blocks
+    tiny = None
+    if len(pieces) > sz.blocks:
+        tiny, pieces = pieces[0][...] + pieces[1][...], pieces[2:]
+        row = lax.broadcasted_iota(jnp.int32, (8, LANES), 0)
+        lane = lax.broadcasted_iota(jnp.int32, (8, LANES), 1)
+    for dist, piece in enumerate(pieces):
+        owner = meta[0] ^ dist
+        for group in range(count):
+            rows = pl.ds(pl.multiple_of(group * sz.states + owner * own, own), own)
+            piece[group * own : (group + 1) * own, :] = (keep[rows, :].astype(F32) + got[rows, :].astype(F32)).astype(BF)
+        if tiny is not None:
+            value = jnp.zeros((8, LANES), F32)
+            for block in range(sz.blocks):
+                wide = pltpu.roll(tiny, sz.width - block * part, 1) if block else tiny
+                deep = pltpu.roll(tiny, sz.width - block * own, 1) if block else tiny
+                mine = jnp.where(row < 4, jnp.where(lane < part, wide[:, :LANES], 0.0), jnp.where(lane < own, deep[:, :LANES], 0.0))
+                value = jnp.where(owner == block, mine, value)
+            hi, lo = split2(value)
+            rest = jnp.zeros((8, sz.width - 2 * LANES), F32)
+            wide = jnp.concatenate([jnp.concatenate([hi, lo, rest], axis=1), jnp.zeros((8, sz.width), F32)], axis=0)
+            piece[count * own : count * own + 16, :] = wide.astype(BF)
+
+
+def split2(x):
+    hi = x.astype(BF).astype(F32)
+    return hi, x - hi
+
+
+def fold_block_kernel(planes, counts, with_tiny, sz, meta, *refs):
+    lanes = sz.width // LANES
+    groups = len(counts)
+    got, refs = refs[: groups * sz.blocks], refs[groups * sz.blocks :]
+    outs, talls = refs[:planes], refs[planes:]
+    at = 0
+    for index, rows in enumerate(counts):
+        pieces = got[index * sz.blocks : (index + 1) * sz.blocks]
+        total = pieces[0][...].astype(F32)
+        for piece in pieces[1:]:
+            total += piece[...].astype(F32)
+        tall = talls[index]
+        padded = tall.shape[0] // lanes
+        for block in range(lanes):
+            tall[block * padded : block * padded + rows, :] = total[0:rows, block * LANES : (block + 1) * LANES].astype(BF)
+            if padded > rows:
+                tall[block * padded + rows : (block + 1) * padded, :] = jnp.zeros((padded - rows, LANES), BF)
+        part = tall.shape[0] // planes
+        for dist, out in enumerate(outs):
+            out[at : at + part, :] = tall[pl.ds(pl.multiple_of((meta[3] ^ dist) * part, part), part), :]
+        at += part
+    if with_tiny:
+        value = total[counts[-1] : counts[-1] + 8, 0:LANES] + total[counts[-1] : counts[-1] + 8, LANES : 2 * LANES]
+        rows = jnp.concatenate(split2(value), axis=0).astype(BF)
+        for out in outs:
+            out[at : at + 16, :] = rows
+
+
+def fold_plane_kernel(sz, meta, *refs):
+    total = refs[0][...].astype(F32)
+    for piece in refs[1:-1]:
+        total += piece[...].astype(F32)
+    refs[-1][...] = total.astype(BF)
+
+
+def join_plane_kernel(sz, meta, first, *refs):
+    parts, out, tiny = refs[:-2], refs[-2], refs[-1]
+    total = parts[0][...].astype(F32)
+    for piece in parts[1:]:
+        total += piece[...].astype(F32)
+    rows = total.shape[0] - 16
+    out[0 : first.shape[0], :] = first[...]
+    out[first.shape[0] :, :] = total[0:rows].astype(BF)
+    tiny[...] = total[rows : rows + 8] + total[rows + 8 :]
+
+
+def finish_kernel(planes, groups, sz, meta, *refs):
+    count = 2 * planes
+    pieces, refs = refs[:count], refs[count:]
+    tiny, lambda_log, lambda_imag, log_step, input_map = refs[:5]
+    grad_gain, grad_skip, grad_log, grad_imag, grad_step, grad_maps, grad_out = refs[5:12]
+    talls, grad_in, lines = refs[12:-2], refs[-2], refs[-1]
+    own = sz.states // sz.blocks
+    lanes = sz.width // LANES
+    start = 0
+    for tall, group in zip(talls, groups):
+        padded = tall.shape[0] // lanes
+        part = tall.shape[0] // planes
+        for side in range(2):
+            half = meta[2] ^ side
+            for dist in range(planes):
+                rows = pl.ds(pl.multiple_of((meta[3] ^ dist) * part, part), part)
+                tall[rows, :] = pieces[side * planes + dist][start : start + part, :]
+            at = 0
+            for which, layer, maps in group:
+                out = grad_in if which == 0 else grad_out
+                for one in range(maps):
+                    for block in range(lanes):
+                        rows = slice(block * padded + at, block * padded + at + own)
+                        out[layer, half * maps + one, :, block * LANES : (block + 1) * LANES] = tall[rows, :].astype(F32)
+                    at += own
+        start += part
+    width = sz.width // sz.blocks
+    grad_gain[...] = tiny[0:2, 0:width]
+    grad_skip[...] = tiny[2:4, 0:width]
+    dr, di, sr, si = discretize(lambda_log[...], lambda_imag[...], log_step[...])
+    lines[...] = jnp.zeros_like(lines)
+    lines[0:2, 0:own] = sr
+    lines[2:4, 0:own] = si
+    cols = lines[...].T
+    back = []
+    for layer in range(2):
+        qr, qi = cols[0:own, layer : layer + 1], cols[0:own, 2 + layer : 3 + layer]
+        wr, wi = grad_in[layer, 0], grad_in[layer, 1]
+        br, bi = input_map[layer, 0].astype(F32), input_map[layer, 1].astype(F32)
+        grad_maps[layer, 0] = qr * wr + qi * wi
+        grad_maps[layer, 1] = qr * wi - qi * wr
+        back.append(jnp.sum(wr * br + wi * bi, axis=1, keepdims=True))
+        back.append(jnp.sum(wi * br - wr * bi, axis=1, keepdims=True))
+    lines[...] = jnp.zeros_like(lines)
+    for index, col in enumerate(back):
+        lines[0:own, index : index + 1] = col
+    rows = lines[...].T
+    step = jnp.exp(log_step[...])
+    lr, li = -jnp.exp(lambda_log[...]), lambda_imag[...]
+    norm = 1.0 / (lr * lr + li * li)
+    for layer in range(2):
+        at = slice(layer, layer + 1)
+        a, b, h = (lr[at], li[at]), (dr[at], di[at]), step[at]
+        gq = rows[2 * layer : 2 * layer + 1, 0:own], rows[2 * layer + 1 : 2 * layer + 2, 0:own]
+        gd = tiny[4 + 2 * layer : 5 + 2 * layer, 0:own], tiny[5 + 2 * layer : 6 + 2 * layer, 0:own]
+        inverse = a[0] * norm[at], -a[1] * norm[at]
+        through = cmul(inverse[0], -inverse[1], *gq)
+        gd = gd[0] + through[0], gd[1] + through[1]
+        ratio = cmul(*inverse, sr[at], si[at])
+        direct = cmul(ratio[0], -ratio[1], *gq)
+        moved = cmul(b[0] * h, -b[1] * h, *gd)
+        turn = cmul(*a, *b)
+        grad_log[at, :] = (moved[0] - direct[0]) * a[0]
+        grad_imag[at, :] = moved[1] - direct[1]
+        grad_step[at, :] = (turn[0] * gd[0] + turn[1] * gd[1]) * h
+
+
+def spread_kernel(sz, meta, *refs):
+    pieces, outs, wide, sems = refs[: sz.blocks], refs[sz.blocks : -2], refs[-2], refs[-1]
+    part = sz.width // sz.blocks
+    copies = []
+    for dist, piece in enumerate(pieces):
+        owner = meta[0] ^ dist
+        for index, out in enumerate(outs):
+            slot = dist * len(outs) + index
+            wide[slot] = piece[index * part : (index + 1) * part, :].astype(F32)
+            cols = pl.ds(pl.multiple_of(lax.rem(owner, sz.chunks) * sz.toks, LANES), sz.toks)
+            copy = pltpu.make_async_copy(wide.at[slot], out.at[lax.div(owner, sz.chunks), :, cols], sems.at[slot])
+            copy.start()
+            copies.append(copy)
+    for copy in copies:
+        copy.wait()
+
+
+VMEM = pl.BlockSpec(memory_space=pltpu.VMEM)
+SMEM = pl.BlockSpec(memory_space=pltpu.SMEM)
+HBM = pl.BlockSpec(memory_space=pltpu.HBM)
+
+
+def call(name, sz, body, items, args, outs, scratch, limit=10, in_spec=VMEM, out_spec=VMEM, time=0.0):
+    out_shape = [jax.ShapeDtypeStruct(shape, dtype) for shape, dtype in outs]
+
+    def kernel(*refs):
+        body(sz, place_of(sz, refs[0] if items else None), *refs[len(items) :])
+
+    return pl.pallas_call(
+        kernel,
+        out_shape=out_shape,
+        in_specs=[SMEM] * len(items) + [in_spec] * len(args),
+        out_specs=[out_spec] * len(outs),
+        scratch_shapes=[pltpu.VMEM(*item) if isinstance(item, tuple) else item for item in scratch],
+        compiler_params=pltpu.CompilerParams(vmem_limit_bytes=limit << 20),
+        cost_estimate=pl.CostEstimate(flops=int(COST * time), bytes_accessed=1000, transcendentals=0),
+        name=name,
+    )(*items, *args)
 
 
 def on_device(tokens, cotangent, item_lengths, item_offsets, norm_gain, lambda_log, lambda_imag, log_step, input_map, output_map, skip_weight):
     micro, part, run = tokens.shape
     layers = norm_gain.shape[0]
     blocks = lax.axis_size("block")
+    planes = lax.axis_size("plane")
     chunks = blocks // micro
     toks = run // chunks
     own = lambda_log.shape[1]
     width, states = part * blocks, own * blocks
     sz = Sizes(blocks, chunks, toks, run, toks // SEGS, width, states, item_lengths.shape[1])
-    me = lax.axis_index("block")
-    mine, chunk = me // chunks, me % chunks
-
-    def swap(x, dist):
-        return lax.ppermute(x, "block", [(i, i ^ dist) for i in range(blocks)])
-
-    def to_chunks(x):
-        out = []
-        for dist in range(blocks):
-            to = me ^ dist
-            piece = lax.dynamic_slice(x, (to // chunks, 0, (to % chunks) * toks), (1, part, toks))[0].astype(BF)
-            out.append(swap(piece, dist) if dist else piece)
-        return out
-
-    def from_chunks(pieces):
-        out = jnp.zeros((micro, part, run), F32)
-        for dist, piece in enumerate(pieces):
-            got = swap(piece, dist) if dist else piece
-            owner = me ^ dist
-            out = lax.dynamic_update_slice(out, got.astype(F32)[None], (owner // chunks, 0, (owner % chunks) * toks))
-        return out
+
+    def swap(x, dist, axis="block"):
+        return lax.ppermute(x, axis, [(i, i ^ dist) for i in range(lax.axis_size(axis))])
+
+    def across(x, dist, back):
+        pairs = []
+        for c in range(2):
+            for b in range(blocks):
+                q = b ^ dist
+                pairs.append((c * blocks + b, (q % 2) * blocks + (q // 2) * 2 + c))
+        return lax.ppermute(x, ("core", "block"), [pair[::-1] for pair in pairs] if back else pairs)
+
+    def across_all(pieces, back=False):
+        return [across(piece, dist, back) for dist, piece in enumerate(pieces)]
+
+    table = jnp.stack([item_lengths, item_offsets])
+    items = [jnp.stack([table, swap(table, 1, "core")])]
+
+    def neighbour(x, dist):
+        pairs = []
+        for c in range(2):
+            for b in range(blocks):
+                q = ((b // 2) * 2 + c) ^ dist
+                pairs.append((c * blocks + b, (q % 2) * blocks + (q // 2) * 2 + b % 2))
+        return lax.ppermute(x, ("core", "block"), pairs)
+
+    def swap_all(pieces, axis="block"):
+        return [swap(piece, dist, axis) if dist else piece for dist, piece in enumerate(pieces)]
 
     def exchange(send):
-        return jnp.stack([swap(send[dist - 1], dist) for dist in range(1, chunks)])
-
-    meta = jnp.concatenate([
-        jnp.stack([me, chunk]).astype(jnp.int32),
-        lax.dynamic_index_in_dim(item_lengths, mine, 0, keepdims=False),
-        lax.dynamic_index_in_dim(item_offsets, mine, 0, keepdims=False),
-    ])
+        return jnp.stack([neighbour(send[dist - 1], dist) for dist in range(1, chunks)])
+
     row = jnp.arange(toks, dtype=jnp.int32)[:, None]
     col = jnp.arange(toks, dtype=jnp.int32)[None, :]
     perm = ((row % SEGS) * sz.steps + row // SEGS == col).astype(BF)
 
-    token_pieces = to_chunks(tokens)
-    discrete, pulls = [], []
-    for layer in range(layers):
-        values, pull = jax.vjp(discretize, lambda_log[layer], lambda_imag[layer], log_step[layer], input_map[layer].astype(F32))
-        discrete.append(values)
-        pulls.append(pull)
-    small = jnp.concatenate(
-        [norm_gain, skip_weight, jnp.stack([v[0] for v in discrete]), jnp.stack([v[1] for v in discrete])], axis=1
-    )
-    small = lax.all_gather(small, "block", axis=0)
-    joined = lambda lo, n: jnp.swapaxes(small[:, :, lo : lo + n], 0, 1).reshape(layers, blocks * n)
-    gains = joined(0, part)
-    skips = joined(part, part)
-    decays = jnp.stack([joined(2 * part, own), joined(2 * part + own, own)], axis=1)
-    w_in = [lax.all_gather(v[2].astype(BF), "block", axis=1, tiled=True).reshape(2 * states, width) for v in discrete]
-    w_out = [lax.all_gather(output_map[l], "block", axis=1, tiled=True).reshape(4 * states, width) for l in range(layers)]
-    gain = [gains[l : l + 1] for l in range(layers)]
-    skip = [skips[l : l + 1] for l in range(layers)]
-    decay = [decays[l] for l in range(layers)]
+    maps_own = ((2, own, width), BF)
+    half_own = ((3, own, width), BF)
+    given = [norm_gain, skip_weight, lambda_log, lambda_imag, log_step, input_map, output_map]
+    *first_pieces, drive_b, half_b, half_c = call(
+        "prepare", sz, prepare_kernel, [], [pltpu.with_memory_space_constraint(x, pltpu.HBM) for x in [tokens, *given]],
+        [((first_rows(sz)[1] + 16, toks), BF)] * blocks + [maps_own, half_own, maps_own],
+        [(x.shape, x.dtype) for x in given] + [((8, LANES), F32), ((8, LANES), F32), maps_own, pltpu.SemaphoreType.DMA((len(given) + blocks,))],
+        limit=6, in_spec=HBM)
+    first_pieces = across_all(first_pieces)
+    maps_a, params = call("join", sz, join_kernel, [], first_pieces, [((states, width), BF), ((8, width), F32)], [])
+    half_b, params = after(half_b, params)
+    cot_cut = call("cut_cotangent", sz, cut_kernel, [], [pltpu.with_memory_space_constraint(cotangent, pltpu.HBM)],
+                   [((part, toks), BF)] * blocks, [((blocks, part, toks), F32), pltpu.SemaphoreType.DMA((blocks,))], limit=4, in_spec=HBM)
+    params, cot_cut = after(params, cot_cut)
+    second_mine = [swap(half_b, dist) for dist in range(1, blocks)]
 
     mask = ((toks, LANES), F32)
     enter = ((4, SEGS, states), F32)
@@ -551,70 +910,112 @@
     sts = ((toks, 4 * states), BF)
     gst = ((toks, 4 * states), F32)
     snd = ((chunks - 1, 2, states), F32)
+    w_in, w_out = ((2 * states, width), BF), ((4 * states, width), BF)
     line, gdec = ((1, width), F32), ((2, states), F32)
     piece_out = [((part, toks), BF)] * blocks
-    unit = 2 * toks * width * states
-
-    hidden_a, normed_a, driven_a, ends_a, send_a = call(
-        "enter", partial(enter_kernel, sz), meta, [gain[0], w_in[0], decay[0], perm, *token_pieces],
-        [rows_b, rows_b, drv, enter, snd], [stacked, mask, mask, mask, enter], 4 * unit)
-    cot_pieces = to_chunks(cotangent)
+
+    w_in_a, hidden_a, normed_a, driven_a, ends_a, send_a = call(
+        "enter", sz, enter_kernel, items, [perm, params, maps_a, swap(maps_a, 1, "core"), *first_pieces],
+        [w_in, rows_b, rows_b, drv, enter, snd], [stacked, mask, mask, mask, enter], time=7)
     recv = exchange(send_a)
-    states_a, slope_a, hidden_b, normed_b, driven_b, ends_b, send_b = call(
-        "middle", partial(middle_kernel, sz), meta,
-        [recv, decay[0], ends_a, driven_a, normed_a, hidden_a, w_out[0], skip[0], gain[1], w_in[1], decay[1]],
-        [sts, rows_b, rows_f, rows_b, drv, enter, snd], [mask, mask, mask, enter, rows_f], 8 * unit)
+    second_mine, half_c, _ = after(second_mine, half_c, send_a)
+    second_maps = second_mine, [swap(piece, 1, "core") for piece in second_mine]
+    third_mine = [swap(half_c, dist) for dist in range(1, blocks)]
+    w_out_a, w_in_b, states_a, slope_a, hidden_b, normed_b, driven_b, ends_b, send_b = call(
+        "middle", sz, middle_kernel, items,
+        [recv, params, ends_a, driven_a, normed_a, hidden_a, output_map[0], drive_b, *second_maps[0], *second_maps[1]],
+        [w_out, w_in, sts, rows_b, rows_f, rows_b, drv, enter, snd], [mask, mask, mask, enter, rows_f], time=11)
     recv = exchange(send_b)
-    states_b, slope_b, *out_pieces = call(
-        "leave", partial(leave_kernel, sz), meta, [recv, decay[1], ends_b, driven_b, normed_b, hidden_b, w_out[1], skip[1], perm],
-        [sts, rows_b, *piece_out], [mask, mask, mask, enter, rows_f, rows_b, stacked], 7 * unit)
-    output = from_chunks(out_pieces)
+    third_mine, cot_cut, _ = after(third_mine, cot_cut, send_b)
+    cot_pieces = across_all(cot_cut)
+    third_maps = third_mine, [swap(piece, 1, "core") for piece in third_mine]
+    w_out_b, states_b, slope_b, *out_pieces = call(
+        "leave", sz, leave_kernel, items,
+        [recv, params, ends_b, driven_b, normed_b, hidden_b, perm, output_map[1], *third_maps[0], *third_maps[1]],
+        [w_out, sts, rows_b, *piece_out], [mask, mask, mask, enter, rows_f, rows_b, stacked], time=8)
+
+    def half_grads(name, pairs, counts, first=()):
+        args = [x for pair in pairs for x in pair]
+        send, keep = call(name, sz, partial(weight_kernel, counts), [], args, [((sum(counts) * states, width), BF)] * 2, [])
+        send, keep, first = after(send, keep, first)
+        return (keep, swap(send, 1, "core")), first
+
+    def fold_core(name, group):
+        total = group[0].shape[0] // states
+        rows = total * own + (16 if len(group) > 2 else 0)
+        return swap_all(call(name, sz, partial(fold_core_kernel, total), [], group, [((rows, width), BF)] * blocks, []))
+
+    def spread(pieces):
+        return call("spread", sz, spread_kernel, [], pieces, [((micro, part, run), F32)] * 2,
+                    [((2 * blocks, part, toks), F32), pltpu.SemaphoreType.DMA((2 * blocks,))], limit=6, out_spec=HBM)
+
+    lanes = width // LANES
+
+    def tall_of(rows):
+        step = max(SEGS * planes // lanes, SEGS)
+        return ((lanes * (-(-rows // step) * step), LANES), BF)
+
+    def over_planes(name, groups, rows, with_tiny):
+        talls = [tall_of(n) for n in rows]
+        cut = sum(t[0][0] for t in talls) // planes + (16 if with_tiny else 0)
+        parts = call(name, sz, partial(fold_block_kernel, planes, rows, with_tiny), [], [x for g in groups for x in g],
+                     [((cut, LANES), BF)] * planes, talls)
+        return swap_all(parts, "plane")
 
     up_b, twice_b, gstates_b, gskip_b, ends, send = call(
-        "turn", partial(turn_kernel, sz), meta, [slope_b, normed_b, w_out[1], decay[1], perm, *cot_pieces],
-        [rows_f, rows_b, gst, line, enter, snd], [stacked, mask, mask, enter], 7 * unit)
+        "turn", sz, turn_kernel, items, [slope_b, normed_b, w_out_b, params, perm, *cot_pieces],
+        [rows_f, rows_b, gst, line, enter, snd], [stacked, mask, mask, enter], time=6)
     recv = exchange(send)
-    (gout_b,) = call("grad_out_b", weight_kernel, None, [states_b, twice_b], [((4 * states, width), BF)], [], 4 * unit)
+    group_a, _ = half_grads("grads_a", [(states_b, twice_b)], (2,))
+    sums_a = fold_core("fold_a", group_a)
+    recv, sums_a[0] = after(recv, sums_a[0])
     gdriven_b, gdecay_b, ggain_b, up_a, twice_a, gstates_a, gskip_a, ends, send = call(
-        "back_middle", partial(back_middle_kernel, sz), meta,
-        [recv, decay[1], ends, gstates_b, states_b, up_b, slope_b, skip[1], hidden_b, gain[1], w_in[1], slope_a, normed_a, w_out[0], decay[0]],
-        [((toks, 2 * states), BF), gdec, line, rows_f, rows_b, gst, line, enter, snd], [mask, mask, enter, drv, rows_f], 10 * unit)
+        "back_middle", sz, back_middle_kernel, items,
+        [recv, params, ends, gstates_b, states_b, up_b, slope_b, hidden_b, w_in_b, slope_a, normed_a, w_out_a],
+        [((toks, 2 * states), BF), gdec, line, rows_f, rows_b, gst, line, enter, snd], [mask, mask, enter, drv, rows_f], limit=12, time=11)
     recv = exchange(send)
-    (gin_b,) = call("grad_in_b", weight_kernel, None, [gdriven_b, normed_b], [((2 * states, width), BF)], [], 2 * unit)
-    (gout_a,) = call("grad_out_a", weight_kernel, None, [states_a, twice_a], [((4 * states, width), BF)], [], 4 * unit)
-    gdriven_a, gdecay_a, ggain_a, *grad_pieces = call(
-        "back_leave", partial(back_leave_kernel, sz), meta,
-        [recv, decay[0], ends, gstates_a, states_a, up_a, slope_a, skip[0], hidden_a, gain[0], w_in[0], perm],
-        [((toks, 2 * states), BF), gdec, line, *piece_out], [mask, mask, enter, drv, rows_f, rows_b, stacked], 6 * unit)
-    input_grad = from_chunks(grad_pieces)
-    (gin_a,) = call("grad_in_a", weight_kernel, None, [gdriven_a, normed_a], [((2 * states, width), BF)], [], 2 * unit)
-
-    def reduce_weights(gin, gout):
-        whole = jnp.concatenate([gin.reshape(2, states, width), gout.reshape(4, states, width)])
-        shard = lax.psum_scatter(whole, "block", scatter_dimension=1, tiled=True)
-        return lax.psum(shard, "dp").astype(F32)
-
-    big = jnp.stack([reduce_weights(gin_a, gout_a), reduce_weights(gin_b, gout_b)])
-    tiny = jnp.concatenate([
-        jnp.concatenate([ggain_a, ggain_b]), jnp.concatenate([gskip_a, gskip_b]),
-        jnp.stack([gdecay_a, gdecay_b]).reshape(layers, 2 * states)], axis=1)
-    tiny = lax.psum(tiny, ("dp", "block"))
-    cut = lambda lo, n: lax.dynamic_slice_in_dim(tiny, lo + me * n, n, 1)
-    grad_gain, grad_skip = cut(0, part), cut(width, part)
-    gdr, gdi = cut(2 * width, own), cut(2 * width + states, own)
-    pulled = [pulls[l]((gdr[l], gdi[l], big[l, :2])) for l in range(layers)]
-    grad_log, grad_imag, grad_step, grad_in = (jnp.stack([p[i] for p in pulled]) for i in range(4))
-    return output, input_grad, grad_gain, grad_log, grad_imag, grad_step, grad_in, big[:, 2:], grad_skip
+    gdriven_b, sums_a = after(gdriven_b, sums_a)
+    group_b, _ = half_grads("grads_b", [(gdriven_b, normed_b), (states_a, twice_a)], (1, 2))
+    sums_b = fold_core("fold_b", group_b)
+    recv, sums_b[0] = after(recv, sums_b[0])
+    gdriven_a, tiny, *last_pieces = call(
+        "back_leave", sz, back_leave_kernel, items,
+        [recv, params, ends, gstates_a, states_a, up_a, slope_a, hidden_a, w_in_a, perm, ggain_b, gskip_a, gskip_b, gdecay_b, *out_pieces],
+        [((toks, 2 * states), BF), ((8, width), F32)] + [((2 * part, toks), BF)] * blocks,
+        [mask, mask, enter, drv, rows_f, rows_b, stacked, gdec, line], limit=12, time=9)
+    group_c, sums_b = half_grads("grads_c", [(gdriven_a, normed_a)], (1,), sums_b)
+    sums_c = fold_core("fold_c", [*group_c, tiny, swap(tiny, 1, "core")])
+    parts_ab = over_planes("planes_ab", [sums_a, sums_b], (2 * own, 3 * own), False)
+    (sum_ab,) = call("sum_ab", sz, fold_plane_kernel, [], parts_ab, [(parts_ab[0].shape, BF)], [])
+    parts_c = over_planes("planes_c", [sums_c], (own,), True)
+    last_pieces, parts_c[0] = after(last_pieces, parts_c[0])
+    last_pieces = across_all(last_pieces, back=True)
+    rows = parts_ab[0].shape[0] + parts_c[0].shape[0] - 16
+    sum_all, tiny = call("sum_c", sz, join_plane_kernel, [], [sum_ab, *parts_c], [((rows, LANES), BF), ((8, LANES), F32)], [])
+    whole = swap_all([sum_all] * planes, "plane")
+    whole, last_pieces = after(whole, last_pieces)
+    whole += [swap(x, 1, "core") for x in whole]
+    output, input_grad = spread(last_pieces)
+    small_out = ((layers, own), F32)
+    grad_gain, grad_skip, grad_log, grad_imag, grad_step, grad_in, grad_out = call(
+        "finish", sz, partial(finish_kernel, planes, ([(1, 1, 2)], [(0, 1, 1), (1, 0, 2)], [(0, 0, 1)])), [],
+        [*whole, tiny, lambda_log, lambda_imag, log_step, input_map],
+        [((layers, part), F32)] * 2 + [small_out] * 3 + [((layers, 2, own, width), F32), ((layers, 4, own, width), F32)],
+        [tall_of(n * own) for n in (2, 3, 1)] + [((layers, 2, own, width), F32), ((LANES, LANES), F32)])
+    return output, input_grad, grad_gain, grad_log, grad_imag, grad_step, grad_in, grad_out, grad_skip
 
 
 def solution(mesh):
+    rows, blocks = mesh.devices.shape
+    inner = Mesh(mesh.devices.reshape(rows // 2, 2, blocks), ("plane", "core", "block"))
+    dp = ("plane", "core")
     half = P(None, "block")
     maps = P(None, None, "block", None)
-    acts = P(None, "block", "dp")
-    items = P(None, "dp")
+    acts = P(None, "block", dp)
+    items = P(None, dp)
     return jax.shard_map(
         on_device,
-        mesh=mesh,
+        mesh=inner,
         in_specs=(acts, acts, items, items, half, half, half, half, maps, maps, half),
         out_specs=(acts, acts, half, half, half, half, maps, maps, half),
         check_vma=False,

time: 315 us -> 186 us (0.59)
  blocking collectives: 91.6 us -> 0 us
  local copies, waits for them, and re-layouts: 43.5 us -> 0.09 us
  starting transfers between devices: 20.7 us -> 53.5 us
  other arithmetic: 16.6 us -> 0.42 us
  between operations: 15 us -> 1.13 us
  Pallas kernels: 57.1 us -> 66.7 us
  waiting for transfers between devices: 69.6 us -> 64.1 us
    ppermute x16 -> x56, waiting for transfers between devices: 0.49 us -> 64.1 us  [the longest x40 42.1 us: swap(): lax.ppermute(x, axis, [(i, i ^ dist) for i in range(lax.axis_size(axis))])]
    psum x1 -> x0, waiting for transfers between devices: 59.3 us -> none  [reduce_weights(): return lax.psum(shard, 'dp').astype(F32)]
    all_gather x3 -> x0, blocking collectives: 46.6 us -> none  [the longest x2 29.9 us: on_device(): lax.all_gather(v[2].astype(BF), 'block', axis=1, tiled=True)]
    psum x1 -> x0, blocking collectives: 45 us -> none  [on_device(): tiny = lax.psum(tiny, ('dp', 'block'))]
    unnamed x174 -> x14, local copies, waits for them, and re-layouts: 36.6 us -> 0.04 us
    ppermute x16 -> x56, starting transfers between devices: 20.5 us -> 53.5 us  [the longest x40 35.7 us: swap(): lax.ppermute(x, axis, [(i, i ^ dist) for i in range(lax.axis_size(axis))])]
    reduce_scatter x2 -> x0, waiting for transfers between devices: 9.68 us -> none  [reduce_weights(): shard = lax.psum_scatter(whole, 'block', scatter_dimension=1, tiled=True)]
    pallas_call x10 -> x21, Pallas kernels: 57.1 us -> 66.7 us  [call(): pl.pallas_call(kernel, out_shape=out_shape, in_specs=[SMEM] * len(items)...]
  transfers between devices with their start and end apart: 21 -> 56, of which waited for: 3 -> 18; matrix products, arithmetic and copies ran while one was open for 4% -> 0% of each run, Pallas kernels for 12% -> 28%
where the time goes in v1:
time: 186 us
  Pallas kernels  66.7 us (36%)
  waiting for transfers between devices  64.1 us (34%)
  starting transfers between devices  53.5 us (29%)
    pallas_call x21, Pallas kernels, call(): pl.pallas_call(kernel, out_shape=out_shape, in_specs=[SMEM] * len(items)...  66.7 us
    ppermute x40, waiting for transfers between devices, swap(): lax.ppermute(x, axis, [(i, i ^ dist) for i in range(lax.axis_size(axis))])  42.1 us
    ppermute x40, starting transfers between devices, swap(): lax.ppermute(x, axis, [(i, i ^ dist) for i in range(lax.axis_size(axis))])  35.7 us
    ppermute x12, waiting for transfers between devices, across(): lax.ppermute(x, ('core', 'block'), [pair[::-1] for pair in pairs] if back...  21.4 us
    ppermute x12, starting transfers between devices, across(): lax.ppermute(x, ('core', 'block'), [pair[::-1] for pair in pairs] if back...  16.3 us
  transfers between devices with their start and end apart: 56, of which 18 were waited for; matrix products, arithmetic and copies ran while one was open for 0% of the time, Pallas kernels for 28%

profile of v1, /device:TPU:0, one launch (start us, length us, event | category | flops | bytes accessed | tf_op | source)
XLA Modules:
  0.0 185.9 jit_solution(2957473922634970494)
XLA Ops:
  0.7 1.9 %prepare.1 = (bf16[192,1024]{1,0:T(8,128)(2,1)S(1)}, bf16[192,1024]{1,0:T(8,128)(2,1)S(1)}, bf16[192,1024]{1,0:T(8,128)(2,1)S(1)}, bf16[192,1024]{1,0:T(8,128)(2...) custom-call(bf16[2,128,2048]{2,1,0:T(8,128)(2,1)} %refs_0_.2, ...), custom_call_target="tpu_custom_call" | custom-call | bytes 1000 | tf_op jit(solution)/shard_map/prepare/pallas_call | solution.py:831
  3.2 4.3 %collective-permute-start.2 = (bf16[192,1024]{1,0:T(8,128)(2,1)S(1)}, bf16[192,1024]{1,0:T(8,128)(2,1)S(1)}, u32[]{:S(2)}, u32[]{:S(2)}) collective-permute-start(bf16[192,1024]{1,0:T(8,128)(2,1)S(1)} %get-tuple-element.150), channel_id=1, source_target_pairs={{0,4},{1,0},{2,6},{3,2},{4,5},{5,1},{6,7},{7,3},{8,12},{9,8},{10,1... | collective-permute-start | bytes 1179656 | tf_op jit(solution)/shard_map/ppermute | solution.py:863
  9.2 8.2 %collective-permute-done.2.refs_1_.refs_6_ = bf16[192,1024]{1,0:T(8,128)(2,1)S(1)} collective-permute-done((bf16[192,1024]{1,0:T(8,128)(2,1)S(1)}, bf16[192,1024]{1,0:T(8,128)(2,1)S(1)}, u32[]{:S(2)}, u32[]{:S(2)}) %collective-permute-start.2) | collective-permute-done | bytes 393248 | tf_op jit(solution)/shard_map/ppermute | solution.py:863
  17.4 9.6 %collective-permute-done.4.refs_3_.refs_8_ = bf16[192,1024]{1,0:T(8,128)(2,1)S(1)} collective-permute-done((bf16[192,1024]{1,0:T(8,128)(2,1)S(1)}, bf16[192,1024]{1,0:T(8,128)(2,1)S(1)}, u32[]{:S(2)}, u32[]{:S(2)}) %collective-permute-start.4) | collective-permute-done | bytes 393248 | tf_op jit(solution)/shard_map/ppermute | solution.py:863
  31.6 1.8 collective-permute-start.7
  33.5 7.1 %enter.1 = (bf16[768,512]{1,0:T(8,128)(2,1)S(1)}, bf16[1024,512]{1,0:T(8,128)(2,1)S(1)}, bf16[1024,512]{1,0:T(8,128)(2,1)S(1)}, f32[1024,768]{1,0:T(8,128)S(1)},...) custom-call(s32[2,2,2,2]{3,2,1,0:T(2,128)S(1)} %pad_add_fusion.refs_0_, ...), custom_call_target="tpu_custom_call" | custom-call | flops 2800000000 | bytes 1000 | tf_op jit(solution)/shard_map/enter/pallas_call | solution.py:831
  40.8 5.2 %collective-permute-done.8.refs_10_ = bf16[3,96,512]{2,1,0:T(8,128)(2,1)S(1)} collective-permute-done((bf16[3,96,512]{2,1,0:T(8,128)(2,1)S(1)}, bf16[3,96,512]{2,1,0:T(8,128)(2,1)S(1)}, u32[]{:S(2)}, u32[]{:S(2)}) %collective-permute-start.8) | collective-permute-done | bytes 294944 | tf_op jit(solution)/shard_map/ppermute | solution.py:855
  50.9 11.4 %middle.1 = (bf16[1536,512]{1,0:T(8,128)(2,1)S(1)}, bf16[768,512]{1,0:T(8,128)(2,1)S(1)}, bf16[1024,1536]{1,0:T(8,128)(2,1)S(1)}, bf16[1024,512]{1,0:T(8,128)(2,...) custom-call(s32[2,2,2,2]{3,2,1,0:T(2,128)S(1)} %pad_add_fusion.refs_, ...), custom_call_target="tpu_custom_call" | custom-call | flops 4400000000 | bytes 1000 | tf_op jit(solution)/shard_map/middle/pallas_call | solution.py:831
  68.3 8.0 %leave.1 = (bf16[1536,512]{1,0:T(8,128)(2,1)S(1)}, bf16[1024,1536]{1,0:T(8,128)(2,1)S(1)}, bf16[1024,512]{1,0:T(8,128)(2,1)S(1)}, bf16[128,1024]{1,0:T(8,128)(2,...) custom-call(s32[2,2,2,2]{3,2,1,0:T(2,128)S(1)} %pad_add_fusion.refs_0_, ...), custom_call_target="tpu_custom_call" | custom-call | flops 3200000000 | bytes 1000 | tf_op jit(solution)/shard_map/leave/pallas_call | solution.py:831
  76.3 3.5 %collective-permute-done.23.refs_9_ = bf16[128,1024]{1,0:T(8,128)(2,1)S(1)} collective-permute-done((bf16[128,1024]{1,0:T(8,128)(2,1)S(1)}, bf16[128,1024]{1,0:T(8,128)(2,1)S(1)}, u32[]{:S(2)}, u32[]{:S(2)}) %collective-permute-start.23) | collective-permute-done | bytes 262176 | tf_op jit(solution)/shard_map/ppermute | solution.py:863
  79.9 6.1 %turn.1 = (f32[1024,512]{1,0:T(8,128)S(1)}, bf16[1024,512]{1,0:T(8,128)(2,1)S(1)}, f32[1024,1536]{1,0:T(8,128)S(1)}, f32[1,512]{1,0:T(1,128)S(1)}, f32[4,16,384]{2,1,0:T(8,128)S(1)}, /*index=5*/f32[1,2,384]{2,1,0:T(2,128)S(1)}) custom-call(s32[2,2,2,2]{3,2,1,0:T(2,128)S(1)} %pad_add_fusion.refs_0_, bf16[1024,512]{1,0:T(8,128)(2,1)S(1)} %get-tuple-element.185.refs_1_.refs_7_, ...), custom_call_target="tpu_custom_call" | custom-call | flops 2400000000 | bytes 1000 | tf_op jit(solution)/shard_map/turn/pallas_call | solution.py:831
  85.9 1.8 grads_a.1
  88.5 1.8 collective-permute-done.25.refs_1_
  94.1 11.1 %back_middle.1 = (bf16[1024,768]{1,0:T(8,128)(2,1)S(1)}, f32[2,384]{1,0:T(2,128)S(1)}, f32[1,512]{1,0:T(1,128)S(1)}, f32[1024,512]{1,0:T(8,128)S(1)}, bf16[1024,...) custom-call(s32[2,2,2,2]{3,2,1,0:T(2,128)S(1)} %pad_add_fusion.refs_, ...), custom_call_target="tpu_custom_call" | custom-call | flops 4400000000 | bytes 1000 | tf_op jit(solution)/shard_map/back_middle/pallas_call | solution.py:831
  105.3 2.7 %grads_b.1 = (bf16[1152,512]{1,0:T(8,128)(2,1)S(1)}, bf16[1152,512]{1,0:T(8,128)(2,1)S(1)}) custom-call(bf16[1024,768]{1,0:T(8,128)(2,1)S(1)} %get-tuple-element.214.refs_0_, bf16[1024,512]{1,0:T(8,128)(2,1)S(1)} %get-tuple-element.175.refs_5_.refs_2_.refs_1_, bf16[1024,1536]{1,0:T(8,128)(2,1)S(1)} %get-tuple-element.215.refs_2_.refs_5_, ...), custom_call_target="tpu_custom_call" | custom-call | bytes 1000 | tf_op jit(solution)/shard_map/grads_b/pallas_call | solution.py:831
  108.6 2.3 %collective-permute-done.30.refs_1_ = bf16[1152,512]{1,0:T(8,128)(2,1)S(1)} collective-permute-done((bf16[1152,512]{1,0:T(8,128)(2,1)S(1)}, bf16[1152,512]{1,0:T(8,128)(2,1)S(1)}, u32[]{:S(2)}, u32[]{:S(2)}) %collective-permute-start.30) | collective-permute-done | bytes 1179680 | tf_op jit(solution)/shard_map/ppermute | solution.py:855
  114.7 8.5 %back_leave.1 = (bf16[1024,768]{1,0:T(8,128)(2,1)S(1)}, f32[8,512]{1,0:T(8,128)S(1)}, bf16[256,1024]{1,0:T(8,128)(2,1)S(1)}, bf16[256,1024]{1,0:T(8,128)(2,1)S(1...) custom-call(s32[2,2,2,2]{3,2,1,0:T(2,128)S(1)} %pad_add_fusion.refs_0_, f32[1,2,384]{2,1,0:T(2,128)S(1)} %bitcast.17, ...), custom_call_target="tpu_custom_call" | custom-call | flops 3600000000 | bytes 1000 | tf_op jit(solution)/shard_map/back_leave/pallas_call | solution.py:831
  124.3 3.3 %collective-permute-done.32.refs_6_ = bf16[288,512]{1,0:T(8,128)(2,1)S(1)} collective-permute-done((bf16[288,512]{1,0:T(8,128)(2,1)S(1)}, bf16[288,512]{1,0:T(8,128)(2,1)S(1)}, u32[]{:S(2)}, u32[]{:S(2)}) %collective-permute-start.32) | collective-permute-done | bytes 294944 | tf_op jit(solution)/shard_map/ppermute | solution.py:855
  130.8 1.6 collective-permute-start.34
  132.5 2.6 %collective-permute-start.35 = (bf16[480,128]{1,0:T(8,128)(2,1)S(1)}, bf16[480,128]{1,0:T(8,128)(2,1)S(1)}, u32[]{:S(2)}, u32[]{:S(2)}) collective-permute-start(bf16[480,128]{1,0:T(8,128)(2,1)S(1)} %get-tuple-element.246), channel_id=1, source_target_pairs={{0,16},{8,24},{16,0},{24,8},{1,17},{9,25},{17,1},{25,9},{2,18},{10... | collective-permute-start | bytes 368648 | tf_op jit(solution)/shard_map/ppermute | solution.py:855
  138.0 4.5 %collective-permute-done.40.refs_2_ = bf16[112,512]{1,0:T(8,128)(2,1)S(1)} collective-permute-done((bf16[112,512]{1,0:T(8,128)(2,1)S(1)}, bf16[112,512]{1,0:T(8,128)(2,1)S(1)}, u32[]{:S(2)}, u32[]{:S(2)}) %collective-permute-start.40) | collective-permute-done | bytes 114720 | tf_op jit(solution)/shard_map/ppermute | solution.py:855
  144.0 1.8 collective-permute-start.49
  148.6 3.5 %collective-permute-start.43 = (bf16[112,128]{1,0:T(8,128)(2,1)S(1)}, bf16[112,128]{1,0:T(8,128)(2,1)S(1)}, u32[]{:S(2)}, u32[]{:S(2)}) collective-permute-start(bf16[112,128]{1,0:T(8,128)(2,1)S(1)} %get-tuple-element.262), channel_id=1, source_target_pairs={{0,16},{8,24},{16,0},{24,8},{1,17},{9,25},{17,1},{25,9},{2,18},{10... | collective-permute-start | bytes 86024 | tf_op jit(solution)/shard_map/ppermute | solution.py:855
  152.0 1.9 collective-permute-done.43.refs_3_
  153.9 2.6 %collective-permute-start.44 = (bf16[112,128]{1,0:T(8,128)(2,1)S(1)}, bf16[112,128]{1,0:T(8,128)(2,1)S(1)}, u32[]{:S(2)}, u32[]{:S(2)}) collective-permute-start(bf16[112,128]{1,0:T(8,128)(2,1)S(1)} %get-tuple-element.263), channel_id=1, source_target_pairs={{0,24},{8,16},{16,8},{24,0},{1,25},{9,17},{17,9},{25,1},{2,26},{10... | collective-permute-start | bytes 86024 | tf_op jit(solution)/shard_map/ppermute | solution.py:855
  156.5 3.1 %collective-permute-done.44.refs_4_ = bf16[112,128]{1,0:T(8,128)(2,1)S(1)} collective-permute-done((bf16[112,128]{1,0:T(8,128)(2,1)S(1)}, bf16[112,128]{1,0:T(8,128)(2,1)S(1)}, u32[]{:S(2)}, u32[]{:S(2)}) %collective-permute-start.44) | collective-permute-done | bytes 28704 | tf_op jit(solution)/shard_map/ppermute | solution.py:855
  159.7 2.6 %collective-permute-start.47 = (bf16[576,128]{1,0:T(8,128)(2,1)S(1)}, bf16[576,128]{1,0:T(8,128)(2,1)S(1)}, u32[]{:S(2)}, u32[]{:S(2)}) collective-permute-start(bf16[576,128]{1,0:T(8,128)(2,1)S(1)} %get-tuple-element.275.refs_0_), channel_id=1, source_target_pairs={{0,24},{8,16},{16,8},{24,0},{1,25},{9,17},{17,9},{25,1},{2,26},{10... | collective-permute-start | bytes 442376 | tf_op jit(solution)/shard_map/ppermute | solution.py:855
  162.3 5.4 %collective-permute-done.47.refs_3_ = bf16[576,128]{1,0:T(8,128)(2,1)S(1)} collective-permute-done((bf16[576,128]{1,0:T(8,128)(2,1)S(1)}, bf16[576,128]{1,0:T(8,128)(2,1)S(1)}, u32[]{:S(2)}, u32[]{:S(2)}) %collective-permute-start.47) | collective-permute-done | bytes 147488 | tf_op jit(solution)/shard_map/ppermute | solution.py:855
  167.7 7.6 %collective-permute-done.46.refs_2_ = bf16[576,128]{1,0:T(8,128)(2,1)S(1)} collective-permute-done((bf16[576,128]{1,0:T(8,128)(2,1)S(1)}, bf16[576,128]{1,0:T(8,128)(2,1)S(1)}, u32[]{:S(2)}, u32[]{:S(2)}) %collective-permute-start.46) | collective-permute-done | bytes 147488 | tf_op jit(solution)/shard_map/ppermute | solution.py:855
  175.4 5.1 %collective-permute-done.45.refs_1_ = bf16[576,128]{1,0:T(8,128)(2,1)S(1)} collective-permute-done((bf16[576,128]{1,0:T(8,128)(2,1)S(1)}, bf16[576,128]{1,0:T(8,128)(2,1)S(1)}, u32[]{:S(2)}, u32[]{:S(2)}) %collective-permute-start.45) | collective-permute-done | bytes 147488 | tf_op jit(solution)/shard_map/ppermute | solution.py:855
  181.6 2.1 %spread.1 = (f32[2,128,2048]{2,1,0:T(8,128)}, f32[2,128,2048]{2,1,0:T(8,128)}) custom-call(bf16[256,1024]{1,0:T(8,128)(2,1)S(1)} %collective-permute-done.48.refs_0_, bf16[256,1024]{1,0:T(8,128)(2,1)S(1)} %collective-permute-done.49.refs_1_, bf16[256,1024]{1,0:T(8,128)(2,1)S(1)} %collective-permute-done.50.refs_2_, ...), custom_call_target="tpu_custom_call" | custom-call | bytes 1000 | tf_op jit(solution)/shard_map/spread/pallas_call | solution.py:831
  183.8 2.1 %finish.1 = (f32[2,128]{1,0:T(2,128)}, f32[2,128]{1,0:T(2,128)}, f32[2,96]{1,0:T(2,128)}, f32[2,96]{1,0:T(2,128)}, f32[2,96]{1,0:T(2,128)}, /*index=5*/f32[2,2,96,512]{3,2,1,0:T(8,128)}, f32[2,4,96,512]{3,2,1,0:T(8,128)}) custom-call(bf16[576,128]{1,0:T(8,128)(2,1)S(1)} %get-tuple-element.275.refs_0_, bf16[576,128]{1,0:T(8,128)(2,1)S(1)} %collective-permute-done.45.refs_1_, ...), custom_call_target="tpu_custom_call" | custom-call | bytes 1000 | tf_op jit(solution)/shard_map/finish/pallas_call | solution.py:831
  (120 shorter events, 39.6 us)
Async XLA Ops:
  2.5 6.6 %collective-permute-start.1 = (bf16[192,1024]{1,0:T(8,128)(2,1)S(1)}, bf16[192,1024]{1,0:T(8,128)(2,1)S(1)}, u32[]{:S(2)}, u32[]{:S(2)}) collective-permute-start(bf16[192,1024]{1,0:T(8,128)(2,1)S(1)} %get-tuple-element.149), channel_id=1, source_target_pairs={{0,0},{1,4},{2,2},{3,6},{4,1},{5,5},{6,3},{7,7},{8,8},{9,12},{10,1... | collective-permute-start | bytes 1179656 | tf_op jit(solution)/shard_map/ppermute | solution.py:863
  3.2 14.1 %collective-permute-start.2 = (bf16[192,1024]{1,0:T(8,128)(2,1)S(1)}, bf16[192,1024]{1,0:T(8,128)(2,1)S(1)}, u32[]{:S(2)}, u32[]{:S(2)}) collective-permute-start(bf16[192,1024]{1,0:T(8,128)(2,1)S(1)} %get-tuple-element.150), channel_id=1, source_target_pairs={{0,4},{1,0},{2,6},{3,2},{4,5},{5,1},{6,7},{7,3},{8,12},{9,8},{10,1... | collective-permute-start | bytes 1179656 | tf_op jit(solution)/shard_map/ppermute | solution.py:863
  7.5 9.8 %collective-permute-start.3 = (bf16[192,1024]{1,0:T(8,128)(2,1)S(1)}, bf16[192,1024]{1,0:T(8,128)(2,1)S(1)}, u32[]{:S(2)}, u32[]{:S(2)}) collective-permute-start(bf16[192,1024]{1,0:T(8,128)(2,1)S(1)} %get-tuple-element.151), channel_id=1, source_target_pairs={{0,2},{1,6},{2,0},{3,4},{4,3},{5,7},{6,1},{7,5},{8,10},{9,14},{10,... | collective-permute-start | bytes 1179656 | tf_op jit(solution)/shard_map/ppermute | solution.py:863
  9.1 17.9 %collective-permute-start.4 = (bf16[192,1024]{1,0:T(8,128)(2,1)S(1)}, bf16[192,1024]{1,0:T(8,128)(2,1)S(1)}, u32[]{:S(2)}, u32[]{:S(2)}) collective-permute-start(bf16[192,1024]{1,0:T(8,128)(2,1)S(1)} %get-tuple-element.152), channel_id=1, source_target_pairs={{0,6},{1,2},{2,4},{3,0},{4,7},{5,3},{6,5},{7,1},{8,14},{9,10},{10,... | collective-permute-start | bytes 1179656 | tf_op jit(solution)/shard_map/ppermute | solution.py:863
  9.1 24.4 %collective-permute-start = (s32[2,2,2]{2,1,0:T(2,128)S(1)}, s32[2,2,2]{2,1,0:T(2,128)S(1)}, u32[]{:S(2)}, u32[]{:S(2)}) collective-permute-start(s32[2,2,2]{2,1,0:T(2,128)S(1)} %get-tuple-element.290), channel_id=1, source_target_pairs={{0,4},{4,0},{1,5},{5,1},{2,6},{6,2},{3,7},{7,3},{8,12},{12,8},{9,1... | collective-permute-start | bytes 104 | tf_op jit(solution)/shard_map/ppermute | solution.py:855
  29.9 10.9 %collective-permute-start.9 = (bf16[3,96,512]{2,1,0:T(8,128)(2,1)S(1)}, bf16[3,96,512]{2,1,0:T(8,128)(2,1)S(1)}, u32[]{:S(2)}, u32[]{:S(2)}) collective-permute-start(bf16[3,96,512]{2,1,0:T(8,128)(2,1)S(1)} %get-tuple-element.167), channel_id=1, source_target_pairs={{0,3},{1,2},{2,1},{3,0},{4,7},{5,6},{6,5},{7,4},{8,11},{9,10},{10,... | collective-permute-start | bytes 884744 | tf_op jit(solution)/shard_map/ppermute | solution.py:855
  30.6 15.4 %collective-permute-start.8 = (bf16[3,96,512]{2,1,0:T(8,128)(2,1)S(1)}, bf16[3,96,512]{2,1,0:T(8,128)(2,1)S(1)}, u32[]{:S(2)}, u32[]{:S(2)}) collective-permute-start(bf16[3,96,512]{2,1,0:T(8,128)(2,1)S(1)} %get-tuple-element.167), channel_id=1, source_target_pairs={{0,2},{1,3},{2,0},{3,1},{4,6},{5,7},{6,4},{7,5},{8,10},{9,11},{10,... | collective-permute-start | bytes 884744 | tf_op jit(solution)/shard_map/ppermute | solution.py:855
  31.6 14.6 %collective-permute-start.7 = (bf16[3,96,512]{2,1,0:T(8,128)(2,1)S(1)}, bf16[3,96,512]{2,1,0:T(8,128)(2,1)S(1)}, u32[]{:S(2)}, u32[]{:S(2)}) collective-permute-start(bf16[3,96,512]{2,1,0:T(8,128)(2,1)S(1)} %get-tuple-element.167), channel_id=1, source_target_pairs={{0,1},{1,0},{2,3},{3,2},{4,5},{5,4},{6,7},{7,6},{8,9},{9,8},{10,11... | collective-permute-start | bytes 884744 | tf_op jit(solution)/shard_map/ppermute | solution.py:855
  47.3 14.9 %collective-permute-start.16 = (bf16[2,96,512]{2,1,0:T(8,128)(2,1)S(1)}, bf16[2,96,512]{2,1,0:T(8,128)(2,1)S(1)}, u32[]{:S(2)}, u32[]{:S(2)}) collective-permute-start(bf16[2,96,512]{2,1,0:T(8,128)(2,1)S(1)} %get-tuple-element.177), channel_id=1, source_target_pairs={{0,3},{1,2},{2,1},{3,0},{4,7},{5,6},{6,5},{7,4},{8,11},{9,10},{10,... | collective-permute-start | bytes 589832 | tf_op jit(solution)/shard_map/ppermute | solution.py:855
  48.7 13.6 %collective-permute-start.15 = (bf16[2,96,512]{2,1,0:T(8,128)(2,1)S(1)}, bf16[2,96,512]{2,1,0:T(8,128)(2,1)S(1)}, u32[]{:S(2)}, u32[]{:S(2)}) collective-permute-start(bf16[2,96,512]{2,1,0:T(8,128)(2,1)S(1)} %get-tuple-element.177), channel_id=1, source_target_pairs={{0,2},{1,3},{2,0},{3,1},{4,6},{5,7},{6,4},{7,5},{8,10},{9,11},{10,... | collective-permute-start | bytes 589832 | tf_op jit(solution)/shard_map/ppermute | solution.py:855
  49.3 13.0 %collective-permute-start.14 = (bf16[2,96,512]{2,1,0:T(8,128)(2,1)S(1)}, bf16[2,96,512]{2,1,0:T(8,128)(2,1)S(1)}, u32[]{:S(2)}, u32[]{:S(2)}) collective-permute-start(bf16[2,96,512]{2,1,0:T(8,128)(2,1)S(1)} %get-tuple-element.177), channel_id=1, source_target_pairs={{0,1},{1,0},{2,3},{3,2},{4,5},{5,4},{6,7},{7,6},{8,9},{9,8},{10,11... | collective-permute-start | bytes 589832 | tf_op jit(solution)/shard_map/ppermute | solution.py:855
  63.4 12.9 %collective-permute-start.20 = (bf16[128,1024]{1,0:T(8,128)(2,1)S(1)}, bf16[128,1024]{1,0:T(8,128)(2,1)S(1)}, u32[]{:S(2)}, u32[]{:S(2)}) collective-permute-start(bf16[128,1024]{1,0:T(8,128)(2,1)S(1)} %get-tuple-element.187), channel_id=1, source_target_pairs={{0,0},{1,4},{2,2},{3,6},{4,1},{5,5},{6,3},{7,7},{8,8},{9,12},{10,1... | collective-permute-start | bytes 786440 | tf_op jit(solution)/shard_map/ppermute | solution.py:863
  64.3 12.0 %collective-permute-start.21 = (bf16[128,1024]{1,0:T(8,128)(2,1)S(1)}, bf16[128,1024]{1,0:T(8,128)(2,1)S(1)}, u32[]{:S(2)}, u32[]{:S(2)}) collective-permute-start(bf16[128,1024]{1,0:T(8,128)(2,1)S(1)} %get-tuple-element.188), channel_id=1, source_target_pairs={{0,4},{1,0},{2,6},{3,2},{4,5},{5,1},{6,7},{7,3},{8,12},{9,8},{10,1... | collective-permute-start | bytes 786440 | tf_op jit(solution)/shard_map/ppermute | solution.py:863
  65.8 10.5 %collective-permute-start.22 = (bf16[128,1024]{1,0:T(8,128)(2,1)S(1)}, bf16[128,1024]{1,0:T(8,128)(2,1)S(1)}, u32[]{:S(2)}, u32[]{:S(2)}) collective-permute-start(bf16[128,1024]{1,0:T(8,128)(2,1)S(1)} %get-tuple-element.189), channel_id=1, source_target_pairs={{0,2},{1,6},{2,0},{3,4},{4,3},{5,7},{6,1},{7,5},{8,10},{9,14},{10,... | collective-permute-start | bytes 786440 | tf_op jit(solution)/shard_map/ppermute | solution.py:863
  67.3 12.6 %collective-permute-start.23 = (bf16[128,1024]{1,0:T(8,128)(2,1)S(1)}, bf16[128,1024]{1,0:T(8,128)(2,1)S(1)}, u32[]{:S(2)}, u32[]{:S(2)}) collective-permute-start(bf16[128,1024]{1,0:T(8,128)(2,1)S(1)} %get-tuple-element.190), channel_id=1, source_target_pairs={{0,6},{1,2},{2,4},{3,0},{4,7},{5,3},{6,5},{7,1},{8,14},{9,10},{10,... | collective-permute-start | bytes 786440 | tf_op jit(solution)/shard_map/ppermute | solution.py:863
  90.6 14.7 %collective-permute-start.26 = (bf16[192,512]{1,0:T(8,128)(2,1)S(1)}, bf16[192,512]{1,0:T(8,128)(2,1)S(1)}, u32[]{:S(2)}, u32[]{:S(2)}) collective-permute-start(bf16[192,512]{1,0:T(8,128)(2,1)S(1)} %get-tuple-element.206), channel_id=1, source_target_pairs={{0,1},{1,0},{2,3},{3,2},{4,5},{5,4},{6,7},{7,6},{8,9},{9,8},{10,11... | collective-permute-start | bytes 589832 | tf_op jit(solution)/shard_map/ppermute | solution.py:855
  91.9 13.4 %collective-permute-start.27 = (bf16[192,512]{1,0:T(8,128)(2,1)S(1)}, bf16[192,512]{1,0:T(8,128)(2,1)S(1)}, u32[]{:S(2)}, u32[]{:S(2)}) collective-permute-start(bf16[192,512]{1,0:T(8,128)(2,1)S(1)} %get-tuple-element.207), channel_id=1, source_target_pairs={{0,2},{1,3},{2,0},{3,1},{4,6},{5,7},{6,4},{7,5},{8,10},{9,11},{10,... | collective-permute-start | bytes 589832 | tf_op jit(solution)/shard_map/ppermute | solution.py:855
  92.5 12.8 %collective-permute-start.28 = (bf16[192,512]{1,0:T(8,128)(2,1)S(1)}, bf16[192,512]{1,0:T(8,128)(2,1)S(1)}, u32[]{:S(2)}, u32[]{:S(2)}) collective-permute-start(bf16[192,512]{1,0:T(8,128)(2,1)S(1)} %get-tuple-element.208), channel_id=1, source_target_pairs={{0,3},{1,2},{2,1},{3,0},{4,7},{5,6},{6,5},{7,4},{8,11},{9,10},{10,... | collective-permute-start | bytes 589832 | tf_op jit(solution)/shard_map/ppermute | solution.py:855
  111.2 13.1 %collective-permute-start.31 = (bf16[288,512]{1,0:T(8,128)(2,1)S(1)}, bf16[288,512]{1,0:T(8,128)(2,1)S(1)}, u32[]{:S(2)}, u32[]{:S(2)}) collective-permute-start(bf16[288,512]{1,0:T(8,128)(2,1)S(1)} %get-tuple-element.237), channel_id=1, source_target_pairs={{0,1},{1,0},{2,3},{3,2},{4,5},{5,4},{6,7},{7,6},{8,9},{9,8},{10,11... | collective-permute-start | bytes 884744 | tf_op jit(solution)/shard_map/ppermute | solution.py:855
  112.5 15.1 %collective-permute-start.32 = (bf16[288,512]{1,0:T(8,128)(2,1)S(1)}, bf16[288,512]{1,0:T(8,128)(2,1)S(1)}, u32[]{:S(2)}, u32[]{:S(2)}) collective-permute-start(bf16[288,512]{1,0:T(8,128)(2,1)S(1)} %get-tuple-element.238), channel_id=1, source_target_pairs={{0,2},{1,3},{2,0},{3,1},{4,6},{5,7},{6,4},{7,5},{8,10},{9,11},{10,... | collective-permute-start | bytes 884744 | tf_op jit(solution)/shard_map/ppermute | solution.py:855
  113.1 14.5 %collective-permute-start.33 = (bf16[288,512]{1,0:T(8,128)(2,1)S(1)}, bf16[288,512]{1,0:T(8,128)(2,1)S(1)}, u32[]{:S(2)}, u32[]{:S(2)}) collective-permute-start(bf16[288,512]{1,0:T(8,128)(2,1)S(1)} %get-tuple-element.239), channel_id=1, source_target_pairs={{0,3},{1,2},{2,1},{3,0},{4,7},{5,6},{6,5},{7,4},{8,11},{9,10},{10,... | collective-permute-start | bytes 884744 | tf_op jit(solution)/shard_map/ppermute | solution.py:855
  129.5 7.2 %collective-permute-start.39 = (bf16[112,512]{1,0:T(8,128)(2,1)S(1)}, bf16[112,512]{1,0:T(8,128)(2,1)S(1)}, u32[]{:S(2)}, u32[]{:S(2)}) collective-permute-start(bf16[112,512]{1,0:T(8,128)(2,1)S(1)} %get-tuple-element.256), channel_id=1, source_target_pairs={{0,1},{1,0},{2,3},{3,2},{4,5},{5,4},{6,7},{7,6},{8,9},{9,8},{10,11... | collective-permute-start | bytes 344072 | tf_op jit(solution)/shard_map/ppermute | solution.py:855
  130.8 13.2 %collective-permute-start.34 = (bf16[480,128]{1,0:T(8,128)(2,1)S(1)}, bf16[480,128]{1,0:T(8,128)(2,1)S(1)}, u32[]{:S(2)}, u32[]{:S(2)}) collective-permute-start(bf16[480,128]{1,0:T(8,128)(2,1)S(1)} %get-tuple-element.245), channel_id=1, source_target_pairs={{0,8},{8,0},{16,24},{24,16},{1,9},{9,1},{17,25},{25,17},{2,10},{10... | collective-permute-start | bytes 368648 | tf_op jit(solution)/shard_map/ppermute | solution.py:855
  132.5 13.4 %collective-permute-start.35 = (bf16[480,128]{1,0:T(8,128)(2,1)S(1)}, bf16[480,128]{1,0:T(8,128)(2,1)S(1)}, u32[]{:S(2)}, u32[]{:S(2)}) collective-permute-start(bf16[480,128]{1,0:T(8,128)(2,1)S(1)} %get-tuple-element.246), channel_id=1, source_target_pairs={{0,16},{8,24},{16,0},{24,8},{1,17},{9,25},{17,1},{25,9},{2,18},{10... | collective-permute-start | bytes 368648 | tf_op jit(solution)/shard_map/ppermute | solution.py:855
  135.0 12.1 %collective-permute-start.36 = (bf16[480,128]{1,0:T(8,128)(2,1)S(1)}, bf16[480,128]{1,0:T(8,128)(2,1)S(1)}, u32[]{:S(2)}, u32[]{:S(2)}) collective-permute-start(bf16[480,128]{1,0:T(8,128)(2,1)S(1)} %get-tuple-element.247), channel_id=1, source_target_pairs={{0,24},{8,16},{16,8},{24,0},{1,25},{9,17},{17,9},{25,1},{2,26},{10... | collective-permute-start | bytes 368648 | tf_op jit(solution)/shard_map/ppermute | solution.py:855
  135.3 7.2 %collective-permute-start.40 = (bf16[112,512]{1,0:T(8,128)(2,1)S(1)}, bf16[112,512]{1,0:T(8,128)(2,1)S(1)}, u32[]{:S(2)}, u32[]{:S(2)}) collective-permute-start(bf16[112,512]{1,0:T(8,128)(2,1)S(1)} %get-tuple-element.257), channel_id=1, source_target_pairs={{0,2},{1,3},{2,0},{3,1},{4,6},{5,7},{6,4},{7,5},{8,10},{9,11},{10,... | collective-permute-start | bytes 344072 | tf_op jit(solution)/shard_map/ppermute | solution.py:855
  143.3 37.2 %collective-permute-start.48 = (bf16[256,1024]{1,0:T(8,128)(2,1)S(1)}, bf16[256,1024]{1,0:T(8,128)(2,1)S(1)}, u32[]{:S(2)}, u32[]{:S(2)}) collective-permute-start(bf16[256,1024]{1,0:T(8,128)(2,1)S(1)} %get-tuple-element.265), channel_id=1, source_target_pairs={{0,0},{4,1},{2,2},{6,3},{1,4},{5,5},{3,6},{7,7},{8,8},{12,9},{10,1... | collective-permute-start | bytes 1572872 | tf_op jit(solution)/shard_map/ppermute | solution.py:863
  144.0 36.5 %collective-permute-start.49 = (bf16[256,1024]{1,0:T(8,128)(2,1)S(1)}, bf16[256,1024]{1,0:T(8,128)(2,1)S(1)}, u32[]{:S(2)}, u32[]{:S(2)}) collective-permute-start(bf16[256,1024]{1,0:T(8,128)(2,1)S(1)} %get-tuple-element.266), channel_id=1, source_target_pairs={{4,0},{0,1},{6,2},{2,3},{5,4},{1,5},{7,6},{3,7},{12,8},{8,9},{14,1... | collective-permute-start | bytes 1572872 | tf_op jit(solution)/shard_map/ppermute | solution.py:863
  145.8 34.7 %collective-permute-start.50 = (bf16[256,1024]{1,0:T(8,128)(2,1)S(1)}, bf16[256,1024]{1,0:T(8,128)(2,1)S(1)}, u32[]{:S(2)}, u32[]{:S(2)}) collective-permute-start(bf16[256,1024]{1,0:T(8,128)(2,1)S(1)} %get-tuple-element.267), channel_id=1, source_target_pairs={{2,0},{6,1},{0,2},{4,3},{3,4},{7,5},{1,6},{5,7},{10,8},{14,9},{8,1... | collective-permute-start | bytes 1572872 | tf_op jit(solution)/shard_map/ppermute | solution.py:863
  147.2 33.4 %collective-permute-start.51 = (bf16[256,1024]{1,0:T(8,128)(2,1)S(1)}, bf16[256,1024]{1,0:T(8,128)(2,1)S(1)}, u32[]{:S(2)}, u32[]{:S(2)}) collective-permute-start(bf16[256,1024]{1,0:T(8,128)(2,1)S(1)} %get-tuple-element.268), channel_id=1, source_target_pairs={{6,0},{2,1},{4,2},{0,3},{7,4},{3,5},{5,6},{1,7},{14,8},{10,9},{12,... | collective-permute-start | bytes 1572872 | tf_op jit(solution)/shard_map/ppermute | solution.py:863
  159.7 8.0 %collective-permute-start.47 = (bf16[576,128]{1,0:T(8,128)(2,1)S(1)}, bf16[576,128]{1,0:T(8,128)(2,1)S(1)}, u32[]{:S(2)}, u32[]{:S(2)}) collective-permute-start(bf16[576,128]{1,0:T(8,128)(2,1)S(1)} %get-tuple-element.275.refs_0_), channel_id=1, source_target_pairs={{0,24},{8,16},{16,8},{24,0},{1,25},{9,17},{17,9},{25,1},{2,26},{10... | collective-permute-start | bytes 442376 | tf_op jit(solution)/shard_map/ppermute | solution.py:855
  167.7 7.6 %collective-permute-start.46 = (bf16[576,128]{1,0:T(8,128)(2,1)S(1)}, bf16[576,128]{1,0:T(8,128)(2,1)S(1)}, u32[]{:S(2)}, u32[]{:S(2)}) collective-permute-start(bf16[576,128]{1,0:T(8,128)(2,1)S(1)} %get-tuple-element.275.refs_0_), channel_id=1, source_target_pairs={{0,16},{8,24},{16,0},{24,8},{1,17},{9,25},{17,1},{25,9},{2,18},{10... | collective-permute-start | bytes 442376 | tf_op jit(solution)/shard_map/ppermute | solution.py:855
  (31 other events, 331.8 us)

commit v2 on v1

--- a/solution.py
+++ b/solution.py
@@ -91,8 +91,9 @@
         onward_next = jnp.where(pos + 1 < sz.run, onward_next, 0.0)
         if live is not None:
             live[rows_of(step), :] = inside
-        ahead[rows_of(step), :] = onward
-        behind[rows_of(step), :] = onward_next
+        if ahead is not None:
+            ahead[rows_of(step), :] = onward
+            behind[rows_of(step), :] = onward_next
         return carry
 
     lax.fori_loop(0, sz.steps, body, 0, unroll=4)
@@ -289,7 +290,7 @@
         grad_decay[1:2, cols] = jnp.sum(carry[1][q][1], axis=0, keepdims=True)
 
 
-ROWS = 64
+ROWS = 256
 
 
 def over_rows(sz, body, init=0):
@@ -467,8 +468,8 @@
 def prepare_kernel(sz, meta, tokens, *refs):
     inputs, refs = refs[:7], refs[7:]
     outs, refs = refs[: sz.blocks], refs[sz.blocks :]
-    drive_b, half_b, half_c = refs[:3]
-    held, small, lines, drive_a, sems = refs[3:10], refs[10], refs[11], refs[12], refs[13]
+    drive_b, half_b = refs[:2]
+    held, small, lines, drive_a, sems = refs[2:9], refs[9], refs[10], refs[11], refs[12]
     top, end = first_rows(sz)
     own, part = sz.states // sz.blocks, sz.width // sz.blocks
     loads, copies = [], []
@@ -511,7 +512,7 @@
     core = meta[2]
     for index in range(2):
         half_b[index] = output_map[0, 2 * core + index]
-        half_c[index] = output_map[1, 2 * core + index]
+        half_b[3 + index] = output_map[1, 2 * core + index]
     half_b[2] = drive_b[core]
     for copy in copies:
         copy.wait()
@@ -566,16 +567,22 @@
                 put(side * count + index, meta[0] ^ (dist + 1), piece[skip + index])
 
 
-def enter_kernel(sz, meta, perm, params, maps, other, *refs):
-    pieces, refs = refs[: sz.blocks], refs[sz.blocks :]
-    w_in, hidden, normed, driven, ends, send, stacked, live, ahead, behind, enter = refs
-    gain, decay = gain_of(params, 0), decay_of(sz, params, 0)
+def open_kernel(sz, meta, perm, params, *refs):
+    pieces, (hidden, normed, stacked, live) = refs[: sz.blocks], refs[sz.blocks :]
     place_pieces(sz, meta, pieces, stacked)
     matmul_nt(perm, stacked, hidden)
+    fill_masks(sz, meta, live, None, None)
+    norm_rows(sz, hidden, gain_of(params, 0), live, normed)
+
+
+def enter_kernel(sz, meta, params, normed, maps, other, w_in, driven, ends, send, ahead, behind, enter):
+    decay = decay_of(sz, params, 0)
     for side, half in ((meta[2], maps), (1 - meta[2], other)):
         w_in[pl.ds(pl.multiple_of(side * sz.states, sz.states), sz.states), :] = half[...]
-    fill_masks(sz, meta, live, ahead, behind)
-    layer_open(sz, meta, hidden, gain, w_in, decay, live, ahead, behind, normed, driven, ends, enter, send)
+    fill_masks(sz, meta, None, ahead, behind)
+    matmul_nt(normed, w_in, driven)
+    chain_ends(sz, decay, ahead, behind, driven, 0, 0, ends)
+    send_ends(sz, meta, decay, ends, enter, send)
 
 
 def middle_kernel(sz, meta, recv, params, ends, driven, normed, hidden, own_out, own_in, *refs):
@@ -595,7 +602,7 @@
     far = sz.blocks - 1
     mine, other, refs = refs[:far], refs[far : 2 * far], refs[2 * far :]
     w_out, states, slope, refs = *refs[:3], refs[3:]
-    place_maps(sz, meta, own_out, mine, other, 0, w_out)
+    place_maps(sz, meta, own_out, mine, other, 3, w_out)
     pieces, refs = refs[: sz.blocks], refs[sz.blocks :]
     live, ahead, behind, enter, mixed, last, stacked = refs
     fill_masks(sz, meta, live, ahead, behind)
@@ -645,15 +652,15 @@
     cut_pieces(sz, meta, last, perm, stacked, [piece.at[part : 2 * part, :] for piece in pieces])
 
 
-def weight_kernel(counts, sz, meta, *refs):
-    for half, out in ((1 - meta[2], refs[-2]), (meta[2], refs[-1])):
-        at = 0
-        for index, count in enumerate(counts):
-            left, right = refs[2 * index], refs[2 * index + 1]
-            for group in range(count):
-                cols = pl.ds(pl.multiple_of((half * count + group) * sz.states, LANES), sz.states)
-                out[at : at + sz.states, :] = tn(left[:, cols], right[...]).astype(out.dtype)
-                at += sz.states
+def weight_kernel(counts, other, sz, meta, *refs):
+    half, out = (1 - meta[2] if other else meta[2]), refs[-1]
+    at = 0
+    for index, count in enumerate(counts):
+        left, right = refs[2 * index], refs[2 * index + 1]
+        for group in range(count):
+            cols = pl.ds(pl.multiple_of((half * count + group) * sz.states, LANES), sz.states)
+            out[at : at + sz.states, :] = tn(left[:, cols], right[...]).astype(out.dtype)
+            at += sz.states
 
 
 def fold_core_kernel(count, sz, meta, keep, got, *pieces):
@@ -687,7 +694,7 @@
     return hi, x - hi
 
 
-def fold_block_kernel(planes, counts, with_tiny, sz, meta, *refs):
+def fold_block_kernel(planes, counts, sz, meta, *refs):
     lanes = sz.width // LANES
     groups = len(counts)
     got, refs = refs[: groups * sz.blocks], refs[groups * sz.blocks :]
@@ -708,28 +715,19 @@
         for dist, out in enumerate(outs):
             out[at : at + part, :] = tall[pl.ds(pl.multiple_of((meta[3] ^ dist) * part, part), part), :]
         at += part
-    if with_tiny:
-        value = total[counts[-1] : counts[-1] + 8, 0:LANES] + total[counts[-1] : counts[-1] + 8, LANES : 2 * LANES]
-        rows = jnp.concatenate(split2(value), axis=0).astype(BF)
-        for out in outs:
-            out[at : at + 16, :] = rows
+    value = total[counts[-1] : counts[-1] + 8, 0:LANES] + total[counts[-1] : counts[-1] + 8, LANES : 2 * LANES]
+    rows = jnp.concatenate(split2(value), axis=0).astype(BF)
+    for out in outs:
+        out[at : at + 16, :] = rows
 
 
 def fold_plane_kernel(sz, meta, *refs):
-    total = refs[0][...].astype(F32)
-    for piece in refs[1:-1]:
-        total += piece[...].astype(F32)
-    refs[-1][...] = total.astype(BF)
-
-
-def join_plane_kernel(sz, meta, first, *refs):
     parts, out, tiny = refs[:-2], refs[-2], refs[-1]
     total = parts[0][...].astype(F32)
     for piece in parts[1:]:
         total += piece[...].astype(F32)
     rows = total.shape[0] - 16
-    out[0 : first.shape[0], :] = first[...]
-    out[first.shape[0] :, :] = total[0:rows].astype(BF)
+    out[...] = total[0:rows].astype(BF)
     tiny[...] = total[rows : rows + 8] + total[rows + 8 :]
 
 
@@ -887,19 +885,18 @@
     perm = ((row % SEGS) * sz.steps + row // SEGS == col).astype(BF)
 
     maps_own = ((2, own, width), BF)
-    half_own = ((3, own, width), BF)
+    half_own = ((5, own, width), BF)
     given = [norm_gain, skip_weight, lambda_log, lambda_imag, log_step, input_map, output_map]
-    *first_pieces, drive_b, half_b, half_c = call(
+    *first_pieces, drive_b, half_b = call(
         "prepare", sz, prepare_kernel, [], [pltpu.with_memory_space_constraint(x, pltpu.HBM) for x in [tokens, *given]],
-        [((first_rows(sz)[1] + 16, toks), BF)] * blocks + [maps_own, half_own, maps_own],
+        [((first_rows(sz)[1] + 16, toks), BF)] * blocks + [maps_own, half_own],
         [(x.shape, x.dtype) for x in given] + [((8, LANES), F32), ((8, LANES), F32), maps_own, pltpu.SemaphoreType.DMA((len(given) + blocks,))],
         limit=6, in_spec=HBM)
     first_pieces = across_all(first_pieces)
-    maps_a, params = call("join", sz, join_kernel, [], first_pieces, [((states, width), BF), ((8, width), F32)], [])
-    half_b, params = after(half_b, params)
     cot_cut = call("cut_cotangent", sz, cut_kernel, [], [pltpu.with_memory_space_constraint(cotangent, pltpu.HBM)],
                    [((part, toks), BF)] * blocks, [((blocks, part, toks), F32), pltpu.SemaphoreType.DMA((blocks,))], limit=4, in_spec=HBM)
-    params, cot_cut = after(params, cot_cut)
+    half_b, first_pieces[1], perm, cot_cut = after(half_b, first_pieces[1], perm, cot_cut)
+    maps_a, params = call("join", sz, join_kernel, [], first_pieces, [((states, width), BF), ((8, width), F32)], [])
     second_mine = [swap(half_b, dist) for dist in range(1, blocks)]
 
     mask = ((toks, LANES), F32)
@@ -914,31 +911,34 @@
     line, gdec = ((1, width), F32), ((2, states), F32)
     piece_out = [((part, toks), BF)] * blocks
 
-    w_in_a, hidden_a, normed_a, driven_a, ends_a, send_a = call(
-        "enter", sz, enter_kernel, items, [perm, params, maps_a, swap(maps_a, 1, "core"), *first_pieces],
-        [w_in, rows_b, rows_b, drv, enter, snd], [stacked, mask, mask, mask, enter], time=7)
+    other_a = swap(maps_a, 1, "core")
+    hidden_a, normed_a = call("open", sz, open_kernel, items, [perm, params, *first_pieces], [rows_b, rows_b], [stacked, mask], time=3)
+    w_in_a, driven_a, ends_a, send_a = call(
+        "enter", sz, enter_kernel, items, [params, normed_a, maps_a, other_a], [w_in, drv, enter, snd], [mask, mask, enter])
     recv = exchange(send_a)
-    second_mine, half_c, _ = after(second_mine, half_c, send_a)
+    second_mine, _ = after(second_mine, send_a)
     second_maps = second_mine, [swap(piece, 1, "core") for piece in second_mine]
-    third_mine = [swap(half_c, dist) for dist in range(1, blocks)]
     w_out_a, w_in_b, states_a, slope_a, hidden_b, normed_b, driven_b, ends_b, send_b = call(
         "middle", sz, middle_kernel, items,
         [recv, params, ends_a, driven_a, normed_a, hidden_a, output_map[0], drive_b, *second_maps[0], *second_maps[1]],
         [w_out, w_in, sts, rows_b, rows_f, rows_b, drv, enter, snd], [mask, mask, mask, enter, rows_f], time=11)
     recv = exchange(send_b)
-    third_mine, cot_cut, _ = after(third_mine, cot_cut, send_b)
+    cot_cut, _ = after(cot_cut, send_a)
     cot_pieces = across_all(cot_cut)
-    third_maps = third_mine, [swap(piece, 1, "core") for piece in third_mine]
+    recv, cot_pieces = after(recv, cot_pieces)
     w_out_b, states_b, slope_b, *out_pieces = call(
         "leave", sz, leave_kernel, items,
-        [recv, params, ends_b, driven_b, normed_b, hidden_b, perm, output_map[1], *third_maps[0], *third_maps[1]],
+        [recv, params, ends_b, driven_b, normed_b, hidden_b, perm, output_map[1], *second_maps[0], *second_maps[1]],
         [w_out, sts, rows_b, *piece_out], [mask, mask, mask, enter, rows_f, rows_b, stacked], time=8)
 
     def half_grads(name, pairs, counts, first=()):
         args = [x for pair in pairs for x in pair]
-        send, keep = call(name, sz, partial(weight_kernel, counts), [], args, [((sum(counts) * states, width), BF)] * 2, [])
-        send, keep, first = after(send, keep, first)
-        return (keep, swap(send, 1, "core")), first
+        shape = [((sum(counts) * states, width), BF)]
+        (send,) = call(name + "_send", sz, partial(weight_kernel, counts, True), [], args, shape, [])
+        send, first = after(send, first)
+        got = swap(send, 1, "core")
+        (keep,) = call(name + "_keep", sz, partial(weight_kernel, counts, False), [], args, shape, [], time=sum(counts))
+        return (keep, got), first
 
     def fold_core(name, group):
         total = group[0].shape[0] // states
@@ -955,10 +955,10 @@
         step = max(SEGS * planes // lanes, SEGS)
         return ((lanes * (-(-rows // step) * step), LANES), BF)
 
-    def over_planes(name, groups, rows, with_tiny):
+    def over_planes(name, groups, rows):
         talls = [tall_of(n) for n in rows]
-        cut = sum(t[0][0] for t in talls) // planes + (16 if with_tiny else 0)
-        parts = call(name, sz, partial(fold_block_kernel, planes, rows, with_tiny), [], [x for g in groups for x in g],
+        cut = sum(t[0][0] for t in talls) // planes + 16
+        parts = call(name, sz, partial(fold_block_kernel, planes, rows), [], [x for g in groups for x in g],
                      [((cut, LANES), BF)] * planes, talls)
         return swap_all(parts, "plane")
 
@@ -985,17 +985,16 @@
         [mask, mask, enter, drv, rows_f, rows_b, stacked, gdec, line], limit=12, time=9)
     group_c, sums_b = half_grads("grads_c", [(gdriven_a, normed_a)], (1,), sums_b)
     sums_c = fold_core("fold_c", [*group_c, tiny, swap(tiny, 1, "core")])
-    parts_ab = over_planes("planes_ab", [sums_a, sums_b], (2 * own, 3 * own), False)
-    (sum_ab,) = call("sum_ab", sz, fold_plane_kernel, [], parts_ab, [(parts_ab[0].shape, BF)], [])
-    parts_c = over_planes("planes_c", [sums_c], (own,), True)
-    last_pieces, parts_c[0] = after(last_pieces, parts_c[0])
-    last_pieces = across_all(last_pieces, back=True)
-    rows = parts_ab[0].shape[0] + parts_c[0].shape[0] - 16
-    sum_all, tiny = call("sum_c", sz, join_plane_kernel, [], [sum_ab, *parts_c], [((rows, LANES), BF), ((8, LANES), F32)], [])
+    parts = over_planes("planes", [sums_a, sums_b, sums_c], (2 * own, 3 * own, own))
+    last_pieces, parts[0] = after(last_pieces, parts[0])
+    early = [across(piece, 2 * dist, True) for dist, piece in enumerate(last_pieces[0::2])]
+    sum_all, tiny = call("sum", sz, fold_plane_kernel, [], parts, [((parts[0].shape[0] - 16, LANES), BF), ((8, LANES), F32)], [])
     whole = swap_all([sum_all] * planes, "plane")
-    whole, last_pieces = after(whole, last_pieces)
+    late, _ = after(last_pieces[1::2], sum_all)
+    late = [across(piece, 2 * dist + 1, True) for dist, piece in enumerate(late)]
+    output, input_grad = spread([piece for pair in zip(early, late) for piece in pair])
+    whole, output = after(whole, output)
     whole += [swap(x, 1, "core") for x in whole]
-    output, input_grad = spread(last_pieces)
     small_out = ((layers, own), F32)
     grad_gain, grad_skip, grad_log, grad_imag, grad_step, grad_in, grad_out = call(
         "finish", sz, partial(finish_kernel, planes, ([(1, 1, 2)], [(0, 1, 1), (1, 0, 2)], [(0, 0, 1)])), [],

time: 186 us -> 169 us (0.909)
  starting transfers between devices: 53.5 us -> 43.2 us
  waiting for transfers between devices: 64.1 us -> 60.4 us
  Pallas kernels: 66.7 us -> 63.8 us
    ppermute x40 -> x31, waiting for transfers between devices: 42.1 us -> 25.8 us  [swap(): lax.ppermute(x, axis, [(i, i ^ dist) for i in range(lax.axis_size(axis))])]
    ppermute x12, waiting for transfers between devices: 21.4 us -> 33.1 us  [across(): lax.ppermute(x, ('core', 'block'), [pair[::-1] for pair in pairs] if back...]
    ppermute x40 -> x31, starting transfers between devices: 35.7 us -> 27.3 us  [swap(): lax.ppermute(x, axis, [(i, i ^ dist) for i in range(lax.axis_size(axis))])]
    pallas_call x21 -> x23, Pallas kernels: 66.7 us -> 63.8 us  [call(): pl.pallas_call(kernel, out_shape=out_shape, in_specs=[SMEM] * len(items)...]
    ppermute x12, starting transfers between devices: 16.3 us -> 14.4 us  [across(): lax.ppermute(x, ('core', 'block'), [pair[::-1] for pair in pairs] if back...]
  transfers between devices with their start and end apart: 56 -> 47, of which waited for: 18 -> 19; matrix products, arithmetic and copies ran while one was open for 0% -> 0% of each run, Pallas kernels for 28% -> 25%
where the time goes in v2:
time: 169 us
  Pallas kernels  63.8 us (38%)
  waiting for transfers between devices  60.4 us (36%)
  starting transfers between devices  43.2 us (26%)
    pallas_call x23, Pallas kernels, call(): pl.pallas_call(kernel, out_shape=out_shape, in_specs=[SMEM] * len(items)...  63.8 us
    ppermute x12, waiting for transfers between devices, across(): lax.ppermute(x, ('core', 'block'), [pair[::-1] for pair in pairs] if back...  33.1 us
    ppermute x31, starting transfers between devices, swap(): lax.ppermute(x, axis, [(i, i ^ dist) for i in range(lax.axis_size(axis))])  27.3 us
    ppermute x31, waiting for transfers between devices, swap(): lax.ppermute(x, axis, [(i, i ^ dist) for i in range(lax.axis_size(axis))])  25.8 us
    ppermute x12, starting transfers between devices, across(): lax.ppermute(x, ('core', 'block'), [pair[::-1] for pair in pairs] if back...  14.4 us
  transfers between devices with their start and end apart: 47, of which 19 were waited for; matrix products, arithmetic and copies ran while one was open for 0% of the time, Pallas kernels for 25%

profile of v2, /device:TPU:0, one launch (start us, length us, event | category | flops | bytes accessed | tf_op | source)
XLA Modules:
  0.0 169.0 jit_solution(14844009491416831184)
XLA Ops:
  0.6 1.9 %prepare.1 = (bf16[192,1024]{1,0:T(8,128)(2,1)S(1)}, bf16[192,1024]{1,0:T(8,128)(2,1)S(1)}, bf16[192,1024]{1,0:T(8,128)(2,1)S(1)}, bf16[192,1024]{1,0:T(8,128)(2...) custom-call(bf16[2,128,2048]{2,1,0:T(8,128)(2,1)} %refs_0_.2, f32[2,128]{1,0:T(2,128)} %refs_1_.1, ...), custom_call_target="tpu_custom_call" | custom-call | bytes 1000 | tf_op jit(solution)/shard_map/prepare/pallas_call | solution.py:829
  3.7 2.6 %collective-permute-start.3 = (bf16[192,1024]{1,0:T(8,128)(2,1)S(1)}, bf16[192,1024]{1,0:T(8,128)(2,1)S(1)}, u32[]{:S(2)}, u32[]{:S(2)}) collective-permute-start(bf16[192,1024]{1,0:T(8,128)(2,1)S(1)} %get-tuple-element.144), channel_id=1, source_target_pairs={{0,2},{1,6},{2,0},{3,4},{4,3},{5,7},{6,1},{7,5},{8,10},{9,14},{10,... | collective-permute-start | bytes 1179656 | tf_op jit(solution)/shard_map/ppermute | solution.py:861
  6.3 3.5 %collective-permute-start.4 = (bf16[192,1024]{1,0:T(8,128)(2,1)S(1)}, bf16[192,1024]{1,0:T(8,128)(2,1)S(1)}, u32[]{:S(2)}, u32[]{:S(2)}) collective-permute-start(bf16[192,1024]{1,0:T(8,128)(2,1)S(1)} %get-tuple-element.145), channel_id=1, source_target_pairs={{0,6},{1,2},{2,4},{3,0},{4,7},{5,3},{6,5},{7,1},{8,14},{9,10},{10,... | collective-permute-start | bytes 1179656 | tf_op jit(solution)/shard_map/ppermute | solution.py:861
  9.8 1.6 cut_cotangent.1
  12.3 2.0 %collective-permute-start.8 = (bf16[5,96,512]{2,1,0:T(8,128)(2,1)S(1)}, bf16[5,96,512]{2,1,0:T(8,128)(2,1)S(1)}, u32[]{:S(2)}, u32[]{:S(2)}) collective-permute-start(bf16[5,96,512]{2,1,0:T(8,128)(2,1)S(1)} %get-tuple-element.155), channel_id=1, source_target_pairs={{0,2},{1,3},{2,0},{3,1},{4,6},{5,7},{6,4},{7,5},{8,10},{9,11},{10,... | collective-permute-start | bytes 1474568 | tf_op jit(solution)/shard_map/ppermute | solution.py:853
  14.2 2.5 %collective-permute-start.7 = (bf16[5,96,512]{2,1,0:T(8,128)(2,1)S(1)}, bf16[5,96,512]{2,1,0:T(8,128)(2,1)S(1)}, u32[]{:S(2)}, u32[]{:S(2)}) collective-permute-start(bf16[5,96,512]{2,1,0:T(8,128)(2,1)S(1)} %get-tuple-element.155), channel_id=1, source_target_pairs={{0,1},{1,0},{2,3},{3,2},{4,5},{5,4},{6,7},{7,6},{8,9},{9,8},{10,11... | collective-permute-start | bytes 1474568 | tf_op jit(solution)/shard_map/ppermute | solution.py:853
  16.8 18.6 %collective-permute-done.4.refs_3_.refs_6_ = bf16[192,1024]{1,0:T(8,128)(2,1)S(1)} collective-permute-done((bf16[192,1024]{1,0:T(8,128)(2,1)S(1)}, bf16[192,1024]{1,0:T(8,128)(2,1)S(1)}, u32[]{:S(2)}, u32[]{:S(2)}) %collective-permute-start.4) | collective-permute-done | bytes 393248 | tf_op jit(solution)/shard_map/ppermute | solution.py:861
  37.2 2.8 %open.1 = (bf16[1024,512]{1,0:T(8,128)(2,1)S(1)}, bf16[1024,512]{1,0:T(8,128)(2,1)S(1)}) custom-call(s32[2,2,2,2]{3,2,1,0:T(2,128)S(1)} %pad_add_fusion.refs_0_, bf16[1024,1024]{1,0:T(8,128)(2,1)S(1)} %fusion.refs_1_.refs_7_.refs_5_.refs_10_, f32[8,512]{1,0:T(8,128)S(1)} %get-tuple-element.146.refs_2_.refs_1_.refs_4_, ...), custom_call_target="tpu_custom_call" | custom-call | flops 1200000000 | bytes 1000 | tf_op jit(solution)/shard_map/open/pallas_call | solution.py:829
  40.1 3.4 %enter.1 = (bf16[768,512]{1,0:T(8,128)(2,1)S(1)}, f32[1024,768]{1,0:T(8,128)S(1)}, f32[4,16,384]{2,1,0:T(8,128)S(1)}, f32[1,2,384]{2,1,0:T(2,128)S(1)}) custom-call(s32[2,2,2,2]{3,2,1,0:T(2,128)S(1)} %pad_add_fusion.refs_0_, f32[8,512]{1,0:T(8,128)S(1)} %get-tuple-element.146.refs_2_.refs_1_.refs_4_, ...), custom_call_target="tpu_custom_call" | custom-call | bytes 1000 | tf_op jit(solution)/shard_map/enter/pallas_call | solution.py:829
  43.5 3.1 %collective-permute-done.8.refs_10_ = bf16[5,96,512]{2,1,0:T(8,128)(2,1)S(1)} collective-permute-done((bf16[5,96,512]{2,1,0:T(8,128)(2,1)S(1)}, bf16[5,96,512]{2,1,0:T(8,128)(2,1)S(1)}, u32[]{:S(2)}, u32[]{:S(2)}) %collective-permute-start.8) | collective-permute-done | bytes 491552 | tf_op jit(solution)/shard_map/ppermute | solution.py:853
  48.4 1.5 collective-permute-done.6
  51.3 1.8 %collective-permute-start.17 = (bf16[128,1024]{1,0:T(8,128)(2,1)S(1)}, bf16[128,1024]{1,0:T(8,128)(2,1)S(1)}, u32[]{:S(2)}, u32[]{:S(2)}) collective-permute-start(bf16[128,1024]{1,0:T(8,128)(2,1)S(1)} %get-tuple-element.167), channel_id=1, source_target_pairs={{0,6},{1,2},{2,4},{3,0},{4,7},{5,3},{6,5},{7,1},{8,14},{9,10},{10,... | collective-permute-start | bytes 786440 | tf_op jit(solution)/shard_map/ppermute | solution.py:861
  53.1 10.2 %middle.1 = (bf16[1536,512]{1,0:T(8,128)(2,1)S(1)}, bf16[768,512]{1,0:T(8,128)(2,1)S(1)}, bf16[1024,1536]{1,0:T(8,128)(2,1)S(1)}, bf16[1024,512]{1,0:T(8,128)(2,...) custom-call(s32[2,2,2,2]{3,2,1,0:T(2,128)S(1)} %pad_add_fusion.refs_, ...), custom_call_target="tpu_custom_call" | custom-call | flops 4400000000 | bytes 1000 | tf_op jit(solution)/shard_map/middle/pallas_call | solution.py:829
  64.7 8.0 %leave.1 = (bf16[1536,512]{1,0:T(8,128)(2,1)S(1)}, bf16[1024,1536]{1,0:T(8,128)(2,1)S(1)}, bf16[1024,512]{1,0:T(8,128)(2,1)S(1)}, bf16[128,1024]{1,0:T(8,128)(2,...) custom-call(s32[2,2,2,2]{3,2,1,0:T(2,128)S(1)} %pad_add_fusion.refs_0_, ...), custom_call_target="tpu_custom_call" | custom-call | flops 3200000000 | bytes 1000 | tf_op jit(solution)/shard_map/leave/pallas_call | solution.py:829
  72.8 6.1 %turn.1 = (f32[1024,512]{1,0:T(8,128)S(1)}, bf16[1024,512]{1,0:T(8,128)(2,1)S(1)}, f32[1024,1536]{1,0:T(8,128)S(1)}, f32[1,512]{1,0:T(1,128)S(1)}, f32[4,16,384]{2,1,0:T(8,128)S(1)}, /*index=5*/f32[1,2,384]{2,1,0:T(2,128)S(1)}) custom-call(s32[2,2,2,2]{3,2,1,0:T(2,128)S(1)} %pad_add_fusion.refs_0_, bf16[1024,512]{1,0:T(8,128)(2,1)S(1)} %get-tuple-element.173.refs_1_.refs_7_, ...), custom_call_target="tpu_custom_call" | custom-call | flops 2400000000 | bytes 1000 | tf_op jit(solution)/shard_map/turn/pallas_call | solution.py:829
  84.5 1.4 collective-permute-start.23
  86.0 10.4 %back_middle.1 = (bf16[1024,768]{1,0:T(8,128)(2,1)S(1)}, f32[2,384]{1,0:T(2,128)S(1)}, f32[1,512]{1,0:T(1,128)S(1)}, f32[1024,512]{1,0:T(8,128)S(1)}, bf16[1024,...) custom-call(s32[2,2,2,2]{3,2,1,0:T(2,128)S(1)} %pad_add_fusion.refs_, ...), custom_call_target="tpu_custom_call" | custom-call | flops 4400000000 | bytes 1000 | tf_op jit(solution)/shard_map/back_middle/pallas_call | solution.py:829
  96.4 1.4 grads_b_send.1
  98.4 1.4 grads_b_keep.1.refs_0_
  103.2 1.4 collective-permute-start.27
  104.6 7.8 %back_leave.1 = (bf16[1024,768]{1,0:T(8,128)(2,1)S(1)}, f32[8,512]{1,0:T(8,128)S(1)}, bf16[256,1024]{1,0:T(8,128)(2,1)S(1)}, bf16[256,1024]{1,0:T(8,128)(2,1)S(1...) custom-call(s32[2,2,2,2]{3,2,1,0:T(2,128)S(1)} %pad_add_fusion.refs_0_, f32[1,2,384]{2,1,0:T(2,128)S(1)} %bitcast.18, ...), custom_call_target="tpu_custom_call" | custom-call | flops 3600000000 | bytes 1000 | tf_op jit(solution)/shard_map/back_leave/pallas_call | solution.py:829
  113.0 4.1 %collective-permute-done.26.refs_6_ = bf16[288,512]{1,0:T(8,128)(2,1)S(1)} collective-permute-done((bf16[288,512]{1,0:T(8,128)(2,1)S(1)}, bf16[288,512]{1,0:T(8,128)(2,1)S(1)}, u32[]{:S(2)}, u32[]{:S(2)}) %collective-permute-start.26) | collective-permute-done | bytes 294944 | tf_op jit(solution)/shard_map/ppermute | solution.py:853
  122.5 2.1 %collective-permute-done.30.refs_9_ = bf16[112,512]{1,0:T(8,128)(2,1)S(1)} collective-permute-done((bf16[112,512]{1,0:T(8,128)(2,1)S(1)}, bf16[112,512]{1,0:T(8,128)(2,1)S(1)}, u32[]{:S(2)}, u32[]{:S(2)}) %collective-permute-start.30) | collective-permute-done | bytes 114720 | tf_op jit(solution)/shard_map/ppermute | solution.py:853
  124.6 2.9 %collective-permute-done.31.refs_10_ = bf16[112,512]{1,0:T(8,128)(2,1)S(1)} collective-permute-done((bf16[112,512]{1,0:T(8,128)(2,1)S(1)}, bf16[112,512]{1,0:T(8,128)(2,1)S(1)}, u32[]{:S(2)}, u32[]{:S(2)}) %collective-permute-start.31) | collective-permute-done | bytes 114720 | tf_op jit(solution)/shard_map/ppermute | solution.py:853
  128.1 1.6 collective-permute-start.33
  129.7 2.6 %collective-permute-start.34 = (bf16[592,128]{1,0:T(8,128)(2,1)S(1)}, bf16[592,128]{1,0:T(8,128)(2,1)S(1)}, u32[]{:S(2)}, u32[]{:S(2)}) collective-permute-start(bf16[592,128]{1,0:T(8,128)(2,1)S(1)} %get-tuple-element.239), channel_id=1, source_target_pairs={{0,16},{8,24},{16,0},{24,8},{1,17},{9,25},{17,1},{25,9},{2,18},{10... | collective-permute-start | bytes 454664 | tf_op jit(solution)/shard_map/ppermute | solution.py:853
  135.2 8.2 %collective-permute-done.34.refs_2_ = bf16[592,128]{1,0:T(8,128)(2,1)S(1)} collective-permute-done((bf16[592,128]{1,0:T(8,128)(2,1)S(1)}, bf16[592,128]{1,0:T(8,128)(2,1)S(1)}, u32[]{:S(2)}, u32[]{:S(2)}) %collective-permute-start.34) | collective-permute-done | bytes 151584 | tf_op jit(solution)/shard_map/ppermute | solution.py:853
  145.0 2.5 %collective-permute-start.38 = (bf16[576,128]{1,0:T(8,128)(2,1)S(1)}, bf16[576,128]{1,0:T(8,128)(2,1)S(1)}, u32[]{:S(2)}, u32[]{:S(2)}) collective-permute-start(bf16[576,128]{1,0:T(8,128)(2,1)S(1)} %get-tuple-element.251.refs_0_), channel_id=1, source_target_pairs={{0,24},{8,16},{16,8},{24,0},{1,25},{9,17},{17,9},{25,1},{2,26},{10... | collective-permute-start | bytes 442376 | tf_op jit(solution)/shard_map/ppermute | solution.py:853
  149.4 3.3 %collective-permute-done.40.refs_1_ = bf16[256,1024]{1,0:T(8,128)(2,1)S(1)} collective-permute-done((bf16[256,1024]{1,0:T(8,128)(2,1)S(1)}, bf16[256,1024]{1,0:T(8,128)(2,1)S(1)}, u32[]{:S(2)}, u32[]{:S(2)}) %collective-permute-start.40) | collective-permute-done | bytes 524320 | tf_op jit(solution)/shard_map/ppermute | solution.py:861
  152.7 9.9 %collective-permute-done.42.refs_3_ = bf16[256,1024]{1,0:T(8,128)(2,1)S(1)} collective-permute-done((bf16[256,1024]{1,0:T(8,128)(2,1)S(1)}, bf16[256,1024]{1,0:T(8,128)(2,1)S(1)}, u32[]{:S(2)}, u32[]{:S(2)}) %collective-permute-start.42) | collective-permute-done | bytes 524320 | tf_op jit(solution)/shard_map/ppermute | solution.py:861
  162.6 2.1 %spread.1 = (f32[2,128,2048]{2,1,0:T(8,128)}, f32[2,128,2048]{2,1,0:T(8,128)}) custom-call(bf16[256,1024]{1,0:T(8,128)(2,1)S(1)} %collective-permute-done.39.refs_0_, bf16[256,1024]{1,0:T(8,128)(2,1)S(1)} %collective-permute-done.40.refs_1_, bf16[256,1024]{1,0:T(8,128)(2,1)S(1)} %collective-permute-done.41.refs_2_, ...), custom_call_target="tpu_custom_call" | custom-call | bytes 1000 | tf_op jit(solution)/shard_map/spread/pallas_call | solution.py:829
  166.9 2.1 %finish.1 = (f32[2,128]{1,0:T(2,128)}, f32[2,128]{1,0:T(2,128)}, f32[2,96]{1,0:T(2,128)}, f32[2,96]{1,0:T(2,128)}, f32[2,96]{1,0:T(2,128)}, /*index=5*/f32[2,2,96,512]{3,2,1,0:T(8,128)}, f32[2,4,96,512]{3,2,1,0:T(8,128)}) custom-call(bf16[576,128]{1,0:T(8,128)(2,1)S(1)} %get-tuple-element.251.refs_0_, bf16[576,128]{1,0:T(8,128)(2,1)S(1)} %collective-permute-done.36.refs_1_, ...), custom_call_target="tpu_custom_call" | custom-call | bytes 1000 | tf_op jit(solution)/shard_map/finish/pallas_call | solution.py:829
  (104 shorter events, 33.0 us)
Async XLA Ops:
  2.5 9.3 %collective-permute-start.2 = (bf16[192,1024]{1,0:T(8,128)(2,1)S(1)}, bf16[192,1024]{1,0:T(8,128)(2,1)S(1)}, u32[]{:S(2)}, u32[]{:S(2)}) collective-permute-start(bf16[192,1024]{1,0:T(8,128)(2,1)S(1)} %get-tuple-element.138), channel_id=1, source_target_pairs={{0,4},{1,0},{2,6},{3,2},{4,5},{5,1},{6,7},{7,3},{8,12},{9,8},{10,1... | collective-permute-start | bytes 1179656 | tf_op jit(solution)/shard_map/ppermute | solution.py:861
  3.0 11.3 %collective-permute-start.1 = (bf16[192,1024]{1,0:T(8,128)(2,1)S(1)}, bf16[192,1024]{1,0:T(8,128)(2,1)S(1)}, u32[]{:S(2)}, u32[]{:S(2)}) collective-permute-start(bf16[192,1024]{1,0:T(8,128)(2,1)S(1)} %get-tuple-element.136), channel_id=1, source_target_pairs={{0,0},{1,4},{2,2},{3,6},{4,1},{5,5},{6,3},{7,7},{8,8},{9,12},{10,1... | collective-permute-start | bytes 1179656 | tf_op jit(solution)/shard_map/ppermute | solution.py:861
  3.7 13.1 %collective-permute-start.3 = (bf16[192,1024]{1,0:T(8,128)(2,1)S(1)}, bf16[192,1024]{1,0:T(8,128)(2,1)S(1)}, u32[]{:S(2)}, u32[]{:S(2)}) collective-permute-start(bf16[192,1024]{1,0:T(8,128)(2,1)S(1)} %get-tuple-element.144), channel_id=1, source_target_pairs={{0,2},{1,6},{2,0},{3,4},{4,3},{5,7},{6,1},{7,5},{8,10},{9,14},{10,... | collective-permute-start | bytes 1179656 | tf_op jit(solution)/shard_map/ppermute | solution.py:861
  6.3 29.1 %collective-permute-start.4 = (bf16[192,1024]{1,0:T(8,128)(2,1)S(1)}, bf16[192,1024]{1,0:T(8,128)(2,1)S(1)}, u32[]{:S(2)}, u32[]{:S(2)}) collective-permute-start(bf16[192,1024]{1,0:T(8,128)(2,1)S(1)} %get-tuple-element.145), channel_id=1, source_target_pairs={{0,6},{1,2},{2,4},{3,0},{4,7},{5,3},{6,5},{7,1},{8,14},{9,10},{10,... | collective-permute-start | bytes 1179656 | tf_op jit(solution)/shard_map/ppermute | solution.py:861
  11.8 31.6 %collective-permute-start.9 = (bf16[5,96,512]{2,1,0:T(8,128)(2,1)S(1)}, bf16[5,96,512]{2,1,0:T(8,128)(2,1)S(1)}, u32[]{:S(2)}, u32[]{:S(2)}) collective-permute-start(bf16[5,96,512]{2,1,0:T(8,128)(2,1)S(1)} %get-tuple-element.155), channel_id=1, source_target_pairs={{0,3},{1,2},{2,1},{3,0},{4,7},{5,6},{6,5},{7,4},{8,11},{9,10},{10,... | collective-permute-start | bytes 1474568 | tf_op jit(solution)/shard_map/ppermute | solution.py:853
  12.3 34.3 %collective-permute-start.8 = (bf16[5,96,512]{2,1,0:T(8,128)(2,1)S(1)}, bf16[5,96,512]{2,1,0:T(8,128)(2,1)S(1)}, u32[]{:S(2)}, u32[]{:S(2)}) collective-permute-start(bf16[5,96,512]{2,1,0:T(8,128)(2,1)S(1)} %get-tuple-element.155), channel_id=1, source_target_pairs={{0,2},{1,3},{2,0},{3,1},{4,6},{5,7},{6,4},{7,5},{8,10},{9,11},{10,... | collective-permute-start | bytes 1474568 | tf_op jit(solution)/shard_map/ppermute | solution.py:853
  14.2 32.3 %collective-permute-start.7 = (bf16[5,96,512]{2,1,0:T(8,128)(2,1)S(1)}, bf16[5,96,512]{2,1,0:T(8,128)(2,1)S(1)}, u32[]{:S(2)}, u32[]{:S(2)}) collective-permute-start(bf16[5,96,512]{2,1,0:T(8,128)(2,1)S(1)} %get-tuple-element.155), channel_id=1, source_target_pairs={{0,1},{1,0},{2,3},{3,2},{4,5},{5,4},{6,7},{7,6},{8,9},{9,8},{10,11... | collective-permute-start | bytes 1474568 | tf_op jit(solution)/shard_map/ppermute | solution.py:853
  46.6 4.7 %collective-permute-start.11 = (bf16[5,96,512]{2,1,0:T(8,128)(2,1)S(1)}, bf16[5,96,512]{2,1,0:T(8,128)(2,1)S(1)}, u32[]{:S(2)}, u32[]{:S(2)}) collective-permute-start(bf16[5,96,512]{2,1,0:T(8,128)(2,1)S(1)} %collective-permute-done.8.refs_10_), channel_id=1, source_target_pairs={{0,4},{4,0},{1,5},{5,1},{2,6},{6,2},{3,7},{7,3},{8,12},{12,8},{9,1... | collective-permute-start | bytes 1474568 | tf_op jit(solution)/shard_map/ppermute | solution.py:853
  47.1 6.0 %collective-permute-start.12 = (bf16[5,96,512]{2,1,0:T(8,128)(2,1)S(1)}, bf16[5,96,512]{2,1,0:T(8,128)(2,1)S(1)}, u32[]{:S(2)}, u32[]{:S(2)}) collective-permute-start(bf16[5,96,512]{2,1,0:T(8,128)(2,1)S(1)} %collective-permute-done.9.refs_11_), channel_id=1, source_target_pairs={{0,4},{4,0},{1,5},{5,1},{2,6},{6,2},{3,7},{7,3},{8,12},{12,8},{9,1... | collective-permute-start | bytes 1474568 | tf_op jit(solution)/shard_map/ppermute | solution.py:853
  47.7 15.7 %collective-permute-start.14 = (bf16[128,1024]{1,0:T(8,128)(2,1)S(1)}, bf16[128,1024]{1,0:T(8,128)(2,1)S(1)}, u32[]{:S(2)}, u32[]{:S(2)}) collective-permute-start(bf16[128,1024]{1,0:T(8,128)(2,1)S(1)} %get-tuple-element.164), channel_id=1, source_target_pairs={{0,0},{1,4},{2,2},{3,6},{4,1},{5,5},{6,3},{7,7},{8,8},{9,12},{10,1... | collective-permute-start | bytes 786440 | tf_op jit(solution)/shard_map/ppermute | solution.py:861
  49.9 13.5 %collective-permute-start.15 = (bf16[128,1024]{1,0:T(8,128)(2,1)S(1)}, bf16[128,1024]{1,0:T(8,128)(2,1)S(1)}, u32[]{:S(2)}, u32[]{:S(2)}) collective-permute-start(bf16[128,1024]{1,0:T(8,128)(2,1)S(1)} %get-tuple-element.165), channel_id=1, source_target_pairs={{0,4},{1,0},{2,6},{3,2},{4,5},{5,1},{6,7},{7,3},{8,12},{9,8},{10,1... | collective-permute-start | bytes 786440 | tf_op jit(solution)/shard_map/ppermute | solution.py:861
  50.1 13.3 %collective-permute-start.16 = (bf16[128,1024]{1,0:T(8,128)(2,1)S(1)}, bf16[128,1024]{1,0:T(8,128)(2,1)S(1)}, u32[]{:S(2)}, u32[]{:S(2)}) collective-permute-start(bf16[128,1024]{1,0:T(8,128)(2,1)S(1)} %get-tuple-element.166), channel_id=1, source_target_pairs={{0,2},{1,6},{2,0},{3,4},{4,3},{5,7},{6,1},{7,5},{8,10},{9,14},{10,... | collective-permute-start | bytes 786440 | tf_op jit(solution)/shard_map/ppermute | solution.py:861
  51.3 13.5 %collective-permute-start.17 = (bf16[128,1024]{1,0:T(8,128)(2,1)S(1)}, bf16[128,1024]{1,0:T(8,128)(2,1)S(1)}, u32[]{:S(2)}, u32[]{:S(2)}) collective-permute-start(bf16[128,1024]{1,0:T(8,128)(2,1)S(1)} %get-tuple-element.167), channel_id=1, source_target_pairs={{0,6},{1,2},{2,4},{3,0},{4,7},{5,3},{6,5},{7,1},{8,14},{9,10},{10,... | collective-permute-start | bytes 786440 | tf_op jit(solution)/shard_map/ppermute | solution.py:861
  82.4 13.9 %collective-permute-start.21 = (bf16[192,512]{1,0:T(8,128)(2,1)S(1)}, bf16[192,512]{1,0:T(8,128)(2,1)S(1)}, u32[]{:S(2)}, u32[]{:S(2)}) collective-permute-start(bf16[192,512]{1,0:T(8,128)(2,1)S(1)} %get-tuple-element.193), channel_id=1, source_target_pairs={{0,1},{1,0},{2,3},{3,2},{4,5},{5,4},{6,7},{7,6},{8,9},{9,8},{10,11... | collective-permute-start | bytes 589832 | tf_op jit(solution)/shard_map/ppermute | solution.py:853
  83.4 13.0 %collective-permute-start.22 = (bf16[192,512]{1,0:T(8,128)(2,1)S(1)}, bf16[192,512]{1,0:T(8,128)(2,1)S(1)}, u32[]{:S(2)}, u32[]{:S(2)}) collective-permute-start(bf16[192,512]{1,0:T(8,128)(2,1)S(1)} %get-tuple-element.194), channel_id=1, source_target_pairs={{0,2},{1,3},{2,0},{3,1},{4,6},{5,7},{6,4},{7,5},{8,10},{9,11},{10,... | collective-permute-start | bytes 589832 | tf_op jit(solution)/shard_map/ppermute | solution.py:853
  84.5 11.8 %collective-permute-start.23 = (bf16[192,512]{1,0:T(8,128)(2,1)S(1)}, bf16[192,512]{1,0:T(8,128)(2,1)S(1)}, u32[]{:S(2)}, u32[]{:S(2)}) collective-permute-start(bf16[192,512]{1,0:T(8,128)(2,1)S(1)} %get-tuple-element.195), channel_id=1, source_target_pairs={{0,3},{1,2},{2,1},{3,0},{4,7},{5,6},{6,5},{7,4},{8,11},{9,10},{10,... | collective-permute-start | bytes 589832 | tf_op jit(solution)/shard_map/ppermute | solution.py:853
  101.0 12.0 %collective-permute-start.25 = (bf16[288,512]{1,0:T(8,128)(2,1)S(1)}, bf16[288,512]{1,0:T(8,128)(2,1)S(1)}, u32[]{:S(2)}, u32[]{:S(2)}) collective-permute-start(bf16[288,512]{1,0:T(8,128)(2,1)S(1)} %get-tuple-element.223), channel_id=1, source_target_pairs={{0,1},{1,0},{2,3},{3,2},{4,5},{5,4},{6,7},{7,6},{8,9},{9,8},{10,11... | collective-permute-start | bytes 884744 | tf_op jit(solution)/shard_map/ppermute | solution.py:853
  102.0 15.1 %collective-permute-start.26 = (bf16[288,512]{1,0:T(8,128)(2,1)S(1)}, bf16[288,512]{1,0:T(8,128)(2,1)S(1)}, u32[]{:S(2)}, u32[]{:S(2)}) collective-permute-start(bf16[288,512]{1,0:T(8,128)(2,1)S(1)} %get-tuple-element.224), channel_id=1, source_target_pairs={{0,2},{1,3},{2,0},{3,1},{4,6},{5,7},{6,4},{7,5},{8,10},{9,11},{10,... | collective-permute-start | bytes 884744 | tf_op jit(solution)/shard_map/ppermute | solution.py:853
  103.2 13.9 %collective-permute-start.27 = (bf16[288,512]{1,0:T(8,128)(2,1)S(1)}, bf16[288,512]{1,0:T(8,128)(2,1)S(1)}, u32[]{:S(2)}, u32[]{:S(2)}) collective-permute-start(bf16[288,512]{1,0:T(8,128)(2,1)S(1)} %get-tuple-element.225), channel_id=1, source_target_pairs={{0,3},{1,2},{2,1},{3,0},{4,7},{5,6},{6,5},{7,4},{8,11},{9,10},{10,... | collective-permute-start | bytes 884744 | tf_op jit(solution)/shard_map/ppermute | solution.py:853
  119.0 5.6 %collective-permute-start.30 = (bf16[112,512]{1,0:T(8,128)(2,1)S(1)}, bf16[112,512]{1,0:T(8,128)(2,1)S(1)}, u32[]{:S(2)}, u32[]{:S(2)}) collective-permute-start(bf16[112,512]{1,0:T(8,128)(2,1)S(1)} %get-tuple-element.233), channel_id=1, source_target_pairs={{0,1},{1,0},{2,3},{3,2},{4,5},{5,4},{6,7},{7,6},{8,9},{9,8},{10,11... | collective-permute-start | bytes 344072 | tf_op jit(solution)/shard_map/ppermute | solution.py:853
  120.2 7.4 %collective-permute-start.31 = (bf16[112,512]{1,0:T(8,128)(2,1)S(1)}, bf16[112,512]{1,0:T(8,128)(2,1)S(1)}, u32[]{:S(2)}, u32[]{:S(2)}) collective-permute-start(bf16[112,512]{1,0:T(8,128)(2,1)S(1)} %get-tuple-element.234), channel_id=1, source_target_pairs={{0,2},{1,3},{2,0},{3,1},{4,6},{5,7},{6,4},{7,5},{8,10},{9,11},{10,... | collective-permute-start | bytes 344072 | tf_op jit(solution)/shard_map/ppermute | solution.py:853
  121.1 6.4 %collective-permute-start.32 = (bf16[112,512]{1,0:T(8,128)(2,1)S(1)}, bf16[112,512]{1,0:T(8,128)(2,1)S(1)}, u32[]{:S(2)}, u32[]{:S(2)}) collective-permute-start(bf16[112,512]{1,0:T(8,128)(2,1)S(1)} %get-tuple-element.235), channel_id=1, source_target_pairs={{0,3},{1,2},{2,1},{3,0},{4,7},{5,6},{6,5},{7,4},{8,11},{9,10},{10,... | collective-permute-start | bytes 344072 | tf_op jit(solution)/shard_map/ppermute | solution.py:853
  128.1 7.1 %collective-permute-start.33 = (bf16[592,128]{1,0:T(8,128)(2,1)S(1)}, bf16[592,128]{1,0:T(8,128)(2,1)S(1)}, u32[]{:S(2)}, u32[]{:S(2)}) collective-permute-start(bf16[592,128]{1,0:T(8,128)(2,1)S(1)} %get-tuple-element.238), channel_id=1, source_target_pairs={{0,8},{8,0},{16,24},{24,16},{1,9},{9,1},{17,25},{25,17},{2,10},{10... | collective-permute-start | bytes 454664 | tf_op jit(solution)/shard_map/ppermute | solution.py:853
  129.7 13.7 %collective-permute-start.34 = (bf16[592,128]{1,0:T(8,128)(2,1)S(1)}, bf16[592,128]{1,0:T(8,128)(2,1)S(1)}, u32[]{:S(2)}, u32[]{:S(2)}) collective-permute-start(bf16[592,128]{1,0:T(8,128)(2,1)S(1)} %get-tuple-element.239), channel_id=1, source_target_pairs={{0,16},{8,24},{16,0},{24,8},{1,17},{9,25},{17,1},{25,9},{2,18},{10... | collective-permute-start | bytes 454664 | tf_op jit(solution)/shard_map/ppermute | solution.py:853
  132.3 11.1 %collective-permute-start.35 = (bf16[592,128]{1,0:T(8,128)(2,1)S(1)}, bf16[592,128]{1,0:T(8,128)(2,1)S(1)}, u32[]{:S(2)}, u32[]{:S(2)}) collective-permute-start(bf16[592,128]{1,0:T(8,128)(2,1)S(1)} %get-tuple-element.240), channel_id=1, source_target_pairs={{0,24},{8,16},{16,8},{24,0},{1,25},{9,17},{17,9},{25,1},{2,26},{10... | collective-permute-start | bytes 454664 | tf_op jit(solution)/shard_map/ppermute | solution.py:853
  132.5 14.9 %collective-permute-start.39 = (bf16[256,1024]{1,0:T(8,128)(2,1)S(1)}, bf16[256,1024]{1,0:T(8,128)(2,1)S(1)}, u32[]{:S(2)}, u32[]{:S(2)}) collective-permute-start(bf16[256,1024]{1,0:T(8,128)(2,1)S(1)} %get-tuple-element.242), channel_id=1, source_target_pairs={{0,0},{4,1},{2,2},{6,3},{1,4},{5,5},{3,6},{7,7},{8,8},{12,9},{10,1... | collective-permute-start | bytes 1572872 | tf_op jit(solution)/shard_map/ppermute | solution.py:861
  133.2 15.4 %collective-permute-start.41 = (bf16[256,1024]{1,0:T(8,128)(2,1)S(1)}, bf16[256,1024]{1,0:T(8,128)(2,1)S(1)}, u32[]{:S(2)}, u32[]{:S(2)}) collective-permute-start(bf16[256,1024]{1,0:T(8,128)(2,1)S(1)} %get-tuple-element.246), channel_id=1, source_target_pairs={{2,0},{6,1},{0,2},{4,3},{3,4},{7,5},{1,6},{5,7},{10,8},{14,9},{8,1... | collective-permute-start | bytes 1572872 | tf_op jit(solution)/shard_map/ppermute | solution.py:861
  143.5 9.2 %collective-permute-start.40 = (bf16[256,1024]{1,0:T(8,128)(2,1)S(1)}, bf16[256,1024]{1,0:T(8,128)(2,1)S(1)}, u32[]{:S(2)}, u32[]{:S(2)}) collective-permute-start(bf16[256,1024]{1,0:T(8,128)(2,1)S(1)} %get-tuple-element.245), channel_id=1, source_target_pairs={{4,0},{0,1},{6,2},{2,3},{5,4},{1,5},{7,6},{3,7},{12,8},{8,9},{14,1... | collective-permute-start | bytes 1572872 | tf_op jit(solution)/shard_map/ppermute | solution.py:861
  144.3 18.3 %collective-permute-start.42 = (bf16[256,1024]{1,0:T(8,128)(2,1)S(1)}, bf16[256,1024]{1,0:T(8,128)(2,1)S(1)}, u32[]{:S(2)}, u32[]{:S(2)}) collective-permute-start(bf16[256,1024]{1,0:T(8,128)(2,1)S(1)} %get-tuple-element.247), channel_id=1, source_target_pairs={{6,0},{2,1},{4,2},{0,3},{7,4},{3,5},{5,6},{1,7},{14,8},{10,9},{12,... | collective-permute-start | bytes 1572872 | tf_op jit(solution)/shard_map/ppermute | solution.py:861
  145.0 19.7 %collective-permute-start.38 = (bf16[576,128]{1,0:T(8,128)(2,1)S(1)}, bf16[576,128]{1,0:T(8,128)(2,1)S(1)}, u32[]{:S(2)}, u32[]{:S(2)}) collective-permute-start(bf16[576,128]{1,0:T(8,128)(2,1)S(1)} %get-tuple-element.251.refs_0_), channel_id=1, source_target_pairs={{0,24},{8,16},{16,8},{24,0},{1,25},{9,17},{17,9},{25,1},{2,26},{10... | collective-permute-start | bytes 442376 | tf_op jit(solution)/shard_map/ppermute | solution.py:853
  147.5 17.2 %collective-permute-start.37 = (bf16[576,128]{1,0:T(8,128)(2,1)S(1)}, bf16[576,128]{1,0:T(8,128)(2,1)S(1)}, u32[]{:S(2)}, u32[]{:S(2)}) collective-permute-start(bf16[576,128]{1,0:T(8,128)(2,1)S(1)} %get-tuple-element.251.refs_0_), channel_id=1, source_target_pairs={{0,16},{8,24},{16,0},{24,8},{1,17},{9,25},{17,1},{25,9},{2,18},{10... | collective-permute-start | bytes 442376 | tf_op jit(solution)/shard_map/ppermute | solution.py:853
  148.7 16.0 %collective-permute-start.36 = (bf16[576,128]{1,0:T(8,128)(2,1)S(1)}, bf16[576,128]{1,0:T(8,128)(2,1)S(1)}, u32[]{:S(2)}, u32[]{:S(2)}) collective-permute-start(bf16[576,128]{1,0:T(8,128)(2,1)S(1)} %get-tuple-element.251.refs_0_), channel_id=1, source_target_pairs={{0,8},{8,0},{16,24},{24,16},{1,9},{9,1},{17,25},{25,17},{2,10},{10... | collective-permute-start | bytes 442376 | tf_op jit(solution)/shard_map/ppermute | solution.py:853
  (22 other events, 250.1 us)

commit v3 on v2

--- a/solution.py
+++ b/solution.py
@@ -27,6 +27,14 @@
     width: int
     states: int
     items: int
+
+
+def turned(sz, index):
+    return sz.blocks - 1 - index
+
+
+def farthest(index, count):
+    return count - index if index else 0
 
 
 def place_of(sz, table):
@@ -89,11 +97,9 @@
             onward = jnp.where((pos > begin) & (pos < end), 1.0, onward)
             onward_next = jnp.where((pos >= begin) & (pos + 1 < end), 1.0, onward_next)
         onward_next = jnp.where(pos + 1 < sz.run, onward_next, 0.0)
-        if live is not None:
-            live[rows_of(step), :] = inside
-        if ahead is not None:
-            ahead[rows_of(step), :] = onward
-            behind[rows_of(step), :] = onward_next
+        live[rows_of(step), :] = inside
+        ahead[rows_of(step), :] = onward
+        behind[rows_of(step), :] = onward_next
         return carry
 
     lax.fori_loop(0, sz.steps, body, 0, unroll=4)
@@ -290,25 +296,12 @@
         grad_decay[1:2, cols] = jnp.sum(carry[1][q][1], axis=0, keepdims=True)
 
 
-ROWS = 256
-
-
-def over_rows(sz, body, init=0):
-    def step(index, carry):
-        return body(pl.ds(pl.multiple_of(index * ROWS, ROWS), ROWS), carry)
-
-    return lax.fori_loop(0, sz.toks // ROWS, step, init)
-
-
-def norm_rows(sz, hidden, gain, live, normed):
-    def body(rows, carry):
-        u = hidden[rows, :].astype(F32)
-        scale = lax.rsqrt(jnp.mean(u * u, axis=1, keepdims=True) + EPSILON)
-        v = u * scale * gain[...]
-        normed[rows, :] = (v * widen(live[rows, :], sz.width // LANES)).astype(BF)
-        return carry
-
-    over_rows(sz, body)
+ROWS = 512
+
+
+def row_parts(sz):
+    size = min(ROWS, sz.toks)
+    return [slice(lo, lo + size) for lo in range(0, sz.toks, size)]
 
 
 def matmul_nt(a, b, out, tile=256):
@@ -316,79 +309,55 @@
         out[:, lo : lo + tile] = nt(a[...], b[lo : lo + tile, :]).astype(out.dtype)
 
 
-def matmul_nn(a, b, out, tile=256):
-    for lo in range(0, b.shape[1], tile):
-        out[:, lo : lo + tile] = nn(a[...], b[:, lo : lo + tile]).astype(out.dtype)
-
-
 def matmul_tn(a, b, out, tile=256):
     for lo in range(0, a.shape[1], tile):
         out[lo : lo + tile, :] = tn(a[:, lo : lo + tile], b[...]).astype(out.dtype)
 
 
-def finish_rows(sz, mixed, skip, normed, live, hidden, slope, result):
-    def body(rows, carry):
-        pre = 2.0 * mixed[rows, :] + skip[...] * normed[rows, :].astype(F32)
-        square = pre * pre
-        th = jnp.tanh(pre * (GELU_C + (GELU_C * GELU_A) * square))
-        on = widen(live[rows, :], sz.width // LANES)
-        part = 0.5 * (1.0 + th)
-        deriv = part + 0.5 * pre * (1.0 - th * th) * (GELU_C + (3.0 * GELU_C * GELU_A) * square)
-        slope[rows, :] = (on * deriv).astype(slope.dtype)
-        result[rows, :] = (hidden[rows, :].astype(F32) + on * (pre * part)).astype(result.dtype)
-        return carry
-
-    over_rows(sz, body)
-
-
-def layer_open(sz, meta, hidden, gain, w_in, decay, live, ahead, behind, normed, driven, ends, enter, send):
-    norm_rows(sz, hidden, gain, live, normed)
-    matmul_nt(normed, w_in, driven)
-    chain_ends(sz, decay, ahead, behind, driven, 0, 0, ends)
-    send_ends(sz, meta, decay, ends, enter, send)
-
-
-def layer_close(sz, meta, recv, decay, ends, driven, normed, hidden, w_out, skip, live, ahead, behind, enter, mixed, states, slope, result):
+def column_sum(x):
+    return jnp.sum(x.reshape(x.shape[0] // 8, 8, x.shape[1]), axis=0)
+
+
+def scale_of(u):
+    return lax.rsqrt(jnp.mean(u * u, axis=1, keepdims=True) + EPSILON)
+
+
+def normed_rows(sz, u, gain, on):
+    return (u * scale_of(u) * gain * on).astype(BF)
+
+
+def finish_rows(sz, rows, states, w_out, skip, normed, on, slope):
+    pre = 2.0 * nn(states[rows, :], w_out[...]) + skip * normed[rows, :].astype(F32)
+    square = pre * pre
+    th = jnp.tanh(pre * (GELU_C + (GELU_C * GELU_A) * square))
+    part = 0.5 + 0.5 * th
+    deriv = part + pre * (1.0 - th * th) * (0.5 * GELU_C + (1.5 * GELU_C * GELU_A) * square)
+    slope[rows, :] = (on * deriv).astype(slope.dtype)
+    return on * (pre * part)
+
+
+def enter_chunk(sz, meta, recv, decay, ends, enter):
     enter_states(sz, meta, decay, ends, received(sz, meta, decay, recv), enter)
-    chain_states(sz, decay, ahead, behind, driven, enter, states)
-    matmul_nn(states, w_out, mixed)
-    finish_rows(sz, mixed, skip, normed, live, hidden, slope, result)
-
-
-def back_open(sz, meta, upstream, slope, normed, w_out, decay, ahead, behind, twice, grad_states, grad_skip, ends, enter, send):
-    def body(rows, total):
-        e = upstream[rows, :] * slope[rows, :].astype(F32)
-        low = e.astype(BF)
-        twice[rows, :] = low + low
-        part = e * normed[rows, :].astype(F32)
-        return total + jnp.sum(part.reshape(ROWS // 8, 8, sz.width), axis=0)
-
-    total = over_rows(sz, body, jnp.zeros((8, sz.width), F32))
-    grad_skip[...] = jnp.sum(total, axis=0, keepdims=True)
-    matmul_nt(twice, w_out, grad_states)
-    chain_ends(sz, decay, ahead, behind, grad_states, 2 * sz.states, 0, ends)
-    send_ends(sz, meta, decay, ends, enter, send)
-
-
-def back_close(sz, meta, recv, decay, ends, grad_states, states, upstream, slope, skip, hidden, gain, w_in, ahead, behind,
-               enter, half, grad_normed, grad_driven, grad_decay, grad_gain, result):
-    enter_states(sz, meta, decay, ends, received(sz, meta, decay, recv), enter)
-    adjoint_chains(sz, decay, ahead, behind, grad_states, enter, states, half, grad_driven, grad_decay)
-    matmul_nn(grad_driven, w_in, grad_normed)
-
-    def body(rows, total):
-        u = hidden[rows, :].astype(F32)
-        r = upstream[rows, :]
-        gn = grad_normed[rows, :] + r * slope[rows, :].astype(F32) * skip[...]
-        scale = lax.rsqrt(jnp.mean(u * u, axis=1, keepdims=True) + EPSILON)
-        part = gn * u * scale
-        dn = gn * gain[...]
-        inner = jnp.sum(dn * u, axis=1, keepdims=True) * (1.0 / sz.width)
-        result[rows, :] = (r + scale * dn - u * (scale * scale * scale * inner)).astype(result.dtype)
-        return total + jnp.sum(part.reshape(ROWS // 8, 8, sz.width), axis=0)
-
-    total = over_rows(sz, body, jnp.zeros((8, sz.width), F32))
-    grad_gain[...] = jnp.sum(total, axis=0, keepdims=True)
+
+
+def back_rows(sz, rows, grad_driven, w_in, upstream, slope, skip, hidden, gain):
+    u = hidden[rows, :].astype(F32)
+    r = upstream[rows, :]
+    gn = nn(grad_driven[rows, :], w_in[...]) + r * slope[rows, :].astype(F32) * skip
+    scale = scale_of(u)
+    moved = u * scale
+    dn = gn * gain
+    inner = jnp.sum(dn * moved, axis=1, keepdims=True) * (1.0 / sz.width)
+    return r + scale * (dn - moved * inner), column_sum(gn * moved)
+
+
+def open_rows(sz, rows, r, slope, normed, w_out, twice, grad_states):
+    e = r * slope[rows, :].astype(F32)
+    low = e.astype(BF)
+    double = low + low
+    twice[rows, :] = double
+    grad_states[rows, :] = nt(double, w_out[...])
+    return column_sum(e * normed[rows, :].astype(F32))
 
 
 def gain_of(params, layer):
@@ -406,7 +375,7 @@
 def place_pieces(sz, meta, pieces, stacked):
     part = sz.width // sz.blocks
     for dist, piece in enumerate(pieces):
-        owner = meta[4] ^ dist
+        owner = meta[4] ^ turned(sz, dist)
         stacked[pl.ds(pl.multiple_of(owner * part, part), part), :] = piece[0:part, :]
 
 
@@ -414,7 +383,7 @@
     part = sz.width // sz.blocks
     matmul_tn(rows, perm, stacked)
     for dist, piece in enumerate(pieces):
-        owner = meta[4] ^ dist
+        owner = meta[4] ^ turned(sz, dist)
         piece[...] = stacked[pl.ds(pl.multiple_of(owner * part, part), part), :]
 
 
@@ -423,7 +392,7 @@
     straight = whole.dtype == BF
     copies = []
     for dist in range(sz.blocks):
-        to = meta[0] ^ dist
+        to = meta[0] ^ turned(sz, dist)
         cols = pl.ds(pl.multiple_of(lax.rem(to, sz.chunks) * sz.toks, LANES), sz.toks)
         source = whole.at[lax.div(to, sz.chunks), :, cols]
         copy = pltpu.make_async_copy(source, outs[dist] if straight else wide.at[dist], sems.at[dist])
@@ -476,7 +445,7 @@
     for index, (source, target) in enumerate(zip(inputs, held)):
         loads.append(pltpu.make_async_copy(source, target, sems.at[index]))
     for dist in range(sz.blocks):
-        to = meta[0] ^ dist
+        to = meta[0] ^ turned(sz, dist)
         cols = pl.ds(pl.multiple_of(lax.rem(to, sz.chunks) * sz.toks, LANES), sz.toks)
         source = tokens.at[lax.div(to, sz.chunks), :, cols]
         copies.append(pltpu.make_async_copy(source, outs[dist].at[0:top, :], sems.at[len(inputs) + dist]))
@@ -504,7 +473,7 @@
     rows = jnp.concatenate([*split3(small[...]), jnp.zeros((8, sz.toks - 3 * LANES), F32)], axis=1)
     rows = jnp.concatenate([rows, jnp.zeros((8, sz.toks), F32)], axis=0).astype(BF)
     for dist, out in enumerate(outs):
-        half = lax.rem(meta[0] ^ dist, 2)
+        half = lax.rem(meta[0] ^ turned(sz, dist), 2)
         for from_rows, to_rows, lanes in half_map_parts(sz):
             out[to_rows, lanes] = drive_a[half, from_rows, :]
         out[end:, :] = rows
@@ -528,7 +497,7 @@
     own = sz.states // sz.blocks
     collect_params(sz, meta, [params_of(sz, piece) for piece in pieces], params)
     for dist, piece in enumerate(pieces):
-        base = (meta[4] ^ dist) * own
+        base = (meta[4] ^ turned(sz, dist)) * own
         for to_rows, from_rows, lanes in half_map_parts(sz):
             rows = pl.ds(pl.multiple_of(base + to_rows.start, 16), to_rows.stop - to_rows.start)
             maps[rows, :] = piece[from_rows, lanes]
@@ -544,7 +513,7 @@
     for block in range(sz.blocks):
         piece = smalls[0]
         for dist in range(1, sz.blocks):
-            piece = jnp.where((meta[4] ^ dist) == block, smalls[dist], piece)
+            piece = jnp.where((meta[4] ^ turned(sz, dist)) == block, smalls[dist], piece)
         for first, count, size in ((0, 4, part), (4, 4, own)):
             mine = jnp.where((row >= first) & (row < first + count) & (lane < size), piece, 0.0)
             wide = jnp.concatenate([mine, pad], axis=1)
@@ -568,84 +537,107 @@
 
 
 def open_kernel(sz, meta, perm, params, *refs):
-    pieces, (hidden, normed, stacked, live) = refs[: sz.blocks], refs[sz.blocks :]
+    pieces, (hidden, normed, live, ahead, behind, stacked) = refs[: sz.blocks], refs[sz.blocks :]
+    fill_masks(sz, meta, live, ahead, behind)
     place_pieces(sz, meta, pieces, stacked)
-    matmul_nt(perm, stacked, hidden)
-    fill_masks(sz, meta, live, None, None)
-    norm_rows(sz, hidden, gain_of(params, 0), live, normed)
-
-
-def enter_kernel(sz, meta, params, normed, maps, other, w_in, driven, ends, send, ahead, behind, enter):
+    gain = gain_of(params, 0)
+    for rows in row_parts(sz):
+        u = nt(perm[rows, :], stacked[...])
+        hidden[rows, :] = u.astype(BF)
+        normed[rows, :] = normed_rows(sz, u, gain, widen(live[rows, :], sz.width // LANES))
+
+
+def enter_kernel(sz, meta, ahead, behind, params, normed, maps, other, w_in, driven, ends, send, enter):
     decay = decay_of(sz, params, 0)
     for side, half in ((meta[2], maps), (1 - meta[2], other)):
         w_in[pl.ds(pl.multiple_of(side * sz.states, sz.states), sz.states), :] = half[...]
-    fill_masks(sz, meta, None, ahead, behind)
     matmul_nt(normed, w_in, driven)
     chain_ends(sz, decay, ahead, behind, driven, 0, 0, ends)
     send_ends(sz, meta, decay, ends, enter, send)
 
 
-def middle_kernel(sz, meta, recv, params, ends, driven, normed, hidden, own_out, own_in, *refs):
+def middle_kernel(sz, meta, live, ahead, behind, recv, params, ends, driven, normed, hidden, own_out, own_in, *refs):
     decay, skip, gain_b, decay_b = decay_of(sz, params, 0), skip_of(params, 0), gain_of(params, 1), decay_of(sz, params, 1)
     far = sz.blocks - 1
     mine, other, refs = refs[:far], refs[far : 2 * far], refs[2 * far :]
-    w_out, w_in_b, states, slope, hidden_b, normed_b, driven_b, ends_b, send_b, live, ahead, behind, enter, mixed = refs
+    w_out, w_in_b, states, slope, hidden_b, normed_b, driven_b, ends_b, send_b, enter = refs
     place_maps(sz, meta, own_out, mine, other, 0, w_out)
     place_maps(sz, meta, own_in, mine, other, 2, w_in_b)
-    fill_masks(sz, meta, live, ahead, behind)
-    layer_close(sz, meta, recv, decay, ends, driven, normed, hidden, w_out, skip, live, ahead, behind, enter, mixed, states, slope, hidden_b)
-    layer_open(sz, meta, hidden_b, gain_b, w_in_b, decay_b, live, ahead, behind, normed_b, driven_b, ends_b, enter, send_b)
-
-
-def leave_kernel(sz, meta, recv, params, ends, driven, normed, hidden, perm, own_out, *refs):
+    enter_chunk(sz, meta, recv, decay, ends, enter)
+    chain_states(sz, decay, ahead, behind, driven, enter, states)
+    for rows in row_parts(sz):
+        on = widen(live[rows, :], sz.width // LANES)
+        u = hidden[rows, :].astype(F32) + finish_rows(sz, rows, states, w_out, skip, normed, on, slope)
+        hidden_b[rows, :] = u
+        v = normed_rows(sz, u, gain_b, on)
+        normed_b[rows, :] = v
+        driven_b[rows, :] = nt(v, w_in_b[...])
+    chain_ends(sz, decay_b, ahead, behind, driven_b, 0, 0, ends_b)
+    send_ends(sz, meta, decay_b, ends_b, enter, send_b)
+
+
+def leave_kernel(sz, meta, live, ahead, behind, recv, params, ends, driven, normed, hidden, perm, own_out, *refs):
     decay, skip = decay_of(sz, params, 1), skip_of(params, 1)
     far = sz.blocks - 1
     mine, other, refs = refs[:far], refs[far : 2 * far], refs[2 * far :]
     w_out, states, slope, refs = *refs[:3], refs[3:]
     place_maps(sz, meta, own_out, mine, other, 3, w_out)
-    pieces, refs = refs[: sz.blocks], refs[sz.blocks :]
-    live, ahead, behind, enter, mixed, last, stacked = refs
-    fill_masks(sz, meta, live, ahead, behind)
-    layer_close(sz, meta, recv, decay, ends, driven, normed, hidden, w_out, skip, live, ahead, behind, enter, mixed, states, slope, last)
+    pieces, (enter, last, stacked) = refs[: sz.blocks], refs[sz.blocks :]
+    enter_chunk(sz, meta, recv, decay, ends, enter)
+    chain_states(sz, decay, ahead, behind, driven, enter, states)
+    for rows in row_parts(sz):
+        on = widen(live[rows, :], sz.width // LANES)
+        last[rows, :] = (hidden[rows, :] + finish_rows(sz, rows, states, w_out, skip, normed, on, slope)).astype(BF)
     cut_pieces(sz, meta, last, perm, stacked, pieces)
 
 
-def turn_kernel(sz, meta, slope, normed, w_out, params, perm, *refs):
+def turn_kernel(sz, meta, ahead, behind, slope, normed, w_out, params, perm, *refs):
     decay = decay_of(sz, params, 1)
     pieces, refs = refs[: sz.blocks], refs[sz.blocks :]
-    upstream, twice, grad_states, grad_skip, ends, send, stacked, ahead, behind, enter = refs
+    upstream, twice, grad_states, grad_skip, ends, send, stacked, enter = refs
     place_pieces(sz, meta, pieces, stacked)
-    matmul_nt(perm, stacked, upstream)
-    fill_masks(sz, meta, None, ahead, behind)
-    back_open(sz, meta, upstream, slope, normed, w_out, decay, ahead, behind, twice, grad_states, grad_skip, ends, enter, send)
-
-
-def back_middle_kernel(sz, meta, recv, params, ends, grad_states, states, upstream, slope, hidden, w_in,
+    skips = []
+    for rows in row_parts(sz):
+        r = nt(perm[rows, :], stacked[...])
+        upstream[rows, :] = r
+        skips.append(open_rows(sz, rows, r, slope, normed, w_out, twice, grad_states))
+    grad_skip[...] = jnp.sum(sum(skips), axis=0, keepdims=True)
+    chain_ends(sz, decay, ahead, behind, grad_states, 2 * sz.states, 0, ends)
+    send_ends(sz, meta, decay, ends, enter, send)
+
+
+def back_middle_kernel(sz, meta, ahead, behind, recv, params, ends, grad_states, states, upstream, slope, hidden, w_in,
                        slope_b, normed_b, w_out_b,
                        grad_driven, grad_decay, grad_gain, upstream_b, twice_b, grad_states_b, grad_skip_b, ends_b, send_b,
-                       ahead, behind, enter, half, grad_normed):
+                       enter, half):
     decay, skip, gain, decay_b = decay_of(sz, params, 1), skip_of(params, 1), gain_of(params, 1), decay_of(sz, params, 0)
-    fill_masks(sz, meta, None, ahead, behind)
-    back_close(sz, meta, recv, decay, ends, grad_states, states, upstream, slope, skip, hidden, gain, w_in, ahead, behind,
-               enter, half, grad_normed, grad_driven, grad_decay, grad_gain, upstream_b)
-    back_open(sz, meta, upstream_b, slope_b, normed_b, w_out_b, decay_b, ahead, behind, twice_b, grad_states_b, grad_skip_b, ends_b, enter, send_b)
-
-
-def back_leave_kernel(sz, meta, recv, params, ends, grad_states, states, upstream, slope, hidden, w_in, perm,
-                      gain_b, skip_a, skip_b, decay_b, *refs):
+    enter_chunk(sz, meta, recv, decay, ends, enter)
+    adjoint_chains(sz, decay, ahead, behind, grad_states, enter, states, half, grad_driven, grad_decay)
+    gains, skips = [], []
+    for rows in row_parts(sz):
+        r, terms = back_rows(sz, rows, grad_driven, w_in, upstream, slope, skip, hidden, gain)
+        gains.append(terms)
+        upstream_b[rows, :] = r
+        skips.append(open_rows(sz, rows, r, slope_b, normed_b, w_out_b, twice_b, grad_states_b))
+    grad_gain[...] = jnp.sum(sum(gains), axis=0, keepdims=True)
+    grad_skip_b[...] = jnp.sum(sum(skips), axis=0, keepdims=True)
+    chain_ends(sz, decay_b, ahead, behind, grad_states_b, 2 * sz.states, 0, ends_b)
+    send_ends(sz, meta, decay_b, ends_b, enter, send_b)
+
+
+def back_chain_kernel(sz, meta, ahead, behind, recv, params, ends, grad_states, states, grad_driven, grad_decay, enter, half):
+    decay = decay_of(sz, params, 0)
+    enter_chunk(sz, meta, recv, decay, ends, enter)
+    adjoint_chains(sz, decay, ahead, behind, grad_states, enter, states, half, grad_driven, grad_decay)
+
+
+def back_leave_kernel(sz, meta, params, grad_driven, upstream, slope, hidden, w_in, perm, *refs):
     done, refs = refs[: sz.blocks], refs[sz.blocks :]
-    grad_driven, tiny, refs = refs[0], refs[1], refs[2:]
-    decay, skip, gain = decay_of(sz, params, 0), skip_of(params, 0), gain_of(params, 0)
-    pieces, refs = refs[: sz.blocks], refs[sz.blocks :]
-    ahead, behind, enter, half, grad_normed, last, stacked, grad_decay, grad_gain = refs
-    fill_masks(sz, meta, None, ahead, behind)
-    back_close(sz, meta, recv, decay, ends, grad_states, states, upstream, slope, skip, hidden, gain, w_in, ahead, behind,
-               enter, half, grad_normed, grad_driven, grad_decay, grad_gain, last)
-    tiny[...] = jnp.zeros_like(tiny)
-    for row, line in enumerate((grad_gain, gain_b, skip_a, skip_b)):
-        tiny[row : row + 1, :] = line[...]
-    tiny[4:6, 0 : sz.states] = grad_decay[...]
-    tiny[6:8, 0 : sz.states] = decay_b[...]
+    skip, gain = skip_of(params, 0), gain_of(params, 0)
+    pieces, (last, stacked) = refs[: sz.blocks], refs[sz.blocks :]
+    for rows in row_parts(sz):
+        r, _ = back_rows(sz, rows, grad_driven, w_in, upstream, slope, skip, hidden, gain)
+        last[rows, :] = r.astype(BF)
     part = sz.width // sz.blocks
     for piece, first in zip(pieces, done):
         piece[0:part, :] = first[...]
@@ -653,8 +645,16 @@
 
 
 def weight_kernel(counts, other, sz, meta, *refs):
-    half, out = (1 - meta[2] if other else meta[2]), refs[-1]
-    at = 0
+    half = 1 - meta[2] if other else meta[2]
+    pairs = 2 * len(counts)
+    out, at = refs[pairs], 0
+    if len(refs) > pairs + 1:
+        whole, out, terms = refs[pairs:]
+        value = tn(refs[0][:, pl.ds(pl.multiple_of(half * sz.states, LANES), sz.states)], refs[1][...])
+        out[...] = value.astype(out.dtype)
+        rows = whole[pl.ds(pl.multiple_of(half * sz.states, sz.states), sz.states), :].astype(F32)
+        terms[...] = jnp.sum(column_sum(rows * value), axis=0, keepdims=True)
+        return
     for index, count in enumerate(counts):
         left, right = refs[2 * index], refs[2 * index + 1]
         for group in range(count):
@@ -663,80 +663,152 @@
             at += sz.states
 
 
-def fold_core_kernel(count, sz, meta, keep, got, *pieces):
-    own = sz.states // sz.blocks
-    part = sz.width // sz.blocks
-    tiny = None
-    if len(pieces) > sz.blocks:
-        tiny, pieces = pieces[0][...] + pieces[1][...], pieces[2:]
-        row = lax.broadcasted_iota(jnp.int32, (8, LANES), 0)
-        lane = lax.broadcasted_iota(jnp.int32, (8, LANES), 1)
-    for dist, piece in enumerate(pieces):
-        owner = meta[0] ^ dist
-        for group in range(count):
-            rows = pl.ds(pl.multiple_of(group * sz.states + owner * own, own), own)
-            piece[group * own : (group + 1) * own, :] = (keep[rows, :].astype(F32) + got[rows, :].astype(F32)).astype(BF)
-        if tiny is not None:
-            value = jnp.zeros((8, LANES), F32)
-            for block in range(sz.blocks):
-                wide = pltpu.roll(tiny, sz.width - block * part, 1) if block else tiny
-                deep = pltpu.roll(tiny, sz.width - block * own, 1) if block else tiny
-                mine = jnp.where(row < 4, jnp.where(lane < part, wide[:, :LANES], 0.0), jnp.where(lane < own, deep[:, :LANES], 0.0))
-                value = jnp.where(owner == block, mine, value)
-            hi, lo = split2(value)
-            rest = jnp.zeros((8, sz.width - 2 * LANES), F32)
-            wide = jnp.concatenate([jnp.concatenate([hi, lo, rest], axis=1), jnp.zeros((8, sz.width), F32)], axis=0)
-            piece[count * own : count * own + 16, :] = wide.astype(BF)
-
-
 def split2(x):
     hi = x.astype(BF).astype(F32)
     return hi, x - hi
 
 
-def fold_block_kernel(planes, counts, sz, meta, *refs):
+class Group(NamedTuple):
+    first: int
+    counts: tuple
+    tiny: bool
+
+    def rows(self, sz):
+        return sum(self.counts) * (sz.states // sz.blocks) + (16 if self.tiny else 0)
+
+
+def bits_of(sz):
+    return sz.blocks.bit_length() - 1
+
+
+def step_bit(sz, step, core):
+    return 1 << ((step + core) % bits_of(sz))
+
+
+def far_block(sz, group, slot, core):
+    return sum(step_bit(sz, group.first + j, core) for j in range(bits_of(sz)) if (slot >> j) & 1)
+
+
+def own_tiny(sz, params, terms, more, gain_b, skip_a, skip_b, decay_a, decay_b, tiny):
+    gain_a = (terms[...] + more[...] + skip_of(params, 0) * skip_a[...]) / gain_of(params, 0)
+    tiny[...] = jnp.zeros_like(tiny)
+    for index, line in enumerate((gain_a, gain_b[...], skip_a[...], skip_b[...])):
+        tiny[index : index + 1, :] = line
+    tiny[4:6, 0 : sz.states] = decay_a[...]
+    tiny[6:8, 0 : sz.states] = decay_b[...]
+    return tiny[...]
+
+
+def tiny_of(sz, tiny, owner):
+    own, part = sz.states // sz.blocks, sz.width // sz.blocks
+    row = lax.broadcasted_iota(jnp.int32, (8, LANES), 0)
+    lane = lax.broadcasted_iota(jnp.int32, (8, LANES), 1)
+    value = jnp.zeros((8, LANES), F32)
+    for block in range(sz.blocks):
+        wide = pltpu.roll(tiny, sz.width - block * part, 1) if block else tiny
+        deep = pltpu.roll(tiny, sz.width - block * own, 1) if block else tiny
+        mine = jnp.where(row < 4, jnp.where(lane < part, wide[:, :LANES], 0.0), jnp.where(lane < own, deep[:, :LANES], 0.0))
+        value = jnp.where(owner == block, mine, value)
+    return value
+
+
+def put_sums(sz, group, value, tiny, slot, kept, message, at):
+    rows = value.shape[0]
+    if slot % 2 == 0:
+        kept[slot // 2, 0:rows, :] = value
+        if group.tiny:
+            kept[slot // 2, rows : rows + 8, 0:LANES] = tiny
+        return at
+    message[at : at + rows, :] = value.astype(BF)
+    if group.tiny:
+        rest = jnp.zeros((8, sz.width - 2 * LANES), F32)
+        wide = jnp.concatenate([*split2(tiny), rest], axis=1)
+        message[at + rows : at + rows + 16, :] = jnp.concatenate([wide, jnp.zeros_like(wide)], axis=0).astype(BF)
+    return at + group.rows(sz)
+
+
+def add_message(sz, group, kept, slot, message, at):
+    rows = group.rows(sz) - (16 if group.tiny else 0)
+    value = kept[slot, 0:rows, :] + message[at : at + rows, :].astype(F32)
+    if not group.tiny:
+        return value, None
+    got = message[at + rows : at + rows + 16, 0 : 2 * LANES].astype(F32)[0:8]
+    return value, kept[slot, rows : rows + 8, 0:LANES] + got[:, 0:LANES] + got[:, LANES:]
+
+
+def step_kernel(old, new, sz, meta, *refs):
+    came, refs = (refs[0], refs[1:]) if old else (None, refs)
+    held, refs = refs[: len(old)], refs[len(old) :]
+    if new:
+        halves, refs = refs[: 2 * len(new.counts)], refs[2 * len(new.counts) :]
+        if new.tiny:
+            lines, refs, room = refs[:8], refs[8:-1], refs[-1]
+    keeps, message = refs[:-1], refs[-1]
+    at = 0
+    for (group, slots, row), kept, keep in zip(old, held, keeps):
+        for slot in range(slots):
+            value, tiny = add_message(sz, group, kept, slot, came, row + slot * group.rows(sz))
+            at = put_sums(sz, group, value, tiny, slot, keep, message, at)
+    if new:
+        own = sz.states // sz.blocks
+        whole = own_tiny(sz, *lines, room) if new.tiny else None
+        for slot in range(sz.blocks):
+            owner = meta[0] ^ jnp.where(meta[2] == 0, far_block(sz, new, slot, 0), far_block(sz, new, slot, 1))
+            parts = []
+            for index, count in enumerate(new.counts):
+                keep, got = halves[2 * index], halves[2 * index + 1]
+                for one in range(count):
+                    rows = pl.ds(pl.multiple_of(one * sz.states + owner * own, own), own)
+                    parts.append(keep[rows, :].astype(F32) + got[rows, :].astype(F32))
+            tiny = tiny_of(sz, whole, owner) if new.tiny else None
+            at = put_sums(sz, new, jnp.concatenate(parts, axis=0), tiny, slot, keeps[-1], message, at)
+
+
+def fold_block_kernel(planes, groups, sz, meta, *refs):
     lanes = sz.width // LANES
-    groups = len(counts)
-    got, refs = refs[: groups * sz.blocks], refs[groups * sz.blocks :]
+    held, refs = refs[: 2 * len(groups)], refs[2 * len(groups) :]
     outs, talls = refs[:planes], refs[planes:]
     at = 0
-    for index, rows in enumerate(counts):
-        pieces = got[index * sz.blocks : (index + 1) * sz.blocks]
-        total = pieces[0][...].astype(F32)
-        for piece in pieces[1:]:
-            total += piece[...].astype(F32)
+    for index, (group, row) in enumerate(groups):
+        total, tiny = add_message(sz, group, held[2 * index], 0, held[2 * index + 1], row)
+        rows = total.shape[0]
         tall = talls[index]
         padded = tall.shape[0] // lanes
         for block in range(lanes):
-            tall[block * padded : block * padded + rows, :] = total[0:rows, block * LANES : (block + 1) * LANES].astype(BF)
+            tall[block * padded : block * padded + rows, :] = total[:, block * LANES : (block + 1) * LANES].astype(BF)
             if padded > rows:
                 tall[block * padded + rows : (block + 1) * padded, :] = jnp.zeros((padded - rows, LANES), BF)
         part = tall.shape[0] // planes
         for dist, out in enumerate(outs):
-            out[at : at + part, :] = tall[pl.ds(pl.multiple_of((meta[3] ^ dist) * part, part), part), :]
+            out[at : at + part, :] = tall[pl.ds(pl.multiple_of((meta[3] ^ farthest(dist, planes)) * part, part), part), :]
         at += part
-    value = total[counts[-1] : counts[-1] + 8, 0:LANES] + total[counts[-1] : counts[-1] + 8, LANES : 2 * LANES]
-    rows = jnp.concatenate(split2(value), axis=0).astype(BF)
-    for out in outs:
-        out[at : at + 16, :] = rows
-
-
-def fold_plane_kernel(sz, meta, *refs):
-    parts, out, tiny = refs[:-2], refs[-2], refs[-1]
+    if tiny is not None:
+        rows = jnp.concatenate(split2(tiny), axis=0).astype(BF)
+        for out in outs:
+            out[at : at + 16, :] = rows
+
+
+def fold_plane_kernel(early, sz, meta, *refs):
+    parts, out, tiny = refs[early:-2], refs[-2], refs[-1]
+    total = refs[0][...].astype(F32)
+    for piece in refs[1:early]:
+        total += piece[...].astype(F32)
+    top = total.shape[0]
+    out[0:top, :] = total.astype(BF)
     total = parts[0][...].astype(F32)
     for piece in parts[1:]:
         total += piece[...].astype(F32)
     rows = total.shape[0] - 16
-    out[...] = total[0:rows].astype(BF)
+    out[top:, :] = total[0:rows].astype(BF)
     tiny[...] = total[rows : rows + 8] + total[rows + 8 :]
 
 
 def finish_kernel(planes, groups, sz, meta, *refs):
     count = 2 * planes
     pieces, refs = refs[:count], refs[count:]
-    tiny, lambda_log, lambda_imag, log_step, input_map = refs[:5]
-    grad_gain, grad_skip, grad_log, grad_imag, grad_step, grad_maps, grad_out = refs[5:12]
-    talls, grad_in, lines = refs[12:-2], refs[-2], refs[-1]
+    tiny, lambda_log, lambda_imag, log_step, input_map = refs[0][...] + refs[1][...], *refs[2:6]
+    grad_gain, grad_skip, grad_log, grad_imag, grad_step, grad_maps, grad_out = refs[6:13]
+    talls, grad_in, lines = refs[13:-2], refs[-2], refs[-1]
     own = sz.states // sz.blocks
     lanes = sz.width // LANES
     start = 0
@@ -746,7 +818,7 @@
         for side in range(2):
             half = meta[2] ^ side
             for dist in range(planes):
-                rows = pl.ds(pl.multiple_of((meta[3] ^ dist) * part, part), part)
+                rows = pl.ds(pl.multiple_of((meta[3] ^ farthest(dist, planes)) * part, part), part)
                 tall[rows, :] = pieces[side * planes + dist][start : start + part, :]
             at = 0
             for which, layer, maps in group:
@@ -803,7 +875,7 @@
     part = sz.width // sz.blocks
     copies = []
     for dist, piece in enumerate(pieces):
-        owner = meta[0] ^ dist
+        owner = meta[0] ^ turned(sz, dist)
         for index, out in enumerate(outs):
             slot = dist * len(outs) + index
             wide[slot] = piece[index * part : (index + 1) * part, :].astype(F32)
@@ -856,7 +928,7 @@
         pairs = []
         for c in range(2):
             for b in range(blocks):
-                q = b ^ dist
+                q = b ^ turned(sz, dist)
                 pairs.append((c * blocks + b, (q % 2) * blocks + (q // 2) * 2 + c))
         return lax.ppermute(x, ("core", "block"), [pair[::-1] for pair in pairs] if back else pairs)
 
@@ -875,7 +947,8 @@
         return lax.ppermute(x, ("core", "block"), pairs)
 
     def swap_all(pieces, axis="block"):
-        return [swap(piece, dist, axis) if dist else piece for dist, piece in enumerate(pieces)]
+        count = len(pieces)
+        return [swap(piece, farthest(index, count), axis) if index else piece for index, piece in enumerate(pieces)]
 
     def exchange(send):
         return jnp.stack([neighbour(send[dist - 1], dist) for dist in range(1, chunks)])
@@ -912,38 +985,61 @@
     piece_out = [((part, toks), BF)] * blocks
 
     other_a = swap(maps_a, 1, "core")
-    hidden_a, normed_a = call("open", sz, open_kernel, items, [perm, params, *first_pieces], [rows_b, rows_b], [stacked, mask], time=3)
+    hidden_a, normed_a, live, ahead, behind = call(
+        "open", sz, open_kernel, items, [perm, params, *first_pieces], [rows_b, rows_b, mask, mask, mask], [stacked], time=3)
     w_in_a, driven_a, ends_a, send_a = call(
-        "enter", sz, enter_kernel, items, [params, normed_a, maps_a, other_a], [w_in, drv, enter, snd], [mask, mask, enter])
+        "enter", sz, enter_kernel, items, [ahead, behind, params, normed_a, maps_a, other_a], [w_in, drv, enter, snd], [enter])
     recv = exchange(send_a)
-    second_mine, _ = after(second_mine, send_a)
+    second_mine, recv = after(second_mine, recv)
     second_maps = second_mine, [swap(piece, 1, "core") for piece in second_mine]
     w_out_a, w_in_b, states_a, slope_a, hidden_b, normed_b, driven_b, ends_b, send_b = call(
         "middle", sz, middle_kernel, items,
-        [recv, params, ends_a, driven_a, normed_a, hidden_a, output_map[0], drive_b, *second_maps[0], *second_maps[1]],
-        [w_out, w_in, sts, rows_b, rows_f, rows_b, drv, enter, snd], [mask, mask, mask, enter, rows_f], time=11)
+        [live, ahead, behind, recv, params, ends_a, driven_a, normed_a, hidden_a, output_map[0], drive_b, *second_maps[0], *second_maps[1]],
+        [w_out, w_in, sts, rows_b, rows_f, rows_b, drv, enter, snd], [enter], time=11)
     recv = exchange(send_b)
     cot_cut, _ = after(cot_cut, send_a)
     cot_pieces = across_all(cot_cut)
     recv, cot_pieces = after(recv, cot_pieces)
     w_out_b, states_b, slope_b, *out_pieces = call(
         "leave", sz, leave_kernel, items,
-        [recv, params, ends_b, driven_b, normed_b, hidden_b, perm, output_map[1], *second_maps[0], *second_maps[1]],
-        [w_out, sts, rows_b, *piece_out], [mask, mask, mask, enter, rows_f, rows_b, stacked], time=8)
-
-    def half_grads(name, pairs, counts, first=()):
+        [live, ahead, behind, recv, params, ends_b, driven_b, normed_b, hidden_b, perm, output_map[1], *second_maps[0], *second_maps[1]],
+        [w_out, sts, rows_b, *piece_out], [enter, rows_b, stacked], time=8)
+
+    def half_grads(name, other, pairs, counts, more=(), time=0.0):
         args = [x for pair in pairs for x in pair]
-        shape = [((sum(counts) * states, width), BF)]
-        (send,) = call(name + "_send", sz, partial(weight_kernel, counts, True), [], args, shape, [])
-        send, first = after(send, first)
-        got = swap(send, 1, "core")
-        (keep,) = call(name + "_keep", sz, partial(weight_kernel, counts, False), [], args, shape, [], time=sum(counts))
-        return (keep, got), first
-
-    def fold_core(name, group):
-        total = group[0].shape[0] // states
-        rows = total * own + (16 if len(group) > 2 else 0)
-        return swap_all(call(name, sz, partial(fold_core_kernel, total), [], group, [((rows, width), BF)] * blocks, []))
+        outs = [((sum(counts) * states, width), BF)] + [line] * len(more)
+        return call(name, sz, partial(weight_kernel, counts, other), [], [*args, *more], outs, [], time=time)
+
+    groups = [Group(0, (2,), False), Group(1, (3,), False), Group(2, (1,), True)]
+    steps = bits_of(sz)
+    kept, came, place = {}, {}, {}
+
+    def halve(step, halves=(), tiny=()):
+        old, args = [], []
+        for index, group in enumerate(groups):
+            if 0 < step - group.first < steps:
+                slots = 1 << (steps - (step - group.first))
+                old.append((group, slots, place[step - 1, index]))
+                args.append(kept[index])
+        if old:
+            args.insert(0, came[step - 1])
+        new = groups[step] if step < len(groups) else None
+        outs, at = [], 0
+        for index, group in enumerate(groups):
+            if 0 <= step - group.first < steps:
+                slots = 1 << (steps - 1 - (step - group.first))
+                outs.append((index, ((slots, group.rows(sz), width), F32)))
+                place[step, index] = at
+                at += slots * group.rows(sz)
+        results = call("halve_%d" % step, sz, partial(step_kernel, old, new), [], [*args, *halves, *tiny],
+                       [shape for _, shape in outs] + [((at, width), BF)], [((8, width), F32)] if tiny else [])
+        for (index, _), value in zip(outs, results):
+            kept[index] = value
+        return results[-1]
+
+    def send_step(step, message):
+        pairs = [(c * blocks + b, c * blocks + (b ^ step_bit(sz, step, c))) for c in range(2) for b in range(blocks)]
+        came[step] = lax.ppermute(message, ("core", "block"), pairs)
 
     def spread(pieces):
         return call("spread", sz, spread_kernel, [], pieces, [((micro, part, run), F32)] * 2,
@@ -955,50 +1051,75 @@
         step = max(SEGS * planes // lanes, SEGS)
         return ((lanes * (-(-rows // step) * step), LANES), BF)
 
-    def over_planes(name, groups, rows):
-        talls = [tall_of(n) for n in rows]
-        cut = sum(t[0][0] for t in talls) // planes + 16
-        parts = call(name, sz, partial(fold_block_kernel, planes, rows), [], [x for g in groups for x in g],
-                     [((cut, LANES), BF)] * planes, talls)
-        return swap_all(parts, "plane")
+    def over_planes(name, which):
+        ends = [(groups[index], place[groups[index].first + steps - 1, index]) for index in which]
+        talls = [tall_of(sum(group.counts) * own) for group, _ in ends]
+        cut = sum(t[0][0] for t in talls) // planes + (16 if ends[-1][0].tiny else 0)
+        args = [x for index in which for x in (kept[index], came[groups[index].first + steps - 1])]
+        return swap_all(call(name, sz, partial(fold_block_kernel, planes, ends), [], args, [((cut, LANES), BF)] * planes, talls), "plane")
 
     up_b, twice_b, gstates_b, gskip_b, ends, send = call(
-        "turn", sz, turn_kernel, items, [slope_b, normed_b, w_out_b, params, perm, *cot_pieces],
-        [rows_f, rows_b, gst, line, enter, snd], [stacked, mask, mask, enter], time=6)
+        "turn", sz, turn_kernel, items, [ahead, behind, slope_b, normed_b, w_out_b, params, perm, *cot_pieces],
+        [rows_f, rows_b, gst, line, enter, snd], [stacked, enter], time=6)
     recv = exchange(send)
-    group_a, _ = half_grads("grads_a", [(states_b, twice_b)], (2,))
-    sums_a = fold_core("fold_a", group_a)
-    recv, sums_a[0] = after(recv, sums_a[0])
+    pairs = [(states_b, twice_b)]
+    (send_maps,) = half_grads("grads_a_send", True, pairs, (2,))
+    got = swap(send_maps, 1, "core")
+    (keep,) = half_grads("grads_a_keep", False, pairs, (2,), time=2)
+    message = halve(0, (keep, got))
+    recv, message = after(recv, message)
+    send_step(0, message)
     gdriven_b, gdecay_b, ggain_b, up_a, twice_a, gstates_a, gskip_a, ends, send = call(
         "back_middle", sz, back_middle_kernel, items,
-        [recv, params, ends, gstates_b, states_b, up_b, slope_b, hidden_b, w_in_b, slope_a, normed_a, w_out_a],
-        [((toks, 2 * states), BF), gdec, line, rows_f, rows_b, gst, line, enter, snd], [mask, mask, enter, drv, rows_f], limit=12, time=11)
+        [ahead, behind, recv, params, ends, gstates_b, states_b, up_b, slope_b, hidden_b, w_in_b, slope_a, normed_a, w_out_a],
+        [((toks, 2 * states), BF), gdec, line, rows_f, rows_b, gst, line, enter, snd], [enter, drv], limit=12, time=11)
     recv = exchange(send)
-    gdriven_b, sums_a = after(gdriven_b, sums_a)
-    group_b, _ = half_grads("grads_b", [(gdriven_b, normed_b), (states_a, twice_a)], (1, 2))
-    sums_b = fold_core("fold_b", group_b)
-    recv, sums_b[0] = after(recv, sums_b[0])
-    gdriven_a, tiny, *last_pieces = call(
-        "back_leave", sz, back_leave_kernel, items,
-        [recv, params, ends, gstates_a, states_a, up_a, slope_a, hidden_a, w_in_a, perm, ggain_b, gskip_a, gskip_b, gdecay_b, *out_pieces],
-        [((toks, 2 * states), BF), ((8, width), F32)] + [((2 * part, toks), BF)] * blocks,
-        [mask, mask, enter, drv, rows_f, rows_b, stacked, gdec, line], limit=12, time=9)
-    group_c, sums_b = half_grads("grads_c", [(gdriven_a, normed_a)], (1,), sums_b)
-    sums_c = fold_core("fold_c", [*group_c, tiny, swap(tiny, 1, "core")])
-    parts = over_planes("planes", [sums_a, sums_b, sums_c], (2 * own, 3 * own, own))
+    gdriven_b, came[0] = after(gdriven_b, came[0])
+    pairs = [(gdriven_b, normed_b), (states_a, twice_a)]
+    (send_maps,) = half_grads("grads_b_send", True, pairs, (1, 2))
+    got = swap(send_maps, 1, "core")
+    (keep,) = half_grads("grads_b_keep", False, pairs, (1, 2), time=9)
+    message = halve(1, (keep, got))
+    recv, message = after(recv, message)
+    send_step(1, message)
+    gdriven_a, gdecay_a = call(
+        "back_chain", sz, back_chain_kernel, items, [ahead, behind, recv, params, ends, gstates_a, states_a],
+        [((toks, 2 * states), BF), gdec], [enter, drv], limit=12, time=9)
+    send_maps, terms = half_grads("grads_c_send", True, [(gdriven_a, normed_a)], (1,), [w_in_a])
+    gdriven_a, send_maps, came[1] = after(gdriven_a, send_maps, came[1])
+    got = swap(send_maps, 1, "core")
+    keep, more = half_grads("grads_c_keep", False, [(gdriven_a, normed_a)], (1,), [w_in_a], time=5)
+    message = halve(2, (keep, got), (params, terms, more, ggain_b, gskip_a, gskip_b, gdecay_a, gdecay_b))
+    early_sums = steps <= 2
+    first_parts = over_planes("planes_a", [0]) if early_sums else []
+    gdriven_a, message = after(gdriven_a, message)
+    send_step(2, message)
+    last_pieces = call(
+        "back_leave", sz, back_leave_kernel, [], [params, gdriven_a, up_a, slope_a, hidden_a, w_in_a, perm, *out_pieces],
+        [((2 * part, toks), BF)] * blocks, [rows_b, stacked], limit=12, time=9)
+    last_pieces, came[2], first_parts = after(last_pieces, came[2], first_parts)
+    if not early_sums:
+        first_parts = over_planes("planes_a", [0])
+    for step in range(3, steps + 2):
+        send_step(step, halve(step))
+    parts = over_planes("planes", [1, 2])
     last_pieces, parts[0] = after(last_pieces, parts[0])
     early = [across(piece, 2 * dist, True) for dist, piece in enumerate(last_pieces[0::2])]
-    sum_all, tiny = call("sum", sz, fold_plane_kernel, [], parts, [((parts[0].shape[0] - 16, LANES), BF), ((8, LANES), F32)], [])
+    parts[0], early = after(parts[0], early)
+    sum_all, tiny = call(
+        "sum", sz, partial(fold_plane_kernel, planes), [], [*first_parts, *parts],
+        [((first_parts[0].shape[0] + parts[0].shape[0] - 16, LANES), BF), ((8, LANES), F32)], [])
     whole = swap_all([sum_all] * planes, "plane")
     late, _ = after(last_pieces[1::2], sum_all)
     late = [across(piece, 2 * dist + 1, True) for dist, piece in enumerate(late)]
     output, input_grad = spread([piece for pair in zip(early, late) for piece in pair])
     whole, output = after(whole, output)
     whole += [swap(x, 1, "core") for x in whole]
+    tiny_other = swap(tiny, 1, "core")
     small_out = ((layers, own), F32)
     grad_gain, grad_skip, grad_log, grad_imag, grad_step, grad_in, grad_out = call(
         "finish", sz, partial(finish_kernel, planes, ([(1, 1, 2)], [(0, 1, 1), (1, 0, 2)], [(0, 0, 1)])), [],
-        [*whole, tiny, lambda_log, lambda_imag, log_step, input_map],
+        [*whole, tiny, tiny_other, lambda_log, lambda_imag, log_step, input_map],
         [((layers, part), F32)] * 2 + [small_out] * 3 + [((layers, 2, own, width), F32), ((layers, 4, own, width), F32)],
         [tall_of(n * own) for n in (2, 3, 1)] + [((layers, 2, own, width), F32), ((LANES, LANES), F32)])
     return output, input_grad, grad_gain, grad_log, grad_imag, grad_step, grad_in, grad_out, grad_skip

time: 169 us -> 161 us (0.953)
  Pallas kernels: 63.8 us -> 57 us
  starting transfers between devices: 43.2 us -> 41.5 us
    ppermute x31 -> x25, waiting for transfers between devices: 25.8 us -> 9.03 us  [swap(): lax.ppermute(x, axis, [(i, i ^ dist) for i in range(lax.axis_size(axis))])]
    ppermute x0 -> x4, waiting for transfers between devices: none -> 10.8 us  [send_step(): came[step] = lax.ppermute(message, ('core', 'block'), pairs)]
    pallas_call x23 -> x26, Pallas kernels: 63.8 us -> 57 us  [call(): pl.pallas_call(kernel, out_shape=out_shape, in_specs=[SMEM] * len(items)...]
    ppermute x12, waiting for transfers between devices: 33.1 us -> 39.3 us  [across(): lax.ppermute(x, ('core', 'block'), [pair[::-1] for pair in pairs] if back...]
    ppermute x31 -> x25, starting transfers between devices: 27.3 us -> 22.6 us  [swap(): lax.ppermute(x, axis, [(i, i ^ dist) for i in range(lax.axis_size(axis))])]
    ppermute x0 -> x4, starting transfers between devices: none -> 3.74 us  [send_step(): came[step] = lax.ppermute(message, ('core', 'block'), pairs)]
    ppermute x12, starting transfers between devices: 14.4 us -> 12 us  [across(): lax.ppermute(x, ('core', 'block'), [pair[::-1] for pair in pairs] if back...]
  transfers between devices with their start and end apart: 47 -> 45, of which waited for: 19 -> 17; matrix products, arithmetic and copies ran while one was open for 0% -> 0% of each run, Pallas kernels for 25% -> 24%
where the time goes in v3:
time: 161 us
  waiting for transfers between devices  60.9 us (38%)
  Pallas kernels  57 us (35%)
  starting transfers between devices  41.5 us (26%)
    pallas_call x26, Pallas kernels, call(): pl.pallas_call(kernel, out_shape=out_shape, in_specs=[SMEM] * len(items)...  57 us
    ppermute x12, waiting for transfers between devices, across(): lax.ppermute(x, ('core', 'block'), [pair[::-1] for pair in pairs] if back...  39.3 us
    ppermute x25, starting transfers between devices, swap(): lax.ppermute(x, axis, [(i, i ^ dist) for i in range(lax.axis_size(axis))])  22.6 us
    ppermute x12, starting transfers between devices, across(): lax.ppermute(x, ('core', 'block'), [pair[::-1] for pair in pairs] if back...  12 us
    ppermute x4, waiting for transfers between devices, send_step(): came[step] = lax.ppermute(message, ('core', 'block'), pairs)  10.8 us
    ppermute x25, waiting for transfers between devices, swap(): lax.ppermute(x, axis, [(i, i ^ dist) for i in range(lax.axis_size(axis))])  9.03 us
    ppermute x4, starting transfers between devices, send_step(): came[step] = lax.ppermute(message, ('core', 'block'), pairs)  3.74 us
  transfers between devices with their start and end apart: 45, of which 17 were waited for; matrix products, arithmetic and copies ran while one was open for 0% of the time, Pallas kernels for 24%

profile of v3, /device:TPU:0, one launch (start us, length us, event | category | flops | bytes accessed | tf_op | source)
XLA Modules:
  0.0 161.0 jit_solution(16654167869721779246)
XLA Ops:
  0.6 1.9 %prepare.1 = (bf16[192,1024]{1,0:T(8,128)(2,1)S(1)}, bf16[192,1024]{1,0:T(8,128)(2,1)S(1)}, bf16[192,1024]{1,0:T(8,128)(2,1)S(1)}, bf16[192,1024]{1,0:T(8,128)(2...) custom-call(bf16[2,128,2048]{2,1,0:T(8,128)(2,1)} %refs_0_.2, f32[2,128]{1,0:T(2,128)} %refs_1_.1, ...), custom_call_target="tpu_custom_call" | custom-call | bytes 1000 | tf_op jit(solution)/shard_map/prepare/pallas_call | solution.py:901
  2.5 3.0 %collective-permute-start.1 = (bf16[192,1024]{1,0:T(8,128)(2,1)S(1)}, bf16[192,1024]{1,0:T(8,128)(2,1)S(1)}, u32[]{:S(2)}, u32[]{:S(2)}) collective-permute-start(bf16[192,1024]{1,0:T(8,128)(2,1)S(1)} %get-tuple-element.157), channel_id=1, source_target_pairs={{0,2},{1,6},{2,0},{3,4},{4,3},{5,7},{6,1},{7,5},{8,10},{9,14},{10,... | collective-permute-start | bytes 1179656 | tf_op jit(solution)/shard_map/ppermute | solution.py:933
  7.4 1.6 cut_cotangent.1
  9.4 10.3 %collective-permute-done.1.refs_1_.refs_4_ = bf16[192,1024]{1,0:T(8,128)(2,1)S(1)} collective-permute-done((bf16[192,1024]{1,0:T(8,128)(2,1)S(1)}, bf16[192,1024]{1,0:T(8,128)(2,1)S(1)}, u32[]{:S(2)}, u32[]{:S(2)}) %collective-permute-start.1) | collective-permute-done | bytes 393248 | tf_op jit(solution)/shard_map/ppermute | solution.py:933
  19.7 2.0 %collective-permute-start.6 = (bf16[5,96,512]{2,1,0:T(8,128)(2,1)S(1)}, bf16[5,96,512]{2,1,0:T(8,128)(2,1)S(1)}, u32[]{:S(2)}, u32[]{:S(2)}) collective-permute-start(bf16[5,96,512]{2,1,0:T(8,128)(2,1)S(1)} %get-tuple-element.170), channel_id=1, source_target_pairs={{0,2},{1,3},{2,0},{3,1},{4,6},{5,7},{6,4},{7,5},{8,10},{9,11},{10,... | collective-permute-start | bytes 1474568 | tf_op jit(solution)/shard_map/ppermute | solution.py:925
  21.8 12.6 %collective-permute-done.refs_0_.refs_3_ = bf16[192,1024]{1,0:T(8,128)(2,1)S(1)} collective-permute-done((bf16[192,1024]{1,0:T(8,128)(2,1)S(1)}, bf16[192,1024]{1,0:T(8,128)(2,1)S(1)}, u32[]{:S(2)}, u32[]{:S(2)}) %collective-permute-start) | collective-permute-done | bytes 393248 | tf_op jit(solution)/shard_map/ppermute | solution.py:933
  36.2 2.7 %open.1 = (bf16[1024,512]{1,0:T(8,128)(2,1)S(1)}, bf16[1024,512]{1,0:T(8,128)(2,1)S(1)}, f32[1024,128]{1,0:T(8,128)S(1)}, f32[1024,128]{1,0:T(8,128)S(1)}, f32[1024,128]{1,0:T(8,128)S(1)}) custom-call(s32[2,2,2,2]{3,2,1,0:T(2,128)S(1)} %pad_add_fusion.refs_0_, bf16[1024,1024]{1,0:T(8,128)(2,1)S(1)} %fusion.refs_1_.refs_10_.refs_7_.refs_6_, ...), custom_call_target="tpu_custom_call" | custom-call | flops 1200000000 | bytes 1000 | tf_op jit(solution)/shard_map/open/pallas_call | solution.py:901
  38.9 3.0 %enter.1 = (bf16[768,512]{1,0:T(8,128)(2,1)S(1)}, f32[1024,768]{1,0:T(8,128)S(1)}, f32[4,16,384]{2,1,0:T(8,128)S(1)}, f32[1,2,384]{2,1,0:T(2,128)S(1)}) custom-call(s32[2,2,2,2]{3,2,1,0:T(2,128)S(1)} %pad_add_fusion.refs_0_, f32[1024,128]{1,0:T(8,128)S(1)} %get-tuple-element.167.refs_1_.refs_2_, f32[1024,128]{1,0:T(8,128)S(1)} %get-tuple-element.168.refs_2_.refs_3_, ...), custom_call_target="tpu_custom_call" | custom-call | bytes 1000 | tf_op jit(solution)/shard_map/enter/pallas_call | solution.py:901
  43.1 1.9 %collective-permute-done.6.refs_13_ = bf16[5,96,512]{2,1,0:T(8,128)(2,1)S(1)} collective-permute-done((bf16[5,96,512]{2,1,0:T(8,128)(2,1)S(1)}, bf16[5,96,512]{2,1,0:T(8,128)(2,1)S(1)}, u32[]{:S(2)}, u32[]{:S(2)}) %collective-permute-start.6) | collective-permute-done | bytes 491552 | tf_op jit(solution)/shard_map/ppermute | solution.py:925
  50.6 8.4 %middle.1 = (bf16[1536,512]{1,0:T(8,128)(2,1)S(1)}, bf16[768,512]{1,0:T(8,128)(2,1)S(1)}, bf16[1024,1536]{1,0:T(8,128)(2,1)S(1)}, bf16[1024,512]{1,0:T(8,128)(2,...) custom-call(s32[2,2,2,2]{3,2,1,0:T(2,128)S(1)} %pad_add_fusion.refs_, ...), custom_call_target="tpu_custom_call" | custom-call | flops 4400000000 | bytes 1000 | tf_op jit(solution)/shard_map/middle/pallas_call | solution.py:901
  58.9 2.6 %collective-permute-start.13 = (f32[2,384]{1,0:T(2,128)S(1)}, f32[2,384]{1,0:T(2,128)S(1)}, u32[]{:S(2)}, u32[]{:S(2)}) collective-permute-start(f32[2,384]{1,0:T(2,128)S(1)} %bitcast.21), channel_id=1, source_target_pairs={{0,4},{1,5},{2,6},{3,7},{4,0},{5,1},{6,2},{7,3},{8,12},{9,13},{10,... | collective-permute-start | bytes 9224 | tf_op jit(solution)/shard_map/ppermute | solution.py:947
  62.4 6.4 %leave.1 = (bf16[1536,512]{1,0:T(8,128)(2,1)S(1)}, bf16[1024,1536]{1,0:T(8,128)(2,1)S(1)}, bf16[1024,512]{1,0:T(8,128)(2,1)S(1)}, bf16[128,1024]{1,0:T(8,128)(2,...) custom-call(s32[2,2,2,2]{3,2,1,0:T(2,128)S(1)} %pad_add_fusion.refs_0_, ...), custom_call_target="tpu_custom_call" | custom-call | flops 3200000000 | bytes 1000 | tf_op jit(solution)/shard_map/leave/pallas_call | solution.py:901
  68.8 5.4 %turn.1 = (f32[1024,512]{1,0:T(8,128)S(1)}, bf16[1024,512]{1,0:T(8,128)(2,1)S(1)}, f32[1024,1536]{1,0:T(8,128)S(1)}, f32[1,512]{1,0:T(1,128)S(1)}, f32[4,16,384]{2,1,0:T(8,128)S(1)}, /*index=5*/f32[1,2,384]{2,1,0:T(2,128)S(1)}) custom-call(s32[2,2,2,2]{3,2,1,0:T(2,128)S(1)} %pad_add_fusion.refs_0_, f32[1024,128]{1,0:T(8,128)S(1)} %get-tuple-element.167.refs_1_.refs_2_, ...), custom_call_target="tpu_custom_call" | custom-call | flops 2400000000 | bytes 1000 | tf_op jit(solution)/shard_map/turn/pallas_call | solution.py:901
  78.5 9.2 %back_middle.1 = (bf16[1024,768]{1,0:T(8,128)(2,1)S(1)}, f32[2,384]{1,0:T(2,128)S(1)}, f32[1,512]{1,0:T(1,128)S(1)}, f32[1024,512]{1,0:T(8,128)S(1)}, bf16[1024,...) custom-call(s32[2,2,2,2]{3,2,1,0:T(2,128)S(1)} %pad_add_fusion.refs_, ...), custom_call_target="tpu_custom_call" | custom-call | flops 4400000000 | bytes 1000 | tf_op jit(solution)/shard_map/back_middle/pallas_call | solution.py:901
  87.7 1.4 grads_b_send.1
  89.8 1.4 grads_b_keep.1.refs_2_
  93.6 3.9 %back_chain.1 = (bf16[1024,768]{1,0:T(8,128)(2,1)S(1)}, f32[2,384]{1,0:T(2,128)S(1)}) custom-call(s32[2,2,2,2]{3,2,1,0:T(2,128)S(1)} %pad_add_fusion.refs_0_, f32[1024,128]{1,0:T(8,128)S(1)} %get-tuple-element.167.refs_1_.refs_2_, f32[1024,128]{1,0:T(8,128)S(1)} %get-tuple-element.168.refs_2_.refs_3_, f32[1,2,384]{2,1,0:T(2,128)S(1)} %bitcast.22, ...), custom_call_target="tpu_custom_call" | custom-call | flops 3600000000 | bytes 1000 | tf_op jit(solution)/shard_map/back_chain/pallas_call | solution.py:901
  98.1 6.4 %collective-permute-done.23.refs_0_.refs_1_ = bf16[768,512]{1,0:T(8,128)(2,1)S(1)} collective-permute-done((bf16[768,512]{1,0:T(8,128)(2,1)S(1)}, bf16[768,512]{1,0:T(8,128)(2,1)S(1)}, u32[]{:S(2)}, u32[]{:S(2)}) %collective-permute-start.23) | collective-permute-done | bytes 786464 | tf_op jit(solution)/shard_map/ppermute | solution.py:1042
  106.5 1.4 collective-permute-start.25
  108.0 6.9 %collective-permute-start.26 = (bf16[192,128]{1,0:T(8,128)(2,1)S(1)}, bf16[192,128]{1,0:T(8,128)(2,1)S(1)}, u32[]{:S(2)}, u32[]{:S(2)}) collective-permute-start(bf16[192,128]{1,0:T(8,128)(2,1)S(1)} %get-tuple-element.255), channel_id=1, source_target_pairs={{0,24},{8,16},{16,8},{24,0},{1,25},{9,17},{17,9},{25,1},{2,26},{10... | collective-permute-start | bytes 147464 | tf_op jit(solution)/shard_map/ppermute | solution.py:925
  115.6 3.0 %back_leave.1 = (bf16[256,1024]{1,0:T(8,128)(2,1)S(1)}, bf16[256,1024]{1,0:T(8,128)(2,1)S(1)}, bf16[256,1024]{1,0:T(8,128)(2,1)S(1)}, bf16[256,1024]{1,0:T(8,128)(2,1)S(1)}) custom-call(f32[8,512]{1,0:T(8,128)S(1)} %get-tuple-element.165.refs_2_.refs_3_.refs_5_.refs_6_.refs_4_.refs_0_, bf16[1024,768]{1,0:T(8,128)(2,1)S(1)} %get-tuple-element.242.refs_0_.refs_1_, ...), custom_call_target="tpu_custom_call" | custom-call | flops 3600000000 | bytes 1000 | tf_op jit(solution)/shard_map/back_leave/pallas_call | solution.py:901
  118.5 1.4 collective-permute-done.27.refs_2_
  120.5 4.4 %collective-permute-done.29.refs_3_ = bf16[112,512]{1,0:T(8,128)(2,1)S(1)} collective-permute-done((bf16[112,512]{1,0:T(8,128)(2,1)S(1)}, bf16[112,512]{1,0:T(8,128)(2,1)S(1)}, u32[]{:S(2)}, u32[]{:S(2)}) %collective-permute-start.29) | collective-permute-done | bytes 114720 | tf_op jit(solution)/shard_map/ppermute | solution.py:1042
  126.2 2.9 %collective-permute-start.32 = (bf16[400,128]{1,0:T(8,128)(2,1)S(1)}, bf16[400,128]{1,0:T(8,128)(2,1)S(1)}, u32[]{:S(2)}, u32[]{:S(2)}) collective-permute-start(bf16[400,128]{1,0:T(8,128)(2,1)S(1)} %get-tuple-element.276), channel_id=1, source_target_pairs={{0,24},{8,16},{16,8},{24,0},{1,25},{9,17},{17,9},{25,1},{2,26},{10... | collective-permute-start | bytes 307208 | tf_op jit(solution)/shard_map/ppermute | solution.py:925
  129.2 1.5 collective-permute-start.34
  130.6 6.2 %collective-permute-done.30.refs_0_ = bf16[256,1024]{1,0:T(8,128)(2,1)S(1)} collective-permute-done((bf16[256,1024]{1,0:T(8,128)(2,1)S(1)}, bf16[256,1024]{1,0:T(8,128)(2,1)S(1)}, u32[]{:S(2)}, u32[]{:S(2)}) %collective-permute-start.30) | collective-permute-done | bytes 524320 | tf_op jit(solution)/shard_map/ppermute | solution.py:933
  136.8 1.8 %collective-permute-done.31.refs_2_ = bf16[256,1024]{1,0:T(8,128)(2,1)S(1)} collective-permute-done((bf16[256,1024]{1,0:T(8,128)(2,1)S(1)}, bf16[256,1024]{1,0:T(8,128)(2,1)S(1)}, u32[]{:S(2)}, u32[]{:S(2)}) %collective-permute-start.31) | collective-permute-done | bytes 524320 | tf_op jit(solution)/shard_map/ppermute | solution.py:933
  138.7 1.3 collective-permute-start.38
  141.8 2.6 %collective-permute-start.36 = (bf16[576,128]{1,0:T(8,128)(2,1)S(1)}, bf16[576,128]{1,0:T(8,128)(2,1)S(1)}, u32[]{:S(2)}, u32[]{:S(2)}) collective-permute-start(bf16[576,128]{1,0:T(8,128)(2,1)S(1)} %get-tuple-element.289.refs_0_), channel_id=1, source_target_pairs={{0,16},{8,24},{16,0},{24,8},{1,17},{9,25},{17,1},{25,9},{2,18},{10... | collective-permute-start | bytes 442376 | tf_op jit(solution)/shard_map/ppermute | solution.py:925
  145.2 8.4 %collective-permute-done.38.refs_1_ = bf16[256,1024]{1,0:T(8,128)(2,1)S(1)} collective-permute-done((bf16[256,1024]{1,0:T(8,128)(2,1)S(1)}, bf16[256,1024]{1,0:T(8,128)(2,1)S(1)}, u32[]{:S(2)}, u32[]{:S(2)}) %collective-permute-start.38) | collective-permute-done | bytes 524320 | tf_op jit(solution)/shard_map/ppermute | solution.py:933
  153.6 2.1 %spread.1 = (f32[2,128,2048]{2,1,0:T(8,128)}, f32[2,128,2048]{2,1,0:T(8,128)}) custom-call(bf16[256,1024]{1,0:T(8,128)(2,1)S(1)} %collective-permute-done.30.refs_0_, bf16[256,1024]{1,0:T(8,128)(2,1)S(1)} %collective-permute-done.38.refs_1_, bf16[256,1024]{1,0:T(8,128)(2,1)S(1)} %collective-permute-done.31.refs_2_, ...), custom_call_target="tpu_custom_call" | custom-call | bytes 1000 | tf_op jit(solution)/shard_map/spread/pallas_call | solution.py:901
  158.9 2.1 %finish.1 = (f32[2,128]{1,0:T(2,128)}, f32[2,128]{1,0:T(2,128)}, f32[2,96]{1,0:T(2,128)}, f32[2,96]{1,0:T(2,128)}, f32[2,96]{1,0:T(2,128)}, /*index=5*/f32[2,2,96,512]{3,2,1,0:T(8,128)}, f32[2,4,96,512]{3,2,1,0:T(8,128)}) custom-call(bf16[576,128]{1,0:T(8,128)(2,1)S(1)} %get-tuple-element.289.refs_0_, bf16[576,128]{1,0:T(8,128)(2,1)S(1)} %collective-permute-done.35.refs_1_, ...), custom_call_target="tpu_custom_call" | custom-call | bytes 1000 | tf_op jit(solution)/shard_map/finish/pallas_call | solution.py:901
  (103 shorter events, 29.8 us)
Async XLA Ops:
  2.5 17.2 %collective-permute-start.1 = (bf16[192,1024]{1,0:T(8,128)(2,1)S(1)}, bf16[192,1024]{1,0:T(8,128)(2,1)S(1)}, u32[]{:S(2)}, u32[]{:S(2)}) collective-permute-start(bf16[192,1024]{1,0:T(8,128)(2,1)S(1)} %get-tuple-element.157), channel_id=1, source_target_pairs={{0,2},{1,6},{2,0},{3,4},{4,3},{5,7},{6,1},{7,5},{8,10},{9,14},{10,... | collective-permute-start | bytes 1179656 | tf_op jit(solution)/shard_map/ppermute | solution.py:933
  5.6 28.8 %collective-permute-start = (bf16[192,1024]{1,0:T(8,128)(2,1)S(1)}, bf16[192,1024]{1,0:T(8,128)(2,1)S(1)}, u32[]{:S(2)}, u32[]{:S(2)}) collective-permute-start(bf16[192,1024]{1,0:T(8,128)(2,1)S(1)} %get-tuple-element.155), channel_id=1, source_target_pairs={{0,6},{1,2},{2,4},{3,0},{4,7},{5,3},{6,5},{7,1},{8,14},{9,10},{10,... | collective-permute-start | bytes 1179656 | tf_op jit(solution)/shard_map/ppermute | solution.py:933
  6.7 27.7 %collective-permute-start.2 = (bf16[192,1024]{1,0:T(8,128)(2,1)S(1)}, bf16[192,1024]{1,0:T(8,128)(2,1)S(1)}, u32[]{:S(2)}, u32[]{:S(2)}) collective-permute-start(bf16[192,1024]{1,0:T(8,128)(2,1)S(1)} %get-tuple-element.163), channel_id=1, source_target_pairs={{0,4},{1,0},{2,6},{3,2},{4,5},{5,1},{6,7},{7,3},{8,12},{9,8},{10,1... | collective-permute-start | bytes 1179656 | tf_op jit(solution)/shard_map/ppermute | solution.py:933
  6.7 27.7 %collective-permute-start.3 = (bf16[192,1024]{1,0:T(8,128)(2,1)S(1)}, bf16[192,1024]{1,0:T(8,128)(2,1)S(1)}, u32[]{:S(2)}, u32[]{:S(2)}) collective-permute-start(bf16[192,1024]{1,0:T(8,128)(2,1)S(1)} %get-tuple-element.164), channel_id=1, source_target_pairs={{0,0},{1,4},{2,2},{3,6},{4,1},{5,5},{6,3},{7,7},{8,8},{9,12},{10,1... | collective-permute-start | bytes 1179656 | tf_op jit(solution)/shard_map/ppermute | solution.py:933
  19.7 23.4 %collective-permute-start.7 = (bf16[5,96,512]{2,1,0:T(8,128)(2,1)S(1)}, bf16[5,96,512]{2,1,0:T(8,128)(2,1)S(1)}, u32[]{:S(2)}, u32[]{:S(2)}) collective-permute-start(bf16[5,96,512]{2,1,0:T(8,128)(2,1)S(1)} %get-tuple-element.170), channel_id=1, source_target_pairs={{0,3},{1,2},{2,1},{3,0},{4,7},{5,6},{6,5},{7,4},{8,11},{9,10},{10,... | collective-permute-start | bytes 1474568 | tf_op jit(solution)/shard_map/ppermute | solution.py:925
  19.7 25.3 %collective-permute-start.6 = (bf16[5,96,512]{2,1,0:T(8,128)(2,1)S(1)}, bf16[5,96,512]{2,1,0:T(8,128)(2,1)S(1)}, u32[]{:S(2)}, u32[]{:S(2)}) collective-permute-start(bf16[5,96,512]{2,1,0:T(8,128)(2,1)S(1)} %get-tuple-element.170), channel_id=1, source_target_pairs={{0,2},{1,3},{2,0},{3,1},{4,6},{5,7},{6,4},{7,5},{8,10},{9,11},{10,... | collective-permute-start | bytes 1474568 | tf_op jit(solution)/shard_map/ppermute | solution.py:925
  34.4 11.6 %collective-permute-start.5 = (bf16[5,96,512]{2,1,0:T(8,128)(2,1)S(1)}, bf16[5,96,512]{2,1,0:T(8,128)(2,1)S(1)}, u32[]{:S(2)}, u32[]{:S(2)}) collective-permute-start(bf16[5,96,512]{2,1,0:T(8,128)(2,1)S(1)} %get-tuple-element.170), channel_id=1, source_target_pairs={{0,1},{1,0},{2,3},{3,2},{4,5},{5,4},{6,7},{7,6},{8,9},{9,8},{10,11... | collective-permute-start | bytes 1474568 | tf_op jit(solution)/shard_map/ppermute | solution.py:925
  34.5 4.4 %collective-permute-start.8 = (bf16[384,512]{1,0:T(8,128)(2,1)S(1)}, bf16[384,512]{1,0:T(8,128)(2,1)S(1)}, u32[]{:S(2)}, u32[]{:S(2)}) collective-permute-start(bf16[384,512]{1,0:T(8,128)(2,1)S(1)} %get-tuple-element.172.refs_5_), channel_id=1, source_target_pairs={{0,4},{4,0},{1,5},{5,1},{2,6},{6,2},{3,7},{7,3},{8,12},{12,8},{9,1... | collective-permute-start | bytes 1179656 | tf_op jit(solution)/shard_map/ppermute | solution.py:925
  46.0 3.7 %collective-permute-start.11 = (bf16[5,96,512]{2,1,0:T(8,128)(2,1)S(1)}, bf16[5,96,512]{2,1,0:T(8,128)(2,1)S(1)}, u32[]{:S(2)}, u32[]{:S(2)}) collective-permute-start(bf16[5,96,512]{2,1,0:T(8,128)(2,1)S(1)} %collective-permute-done.6.refs_13_), channel_id=1, source_target_pairs={{0,4},{4,0},{1,5},{5,1},{2,6},{6,2},{3,7},{7,3},{8,12},{12,8},{9,1... | collective-permute-start | bytes 1474568 | tf_op jit(solution)/shard_map/ppermute | solution.py:925
  46.5 4.1 %collective-permute-start.12 = (bf16[5,96,512]{2,1,0:T(8,128)(2,1)S(1)}, bf16[5,96,512]{2,1,0:T(8,128)(2,1)S(1)}, u32[]{:S(2)}, u32[]{:S(2)}) collective-permute-start(bf16[5,96,512]{2,1,0:T(8,128)(2,1)S(1)} %collective-permute-done.7.refs_14_), channel_id=1, source_target_pairs={{0,4},{4,0},{1,5},{5,1},{2,6},{6,2},{3,7},{7,3},{8,12},{12,8},{9,1... | collective-permute-start | bytes 1474568 | tf_op jit(solution)/shard_map/ppermute | solution.py:925
  46.6 15.0 %collective-permute-start.14 = (bf16[128,1024]{1,0:T(8,128)(2,1)S(1)}, bf16[128,1024]{1,0:T(8,128)(2,1)S(1)}, u32[]{:S(2)}, u32[]{:S(2)}) collective-permute-start(bf16[128,1024]{1,0:T(8,128)(2,1)S(1)} %get-tuple-element.187), channel_id=1, source_target_pairs={{0,6},{1,2},{2,4},{3,0},{4,7},{5,3},{6,5},{7,1},{8,14},{9,10},{10,... | collective-permute-start | bytes 786440 | tf_op jit(solution)/shard_map/ppermute | solution.py:933
  47.8 13.8 %collective-permute-start.15 = (bf16[128,1024]{1,0:T(8,128)(2,1)S(1)}, bf16[128,1024]{1,0:T(8,128)(2,1)S(1)}, u32[]{:S(2)}, u32[]{:S(2)}) collective-permute-start(bf16[128,1024]{1,0:T(8,128)(2,1)S(1)} %get-tuple-element.188), channel_id=1, source_target_pairs={{0,2},{1,6},{2,0},{3,4},{4,3},{5,7},{6,1},{7,5},{8,10},{9,14},{10,... | collective-permute-start | bytes 786440 | tf_op jit(solution)/shard_map/ppermute | solution.py:933
  48.8 12.8 %collective-permute-start.16 = (bf16[128,1024]{1,0:T(8,128)(2,1)S(1)}, bf16[128,1024]{1,0:T(8,128)(2,1)S(1)}, u32[]{:S(2)}, u32[]{:S(2)}) collective-permute-start(bf16[128,1024]{1,0:T(8,128)(2,1)S(1)} %get-tuple-element.189), channel_id=1, source_target_pairs={{0,4},{1,0},{2,6},{3,2},{4,5},{5,1},{6,7},{7,3},{8,12},{9,8},{10,1... | collective-permute-start | bytes 786440 | tf_op jit(solution)/shard_map/ppermute | solution.py:933
  49.7 11.9 %collective-permute-start.17 = (bf16[128,1024]{1,0:T(8,128)(2,1)S(1)}, bf16[128,1024]{1,0:T(8,128)(2,1)S(1)}, u32[]{:S(2)}, u32[]{:S(2)}) collective-permute-start(bf16[128,1024]{1,0:T(8,128)(2,1)S(1)} %get-tuple-element.190), channel_id=1, source_target_pairs={{0,0},{1,4},{2,2},{3,6},{4,1},{5,5},{6,3},{7,7},{8,8},{9,12},{10,1... | collective-permute-start | bytes 786440 | tf_op jit(solution)/shard_map/ppermute | solution.py:933
  58.9 3.4 %collective-permute-start.13 = (f32[2,384]{1,0:T(2,128)S(1)}, f32[2,384]{1,0:T(2,128)S(1)}, u32[]{:S(2)}, u32[]{:S(2)}) collective-permute-start(f32[2,384]{1,0:T(2,128)S(1)} %bitcast.21), channel_id=1, source_target_pairs={{0,4},{1,5},{2,6},{3,7},{4,0},{5,1},{6,2},{7,3},{8,12},{9,13},{10,... | collective-permute-start | bytes 9224 | tf_op jit(solution)/shard_map/ppermute | solution.py:947
  77.8 10.0 %collective-permute-start.21 = (bf16[384,512]{1,0:T(8,128)(2,1)S(1)}, bf16[384,512]{1,0:T(8,128)(2,1)S(1)}, u32[]{:S(2)}, u32[]{:S(2)}) collective-permute-start(bf16[384,512]{1,0:T(8,128)(2,1)S(1)} %get-tuple-element.215), channel_id=1, source_target_pairs={{0,1},{1,0},{2,3},{3,2},{4,6},{5,7},{6,4},{7,5},{8,9},{9,8},{10,11... | collective-permute-start | bytes 1179656 | tf_op jit(solution)/shard_map/ppermute | solution.py:1042
  92.4 12.1 %collective-permute-start.23 = (bf16[768,512]{1,0:T(8,128)(2,1)S(1)}, bf16[768,512]{1,0:T(8,128)(2,1)S(1)}, u32[]{:S(2)}, u32[]{:S(2)}) collective-permute-start(bf16[768,512]{1,0:T(8,128)(2,1)S(1)} %get-tuple-element.228), channel_id=1, source_target_pairs={{0,2},{1,3},{2,0},{3,1},{4,5},{5,4},{6,7},{7,6},{8,10},{9,11},{10,... | collective-permute-start | bytes 2359304 | tf_op jit(solution)/shard_map/ppermute | solution.py:1042
  106.5 13.4 %collective-permute-start.25 = (bf16[512,512]{1,0:T(8,128)(2,1)S(1)}, bf16[512,512]{1,0:T(8,128)(2,1)S(1)}, u32[]{:S(2)}, u32[]{:S(2)}) collective-permute-start(bf16[512,512]{1,0:T(8,128)(2,1)S(1)} %get-tuple-element.252), channel_id=1, source_target_pairs={{0,1},{1,0},{2,3},{3,2},{4,6},{5,7},{6,4},{7,5},{8,9},{9,8},{10,11... | collective-permute-start | bytes 1572872 | tf_op jit(solution)/shard_map/ppermute | solution.py:1042
  108.0 10.5 %collective-permute-start.26 = (bf16[192,128]{1,0:T(8,128)(2,1)S(1)}, bf16[192,128]{1,0:T(8,128)(2,1)S(1)}, u32[]{:S(2)}, u32[]{:S(2)}) collective-permute-start(bf16[192,128]{1,0:T(8,128)(2,1)S(1)} %get-tuple-element.255), channel_id=1, source_target_pairs={{0,24},{8,16},{16,8},{24,0},{1,25},{9,17},{17,9},{25,1},{2,26},{10... | collective-permute-start | bytes 147464 | tf_op jit(solution)/shard_map/ppermute | solution.py:925
  114.9 5.0 %collective-permute-start.27 = (bf16[192,128]{1,0:T(8,128)(2,1)S(1)}, bf16[192,128]{1,0:T(8,128)(2,1)S(1)}, u32[]{:S(2)}, u32[]{:S(2)}) collective-permute-start(bf16[192,128]{1,0:T(8,128)(2,1)S(1)} %get-tuple-element.256), channel_id=1, source_target_pairs={{0,16},{8,24},{16,0},{24,8},{1,17},{9,25},{17,1},{25,9},{2,18},{10... | collective-permute-start | bytes 147464 | tf_op jit(solution)/shard_map/ppermute | solution.py:925
  114.9 5.0 %collective-permute-start.28 = (bf16[192,128]{1,0:T(8,128)(2,1)S(1)}, bf16[192,128]{1,0:T(8,128)(2,1)S(1)}, u32[]{:S(2)}, u32[]{:S(2)}) collective-permute-start(bf16[192,128]{1,0:T(8,128)(2,1)S(1)} %get-tuple-element.257), channel_id=1, source_target_pairs={{0,8},{8,0},{16,24},{24,16},{1,9},{9,1},{17,25},{25,17},{2,10},{10... | collective-permute-start | bytes 147464 | tf_op jit(solution)/shard_map/ppermute | solution.py:925
  120.0 4.9 %collective-permute-start.29 = (bf16[112,512]{1,0:T(8,128)(2,1)S(1)}, bf16[112,512]{1,0:T(8,128)(2,1)S(1)}, u32[]{:S(2)}, u32[]{:S(2)}) collective-permute-start(bf16[112,512]{1,0:T(8,128)(2,1)S(1)} %get-tuple-element.270), channel_id=1, source_target_pairs={{0,2},{1,3},{2,0},{3,1},{4,5},{5,4},{6,7},{7,6},{8,10},{9,11},{10,... | collective-permute-start | bytes 344072 | tf_op jit(solution)/shard_map/ppermute | solution.py:1042
  125.0 11.8 %collective-permute-start.30 = (bf16[256,1024]{1,0:T(8,128)(2,1)S(1)}, bf16[256,1024]{1,0:T(8,128)(2,1)S(1)}, u32[]{:S(2)}, u32[]{:S(2)}) collective-permute-start(bf16[256,1024]{1,0:T(8,128)(2,1)S(1)} %get-tuple-element.273), channel_id=1, source_target_pairs={{6,0},{2,1},{4,2},{0,3},{7,4},{3,5},{5,6},{1,7},{14,8},{10,9},{12,... | collective-permute-start | bytes 1572872 | tf_op jit(solution)/shard_map/ppermute | solution.py:933
  126.2 12.4 %collective-permute-start.31 = (bf16[256,1024]{1,0:T(8,128)(2,1)S(1)}, bf16[256,1024]{1,0:T(8,128)(2,1)S(1)}, u32[]{:S(2)}, u32[]{:S(2)}) collective-permute-start(bf16[256,1024]{1,0:T(8,128)(2,1)S(1)} %get-tuple-element.274), channel_id=1, source_target_pairs={{4,0},{0,1},{6,2},{2,3},{5,4},{1,5},{7,6},{3,7},{12,8},{8,9},{14,1... | collective-permute-start | bytes 1572872 | tf_op jit(solution)/shard_map/ppermute | solution.py:933
  126.2 12.4 %collective-permute-start.32 = (bf16[400,128]{1,0:T(8,128)(2,1)S(1)}, bf16[400,128]{1,0:T(8,128)(2,1)S(1)}, u32[]{:S(2)}, u32[]{:S(2)}) collective-permute-start(bf16[400,128]{1,0:T(8,128)(2,1)S(1)} %get-tuple-element.276), channel_id=1, source_target_pairs={{0,24},{8,16},{16,8},{24,0},{1,25},{9,17},{17,9},{25,1},{2,26},{10... | collective-permute-start | bytes 307208 | tf_op jit(solution)/shard_map/ppermute | solution.py:925
  129.1 9.5 %collective-permute-start.33 = (bf16[400,128]{1,0:T(8,128)(2,1)S(1)}, bf16[400,128]{1,0:T(8,128)(2,1)S(1)}, u32[]{:S(2)}, u32[]{:S(2)}) collective-permute-start(bf16[400,128]{1,0:T(8,128)(2,1)S(1)} %get-tuple-element.277), channel_id=1, source_target_pairs={{0,16},{8,24},{16,0},{24,8},{1,17},{9,25},{17,1},{25,9},{2,18},{10... | collective-permute-start | bytes 307208 | tf_op jit(solution)/shard_map/ppermute | solution.py:925
  129.2 9.5 %collective-permute-start.34 = (bf16[400,128]{1,0:T(8,128)(2,1)S(1)}, bf16[400,128]{1,0:T(8,128)(2,1)S(1)}, u32[]{:S(2)}, u32[]{:S(2)}) collective-permute-start(bf16[400,128]{1,0:T(8,128)(2,1)S(1)} %get-tuple-element.278), channel_id=1, source_target_pairs={{0,8},{8,0},{16,24},{24,16},{1,9},{9,1},{17,25},{25,17},{2,10},{10... | collective-permute-start | bytes 307208 | tf_op jit(solution)/shard_map/ppermute | solution.py:925
  138.7 14.9 %collective-permute-start.38 = (bf16[256,1024]{1,0:T(8,128)(2,1)S(1)}, bf16[256,1024]{1,0:T(8,128)(2,1)S(1)}, u32[]{:S(2)}, u32[]{:S(2)}) collective-permute-start(bf16[256,1024]{1,0:T(8,128)(2,1)S(1)} %get-tuple-element.283), channel_id=1, source_target_pairs={{2,0},{6,1},{0,2},{4,3},{3,4},{7,5},{1,6},{5,7},{10,8},{14,9},{8,1... | collective-permute-start | bytes 1572872 | tf_op jit(solution)/shard_map/ppermute | solution.py:933
  140.0 13.5 %collective-permute-start.39 = (bf16[256,1024]{1,0:T(8,128)(2,1)S(1)}, bf16[256,1024]{1,0:T(8,128)(2,1)S(1)}, u32[]{:S(2)}, u32[]{:S(2)}) collective-permute-start(bf16[256,1024]{1,0:T(8,128)(2,1)S(1)} %get-tuple-element.285), channel_id=1, source_target_pairs={{0,0},{4,1},{2,2},{6,3},{1,4},{5,5},{3,6},{7,7},{8,8},{12,9},{10,1... | collective-permute-start | bytes 1572872 | tf_op jit(solution)/shard_map/ppermute | solution.py:933
  140.7 15.0 %collective-permute-start.37 = (bf16[576,128]{1,0:T(8,128)(2,1)S(1)}, bf16[576,128]{1,0:T(8,128)(2,1)S(1)}, u32[]{:S(2)}, u32[]{:S(2)}) collective-permute-start(bf16[576,128]{1,0:T(8,128)(2,1)S(1)} %get-tuple-element.289.refs_0_), channel_id=1, source_target_pairs={{0,8},{8,0},{16,24},{24,16},{1,9},{9,1},{17,25},{25,17},{2,10},{10... | collective-permute-start | bytes 442376 | tf_op jit(solution)/shard_map/ppermute | solution.py:925
  141.8 13.8 %collective-permute-start.36 = (bf16[576,128]{1,0:T(8,128)(2,1)S(1)}, bf16[576,128]{1,0:T(8,128)(2,1)S(1)}, u32[]{:S(2)}, u32[]{:S(2)}) collective-permute-start(bf16[576,128]{1,0:T(8,128)(2,1)S(1)} %get-tuple-element.289.refs_0_), channel_id=1, source_target_pairs={{0,16},{8,24},{16,0},{24,8},{1,17},{9,25},{17,1},{25,9},{2,18},{10... | collective-permute-start | bytes 442376 | tf_op jit(solution)/shard_map/ppermute | solution.py:925
  144.4 11.3 %collective-permute-start.35 = (bf16[576,128]{1,0:T(8,128)(2,1)S(1)}, bf16[576,128]{1,0:T(8,128)(2,1)S(1)}, u32[]{:S(2)}, u32[]{:S(2)}) collective-permute-start(bf16[576,128]{1,0:T(8,128)(2,1)S(1)} %get-tuple-element.289.refs_0_), channel_id=1, source_target_pairs={{0,24},{8,16},{16,8},{24,0},{1,25},{9,17},{17,9},{25,1},{2,26},{10... | collective-permute-start | bytes 442376 | tf_op jit(solution)/shard_map/ppermute | solution.py:925
  (20 other events, 241.3 us)

commit v4 on v3

--- a/solution.py
+++ b/solution.py
@@ -556,15 +556,19 @@
     send_ends(sz, meta, decay, ends, enter, send)
 
 
-def middle_kernel(sz, meta, live, ahead, behind, recv, params, ends, driven, normed, hidden, own_out, own_in, *refs):
-    decay, skip, gain_b, decay_b = decay_of(sz, params, 0), skip_of(params, 0), gain_of(params, 1), decay_of(sz, params, 1)
+def chain_kernel(sz, meta, ahead, behind, recv, params, ends, driven, states, enter):
+    decay = decay_of(sz, params, 0)
+    enter_chunk(sz, meta, recv, decay, ends, enter)
+    chain_states(sz, decay, ahead, behind, driven, enter, states)
+
+
+def middle_kernel(sz, meta, live, ahead, behind, states, params, normed, hidden, own_out, own_in, *refs):
+    skip, gain_b, decay_b = skip_of(params, 0), gain_of(params, 1), decay_of(sz, params, 1)
     far = sz.blocks - 1
     mine, other, refs = refs[:far], refs[far : 2 * far], refs[2 * far :]
-    w_out, w_in_b, states, slope, hidden_b, normed_b, driven_b, ends_b, send_b, enter = refs
+    w_out, w_in_b, slope, hidden_b, normed_b, driven_b, ends_b, send_b, enter = refs
     place_maps(sz, meta, own_out, mine, other, 0, w_out)
     place_maps(sz, meta, own_in, mine, other, 2, w_in_b)
-    enter_chunk(sz, meta, recv, decay, ends, enter)
-    chain_states(sz, decay, ahead, behind, driven, enter, states)
     for rows in row_parts(sz):
         on = widen(live[rows, :], sz.width // LANES)
         u = hidden[rows, :].astype(F32) + finish_rows(sz, rows, states, w_out, skip, normed, on, slope)
@@ -990,16 +994,20 @@
     w_in_a, driven_a, ends_a, send_a = call(
         "enter", sz, enter_kernel, items, [ahead, behind, params, normed_a, maps_a, other_a], [w_in, drv, enter, snd], [enter])
     recv = exchange(send_a)
-    second_mine, recv = after(second_mine, recv)
+    (states_a,) = call("chain", sz, chain_kernel, items, [ahead, behind, recv, params, ends_a, driven_a], [sts], [enter])
+    second_mine, states_a = after(second_mine, states_a)
     second_maps = second_mine, [swap(piece, 1, "core") for piece in second_mine]
-    w_out_a, w_in_b, states_a, slope_a, hidden_b, normed_b, driven_b, ends_b, send_b = call(
+    cot_early, _ = after(cot_cut[0::2], recv)
+    cot_early = [across(piece, 2 * index, False) for index, piece in enumerate(cot_early)]
+    w_out_a, w_in_b, slope_a, hidden_b, normed_b, driven_b, ends_b, send_b = call(
         "middle", sz, middle_kernel, items,
-        [live, ahead, behind, recv, params, ends_a, driven_a, normed_a, hidden_a, output_map[0], drive_b, *second_maps[0], *second_maps[1]],
-        [w_out, w_in, sts, rows_b, rows_f, rows_b, drv, enter, snd], [enter], time=11)
+        [live, ahead, behind, states_a, params, normed_a, hidden_a, output_map[0], drive_b, *second_maps[0], *second_maps[1]],
+        [w_out, w_in, rows_b, rows_f, rows_b, drv, enter, snd], [enter], time=11)
+    send_b, cot_early = after(send_b, cot_early)
     recv = exchange(send_b)
-    cot_cut, _ = after(cot_cut, send_a)
-    cot_pieces = across_all(cot_cut)
-    recv, cot_pieces = after(recv, cot_pieces)
+    cot_late, _ = after(cot_cut[1::2], send_b)
+    cot_late = [across(piece, 2 * index + 1, False) for index, piece in enumerate(cot_late)]
+    cot_pieces = [piece for pair in zip(cot_early, cot_late) for piece in pair]
     w_out_b, states_b, slope_b, *out_pieces = call(
         "leave", sz, leave_kernel, items,
         [live, ahead, behind, recv, params, ends_b, driven_b, normed_b, hidden_b, perm, output_map[1], *second_maps[0], *second_maps[1]],
@@ -1086,18 +1094,19 @@
         "back_chain", sz, back_chain_kernel, items, [ahead, behind, recv, params, ends, gstates_a, states_a],
         [((toks, 2 * states), BF), gdec], [enter, drv], limit=12, time=9)
     send_maps, terms = half_grads("grads_c_send", True, [(gdriven_a, normed_a)], (1,), [w_in_a])
-    gdriven_a, send_maps, came[1] = after(gdriven_a, send_maps, came[1])
+    gdriven_a, send_maps = after(gdriven_a, send_maps)
     got = swap(send_maps, 1, "core")
+    last_pieces = call(
+        "back_leave", sz, back_leave_kernel, [], [params, gdriven_a, up_a, slope_a, hidden_a, w_in_a, perm, *out_pieces],
+        [((2 * part, toks), BF)] * blocks, [rows_b, stacked], limit=12, time=3)
+    last_pieces, gdriven_a, came[1] = after(last_pieces, gdriven_a, came[1])
     keep, more = half_grads("grads_c_keep", False, [(gdriven_a, normed_a)], (1,), [w_in_a], time=5)
     message = halve(2, (keep, got), (params, terms, more, ggain_b, gskip_a, gskip_b, gdecay_a, gdecay_b))
     early_sums = steps <= 2
+    kept[0], message = after(kept[0], message)
     first_parts = over_planes("planes_a", [0]) if early_sums else []
-    gdriven_a, message = after(gdriven_a, message)
     send_step(2, message)
-    last_pieces = call(
-        "back_leave", sz, back_leave_kernel, [], [params, gdriven_a, up_a, slope_a, hidden_a, w_in_a, perm, *out_pieces],
-        [((2 * part, toks), BF)] * blocks, [rows_b, stacked], limit=12, time=9)
-    last_pieces, came[2], first_parts = after(last_pieces, came[2], first_parts)
+    came[2], first_parts = after(came[2], first_parts)
     if not early_sums:
         first_parts = over_planes("planes_a", [0])
     for step in range(3, steps + 2):
@@ -1113,9 +1122,11 @@
     late, _ = after(last_pieces[1::2], sum_all)
     late = [across(piece, 2 * dist + 1, True) for dist, piece in enumerate(late)]
     output, input_grad = spread([piece for pair in zip(early, late) for piece in pair])
-    whole, output = after(whole, output)
-    whole += [swap(x, 1, "core") for x in whole]
-    tiny_other = swap(tiny, 1, "core")
+    sum_all, tiny, output = after(sum_all, tiny, output)
+    others = [swap(x, 1, "core") for x in (sum_all, tiny)]
+    whole, others = after(whole, others)
+    whole += [others[0], *(swap(x, 1, "core") for x in whole[1:])]
+    tiny_other = others[1]
     small_out = ((layers, own), F32)
     grad_gain, grad_skip, grad_log, grad_imag, grad_step, grad_in, grad_out = call(
         "finish", sz, partial(finish_kernel, planes, ([(1, 1, 2)], [(0, 1, 1), (1, 0, 2)], [(0, 0, 1)])), [],

time: 161 us -> 159 us (0.988)
  starting transfers between devices: 41.5 us -> 39 us
    ppermute x4, waiting for transfers between devices: 10.8 us -> 8.28 us  [send_step(): came[step] = lax.ppermute(message, ('core', 'block'), pairs)]
    ppermute x12, waiting for transfers between devices: 39.3 us -> 41.7 us  [across(): lax.ppermute(x, ('core', 'block'), [pair[::-1] for pair in pairs] if back...]
    ppermute x4, starting transfers between devices: 3.15 us -> 0.79 us  [neighbour(): return lax.ppermute(x, ('core', 'block'), pairs)]
    pallas_call x26 -> x27, Pallas kernels: 57 us -> 57.3 us  [call(): pl.pallas_call(kernel, out_shape=out_shape, in_specs=[SMEM] * len(items)...]
  transfers between devices with their start and end apart: 45 -> 45, of which waited for: 17 -> 20; matrix products, arithmetic and copies ran while one was open for 0% -> 0% of each run, Pallas kernels for 24% -> 28%
where the time goes in v4:
time: 159 us
  waiting for transfers between devices  60.8 us (38%)
  Pallas kernels  57.3 us (36%)
  starting transfers between devices  39 us (25%)
    pallas_call x27, Pallas kernels, call(): pl.pallas_call(kernel, out_shape=out_shape, in_specs=[SMEM] * len(items)...  57.3 us
    ppermute x12, waiting for transfers between devices, across(): lax.ppermute(x, ('core', 'block'), [pair[::-1] for pair in pairs] if back...  41.7 us
    ppermute x25, starting transfers between devices, swap(): lax.ppermute(x, axis, [(i, i ^ dist) for i in range(lax.axis_size(axis))])  21.5 us
    ppermute x12, starting transfers between devices, across(): lax.ppermute(x, ('core', 'block'), [pair[::-1] for pair in pairs] if back...  13.3 us
    ppermute x25, waiting for transfers between devices, swap(): lax.ppermute(x, axis, [(i, i ^ dist) for i in range(lax.axis_size(axis))])  9.8 us
    ppermute x4, waiting for transfers between devices, send_step(): came[step] = lax.ppermute(message, ('core', 'block'), pairs)  8.28 us
    ppermute x4, starting transfers between devices, send_step(): came[step] = lax.ppermute(message, ('core', 'block'), pairs)  3.44 us
  transfers between devices with their start and end apart: 45, of which 20 were waited for; matrix products, arithmetic and copies ran while one was open for 0% of the time, Pallas kernels for 28%

profile of v4, /device:TPU:0, one launch (start us, length us, event | category | flops | bytes accessed | tf_op | source)
XLA Modules:
  0.0 158.7 jit_solution(10396353878426503367)
XLA Ops:
  0.6 1.9 %prepare.1 = (bf16[192,1024]{1,0:T(8,128)(2,1)S(1)}, bf16[192,1024]{1,0:T(8,128)(2,1)S(1)}, bf16[192,1024]{1,0:T(8,128)(2,1)S(1)}, bf16[192,1024]{1,0:T(8,128)(2...) custom-call(bf16[2,128,2048]{2,1,0:T(8,128)(2,1)} %refs_0_.2, f32[2,128]{1,0:T(2,128)} %refs_1_.1, ...), custom_call_target="tpu_custom_call" | custom-call | bytes 1000 | tf_op jit(solution)/shard_map/prepare/pallas_call | solution.py:905
  2.5 3.0 %collective-permute-start.1 = (bf16[192,1024]{1,0:T(8,128)(2,1)S(1)}, bf16[192,1024]{1,0:T(8,128)(2,1)S(1)}, u32[]{:S(2)}, u32[]{:S(2)}) collective-permute-start(bf16[192,1024]{1,0:T(8,128)(2,1)S(1)} %get-tuple-element.158), channel_id=1, source_target_pairs={{0,2},{1,6},{2,0},{3,4},{4,3},{5,7},{6,1},{7,5},{8,10},{9,14},{10,... | collective-permute-start | bytes 1179656 | tf_op jit(solution)/shard_map/ppermute | solution.py:937
  7.4 1.6 %cut_cotangent.1 = (bf16[128,1024]{1,0:T(8,128)(2,1)S(1)}, bf16[128,1024]{1,0:T(8,128)(2,1)S(1)}, bf16[128,1024]{1,0:T(8,128)(2,1)S(1)}, bf16[128,1024]{1,0:T(8,128)(2,1)S(1)}) custom-call(f32[2,128,2048]{2,1,0:T(8,128)} %refs_0_.3), custom_call_target="tpu_custom_call" | custom-call | bytes 1000 | tf_op jit(solution)/shard_map/cut_cotangent/pallas_call | solution.py:905
  9.4 10.3 %collective-permute-done.1.refs_1_.refs_4_ = bf16[192,1024]{1,0:T(8,128)(2,1)S(1)} collective-permute-done((bf16[192,1024]{1,0:T(8,128)(2,1)S(1)}, bf16[192,1024]{1,0:T(8,128)(2,1)S(1)}, u32[]{:S(2)}, u32[]{:S(2)}) %collective-permute-start.1) | collective-permute-done | bytes 393248 | tf_op jit(solution)/shard_map/ppermute | solution.py:937
  19.7 2.0 %collective-permute-start.6 = (bf16[5,96,512]{2,1,0:T(8,128)(2,1)S(1)}, bf16[5,96,512]{2,1,0:T(8,128)(2,1)S(1)}, u32[]{:S(2)}, u32[]{:S(2)}) collective-permute-start(bf16[5,96,512]{2,1,0:T(8,128)(2,1)S(1)} %get-tuple-element.172), channel_id=1, source_target_pairs={{0,2},{1,3},{2,0},{3,1},{4,6},{5,7},{6,4},{7,5},{8,10},{9,11},{10,... | collective-permute-start | bytes 1474568 | tf_op jit(solution)/shard_map/ppermute | solution.py:929
  21.8 12.6 %collective-permute-done.2.refs_0_.refs_3_ = bf16[192,1024]{1,0:T(8,128)(2,1)S(1)} collective-permute-done((bf16[192,1024]{1,0:T(8,128)(2,1)S(1)}, bf16[192,1024]{1,0:T(8,128)(2,1)S(1)}, u32[]{:S(2)}, u32[]{:S(2)}) %collective-permute-start.2) | collective-permute-done | bytes 393248 | tf_op jit(solution)/shard_map/ppermute | solution.py:937
  36.2 2.7 %open.1 = (bf16[1024,512]{1,0:T(8,128)(2,1)S(1)}, bf16[1024,512]{1,0:T(8,128)(2,1)S(1)}, f32[1024,128]{1,0:T(8,128)S(1)}, f32[1024,128]{1,0:T(8,128)S(1)}, f32[1024,128]{1,0:T(8,128)S(1)}) custom-call(s32[2,2,2,2]{3,2,1,0:T(2,128)S(1)} %pad_add_fusion.refs_0_, bf16[1024,1024]{1,0:T(8,128)(2,1)S(1)} %fusion.refs_1_.refs_10_.refs_7_.refs_6_, ...), custom_call_target="tpu_custom_call" | custom-call | flops 1200000000 | bytes 1000 | tf_op jit(solution)/shard_map/open/pallas_call | solution.py:905
  38.9 3.0 %enter.1 = (bf16[768,512]{1,0:T(8,128)(2,1)S(1)}, f32[1024,768]{1,0:T(8,128)S(1)}, f32[4,16,384]{2,1,0:T(8,128)S(1)}, f32[1,2,384]{2,1,0:T(2,128)S(1)}) custom-call(s32[2,2,2,2]{3,2,1,0:T(2,128)S(1)} %pad_add_fusion.refs_0_, f32[1024,128]{1,0:T(8,128)S(1)} %get-tuple-element.169.refs_1_.refs_2_, f32[1024,128]{1,0:T(8,128)S(1)} %get-tuple-element.170.refs_2_.refs_3_, ...), custom_call_target="tpu_custom_call" | custom-call | bytes 1000 | tf_op jit(solution)/shard_map/enter/pallas_call | solution.py:905
  43.1 2.4 %chain.1.refs_4_.refs_2_.refs_7_ = bf16[1024,1536]{1,0:T(8,128)(2,1)S(1)} custom-call(s32[2,2,2,2]{3,2,1,0:T(2,128)S(1)} %pad_add_fusion.refs_0_, f32[1024,128]{1,0:T(8,128)S(1)} %get-tuple-element.169.refs_1_.refs_2_, f32[1024,128]{1,0:T(8,128)S(1)} %get-tuple-element.170.refs_2_.refs_3_, f32[1,2,384]{2,1,0:T(2,128)S(1)} %bitcast.18, ...), custom_call_target="tpu_custom_call" | custom-call | bytes 1000 | tf_op jit(solution)/shard_map/chain/pallas_call | solution.py:905
  46.6 2.6 %collective-permute-start.13 = (bf16[128,1024]{1,0:T(8,128)(2,1)S(1)}, bf16[128,1024]{1,0:T(8,128)(2,1)S(1)}, u32[]{:S(2)}, u32[]{:S(2)}) collective-permute-start(bf16[128,1024]{1,0:T(8,128)(2,1)S(1)} %get-tuple-element.187), channel_id=1, source_target_pairs={{0,6},{1,2},{2,4},{3,0},{4,7},{5,3},{6,5},{7,1},{8,14},{9,10},{10,... | collective-permute-start | bytes 786440 | tf_op jit(solution)/shard_map/ppermute | solution.py:937
  50.4 6.5 %middle.1 = (bf16[1536,512]{1,0:T(8,128)(2,1)S(1)}, bf16[768,512]{1,0:T(8,128)(2,1)S(1)}, bf16[1024,512]{1,0:T(8,128)(2,1)S(1)}, f32[1024,512]{1,0:T(8,128)S(1)}...) custom-call(s32[2,2,2,2]{3,2,1,0:T(2,128)S(1)} %pad_add_fusion.refs_, ...), custom_call_target="tpu_custom_call" | custom-call | flops 4400000000 | bytes 1000 | tf_op jit(solution)/shard_map/middle/pallas_call | solution.py:905
  59.4 6.4 %leave.1 = (bf16[1536,512]{1,0:T(8,128)(2,1)S(1)}, bf16[1024,1536]{1,0:T(8,128)(2,1)S(1)}, bf16[1024,512]{1,0:T(8,128)(2,1)S(1)}, bf16[128,1024]{1,0:T(8,128)(2,...) custom-call(s32[2,2,2,2]{3,2,1,0:T(2,128)S(1)} %pad_add_fusion.refs_0_, ...), custom_call_target="tpu_custom_call" | custom-call | flops 3200000000 | bytes 1000 | tf_op jit(solution)/shard_map/leave/pallas_call | solution.py:905
  67.2 5.1 %turn.1 = (f32[1024,512]{1,0:T(8,128)S(1)}, bf16[1024,512]{1,0:T(8,128)(2,1)S(1)}, f32[1024,1536]{1,0:T(8,128)S(1)}, f32[1,512]{1,0:T(1,128)S(1)}, f32[4,16,384]{2,1,0:T(8,128)S(1)}, /*index=5*/f32[1,2,384]{2,1,0:T(2,128)S(1)}) custom-call(s32[2,2,2,2]{3,2,1,0:T(2,128)S(1)} %pad_add_fusion.refs_0_, f32[1024,128]{1,0:T(8,128)S(1)} %get-tuple-element.169.refs_1_.refs_2_, ...), custom_call_target="tpu_custom_call" | custom-call | flops 2400000000 | bytes 1000 | tf_op jit(solution)/shard_map/turn/pallas_call | solution.py:905
  73.4 1.4 collective-permute-start.19
  76.9 1.9 %collective-permute-start.20 = (bf16[384,512]{1,0:T(8,128)(2,1)S(1)}, bf16[384,512]{1,0:T(8,128)(2,1)S(1)}, u32[]{:S(2)}, u32[]{:S(2)}) collective-permute-start(bf16[384,512]{1,0:T(8,128)(2,1)S(1)} %get-tuple-element.214), channel_id=1, source_target_pairs={{0,1},{1,0},{2,3},{3,2},{4,6},{5,7},{6,4},{7,5},{8,9},{9,8},{10,11... | collective-permute-start | bytes 1179656 | tf_op jit(solution)/shard_map/ppermute | solution.py:1050
  78.8 9.5 %back_middle.1 = (bf16[1024,768]{1,0:T(8,128)(2,1)S(1)}, f32[2,384]{1,0:T(2,128)S(1)}, f32[1,512]{1,0:T(1,128)S(1)}, f32[1024,512]{1,0:T(8,128)S(1)}, bf16[1024,...) custom-call(s32[2,2,2,2]{3,2,1,0:T(2,128)S(1)} %pad_add_fusion.refs_, ...), custom_call_target="tpu_custom_call" | custom-call | flops 4400000000 | bytes 1000 | tf_op jit(solution)/shard_map/back_middle/pallas_call | solution.py:905
  88.4 1.4 grads_b_send.1
  90.4 1.4 grads_b_keep.1.refs_2_
  93.6 3.7 %back_chain.1 = (bf16[1024,768]{1,0:T(8,128)(2,1)S(1)}, f32[2,384]{1,0:T(2,128)S(1)}) custom-call(s32[2,2,2,2]{3,2,1,0:T(2,128)S(1)} %pad_add_fusion.refs_0_, f32[1024,128]{1,0:T(8,128)S(1)} %get-tuple-element.169.refs_1_.refs_2_, f32[1024,128]{1,0:T(8,128)S(1)} %get-tuple-element.170.refs_2_.refs_3_, f32[1,2,384]{2,1,0:T(2,128)S(1)} %bitcast.21, ...), custom_call_target="tpu_custom_call" | custom-call | flops 3600000000 | bytes 1000 | tf_op jit(solution)/shard_map/back_chain/pallas_call | solution.py:905
  98.0 3.0 %back_leave.1 = (bf16[256,1024]{1,0:T(8,128)(2,1)S(1)}, bf16[256,1024]{1,0:T(8,128)(2,1)S(1)}, bf16[256,1024]{1,0:T(8,128)(2,1)S(1)}, bf16[256,1024]{1,0:T(8,128)(2,1)S(1)}) custom-call(f32[8,512]{1,0:T(8,128)S(1)} %get-tuple-element.168.refs_2_.refs_3_.refs_4_.refs_5_.refs_6_.refs_0_, bf16[1024,768]{1,0:T(8,128)(2,1)S(1)} %get-tuple-element.241.refs_0_.refs_1_, ...), custom_call_target="tpu_custom_call" | custom-call | flops 1200000000 | bytes 1000 | tf_op jit(solution)/shard_map/back_leave/pallas_call | solution.py:905
  101.0 4.1 %collective-permute-done.23.refs_0_.refs_1_ = bf16[768,512]{1,0:T(8,128)(2,1)S(1)} collective-permute-done((bf16[768,512]{1,0:T(8,128)(2,1)S(1)}, bf16[768,512]{1,0:T(8,128)(2,1)S(1)}, u32[]{:S(2)}, u32[]{:S(2)}) %collective-permute-start.23) | collective-permute-done | bytes 786464 | tf_op jit(solution)/shard_map/ppermute | solution.py:1050
  106.3 6.0 %collective-permute-start.26 = (bf16[192,128]{1,0:T(8,128)(2,1)S(1)}, bf16[192,128]{1,0:T(8,128)(2,1)S(1)}, u32[]{:S(2)}, u32[]{:S(2)}) collective-permute-start(bf16[192,128]{1,0:T(8,128)(2,1)S(1)} %get-tuple-element.255), channel_id=1, source_target_pairs={{0,24},{8,16},{16,8},{24,0},{1,25},{9,17},{17,9},{25,1},{2,26},{10... | collective-permute-start | bytes 147464 | tf_op jit(solution)/shard_map/ppermute | solution.py:929
  113.0 1.7 %collective-permute-done.26.refs_1_ = bf16[192,128]{1,0:T(8,128)(2,1)S(1)} collective-permute-done((bf16[192,128]{1,0:T(8,128)(2,1)S(1)}, bf16[192,128]{1,0:T(8,128)(2,1)S(1)}, u32[]{:S(2)}, u32[]{:S(2)}) %collective-permute-start.26) | collective-permute-done | bytes 49184 | tf_op jit(solution)/shard_map/ppermute | solution.py:929
  114.7 2.7 %collective-permute-done.27.refs_2_ = bf16[192,128]{1,0:T(8,128)(2,1)S(1)} collective-permute-done((bf16[192,128]{1,0:T(8,128)(2,1)S(1)}, bf16[192,128]{1,0:T(8,128)(2,1)S(1)}, u32[]{:S(2)}, u32[]{:S(2)}) %collective-permute-start.27) | collective-permute-done | bytes 49184 | tf_op jit(solution)/shard_map/ppermute | solution.py:929
  118.2 4.1 %collective-permute-done.29.refs_3_ = bf16[112,512]{1,0:T(8,128)(2,1)S(1)} collective-permute-done((bf16[112,512]{1,0:T(8,128)(2,1)S(1)}, bf16[112,512]{1,0:T(8,128)(2,1)S(1)}, u32[]{:S(2)}, u32[]{:S(2)}) %collective-permute-start.29) | collective-permute-done | bytes 114720 | tf_op jit(solution)/shard_map/ppermute | solution.py:1050
  123.7 3.0 %collective-permute-start.32 = (bf16[400,128]{1,0:T(8,128)(2,1)S(1)}, bf16[400,128]{1,0:T(8,128)(2,1)S(1)}, u32[]{:S(2)}, u32[]{:S(2)}) collective-permute-start(bf16[400,128]{1,0:T(8,128)(2,1)S(1)} %get-tuple-element.276), channel_id=1, source_target_pairs={{0,24},{8,16},{16,8},{24,0},{1,25},{9,17},{17,9},{25,1},{2,26},{10... | collective-permute-start | bytes 307208 | tf_op jit(solution)/shard_map/ppermute | solution.py:929
  128.1 5.9 %collective-permute-done.30.refs_0_ = bf16[256,1024]{1,0:T(8,128)(2,1)S(1)} collective-permute-done((bf16[256,1024]{1,0:T(8,128)(2,1)S(1)}, bf16[256,1024]{1,0:T(8,128)(2,1)S(1)}, u32[]{:S(2)}, u32[]{:S(2)}) %collective-permute-start.30) | collective-permute-done | bytes 524320 | tf_op jit(solution)/shard_map/ppermute | solution.py:937
  134.0 2.1 %collective-permute-done.31.refs_2_ = bf16[256,1024]{1,0:T(8,128)(2,1)S(1)} collective-permute-done((bf16[256,1024]{1,0:T(8,128)(2,1)S(1)}, bf16[256,1024]{1,0:T(8,128)(2,1)S(1)}, u32[]{:S(2)}, u32[]{:S(2)}) %collective-permute-start.31) | collective-permute-done | bytes 524320 | tf_op jit(solution)/shard_map/ppermute | solution.py:937
  139.3 2.6 %collective-permute-start.38 = (bf16[576,128]{1,0:T(8,128)(2,1)S(1)}, bf16[576,128]{1,0:T(8,128)(2,1)S(1)}, u32[]{:S(2)}, u32[]{:S(2)}) collective-permute-start(bf16[576,128]{1,0:T(8,128)(2,1)S(1)} %get-tuple-element.292.refs_0_), channel_id=1, source_target_pairs={{0,16},{8,24},{16,0},{24,8},{1,17},{9,25},{17,1},{25,9},{2,18},{10... | collective-permute-start | bytes 442376 | tf_op jit(solution)/shard_map/ppermute | solution.py:929
  142.6 8.4 %collective-permute-done.35.refs_1_ = bf16[256,1024]{1,0:T(8,128)(2,1)S(1)} collective-permute-done((bf16[256,1024]{1,0:T(8,128)(2,1)S(1)}, bf16[256,1024]{1,0:T(8,128)(2,1)S(1)}, u32[]{:S(2)}, u32[]{:S(2)}) %collective-permute-start.35) | collective-permute-done | bytes 524320 | tf_op jit(solution)/shard_map/ppermute | solution.py:937
  151.0 2.1 %spread.1 = (f32[2,128,2048]{2,1,0:T(8,128)}, f32[2,128,2048]{2,1,0:T(8,128)}) custom-call(bf16[256,1024]{1,0:T(8,128)(2,1)S(1)} %collective-permute-done.30.refs_0_, bf16[256,1024]{1,0:T(8,128)(2,1)S(1)} %collective-permute-done.35.refs_1_, bf16[256,1024]{1,0:T(8,128)(2,1)S(1)} %collective-permute-done.31.refs_2_, ...), custom_call_target="tpu_custom_call" | custom-call | bytes 1000 | tf_op jit(solution)/shard_map/spread/pallas_call | solution.py:905
  156.6 2.1 %finish.1 = (f32[2,128]{1,0:T(2,128)}, f32[2,128]{1,0:T(2,128)}, f32[2,96]{1,0:T(2,128)}, f32[2,96]{1,0:T(2,128)}, f32[2,96]{1,0:T(2,128)}, /*index=5*/f32[2,2,96,512]{3,2,1,0:T(8,128)}, f32[2,4,96,512]{3,2,1,0:T(8,128)}) custom-call(bf16[576,128]{1,0:T(8,128)(2,1)S(1)} %get-tuple-element.292.refs_0_, bf16[576,128]{1,0:T(8,128)(2,1)S(1)} %collective-permute-done.37.refs_1_, ...), custom_call_target="tpu_custom_call" | custom-call | bytes 1000 | tf_op jit(solution)/shard_map/finish/pallas_call | solution.py:905
  (104 shorter events, 30.4 us)
Async XLA Ops:
  2.5 17.2 %collective-permute-start.1 = (bf16[192,1024]{1,0:T(8,128)(2,1)S(1)}, bf16[192,1024]{1,0:T(8,128)(2,1)S(1)}, u32[]{:S(2)}, u32[]{:S(2)}) collective-permute-start(bf16[192,1024]{1,0:T(8,128)(2,1)S(1)} %get-tuple-element.158), channel_id=1, source_target_pairs={{0,2},{1,6},{2,0},{3,4},{4,3},{5,7},{6,1},{7,5},{8,10},{9,14},{10,... | collective-permute-start | bytes 1179656 | tf_op jit(solution)/shard_map/ppermute | solution.py:937
  5.6 28.8 %collective-permute-start.2 = (bf16[192,1024]{1,0:T(8,128)(2,1)S(1)}, bf16[192,1024]{1,0:T(8,128)(2,1)S(1)}, u32[]{:S(2)}, u32[]{:S(2)}) collective-permute-start(bf16[192,1024]{1,0:T(8,128)(2,1)S(1)} %get-tuple-element.164), channel_id=1, source_target_pairs={{0,6},{1,2},{2,4},{3,0},{4,7},{5,3},{6,5},{7,1},{8,14},{9,10},{10,... | collective-permute-start | bytes 1179656 | tf_op jit(solution)/shard_map/ppermute | solution.py:937
  6.7 27.7 %collective-permute-start.3 = (bf16[192,1024]{1,0:T(8,128)(2,1)S(1)}, bf16[192,1024]{1,0:T(8,128)(2,1)S(1)}, u32[]{:S(2)}, u32[]{:S(2)}) collective-permute-start(bf16[192,1024]{1,0:T(8,128)(2,1)S(1)} %get-tuple-element.166), channel_id=1, source_target_pairs={{0,4},{1,0},{2,6},{3,2},{4,5},{5,1},{6,7},{7,3},{8,12},{9,8},{10,1... | collective-permute-start | bytes 1179656 | tf_op jit(solution)/shard_map/ppermute | solution.py:937
  6.7 27.7 %collective-permute-start.4 = (bf16[192,1024]{1,0:T(8,128)(2,1)S(1)}, bf16[192,1024]{1,0:T(8,128)(2,1)S(1)}, u32[]{:S(2)}, u32[]{:S(2)}) collective-permute-start(bf16[192,1024]{1,0:T(8,128)(2,1)S(1)} %get-tuple-element.167), channel_id=1, source_target_pairs={{0,0},{1,4},{2,2},{3,6},{4,1},{5,5},{6,3},{7,7},{8,8},{9,12},{10,1... | collective-permute-start | bytes 1179656 | tf_op jit(solution)/shard_map/ppermute | solution.py:937
  19.7 25.8 %collective-permute-start.7 = (bf16[5,96,512]{2,1,0:T(8,128)(2,1)S(1)}, bf16[5,96,512]{2,1,0:T(8,128)(2,1)S(1)}, u32[]{:S(2)}, u32[]{:S(2)}) collective-permute-start(bf16[5,96,512]{2,1,0:T(8,128)(2,1)S(1)} %get-tuple-element.172), channel_id=1, source_target_pairs={{0,3},{1,2},{2,1},{3,0},{4,7},{5,6},{6,5},{7,4},{8,11},{9,10},{10,... | collective-permute-start | bytes 1474568 | tf_op jit(solution)/shard_map/ppermute | solution.py:929
  19.7 25.8 %collective-permute-start.6 = (bf16[5,96,512]{2,1,0:T(8,128)(2,1)S(1)}, bf16[5,96,512]{2,1,0:T(8,128)(2,1)S(1)}, u32[]{:S(2)}, u32[]{:S(2)}) collective-permute-start(bf16[5,96,512]{2,1,0:T(8,128)(2,1)S(1)} %get-tuple-element.172), channel_id=1, source_target_pairs={{0,2},{1,3},{2,0},{3,1},{4,6},{5,7},{6,4},{7,5},{8,10},{9,11},{10,... | collective-permute-start | bytes 1474568 | tf_op jit(solution)/shard_map/ppermute | solution.py:929
  34.4 11.6 %collective-permute-start.5 = (bf16[5,96,512]{2,1,0:T(8,128)(2,1)S(1)}, bf16[5,96,512]{2,1,0:T(8,128)(2,1)S(1)}, u32[]{:S(2)}, u32[]{:S(2)}) collective-permute-start(bf16[5,96,512]{2,1,0:T(8,128)(2,1)S(1)} %get-tuple-element.172), channel_id=1, source_target_pairs={{0,1},{1,0},{2,3},{3,2},{4,5},{5,4},{6,7},{7,6},{8,9},{9,8},{10,11... | collective-permute-start | bytes 1474568 | tf_op jit(solution)/shard_map/ppermute | solution.py:929
  34.5 4.4 %collective-permute-start.8 = (bf16[384,512]{1,0:T(8,128)(2,1)S(1)}, bf16[384,512]{1,0:T(8,128)(2,1)S(1)}, u32[]{:S(2)}, u32[]{:S(2)}) collective-permute-start(bf16[384,512]{1,0:T(8,128)(2,1)S(1)} %get-tuple-element.174.refs_5_), channel_id=1, source_target_pairs={{0,4},{4,0},{1,5},{5,1},{2,6},{6,2},{3,7},{7,3},{8,12},{12,8},{9,1... | collective-permute-start | bytes 1179656 | tf_op jit(solution)/shard_map/ppermute | solution.py:929
  46.0 4.4 %collective-permute-start.10 = (bf16[5,96,512]{2,1,0:T(8,128)(2,1)S(1)}, bf16[5,96,512]{2,1,0:T(8,128)(2,1)S(1)}, u32[]{:S(2)}, u32[]{:S(2)}) collective-permute-start(bf16[5,96,512]{2,1,0:T(8,128)(2,1)S(1)} %collective-permute-done.5.refs_10_.refs_12_), channel_id=1, source_target_pairs={{0,4},{4,0},{1,5},{5,1},{2,6},{6,2},{3,7},{7,3},{8,12},{12,8},{9,1... | collective-permute-start | bytes 1474568 | tf_op jit(solution)/shard_map/ppermute | solution.py:929
  46.0 4.4 %collective-permute-start.11 = (bf16[5,96,512]{2,1,0:T(8,128)(2,1)S(1)}, bf16[5,96,512]{2,1,0:T(8,128)(2,1)S(1)}, u32[]{:S(2)}, u32[]{:S(2)}) collective-permute-start(bf16[5,96,512]{2,1,0:T(8,128)(2,1)S(1)} %collective-permute-done.6.refs_11_.refs_13_), channel_id=1, source_target_pairs={{0,4},{4,0},{1,5},{5,1},{2,6},{6,2},{3,7},{7,3},{8,12},{12,8},{9,1... | collective-permute-start | bytes 1474568 | tf_op jit(solution)/shard_map/ppermute | solution.py:929
  46.6 10.4 %collective-permute-start.13 = (bf16[128,1024]{1,0:T(8,128)(2,1)S(1)}, bf16[128,1024]{1,0:T(8,128)(2,1)S(1)}, u32[]{:S(2)}, u32[]{:S(2)}) collective-permute-start(bf16[128,1024]{1,0:T(8,128)(2,1)S(1)} %get-tuple-element.187), channel_id=1, source_target_pairs={{0,6},{1,2},{2,4},{3,0},{4,7},{5,3},{6,5},{7,1},{8,14},{9,10},{10,... | collective-permute-start | bytes 786440 | tf_op jit(solution)/shard_map/ppermute | solution.py:937
  49.1 8.9 %collective-permute-start.14 = (bf16[128,1024]{1,0:T(8,128)(2,1)S(1)}, bf16[128,1024]{1,0:T(8,128)(2,1)S(1)}, u32[]{:S(2)}, u32[]{:S(2)}) collective-permute-start(bf16[128,1024]{1,0:T(8,128)(2,1)S(1)} %get-tuple-element.188), channel_id=1, source_target_pairs={{0,4},{1,0},{2,6},{3,2},{4,5},{5,1},{6,7},{7,3},{8,12},{9,8},{10,1... | collective-permute-start | bytes 786440 | tf_op jit(solution)/shard_map/ppermute | solution.py:937
  58.0 9.2 %collective-permute-start.16 = (bf16[128,1024]{1,0:T(8,128)(2,1)S(1)}, bf16[128,1024]{1,0:T(8,128)(2,1)S(1)}, u32[]{:S(2)}, u32[]{:S(2)}) collective-permute-start(bf16[128,1024]{1,0:T(8,128)(2,1)S(1)} %get-tuple-element.199), channel_id=1, source_target_pairs={{0,2},{1,6},{2,0},{3,4},{4,3},{5,7},{6,1},{7,5},{8,10},{9,14},{10,... | collective-permute-start | bytes 786440 | tf_op jit(solution)/shard_map/ppermute | solution.py:937
  58.6 8.6 %collective-permute-start.17 = (bf16[128,1024]{1,0:T(8,128)(2,1)S(1)}, bf16[128,1024]{1,0:T(8,128)(2,1)S(1)}, u32[]{:S(2)}, u32[]{:S(2)}) collective-permute-start(bf16[128,1024]{1,0:T(8,128)(2,1)S(1)} %get-tuple-element.201), channel_id=1, source_target_pairs={{0,0},{1,4},{2,2},{3,6},{4,1},{5,5},{6,3},{7,7},{8,8},{9,12},{10,1... | collective-permute-start | bytes 786440 | tf_op jit(solution)/shard_map/ppermute | solution.py:937
  76.9 11.5 %collective-permute-start.20 = (bf16[384,512]{1,0:T(8,128)(2,1)S(1)}, bf16[384,512]{1,0:T(8,128)(2,1)S(1)}, u32[]{:S(2)}, u32[]{:S(2)}) collective-permute-start(bf16[384,512]{1,0:T(8,128)(2,1)S(1)} %get-tuple-element.214), channel_id=1, source_target_pairs={{0,1},{1,0},{2,3},{3,2},{4,6},{5,7},{6,4},{7,5},{8,9},{9,8},{10,11... | collective-permute-start | bytes 1179656 | tf_op jit(solution)/shard_map/ppermute | solution.py:1050
  93.1 12.1 %collective-permute-start.23 = (bf16[768,512]{1,0:T(8,128)(2,1)S(1)}, bf16[768,512]{1,0:T(8,128)(2,1)S(1)}, u32[]{:S(2)}, u32[]{:S(2)}) collective-permute-start(bf16[768,512]{1,0:T(8,128)(2,1)S(1)} %get-tuple-element.238), channel_id=1, source_target_pairs={{0,2},{1,3},{2,0},{3,1},{4,5},{5,4},{6,7},{7,6},{8,10},{9,11},{10,... | collective-permute-start | bytes 2359304 | tf_op jit(solution)/shard_map/ppermute | solution.py:1050
  97.9 7.8 %collective-permute-start.24 = (bf16[384,512]{1,0:T(8,128)(2,1)S(1)}, bf16[384,512]{1,0:T(8,128)(2,1)S(1)}, u32[]{:S(2)}, u32[]{:S(2)}) collective-permute-start(bf16[384,512]{1,0:T(8,128)(2,1)S(1)} %get-tuple-element.243), channel_id=1, source_target_pairs={{0,4},{4,0},{1,5},{5,1},{2,6},{6,2},{3,7},{7,3},{8,12},{12,8},{9,1... | collective-permute-start | bytes 1179656 | tf_op jit(solution)/shard_map/ppermute | solution.py:929
  106.0 11.3 %collective-permute-start.25 = (bf16[512,512]{1,0:T(8,128)(2,1)S(1)}, bf16[512,512]{1,0:T(8,128)(2,1)S(1)}, u32[]{:S(2)}, u32[]{:S(2)}) collective-permute-start(bf16[512,512]{1,0:T(8,128)(2,1)S(1)} %get-tuple-element.252), channel_id=1, source_target_pairs={{0,1},{1,0},{2,3},{3,2},{4,6},{5,7},{6,4},{7,5},{8,9},{9,8},{10,11... | collective-permute-start | bytes 1572872 | tf_op jit(solution)/shard_map/ppermute | solution.py:1050
  106.3 8.4 %collective-permute-start.26 = (bf16[192,128]{1,0:T(8,128)(2,1)S(1)}, bf16[192,128]{1,0:T(8,128)(2,1)S(1)}, u32[]{:S(2)}, u32[]{:S(2)}) collective-permute-start(bf16[192,128]{1,0:T(8,128)(2,1)S(1)} %get-tuple-element.255), channel_id=1, source_target_pairs={{0,24},{8,16},{16,8},{24,0},{1,25},{9,17},{17,9},{25,1},{2,26},{10... | collective-permute-start | bytes 147464 | tf_op jit(solution)/shard_map/ppermute | solution.py:929
  112.4 5.0 %collective-permute-start.27 = (bf16[192,128]{1,0:T(8,128)(2,1)S(1)}, bf16[192,128]{1,0:T(8,128)(2,1)S(1)}, u32[]{:S(2)}, u32[]{:S(2)}) collective-permute-start(bf16[192,128]{1,0:T(8,128)(2,1)S(1)} %get-tuple-element.256), channel_id=1, source_target_pairs={{0,16},{8,24},{16,0},{24,8},{1,17},{9,25},{17,1},{25,9},{2,18},{10... | collective-permute-start | bytes 147464 | tf_op jit(solution)/shard_map/ppermute | solution.py:929
  112.4 5.0 %collective-permute-start.28 = (bf16[192,128]{1,0:T(8,128)(2,1)S(1)}, bf16[192,128]{1,0:T(8,128)(2,1)S(1)}, u32[]{:S(2)}, u32[]{:S(2)}) collective-permute-start(bf16[192,128]{1,0:T(8,128)(2,1)S(1)} %get-tuple-element.257), channel_id=1, source_target_pairs={{0,8},{8,0},{16,24},{24,16},{1,9},{9,1},{17,25},{25,17},{2,10},{10... | collective-permute-start | bytes 147464 | tf_op jit(solution)/shard_map/ppermute | solution.py:929
  117.4 4.9 %collective-permute-start.29 = (bf16[112,512]{1,0:T(8,128)(2,1)S(1)}, bf16[112,512]{1,0:T(8,128)(2,1)S(1)}, u32[]{:S(2)}, u32[]{:S(2)}) collective-permute-start(bf16[112,512]{1,0:T(8,128)(2,1)S(1)} %get-tuple-element.270), channel_id=1, source_target_pairs={{0,2},{1,3},{2,0},{3,1},{4,5},{5,4},{6,7},{7,6},{8,10},{9,11},{10,... | collective-permute-start | bytes 344072 | tf_op jit(solution)/shard_map/ppermute | solution.py:1050
  122.5 11.5 %collective-permute-start.30 = (bf16[256,1024]{1,0:T(8,128)(2,1)S(1)}, bf16[256,1024]{1,0:T(8,128)(2,1)S(1)}, u32[]{:S(2)}, u32[]{:S(2)}) collective-permute-start(bf16[256,1024]{1,0:T(8,128)(2,1)S(1)} %get-tuple-element.273), channel_id=1, source_target_pairs={{6,0},{2,1},{4,2},{0,3},{7,4},{3,5},{5,6},{1,7},{14,8},{10,9},{12,... | collective-permute-start | bytes 1572872 | tf_op jit(solution)/shard_map/ppermute | solution.py:937
  123.7 12.4 %collective-permute-start.31 = (bf16[256,1024]{1,0:T(8,128)(2,1)S(1)}, bf16[256,1024]{1,0:T(8,128)(2,1)S(1)}, u32[]{:S(2)}, u32[]{:S(2)}) collective-permute-start(bf16[256,1024]{1,0:T(8,128)(2,1)S(1)} %get-tuple-element.274), channel_id=1, source_target_pairs={{4,0},{0,1},{6,2},{2,3},{5,4},{1,5},{7,6},{3,7},{12,8},{8,9},{14,1... | collective-permute-start | bytes 1572872 | tf_op jit(solution)/shard_map/ppermute | solution.py:937
  123.7 12.4 %collective-permute-start.32 = (bf16[400,128]{1,0:T(8,128)(2,1)S(1)}, bf16[400,128]{1,0:T(8,128)(2,1)S(1)}, u32[]{:S(2)}, u32[]{:S(2)}) collective-permute-start(bf16[400,128]{1,0:T(8,128)(2,1)S(1)} %get-tuple-element.276), channel_id=1, source_target_pairs={{0,24},{8,16},{16,8},{24,0},{1,25},{9,17},{17,9},{25,1},{2,26},{10... | collective-permute-start | bytes 307208 | tf_op jit(solution)/shard_map/ppermute | solution.py:929
  126.7 9.4 %collective-permute-start.33 = (bf16[400,128]{1,0:T(8,128)(2,1)S(1)}, bf16[400,128]{1,0:T(8,128)(2,1)S(1)}, u32[]{:S(2)}, u32[]{:S(2)}) collective-permute-start(bf16[400,128]{1,0:T(8,128)(2,1)S(1)} %get-tuple-element.277), channel_id=1, source_target_pairs={{0,16},{8,24},{16,0},{24,8},{1,17},{9,25},{17,1},{25,9},{2,18},{10... | collective-permute-start | bytes 307208 | tf_op jit(solution)/shard_map/ppermute | solution.py:929
  126.7 9.4 %collective-permute-start.34 = (bf16[400,128]{1,0:T(8,128)(2,1)S(1)}, bf16[400,128]{1,0:T(8,128)(2,1)S(1)}, u32[]{:S(2)}, u32[]{:S(2)}) collective-permute-start(bf16[400,128]{1,0:T(8,128)(2,1)S(1)} %get-tuple-element.278), channel_id=1, source_target_pairs={{0,8},{8,0},{16,24},{24,16},{1,9},{9,1},{17,25},{25,17},{2,10},{10... | collective-permute-start | bytes 307208 | tf_op jit(solution)/shard_map/ppermute | solution.py:929
  136.2 14.9 %collective-permute-start.35 = (bf16[256,1024]{1,0:T(8,128)(2,1)S(1)}, bf16[256,1024]{1,0:T(8,128)(2,1)S(1)}, u32[]{:S(2)}, u32[]{:S(2)}) collective-permute-start(bf16[256,1024]{1,0:T(8,128)(2,1)S(1)} %get-tuple-element.284), channel_id=1, source_target_pairs={{2,0},{6,1},{0,2},{4,3},{3,4},{7,5},{1,6},{5,7},{10,8},{14,9},{8,1... | collective-permute-start | bytes 1572872 | tf_op jit(solution)/shard_map/ppermute | solution.py:937
  137.5 13.6 %collective-permute-start.36 = (bf16[256,1024]{1,0:T(8,128)(2,1)S(1)}, bf16[256,1024]{1,0:T(8,128)(2,1)S(1)}, u32[]{:S(2)}, u32[]{:S(2)}) collective-permute-start(bf16[256,1024]{1,0:T(8,128)(2,1)S(1)} %get-tuple-element.286), channel_id=1, source_target_pairs={{0,0},{4,1},{2,2},{6,3},{1,4},{5,5},{3,6},{7,7},{8,8},{12,9},{10,1... | collective-permute-start | bytes 1572872 | tf_op jit(solution)/shard_map/ppermute | solution.py:937
  138.1 15.6 %collective-permute-start.39 = (bf16[576,128]{1,0:T(8,128)(2,1)S(1)}, bf16[576,128]{1,0:T(8,128)(2,1)S(1)}, u32[]{:S(2)}, u32[]{:S(2)}) collective-permute-start(bf16[576,128]{1,0:T(8,128)(2,1)S(1)} %get-tuple-element.292.refs_0_), channel_id=1, source_target_pairs={{0,8},{8,0},{16,24},{24,16},{1,9},{9,1},{17,25},{25,17},{2,10},{10... | collective-permute-start | bytes 442376 | tf_op jit(solution)/shard_map/ppermute | solution.py:929
  139.3 14.4 %collective-permute-start.38 = (bf16[576,128]{1,0:T(8,128)(2,1)S(1)}, bf16[576,128]{1,0:T(8,128)(2,1)S(1)}, u32[]{:S(2)}, u32[]{:S(2)}) collective-permute-start(bf16[576,128]{1,0:T(8,128)(2,1)S(1)} %get-tuple-element.292.refs_0_), channel_id=1, source_target_pairs={{0,16},{8,24},{16,0},{24,8},{1,17},{9,25},{17,1},{25,9},{2,18},{10... | collective-permute-start | bytes 442376 | tf_op jit(solution)/shard_map/ppermute | solution.py:929
  141.9 11.9 %collective-permute-start.37 = (bf16[576,128]{1,0:T(8,128)(2,1)S(1)}, bf16[576,128]{1,0:T(8,128)(2,1)S(1)}, u32[]{:S(2)}, u32[]{:S(2)}) collective-permute-start(bf16[576,128]{1,0:T(8,128)(2,1)S(1)} %get-tuple-element.292.refs_0_), channel_id=1, source_target_pairs={{0,24},{8,16},{16,8},{24,0},{1,25},{9,17},{17,9},{25,1},{2,26},{10... | collective-permute-start | bytes 442376 | tf_op jit(solution)/shard_map/ppermute | solution.py:929
  (20 other events, 237.7 us)

commit v5 on v4

--- a/solution.py
+++ b/solution.py
@@ -580,19 +580,17 @@
     send_ends(sz, meta, decay_b, ends_b, enter, send_b)
 
 
-def leave_kernel(sz, meta, live, ahead, behind, recv, params, ends, driven, normed, hidden, perm, own_out, *refs):
+def leave_kernel(sz, meta, live, ahead, behind, recv, params, ends, driven, normed, hidden, own_out, *refs):
     decay, skip = decay_of(sz, params, 1), skip_of(params, 1)
     far = sz.blocks - 1
     mine, other, refs = refs[:far], refs[far : 2 * far], refs[2 * far :]
-    w_out, states, slope, refs = *refs[:3], refs[3:]
+    w_out, states, slope, last, enter = refs
     place_maps(sz, meta, own_out, mine, other, 3, w_out)
-    pieces, (enter, last, stacked) = refs[: sz.blocks], refs[sz.blocks :]
     enter_chunk(sz, meta, recv, decay, ends, enter)
     chain_states(sz, decay, ahead, behind, driven, enter, states)
     for rows in row_parts(sz):
         on = widen(live[rows, :], sz.width // LANES)
         last[rows, :] = (hidden[rows, :] + finish_rows(sz, rows, states, w_out, skip, normed, on, slope)).astype(BF)
-    cut_pieces(sz, meta, last, perm, stacked, pieces)
 
 
 def turn_kernel(sz, meta, ahead, behind, slope, normed, w_out, params, perm, *refs):
@@ -635,16 +633,14 @@
     adjoint_chains(sz, decay, ahead, behind, grad_states, enter, states, half, grad_driven, grad_decay)
 
 
-def back_leave_kernel(sz, meta, params, grad_driven, upstream, slope, hidden, w_in, perm, *refs):
-    done, refs = refs[: sz.blocks], refs[sz.blocks :]
+def back_leave_kernel(sz, meta, params, grad_driven, upstream, slope, hidden, w_in, perm, done, *refs):
     skip, gain = skip_of(params, 0), gain_of(params, 0)
     pieces, (last, stacked) = refs[: sz.blocks], refs[sz.blocks :]
     for rows in row_parts(sz):
         r, _ = back_rows(sz, rows, grad_driven, w_in, upstream, slope, skip, hidden, gain)
         last[rows, :] = r.astype(BF)
     part = sz.width // sz.blocks
-    for piece, first in zip(pieces, done):
-        piece[0:part, :] = first[...]
+    cut_pieces(sz, meta, done, perm, stacked, [piece.at[0:part, :] for piece in pieces])
     cut_pieces(sz, meta, last, perm, stacked, [piece.at[part : 2 * part, :] for piece in pieces])
 
 
@@ -675,10 +671,9 @@
 class Group(NamedTuple):
     first: int
     counts: tuple
-    tiny: bool
 
     def rows(self, sz):
-        return sum(self.counts) * (sz.states // sz.blocks) + (16 if self.tiny else 0)
+        return sum(self.counts) * (sz.states // sz.blocks)
 
 
 def bits_of(sz):
@@ -716,28 +711,16 @@
     return value
 
 
-def put_sums(sz, group, value, tiny, slot, kept, message, at):
-    rows = value.shape[0]
+def put_sums(value, slot, kept, message, at):
     if slot % 2 == 0:
-        kept[slot // 2, 0:rows, :] = value
-        if group.tiny:
-            kept[slot // 2, rows : rows + 8, 0:LANES] = tiny
+        kept[slot // 2] = value
         return at
-    message[at : at + rows, :] = value.astype(BF)
-    if group.tiny:
-        rest = jnp.zeros((8, sz.width - 2 * LANES), F32)
-        wide = jnp.concatenate([*split2(tiny), rest], axis=1)
-        message[at + rows : at + rows + 16, :] = jnp.concatenate([wide, jnp.zeros_like(wide)], axis=0).astype(BF)
-    return at + group.rows(sz)
+    message[at : at + value.shape[0], :] = value.astype(BF)
+    return at + value.shape[0]
 
 
 def add_message(sz, group, kept, slot, message, at):
-    rows = group.rows(sz) - (16 if group.tiny else 0)
-    value = kept[slot, 0:rows, :] + message[at : at + rows, :].astype(F32)
-    if not group.tiny:
-        return value, None
-    got = message[at + rows : at + rows + 16, 0 : 2 * LANES].astype(F32)[0:8]
-    return value, kept[slot, rows : rows + 8, 0:LANES] + got[:, 0:LANES] + got[:, LANES:]
+    return kept[slot] + message[at : at + group.rows(sz), :].astype(F32)
 
 
 def step_kernel(old, new, sz, meta, *refs):
@@ -745,17 +728,14 @@
     held, refs = refs[: len(old)], refs[len(old) :]
     if new:
         halves, refs = refs[: 2 * len(new.counts)], refs[2 * len(new.counts) :]
-        if new.tiny:
-            lines, refs, room = refs[:8], refs[8:-1], refs[-1]
     keeps, message = refs[:-1], refs[-1]
     at = 0
     for (group, slots, row), kept, keep in zip(old, held, keeps):
         for slot in range(slots):
-            value, tiny = add_message(sz, group, kept, slot, came, row + slot * group.rows(sz))
-            at = put_sums(sz, group, value, tiny, slot, keep, message, at)
+            value = add_message(sz, group, kept, slot, came, row + slot * group.rows(sz))
+            at = put_sums(value, slot, keep, message, at)
     if new:
         own = sz.states // sz.blocks
-        whole = own_tiny(sz, *lines, room) if new.tiny else None
         for slot in range(sz.blocks):
             owner = meta[0] ^ jnp.where(meta[2] == 0, far_block(sz, new, slot, 0), far_block(sz, new, slot, 1))
             parts = []
@@ -764,19 +744,38 @@
                 for one in range(count):
                     rows = pl.ds(pl.multiple_of(one * sz.states + owner * own, own), own)
                     parts.append(keep[rows, :].astype(F32) + got[rows, :].astype(F32))
-            tiny = tiny_of(sz, whole, owner) if new.tiny else None
-            at = put_sums(sz, new, jnp.concatenate(parts, axis=0), tiny, slot, keeps[-1], message, at)
-
-
-def fold_block_kernel(planes, groups, sz, meta, *refs):
+            at = put_sums(jnp.concatenate(parts, axis=0), slot, keeps[-1], message, at)
+
+
+def direct_kernel(group, sz, meta, keep, got, *refs):
+    own = sz.states // sz.blocks
+    lines, pieces, room = refs[:8], refs[8:-1], refs[-1]
+    whole = own_tiny(sz, *lines, room)
+    for index, piece in enumerate(pieces):
+        owner = meta[0] ^ farthest(index, sz.blocks)
+        rows = pl.ds(pl.multiple_of(owner * own, own), own)
+        piece[0:own, :] = (keep[rows, :].astype(F32) + got[rows, :].astype(F32)).astype(BF)
+        rest = jnp.zeros((8, sz.width - 2 * LANES), F32)
+        wide = jnp.concatenate([*split2(tiny_of(sz, whole, owner)), rest], axis=1)
+        piece[own : own + 16, :] = jnp.concatenate([wide, jnp.zeros_like(wide)], axis=0).astype(BF)
+
+
+def fold_block_kernel(planes, groups, direct, sz, meta, *refs):
     lanes = sz.width // LANES
     held, refs = refs[: 2 * len(groups)], refs[2 * len(groups) :]
+    pieces, refs = (refs[: sz.blocks], refs[sz.blocks :]) if direct else ((), refs)
     outs, talls = refs[:planes], refs[planes:]
+    totals = [add_message(sz, group, held[2 * index], 0, held[2 * index + 1], row) for index, (group, row) in enumerate(groups)]
+    if direct:
+        total = pieces[0][...].astype(F32)
+        for piece in pieces[1:]:
+            total += piece[...].astype(F32)
+        rows = total.shape[0] - 16
+        totals.append(total[0:rows])
+        tiny = total[rows : rows + 8, 0:LANES] + total[rows : rows + 8, LANES : 2 * LANES]
     at = 0
-    for index, (group, row) in enumerate(groups):
-        total, tiny = add_message(sz, group, held[2 * index], 0, held[2 * index + 1], row)
+    for total, tall in zip(totals, talls):
         rows = total.shape[0]
-        tall = talls[index]
         padded = tall.shape[0] // lanes
         for block in range(lanes):
             tall[block * padded : block * padded + rows, :] = total[:, block * LANES : (block + 1) * LANES].astype(BF)
@@ -786,7 +785,7 @@
         for dist, out in enumerate(outs):
             out[at : at + part, :] = tall[pl.ds(pl.multiple_of((meta[3] ^ farthest(dist, planes)) * part, part), part), :]
         at += part
-    if tiny is not None:
+    if direct:
         rows = jnp.concatenate(split2(tiny), axis=0).astype(BF)
         for out in outs:
             out[at : at + 16, :] = rows
@@ -794,11 +793,13 @@
 
 def fold_plane_kernel(early, sz, meta, *refs):
     parts, out, tiny = refs[early:-2], refs[-2], refs[-1]
-    total = refs[0][...].astype(F32)
-    for piece in refs[1:early]:
-        total += piece[...].astype(F32)
-    top = total.shape[0]
-    out[0:top, :] = total.astype(BF)
+    top = 0
+    if early:
+        total = refs[0][...].astype(F32)
+        for piece in refs[1:early]:
+            total += piece[...].astype(F32)
+        top = total.shape[0]
+        out[0:top, :] = total.astype(BF)
     total = parts[0][...].astype(F32)
     for piece in parts[1:]:
         total += piece[...].astype(F32)
@@ -997,32 +998,28 @@
     (states_a,) = call("chain", sz, chain_kernel, items, [ahead, behind, recv, params, ends_a, driven_a], [sts], [enter])
     second_mine, states_a = after(second_mine, states_a)
     second_maps = second_mine, [swap(piece, 1, "core") for piece in second_mine]
-    cot_early, _ = after(cot_cut[0::2], recv)
-    cot_early = [across(piece, 2 * index, False) for index, piece in enumerate(cot_early)]
+    cot_cut, _ = after(cot_cut, recv)
+    cot_pieces = across_all(cot_cut)
     w_out_a, w_in_b, slope_a, hidden_b, normed_b, driven_b, ends_b, send_b = call(
         "middle", sz, middle_kernel, items,
         [live, ahead, behind, states_a, params, normed_a, hidden_a, output_map[0], drive_b, *second_maps[0], *second_maps[1]],
         [w_out, w_in, rows_b, rows_f, rows_b, drv, enter, snd], [enter], time=11)
-    send_b, cot_early = after(send_b, cot_early)
     recv = exchange(send_b)
-    cot_late, _ = after(cot_cut[1::2], send_b)
-    cot_late = [across(piece, 2 * index + 1, False) for index, piece in enumerate(cot_late)]
-    cot_pieces = [piece for pair in zip(cot_early, cot_late) for piece in pair]
-    w_out_b, states_b, slope_b, *out_pieces = call(
+    w_out_b, states_b, slope_b, last_b = call(
         "leave", sz, leave_kernel, items,
-        [live, ahead, behind, recv, params, ends_b, driven_b, normed_b, hidden_b, perm, output_map[1], *second_maps[0], *second_maps[1]],
-        [w_out, sts, rows_b, *piece_out], [enter, rows_b, stacked], time=8)
+        [live, ahead, behind, recv, params, ends_b, driven_b, normed_b, hidden_b, output_map[1], *second_maps[0], *second_maps[1]],
+        [w_out, sts, rows_b, rows_b], [enter])
 
     def half_grads(name, other, pairs, counts, more=(), time=0.0):
         args = [x for pair in pairs for x in pair]
         outs = [((sum(counts) * states, width), BF)] + [line] * len(more)
         return call(name, sz, partial(weight_kernel, counts, other), [], [*args, *more], outs, [], time=time)
 
-    groups = [Group(0, (2,), False), Group(1, (3,), False), Group(2, (1,), True)]
+    groups = [Group(0, (2,)), Group(1, (3,))]
     steps = bits_of(sz)
     kept, came, place = {}, {}, {}
 
-    def halve(step, halves=(), tiny=()):
+    def halve(step, halves=()):
         old, args = [], []
         for index, group in enumerate(groups):
             if 0 < step - group.first < steps:
@@ -1039,8 +1036,8 @@
                 outs.append((index, ((slots, group.rows(sz), width), F32)))
                 place[step, index] = at
                 at += slots * group.rows(sz)
-        results = call("halve_%d" % step, sz, partial(step_kernel, old, new), [], [*args, *halves, *tiny],
-                       [shape for _, shape in outs] + [((at, width), BF)], [((8, width), F32)] if tiny else [])
+        results = call("halve_%d" % step, sz, partial(step_kernel, old, new), [], [*args, *halves],
+                       [shape for _, shape in outs] + [((at, width), BF)], [])
         for (index, _), value in zip(outs, results):
             kept[index] = value
         return results[-1]
@@ -1051,7 +1048,7 @@
 
     def spread(pieces):
         return call("spread", sz, spread_kernel, [], pieces, [((micro, part, run), F32)] * 2,
-                    [((2 * blocks, part, toks), F32), pltpu.SemaphoreType.DMA((2 * blocks,))], limit=6, out_spec=HBM)
+                    [((2 * blocks, part, toks), F32), pltpu.SemaphoreType.DMA((2 * blocks,))], limit=6, out_spec=HBM, time=9)
 
     lanes = width // LANES
 
@@ -1059,12 +1056,13 @@
         step = max(SEGS * planes // lanes, SEGS)
         return ((lanes * (-(-rows // step) * step), LANES), BF)
 
-    def over_planes(name, which):
+    def over_planes(name, which, direct=()):
         ends = [(groups[index], place[groups[index].first + steps - 1, index]) for index in which]
-        talls = [tall_of(sum(group.counts) * own) for group, _ in ends]
-        cut = sum(t[0][0] for t in talls) // planes + (16 if ends[-1][0].tiny else 0)
+        talls = [tall_of(group.rows(sz)) for group, _ in ends] + [tall_of(own)] * bool(direct)
+        cut = sum(t[0][0] for t in talls) // planes + (16 if direct else 0)
         args = [x for index in which for x in (kept[index], came[groups[index].first + steps - 1])]
-        return swap_all(call(name, sz, partial(fold_block_kernel, planes, ends), [], args, [((cut, LANES), BF)] * planes, talls), "plane")
+        return swap_all(call(name, sz, partial(fold_block_kernel, planes, ends, bool(direct)), [], [*args, *direct],
+                             [((cut, LANES), BF)] * planes, talls), "plane")
 
     up_b, twice_b, gstates_b, gskip_b, ends, send = call(
         "turn", sz, turn_kernel, items, [ahead, behind, slope_b, normed_b, w_out_b, params, perm, *cot_pieces],
@@ -1096,36 +1094,42 @@
     send_maps, terms = half_grads("grads_c_send", True, [(gdriven_a, normed_a)], (1,), [w_in_a])
     gdriven_a, send_maps = after(gdriven_a, send_maps)
     got = swap(send_maps, 1, "core")
+    keep, more = half_grads("grads_c_keep", False, [(gdriven_a, normed_a)], (1,), [w_in_a], time=0)
+    sums_c = list(call(
+        "direct", sz, partial(direct_kernel, None), [],
+        [keep, got, params, terms, more, ggain_b, gskip_a, gskip_b, gdecay_a, gdecay_b], [((own + 16, width), BF)] * blocks, [((8, width), F32)]))
+    gdriven_a, sums_c[0] = after(gdriven_a, sums_c[0])
+    sums_c = swap_all(sums_c)
     last_pieces = call(
-        "back_leave", sz, back_leave_kernel, [], [params, gdriven_a, up_a, slope_a, hidden_a, w_in_a, perm, *out_pieces],
-        [((2 * part, toks), BF)] * blocks, [rows_b, stacked], limit=12, time=3)
-    last_pieces, gdriven_a, came[1] = after(last_pieces, gdriven_a, came[1])
-    keep, more = half_grads("grads_c_keep", False, [(gdriven_a, normed_a)], (1,), [w_in_a], time=5)
-    message = halve(2, (keep, got), (params, terms, more, ggain_b, gskip_a, gskip_b, gdecay_a, gdecay_b))
-    early_sums = steps <= 2
+        "back_leave", sz, back_leave_kernel, [], [params, gdriven_a, up_a, slope_a, hidden_a, w_in_a, perm, last_b],
+        [((2 * part, toks), BF)] * blocks, [rows_b, stacked], limit=12, time=6)
+    last_pieces, came[1], sums_c = after(last_pieces, came[1], sums_c)
+    message = halve(2)
     kept[0], message = after(kept[0], message)
-    first_parts = over_planes("planes_a", [0]) if early_sums else []
+    first_parts = over_planes("planes_a", [0]) if steps <= 2 else []
     send_step(2, message)
-    came[2], first_parts = after(came[2], first_parts)
-    if not early_sums:
-        first_parts = over_planes("planes_a", [0])
-    for step in range(3, steps + 2):
+    if first_parts:
+        came[2], first_parts = after(came[2], first_parts)
+    for step in range(3, steps + 1):
         send_step(step, halve(step))
-    parts = over_planes("planes", [1, 2])
+    parts = over_planes("planes", [1] if first_parts else [0, 1], sums_c)
     last_pieces, parts[0] = after(last_pieces, parts[0])
     early = [across(piece, 2 * dist, True) for dist, piece in enumerate(last_pieces[0::2])]
     parts[0], early = after(parts[0], early)
     sum_all, tiny = call(
-        "sum", sz, partial(fold_plane_kernel, planes), [], [*first_parts, *parts],
-        [((first_parts[0].shape[0] + parts[0].shape[0] - 16, LANES), BF), ((8, LANES), F32)], [])
+        "sum", sz, partial(fold_plane_kernel, len(first_parts)), [], [*first_parts, *parts],
+        [((sum(x[0].shape[0] for x in (first_parts, parts) if x) - 16, LANES), BF), ((8, LANES), F32)], [])
     whole = swap_all([sum_all] * planes, "plane")
     late, _ = after(last_pieces[1::2], sum_all)
     late = [across(piece, 2 * dist + 1, True) for dist, piece in enumerate(late)]
+    whole = swap_all([sum_all] * planes, "plane")
+    late, others = after(late, [sum_all, tiny, *whole[planes - 0 :]])
+    others = [swap(x, 1, "core") for x in others]
     output, input_grad = spread([piece for pair in zip(early, late) for piece in pair])
-    sum_all, tiny, output = after(sum_all, tiny, output)
-    others = [swap(x, 1, "core") for x in (sum_all, tiny)]
-    whole, others = after(whole, others)
-    whole += [others[0], *(swap(x, 1, "core") for x in whole[1:])]
+    far = whole[1 : planes - 0]
+    far, others, output = after(far, others, output)
+    far = [swap(x, 1, "core") for x in far]
+    whole += [others[0], *far, *others[2:]]
     tiny_other = others[1]
     small_out = ((layers, own), F32)
     grad_gain, grad_skip, grad_log, grad_imag, grad_step, grad_in, grad_out = call(

time: 159 us -> 156 us (0.981)
  waiting for transfers between devices: 60.8 us -> 52.9 us
  starting transfers between devices: 39 us -> 43.7 us
    ppermute x4 -> x3, waiting for transfers between devices: 8.28 us -> 0.01 us  [send_step(): came[step] = lax.ppermute(message, ('core', 'block'), pairs)]
    ppermute x25 -> x28, starting transfers between devices: 21.5 us -> 24.7 us  [swap(): lax.ppermute(x, axis, [(i, i ^ dist) for i in range(lax.axis_size(axis))])]
    ppermute x12, waiting for transfers between devices: 41.7 us -> 39.5 us  [across(): lax.ppermute(x, ('core', 'block'), [pair[::-1] for pair in pairs] if back...]
    ppermute x4, starting transfers between devices: 0.79 us -> 2.61 us  [neighbour(): return lax.ppermute(x, ('core', 'block'), pairs)]
    ppermute x25 -> x28, waiting for transfers between devices: 9.8 us -> 11.5 us  [swap(): lax.ppermute(x, axis, [(i, i ^ dist) for i in range(lax.axis_size(axis))])]
    ppermute x4 -> x3, starting transfers between devices: 3.44 us -> 3.68 us  [send_step(): came[step] = lax.ppermute(message, ('core', 'block'), pairs)]
  transfers between devices with their start and end apart: 45 -> 47, of which waited for: 20 -> 18; matrix products, arithmetic and copies ran while one was open for 0% -> 0% of each run, Pallas kernels for 28% -> 29%
where the time goes in v5:
time: 156 us
  Pallas kernels  57.7 us (37%)
  waiting for transfers between devices  52.9 us (34%)
  starting transfers between devices  43.7 us (28%)
    pallas_call x27, Pallas kernels, call(): pl.pallas_call(kernel, out_shape=out_shape, in_specs=[SMEM] * len(items)...  57.7 us
    ppermute x12, waiting for transfers between devices, across(): lax.ppermute(x, ('core', 'block'), [pair[::-1] for pair in pairs] if back...  39.5 us
    ppermute x28, starting transfers between devices, swap(): lax.ppermute(x, axis, [(i, i ^ dist) for i in range(lax.axis_size(axis))])  24.7 us
    ppermute x12, starting transfers between devices, across(): lax.ppermute(x, ('core', 'block'), [pair[::-1] for pair in pairs] if back...  12.7 us
    ppermute x28, waiting for transfers between devices, swap(): lax.ppermute(x, axis, [(i, i ^ dist) for i in range(lax.axis_size(axis))])  11.5 us
    ppermute x3, starting transfers between devices, send_step(): came[step] = lax.ppermute(message, ('core', 'block'), pairs)  3.68 us
  transfers between devices with their start and end apart: 47, of which 18 were waited for; matrix products, arithmetic and copies ran while one was open for 0% of the time, Pallas kernels for 29%

profile of v5, /device:TPU:0, one launch (start us, length us, event | category | flops | bytes accessed | tf_op | source)
XLA Modules:
  0.0 155.9 jit_solution(2528394795811712094)
XLA Ops:
  0.6 1.9 %prepare.1 = (bf16[192,1024]{1,0:T(8,128)(2,1)S(1)}, bf16[192,1024]{1,0:T(8,128)(2,1)S(1)}, bf16[192,1024]{1,0:T(8,128)(2,1)S(1)}, bf16[192,1024]{1,0:T(8,128)(2...) custom-call(bf16[2,128,2048]{2,1,0:T(8,128)(2,1)} %refs_0_.2, f32[2,128]{1,0:T(2,128)} %refs_1_.1, ...), custom_call_target="tpu_custom_call" | custom-call | bytes 1000 | tf_op jit(solution)/shard_map/prepare/pallas_call | solution.py:906
  2.5 3.0 %collective-permute-start.1 = (bf16[192,1024]{1,0:T(8,128)(2,1)S(1)}, bf16[192,1024]{1,0:T(8,128)(2,1)S(1)}, u32[]{:S(2)}, u32[]{:S(2)}) collective-permute-start(bf16[192,1024]{1,0:T(8,128)(2,1)S(1)} %get-tuple-element.159), channel_id=1, source_target_pairs={{0,2},{1,6},{2,0},{3,4},{4,3},{5,7},{6,1},{7,5},{8,10},{9,14},{10,... | collective-permute-start | bytes 1179656 | tf_op jit(solution)/shard_map/ppermute | solution.py:938
  7.4 1.6 %cut_cotangent.1 = (bf16[128,1024]{1,0:T(8,128)(2,1)S(1)}, bf16[128,1024]{1,0:T(8,128)(2,1)S(1)}, bf16[128,1024]{1,0:T(8,128)(2,1)S(1)}, bf16[128,1024]{1,0:T(8,128)(2,1)S(1)}) custom-call(f32[2,128,2048]{2,1,0:T(8,128)} %refs_0_.3), custom_call_target="tpu_custom_call" | custom-call | bytes 1000 | tf_op jit(solution)/shard_map/cut_cotangent/pallas_call | solution.py:906
  9.4 10.3 %collective-permute-done.1.refs_1_.refs_4_ = bf16[192,1024]{1,0:T(8,128)(2,1)S(1)} collective-permute-done((bf16[192,1024]{1,0:T(8,128)(2,1)S(1)}, bf16[192,1024]{1,0:T(8,128)(2,1)S(1)}, u32[]{:S(2)}, u32[]{:S(2)}) %collective-permute-start.1) | collective-permute-done | bytes 393248 | tf_op jit(solution)/shard_map/ppermute | solution.py:938
  19.7 2.0 %collective-permute-start.6 = (bf16[5,96,512]{2,1,0:T(8,128)(2,1)S(1)}, bf16[5,96,512]{2,1,0:T(8,128)(2,1)S(1)}, u32[]{:S(2)}, u32[]{:S(2)}) collective-permute-start(bf16[5,96,512]{2,1,0:T(8,128)(2,1)S(1)} %get-tuple-element.173), channel_id=1, source_target_pairs={{0,2},{1,3},{2,0},{3,1},{4,6},{5,7},{6,4},{7,5},{8,10},{9,11},{10,... | collective-permute-start | bytes 1474568 | tf_op jit(solution)/shard_map/ppermute | solution.py:930
  21.8 12.6 %collective-permute-done.2.refs_0_.refs_3_ = bf16[192,1024]{1,0:T(8,128)(2,1)S(1)} collective-permute-done((bf16[192,1024]{1,0:T(8,128)(2,1)S(1)}, bf16[192,1024]{1,0:T(8,128)(2,1)S(1)}, u32[]{:S(2)}, u32[]{:S(2)}) %collective-permute-start.2) | collective-permute-done | bytes 393248 | tf_op jit(solution)/shard_map/ppermute | solution.py:938
  36.2 2.7 %open.1 = (bf16[1024,512]{1,0:T(8,128)(2,1)S(1)}, bf16[1024,512]{1,0:T(8,128)(2,1)S(1)}, f32[1024,128]{1,0:T(8,128)S(1)}, f32[1024,128]{1,0:T(8,128)S(1)}, f32[1024,128]{1,0:T(8,128)S(1)}) custom-call(s32[2,2,2,2]{3,2,1,0:T(2,128)S(1)} %pad_add_fusion.refs_0_, bf16[1024,1024]{1,0:T(8,128)(2,1)S(1)} %fusion.refs_1_.refs_7_.refs_6_, ...), custom_call_target="tpu_custom_call" | custom-call | flops 1200000000 | bytes 1000 | tf_op jit(solution)/shard_map/open/pallas_call | solution.py:906
  38.9 3.0 %enter.1 = (bf16[768,512]{1,0:T(8,128)(2,1)S(1)}, f32[1024,768]{1,0:T(8,128)S(1)}, f32[4,16,384]{2,1,0:T(8,128)S(1)}, f32[1,2,384]{2,1,0:T(2,128)S(1)}) custom-call(s32[2,2,2,2]{3,2,1,0:T(2,128)S(1)} %pad_add_fusion.refs_0_, f32[1024,128]{1,0:T(8,128)S(1)} %get-tuple-element.170.refs_1_.refs_2_, f32[1024,128]{1,0:T(8,128)S(1)} %get-tuple-element.171.refs_2_.refs_3_, ...), custom_call_target="tpu_custom_call" | custom-call | bytes 1000 | tf_op jit(solution)/shard_map/enter/pallas_call | solution.py:906
  43.1 2.4 %chain.1.refs_4_.refs_2_.refs_7_ = bf16[1024,1536]{1,0:T(8,128)(2,1)S(1)} custom-call(s32[2,2,2,2]{3,2,1,0:T(2,128)S(1)} %pad_add_fusion.refs_0_, f32[1024,128]{1,0:T(8,128)S(1)} %get-tuple-element.170.refs_1_.refs_2_, f32[1024,128]{1,0:T(8,128)S(1)} %get-tuple-element.171.refs_2_.refs_3_, f32[1,2,384]{2,1,0:T(2,128)S(1)} %bitcast.18, ...), custom_call_target="tpu_custom_call" | custom-call | bytes 1000 | tf_op jit(solution)/shard_map/chain/pallas_call | solution.py:906
  46.6 2.6 %collective-permute-start.14 = (bf16[128,1024]{1,0:T(8,128)(2,1)S(1)}, bf16[128,1024]{1,0:T(8,128)(2,1)S(1)}, u32[]{:S(2)}, u32[]{:S(2)}) collective-permute-start(bf16[128,1024]{1,0:T(8,128)(2,1)S(1)} %get-tuple-element.196), channel_id=1, source_target_pairs={{0,6},{1,2},{2,4},{3,0},{4,7},{5,3},{6,5},{7,1},{8,14},{9,10},{10,... | collective-permute-start | bytes 786440 | tf_op jit(solution)/shard_map/ppermute | solution.py:938
  51.4 6.7 %middle.1 = (bf16[1536,512]{1,0:T(8,128)(2,1)S(1)}, bf16[768,512]{1,0:T(8,128)(2,1)S(1)}, bf16[1024,512]{1,0:T(8,128)(2,1)S(1)}, f32[1024,512]{1,0:T(8,128)S(1)}...) custom-call(s32[2,2,2,2]{3,2,1,0:T(2,128)S(1)} %pad_add_fusion.refs_, ...), custom_call_target="tpu_custom_call" | custom-call | flops 4400000000 | bytes 1000 | tf_op jit(solution)/shard_map/middle/pallas_call | solution.py:906
  58.1 2.1 %collective-permute-start.13 = (f32[2,384]{1,0:T(2,128)S(1)}, f32[2,384]{1,0:T(2,128)S(1)}, u32[]{:S(2)}, u32[]{:S(2)}) collective-permute-start(f32[2,384]{1,0:T(2,128)S(1)} %bitcast.23), channel_id=1, source_target_pairs={{0,4},{1,5},{2,6},{3,7},{4,0},{5,1},{6,2},{7,3},{8,12},{9,13},{10,... | collective-permute-start | bytes 9224 | tf_op jit(solution)/shard_map/ppermute | solution.py:952
  61.1 5.6 %leave.1 = (bf16[1536,512]{1,0:T(8,128)(2,1)S(1)}, bf16[1024,1536]{1,0:T(8,128)(2,1)S(1)}, bf16[1024,512]{1,0:T(8,128)(2,1)S(1)}, bf16[1024,512]{1,0:T(8,128)(2,1)S(1)}) custom-call(s32[2,2,2,2]{3,2,1,0:T(2,128)S(1)} %pad_add_fusion.refs_0_, f32[1024,128]{1,0:T(8,128)S(1)} %get-tuple-element.172.refs_1_, f32[1024,128]{1,0:T(8,128)S(1)} %get-tuple-element.170.refs_1_.refs_2_, ...), custom_call_target="tpu_custom_call" | custom-call | bytes 1000 | tf_op jit(solution)/shard_map/leave/pallas_call | solution.py:906
  66.7 5.1 %turn.1 = (f32[1024,512]{1,0:T(8,128)S(1)}, bf16[1024,512]{1,0:T(8,128)(2,1)S(1)}, f32[1024,1536]{1,0:T(8,128)S(1)}, f32[1,512]{1,0:T(1,128)S(1)}, f32[4,16,384]{2,1,0:T(8,128)S(1)}, /*index=5*/f32[1,2,384]{2,1,0:T(2,128)S(1)}) custom-call(s32[2,2,2,2]{3,2,1,0:T(2,128)S(1)} %pad_add_fusion.refs_0_, f32[1024,128]{1,0:T(8,128)S(1)} %get-tuple-element.170.refs_1_.refs_2_, ...), custom_call_target="tpu_custom_call" | custom-call | flops 2400000000 | bytes 1000 | tf_op jit(solution)/shard_map/turn/pallas_call | solution.py:906
  76.8 9.4 %back_middle.1 = (bf16[1024,768]{1,0:T(8,128)(2,1)S(1)}, f32[2,384]{1,0:T(2,128)S(1)}, f32[1,512]{1,0:T(1,128)S(1)}, f32[1024,512]{1,0:T(8,128)S(1)}, bf16[1024,...) custom-call(s32[2,2,2,2]{3,2,1,0:T(2,128)S(1)} %pad_add_fusion.refs_, ...), custom_call_target="tpu_custom_call" | custom-call | flops 4400000000 | bytes 1000 | tf_op jit(solution)/shard_map/back_middle/pallas_call | solution.py:906
  86.2 1.4 grads_b_send.1
  88.6 1.4 grads_b_keep.1.refs_2_
  91.3 1.4 collective-permute-start.24
  92.7 3.7 %back_chain.1 = (bf16[1024,768]{1,0:T(8,128)(2,1)S(1)}, f32[2,384]{1,0:T(2,128)S(1)}) custom-call(s32[2,2,2,2]{3,2,1,0:T(2,128)S(1)} %pad_add_fusion.refs_0_, f32[1024,128]{1,0:T(8,128)S(1)} %get-tuple-element.170.refs_1_.refs_2_, f32[1024,128]{1,0:T(8,128)S(1)} %get-tuple-element.171.refs_2_.refs_3_, f32[1,2,384]{2,1,0:T(2,128)S(1)} %bitcast.21, ...), custom_call_target="tpu_custom_call" | custom-call | flops 3600000000 | bytes 1000 | tf_op jit(solution)/shard_map/back_chain/pallas_call | solution.py:906
  100.0 1.5 collective-permute-start.26
  102.5 4.1 %back_leave.1 = (bf16[256,1024]{1,0:T(8,128)(2,1)S(1)}, bf16[256,1024]{1,0:T(8,128)(2,1)S(1)}, bf16[256,1024]{1,0:T(8,128)(2,1)S(1)}, bf16[256,1024]{1,0:T(8,128)(2,1)S(1)}) custom-call(f32[8,512]{1,0:T(8,128)S(1)} %get-tuple-element.169.refs_2_.refs_3_.refs_4_.refs_5_.refs_6_.refs_0_, bf16[1024,768]{1,0:T(8,128)(2,1)S(1)} %get-tuple-element.237.refs_0_.refs_1_, ...), custom_call_target="tpu_custom_call" | custom-call | flops 2400000000 | bytes 1000 | tf_op jit(solution)/shard_map/back_leave/pallas_call | solution.py:906
  106.6 1.7 %collective-permute-done.26.refs_4_ = bf16[112,512]{1,0:T(8,128)(2,1)S(1)} collective-permute-done((bf16[112,512]{1,0:T(8,128)(2,1)S(1)}, bf16[112,512]{1,0:T(8,128)(2,1)S(1)}, u32[]{:S(2)}, u32[]{:S(2)}) %collective-permute-start.26) | collective-permute-done | bytes 114720 | tf_op jit(solution)/shard_map/ppermute | solution.py:930
  109.4 5.8 %collective-permute-start.29 = (bf16[192,128]{1,0:T(8,128)(2,1)S(1)}, bf16[192,128]{1,0:T(8,128)(2,1)S(1)}, u32[]{:S(2)}, u32[]{:S(2)}) collective-permute-start(bf16[192,128]{1,0:T(8,128)(2,1)S(1)} %get-tuple-element.255), channel_id=1, source_target_pairs={{0,24},{8,16},{16,8},{24,0},{1,25},{9,17},{17,9},{25,1},{2,26},{10... | collective-permute-start | bytes 147464 | tf_op jit(solution)/shard_map/ppermute | solution.py:930
  115.9 1.7 %collective-permute-done.29.refs_1_ = bf16[192,128]{1,0:T(8,128)(2,1)S(1)} collective-permute-done((bf16[192,128]{1,0:T(8,128)(2,1)S(1)}, bf16[192,128]{1,0:T(8,128)(2,1)S(1)}, u32[]{:S(2)}, u32[]{:S(2)}) %collective-permute-start.29) | collective-permute-done | bytes 49184 | tf_op jit(solution)/shard_map/ppermute | solution.py:930
  117.6 2.7 %collective-permute-done.30.refs_2_ = bf16[192,128]{1,0:T(8,128)(2,1)S(1)} collective-permute-done((bf16[192,128]{1,0:T(8,128)(2,1)S(1)}, bf16[192,128]{1,0:T(8,128)(2,1)S(1)}, u32[]{:S(2)}, u32[]{:S(2)}) %collective-permute-start.30) | collective-permute-done | bytes 49184 | tf_op jit(solution)/shard_map/ppermute | solution.py:930
  121.7 1.6 %collective-permute-start.34 = (bf16[400,128]{1,0:T(8,128)(2,1)S(1)}, bf16[400,128]{1,0:T(8,128)(2,1)S(1)}, u32[]{:S(2)}, u32[]{:S(2)}) collective-permute-start(bf16[400,128]{1,0:T(8,128)(2,1)S(1)} %get-tuple-element.277), channel_id=1, source_target_pairs={{0,24},{8,16},{16,8},{24,0},{1,25},{9,17},{17,9},{25,1},{2,26},{10... | collective-permute-start | bytes 307208 | tf_op jit(solution)/shard_map/ppermute | solution.py:930
  123.7 2.4 %collective-permute-start.36 = (bf16[400,128]{1,0:T(8,128)(2,1)S(1)}, bf16[400,128]{1,0:T(8,128)(2,1)S(1)}, u32[]{:S(2)}, u32[]{:S(2)}) collective-permute-start(bf16[400,128]{1,0:T(8,128)(2,1)S(1)} %get-tuple-element.279), channel_id=1, source_target_pairs={{0,8},{8,0},{16,24},{24,16},{1,9},{9,1},{17,25},{25,17},{2,10},{10... | collective-permute-start | bytes 307208 | tf_op jit(solution)/shard_map/ppermute | solution.py:930
  126.0 7.1 %collective-permute-done.32.refs_0_ = bf16[256,1024]{1,0:T(8,128)(2,1)S(1)} collective-permute-done((bf16[256,1024]{1,0:T(8,128)(2,1)S(1)}, bf16[256,1024]{1,0:T(8,128)(2,1)S(1)}, u32[]{:S(2)}, u32[]{:S(2)}) %collective-permute-start.32) | collective-permute-done | bytes 524320 | tf_op jit(solution)/shard_map/ppermute | solution.py:938
  136.2 2.8 %collective-permute-start.38 = (bf16[576,128]{1,0:T(8,128)(2,1)S(1)}, bf16[576,128]{1,0:T(8,128)(2,1)S(1)}, u32[]{:S(2)}, u32[]{:S(2)}) collective-permute-start(bf16[576,128]{1,0:T(8,128)(2,1)S(1)} %get-tuple-element.286.refs_0_), channel_id=1, source_target_pairs={{0,16},{8,24},{16,0},{24,8},{1,17},{9,25},{17,1},{25,9},{2,18},{10... | collective-permute-start | bytes 442376 | tf_op jit(solution)/shard_map/ppermute | solution.py:930
  140.4 8.6 %collective-permute-done.40.refs_1_ = bf16[256,1024]{1,0:T(8,128)(2,1)S(1)} collective-permute-done((bf16[256,1024]{1,0:T(8,128)(2,1)S(1)}, bf16[256,1024]{1,0:T(8,128)(2,1)S(1)}, u32[]{:S(2)}, u32[]{:S(2)}) %collective-permute-start.40) | collective-permute-done | bytes 524320 | tf_op jit(solution)/shard_map/ppermute | solution.py:938
  149.6 2.1 %spread.1 = (f32[2,128,2048]{2,1,0:T(8,128)}, f32[2,128,2048]{2,1,0:T(8,128)}) custom-call(bf16[256,1024]{1,0:T(8,128)(2,1)S(1)} %collective-permute-done.32.refs_0_, bf16[256,1024]{1,0:T(8,128)(2,1)S(1)} %collective-permute-done.40.refs_1_, bf16[256,1024]{1,0:T(8,128)(2,1)S(1)} %collective-permute-done.33.refs_2_, ...), custom_call_target="tpu_custom_call" | custom-call | flops 3600000000 | bytes 1000 | tf_op jit(solution)/shard_map/spread/pallas_call | solution.py:906
  153.7 2.1 %finish.1 = (f32[2,128]{1,0:T(2,128)}, f32[2,128]{1,0:T(2,128)}, f32[2,96]{1,0:T(2,128)}, f32[2,96]{1,0:T(2,128)}, f32[2,96]{1,0:T(2,128)}, /*index=5*/f32[2,2,96,512]{3,2,1,0:T(8,128)}, f32[2,4,96,512]{3,2,1,0:T(8,128)}) custom-call(bf16[576,128]{1,0:T(8,128)(2,1)S(1)} %get-tuple-element.286.refs_0_, bf16[576,128]{1,0:T(8,128)(2,1)S(1)} %collective-permute-done.37.refs_1_, ...), custom_call_target="tpu_custom_call" | custom-call | bytes 1000 | tf_op jit(solution)/shard_map/finish/pallas_call | solution.py:906
  (108 shorter events, 31.8 us)
Async XLA Ops:
  2.5 17.2 %collective-permute-start.1 = (bf16[192,1024]{1,0:T(8,128)(2,1)S(1)}, bf16[192,1024]{1,0:T(8,128)(2,1)S(1)}, u32[]{:S(2)}, u32[]{:S(2)}) collective-permute-start(bf16[192,1024]{1,0:T(8,128)(2,1)S(1)} %get-tuple-element.159), channel_id=1, source_target_pairs={{0,2},{1,6},{2,0},{3,4},{4,3},{5,7},{6,1},{7,5},{8,10},{9,14},{10,... | collective-permute-start | bytes 1179656 | tf_op jit(solution)/shard_map/ppermute | solution.py:938
  5.6 28.8 %collective-permute-start.2 = (bf16[192,1024]{1,0:T(8,128)(2,1)S(1)}, bf16[192,1024]{1,0:T(8,128)(2,1)S(1)}, u32[]{:S(2)}, u32[]{:S(2)}) collective-permute-start(bf16[192,1024]{1,0:T(8,128)(2,1)S(1)} %get-tuple-element.165), channel_id=1, source_target_pairs={{0,6},{1,2},{2,4},{3,0},{4,7},{5,3},{6,5},{7,1},{8,14},{9,10},{10,... | collective-permute-start | bytes 1179656 | tf_op jit(solution)/shard_map/ppermute | solution.py:938
  6.7 27.7 %collective-permute-start.3 = (bf16[192,1024]{1,0:T(8,128)(2,1)S(1)}, bf16[192,1024]{1,0:T(8,128)(2,1)S(1)}, u32[]{:S(2)}, u32[]{:S(2)}) collective-permute-start(bf16[192,1024]{1,0:T(8,128)(2,1)S(1)} %get-tuple-element.167), channel_id=1, source_target_pairs={{0,4},{1,0},{2,6},{3,2},{4,5},{5,1},{6,7},{7,3},{8,12},{9,8},{10,1... | collective-permute-start | bytes 1179656 | tf_op jit(solution)/shard_map/ppermute | solution.py:938
  6.7 27.7 %collective-permute-start.4 = (bf16[192,1024]{1,0:T(8,128)(2,1)S(1)}, bf16[192,1024]{1,0:T(8,128)(2,1)S(1)}, u32[]{:S(2)}, u32[]{:S(2)}) collective-permute-start(bf16[192,1024]{1,0:T(8,128)(2,1)S(1)} %get-tuple-element.168), channel_id=1, source_target_pairs={{0,0},{1,4},{2,2},{3,6},{4,1},{5,5},{6,3},{7,7},{8,8},{9,12},{10,1... | collective-permute-start | bytes 1179656 | tf_op jit(solution)/shard_map/ppermute | solution.py:938
  19.7 25.8 %collective-permute-start.7 = (bf16[5,96,512]{2,1,0:T(8,128)(2,1)S(1)}, bf16[5,96,512]{2,1,0:T(8,128)(2,1)S(1)}, u32[]{:S(2)}, u32[]{:S(2)}) collective-permute-start(bf16[5,96,512]{2,1,0:T(8,128)(2,1)S(1)} %get-tuple-element.173), channel_id=1, source_target_pairs={{0,3},{1,2},{2,1},{3,0},{4,7},{5,6},{6,5},{7,4},{8,11},{9,10},{10,... | collective-permute-start | bytes 1474568 | tf_op jit(solution)/shard_map/ppermute | solution.py:930
  19.7 25.8 %collective-permute-start.6 = (bf16[5,96,512]{2,1,0:T(8,128)(2,1)S(1)}, bf16[5,96,512]{2,1,0:T(8,128)(2,1)S(1)}, u32[]{:S(2)}, u32[]{:S(2)}) collective-permute-start(bf16[5,96,512]{2,1,0:T(8,128)(2,1)S(1)} %get-tuple-element.173), channel_id=1, source_target_pairs={{0,2},{1,3},{2,0},{3,1},{4,6},{5,7},{6,4},{7,5},{8,10},{9,11},{10,... | collective-permute-start | bytes 1474568 | tf_op jit(solution)/shard_map/ppermute | solution.py:930
  34.4 11.6 %collective-permute-start.5 = (bf16[5,96,512]{2,1,0:T(8,128)(2,1)S(1)}, bf16[5,96,512]{2,1,0:T(8,128)(2,1)S(1)}, u32[]{:S(2)}, u32[]{:S(2)}) collective-permute-start(bf16[5,96,512]{2,1,0:T(8,128)(2,1)S(1)} %get-tuple-element.173), channel_id=1, source_target_pairs={{0,1},{1,0},{2,3},{3,2},{4,5},{5,4},{6,7},{7,6},{8,9},{9,8},{10,11... | collective-permute-start | bytes 1474568 | tf_op jit(solution)/shard_map/ppermute | solution.py:930
  46.0 4.7 %collective-permute-start.11 = (bf16[5,96,512]{2,1,0:T(8,128)(2,1)S(1)}, bf16[5,96,512]{2,1,0:T(8,128)(2,1)S(1)}, u32[]{:S(2)}, u32[]{:S(2)}) collective-permute-start(bf16[5,96,512]{2,1,0:T(8,128)(2,1)S(1)} %collective-permute-done.6.refs_11_.refs_12_), channel_id=1, source_target_pairs={{0,4},{4,0},{1,5},{5,1},{2,6},{6,2},{3,7},{7,3},{8,12},{12,8},{9,1... | collective-permute-start | bytes 1474568 | tf_op jit(solution)/shard_map/ppermute | solution.py:930
  46.5 4.9 %collective-permute-start.12 = (bf16[5,96,512]{2,1,0:T(8,128)(2,1)S(1)}, bf16[5,96,512]{2,1,0:T(8,128)(2,1)S(1)}, u32[]{:S(2)}, u32[]{:S(2)}) collective-permute-start(bf16[5,96,512]{2,1,0:T(8,128)(2,1)S(1)} %collective-permute-done.7.refs_12_.refs_13_), channel_id=1, source_target_pairs={{0,4},{4,0},{1,5},{5,1},{2,6},{6,2},{3,7},{7,3},{8,12},{12,8},{9,1... | collective-permute-start | bytes 1474568 | tf_op jit(solution)/shard_map/ppermute | solution.py:930
  46.6 20.1 %collective-permute-start.14 = (bf16[128,1024]{1,0:T(8,128)(2,1)S(1)}, bf16[128,1024]{1,0:T(8,128)(2,1)S(1)}, u32[]{:S(2)}, u32[]{:S(2)}) collective-permute-start(bf16[128,1024]{1,0:T(8,128)(2,1)S(1)} %get-tuple-element.196), channel_id=1, source_target_pairs={{0,6},{1,2},{2,4},{3,0},{4,7},{5,3},{6,5},{7,1},{8,14},{9,10},{10,... | collective-permute-start | bytes 786440 | tf_op jit(solution)/shard_map/ppermute | solution.py:938
  49.2 17.5 %collective-permute-start.15 = (bf16[128,1024]{1,0:T(8,128)(2,1)S(1)}, bf16[128,1024]{1,0:T(8,128)(2,1)S(1)}, u32[]{:S(2)}, u32[]{:S(2)}) collective-permute-start(bf16[128,1024]{1,0:T(8,128)(2,1)S(1)} %get-tuple-element.197), channel_id=1, source_target_pairs={{0,2},{1,6},{2,0},{3,4},{4,3},{5,7},{6,1},{7,5},{8,10},{9,14},{10,... | collective-permute-start | bytes 786440 | tf_op jit(solution)/shard_map/ppermute | solution.py:938
  49.5 17.2 %collective-permute-start.16 = (bf16[128,1024]{1,0:T(8,128)(2,1)S(1)}, bf16[128,1024]{1,0:T(8,128)(2,1)S(1)}, u32[]{:S(2)}, u32[]{:S(2)}) collective-permute-start(bf16[128,1024]{1,0:T(8,128)(2,1)S(1)} %get-tuple-element.198), channel_id=1, source_target_pairs={{0,4},{1,0},{2,6},{3,2},{4,5},{5,1},{6,7},{7,3},{8,12},{9,8},{10,1... | collective-permute-start | bytes 786440 | tf_op jit(solution)/shard_map/ppermute | solution.py:938
  50.8 15.9 %collective-permute-start.17 = (bf16[128,1024]{1,0:T(8,128)(2,1)S(1)}, bf16[128,1024]{1,0:T(8,128)(2,1)S(1)}, u32[]{:S(2)}, u32[]{:S(2)}) collective-permute-start(bf16[128,1024]{1,0:T(8,128)(2,1)S(1)} %get-tuple-element.199), channel_id=1, source_target_pairs={{0,0},{1,4},{2,2},{3,6},{4,1},{5,5},{6,3},{7,7},{8,8},{9,12},{10,1... | collective-permute-start | bytes 786440 | tf_op jit(solution)/shard_map/ppermute | solution.py:938
  75.4 10.8 %collective-permute-start.20 = (bf16[384,512]{1,0:T(8,128)(2,1)S(1)}, bf16[384,512]{1,0:T(8,128)(2,1)S(1)}, u32[]{:S(2)}, u32[]{:S(2)}) collective-permute-start(bf16[384,512]{1,0:T(8,128)(2,1)S(1)} %get-tuple-element.212), channel_id=1, source_target_pairs={{0,1},{1,0},{2,3},{3,2},{4,6},{5,7},{6,4},{7,5},{8,9},{9,8},{10,11... | collective-permute-start | bytes 1179656 | tf_op jit(solution)/shard_map/ppermute | solution.py:1047
  91.3 17.0 %collective-permute-start.24 = (bf16[768,512]{1,0:T(8,128)(2,1)S(1)}, bf16[768,512]{1,0:T(8,128)(2,1)S(1)}, u32[]{:S(2)}, u32[]{:S(2)}) collective-permute-start(bf16[768,512]{1,0:T(8,128)(2,1)S(1)} %get-tuple-element.244), channel_id=1, source_target_pairs={{0,2},{1,3},{2,0},{3,1},{4,5},{5,4},{6,7},{7,6},{8,10},{9,11},{10,... | collective-permute-start | bytes 2359304 | tf_op jit(solution)/shard_map/ppermute | solution.py:1047
  99.0 7.6 %collective-permute-start.25 = (bf16[112,512]{1,0:T(8,128)(2,1)S(1)}, bf16[112,512]{1,0:T(8,128)(2,1)S(1)}, u32[]{:S(2)}, u32[]{:S(2)}) collective-permute-start(bf16[112,512]{1,0:T(8,128)(2,1)S(1)} %get-tuple-element.246), channel_id=1, source_target_pairs={{0,3},{1,2},{2,1},{3,0},{4,7},{5,6},{6,5},{7,4},{8,11},{9,10},{10,... | collective-permute-start | bytes 344072 | tf_op jit(solution)/shard_map/ppermute | solution.py:930
  100.0 8.3 %collective-permute-start.26 = (bf16[112,512]{1,0:T(8,128)(2,1)S(1)}, bf16[112,512]{1,0:T(8,128)(2,1)S(1)}, u32[]{:S(2)}, u32[]{:S(2)}) collective-permute-start(bf16[112,512]{1,0:T(8,128)(2,1)S(1)} %get-tuple-element.247), channel_id=1, source_target_pairs={{0,2},{1,3},{2,0},{3,1},{4,6},{5,7},{6,4},{7,5},{8,10},{9,11},{10,... | collective-permute-start | bytes 344072 | tf_op jit(solution)/shard_map/ppermute | solution.py:930
  101.5 6.8 %collective-permute-start.27 = (bf16[112,512]{1,0:T(8,128)(2,1)S(1)}, bf16[112,512]{1,0:T(8,128)(2,1)S(1)}, u32[]{:S(2)}, u32[]{:S(2)}) collective-permute-start(bf16[112,512]{1,0:T(8,128)(2,1)S(1)} %get-tuple-element.248), channel_id=1, source_target_pairs={{0,1},{1,0},{2,3},{3,2},{4,5},{5,4},{6,7},{7,6},{8,9},{9,8},{10,11... | collective-permute-start | bytes 344072 | tf_op jit(solution)/shard_map/ppermute | solution.py:930
  108.5 11.8 %collective-permute-start.28 = (bf16[288,512]{1,0:T(8,128)(2,1)S(1)}, bf16[288,512]{1,0:T(8,128)(2,1)S(1)}, u32[]{:S(2)}, u32[]{:S(2)}) collective-permute-start(bf16[288,512]{1,0:T(8,128)(2,1)S(1)} %get-tuple-element.252), channel_id=1, source_target_pairs={{0,1},{1,0},{2,3},{3,2},{4,6},{5,7},{6,4},{7,5},{8,9},{9,8},{10,11... | collective-permute-start | bytes 884744 | tf_op jit(solution)/shard_map/ppermute | solution.py:1047
  109.4 8.1 %collective-permute-start.29 = (bf16[192,128]{1,0:T(8,128)(2,1)S(1)}, bf16[192,128]{1,0:T(8,128)(2,1)S(1)}, u32[]{:S(2)}, u32[]{:S(2)}) collective-permute-start(bf16[192,128]{1,0:T(8,128)(2,1)S(1)} %get-tuple-element.255), channel_id=1, source_target_pairs={{0,24},{8,16},{16,8},{24,0},{1,25},{9,17},{17,9},{25,1},{2,26},{10... | collective-permute-start | bytes 147464 | tf_op jit(solution)/shard_map/ppermute | solution.py:930
  115.2 5.0 %collective-permute-start.30 = (bf16[192,128]{1,0:T(8,128)(2,1)S(1)}, bf16[192,128]{1,0:T(8,128)(2,1)S(1)}, u32[]{:S(2)}, u32[]{:S(2)}) collective-permute-start(bf16[192,128]{1,0:T(8,128)(2,1)S(1)} %get-tuple-element.256), channel_id=1, source_target_pairs={{0,16},{8,24},{16,0},{24,8},{1,17},{9,25},{17,1},{25,9},{2,18},{10... | collective-permute-start | bytes 147464 | tf_op jit(solution)/shard_map/ppermute | solution.py:930
  115.2 5.0 %collective-permute-start.31 = (bf16[192,128]{1,0:T(8,128)(2,1)S(1)}, bf16[192,128]{1,0:T(8,128)(2,1)S(1)}, u32[]{:S(2)}, u32[]{:S(2)}) collective-permute-start(bf16[192,128]{1,0:T(8,128)(2,1)S(1)} %get-tuple-element.257), channel_id=1, source_target_pairs={{0,8},{8,0},{16,24},{24,16},{1,9},{9,1},{17,25},{25,17},{2,10},{10... | collective-permute-start | bytes 147464 | tf_op jit(solution)/shard_map/ppermute | solution.py:930
  120.4 12.7 %collective-permute-start.32 = (bf16[256,1024]{1,0:T(8,128)(2,1)S(1)}, bf16[256,1024]{1,0:T(8,128)(2,1)S(1)}, u32[]{:S(2)}, u32[]{:S(2)}) collective-permute-start(bf16[256,1024]{1,0:T(8,128)(2,1)S(1)} %get-tuple-element.274), channel_id=1, source_target_pairs={{6,0},{2,1},{4,2},{0,3},{7,4},{3,5},{5,6},{1,7},{14,8},{10,9},{12,... | collective-permute-start | bytes 1572872 | tf_op jit(solution)/shard_map/ppermute | solution.py:938
  121.7 12.4 %collective-permute-start.33 = (bf16[256,1024]{1,0:T(8,128)(2,1)S(1)}, bf16[256,1024]{1,0:T(8,128)(2,1)S(1)}, u32[]{:S(2)}, u32[]{:S(2)}) collective-permute-start(bf16[256,1024]{1,0:T(8,128)(2,1)S(1)} %get-tuple-element.275), channel_id=1, source_target_pairs={{4,0},{0,1},{6,2},{2,3},{5,4},{1,5},{7,6},{3,7},{12,8},{8,9},{14,1... | collective-permute-start | bytes 1572872 | tf_op jit(solution)/shard_map/ppermute | solution.py:938
  121.7 12.4 %collective-permute-start.34 = (bf16[400,128]{1,0:T(8,128)(2,1)S(1)}, bf16[400,128]{1,0:T(8,128)(2,1)S(1)}, u32[]{:S(2)}, u32[]{:S(2)}) collective-permute-start(bf16[400,128]{1,0:T(8,128)(2,1)S(1)} %get-tuple-element.277), channel_id=1, source_target_pairs={{0,24},{8,16},{16,8},{24,0},{1,25},{9,17},{17,9},{25,1},{2,26},{10... | collective-permute-start | bytes 307208 | tf_op jit(solution)/shard_map/ppermute | solution.py:930
  123.3 10.8 %collective-permute-start.35 = (bf16[400,128]{1,0:T(8,128)(2,1)S(1)}, bf16[400,128]{1,0:T(8,128)(2,1)S(1)}, u32[]{:S(2)}, u32[]{:S(2)}) collective-permute-start(bf16[400,128]{1,0:T(8,128)(2,1)S(1)} %get-tuple-element.278), channel_id=1, source_target_pairs={{0,16},{8,24},{16,0},{24,8},{1,17},{9,25},{17,1},{25,9},{2,18},{10... | collective-permute-start | bytes 307208 | tf_op jit(solution)/shard_map/ppermute | solution.py:930
  123.7 10.3 %collective-permute-start.36 = (bf16[400,128]{1,0:T(8,128)(2,1)S(1)}, bf16[400,128]{1,0:T(8,128)(2,1)S(1)}, u32[]{:S(2)}, u32[]{:S(2)}) collective-permute-start(bf16[400,128]{1,0:T(8,128)(2,1)S(1)} %get-tuple-element.279), channel_id=1, source_target_pairs={{0,8},{8,0},{16,24},{24,16},{1,9},{9,1},{17,25},{25,17},{2,10},{10... | collective-permute-start | bytes 307208 | tf_op jit(solution)/shard_map/ppermute | solution.py:930
  134.1 14.9 %collective-permute-start.40 = (bf16[256,1024]{1,0:T(8,128)(2,1)S(1)}, bf16[256,1024]{1,0:T(8,128)(2,1)S(1)}, u32[]{:S(2)}, u32[]{:S(2)}) collective-permute-start(bf16[256,1024]{1,0:T(8,128)(2,1)S(1)} %get-tuple-element.283), channel_id=1, source_target_pairs={{2,0},{6,1},{0,2},{4,3},{3,4},{7,5},{1,6},{5,7},{10,8},{14,9},{8,1... | collective-permute-start | bytes 1572872 | tf_op jit(solution)/shard_map/ppermute | solution.py:938
  135.2 13.8 %collective-permute-start.41 = (bf16[256,1024]{1,0:T(8,128)(2,1)S(1)}, bf16[256,1024]{1,0:T(8,128)(2,1)S(1)}, u32[]{:S(2)}, u32[]{:S(2)}) collective-permute-start(bf16[256,1024]{1,0:T(8,128)(2,1)S(1)} %get-tuple-element.284), channel_id=1, source_target_pairs={{0,0},{4,1},{2,2},{6,3},{1,4},{5,5},{3,6},{7,7},{8,8},{12,9},{10,1... | collective-permute-start | bytes 1572872 | tf_op jit(solution)/shard_map/ppermute | solution.py:938
  135.9 15.8 %collective-permute-start.39 = (bf16[576,128]{1,0:T(8,128)(2,1)S(1)}, bf16[576,128]{1,0:T(8,128)(2,1)S(1)}, u32[]{:S(2)}, u32[]{:S(2)}) collective-permute-start(bf16[576,128]{1,0:T(8,128)(2,1)S(1)} %get-tuple-element.286.refs_0_), channel_id=1, source_target_pairs={{0,8},{8,0},{16,24},{24,16},{1,9},{9,1},{17,25},{25,17},{2,10},{10... | collective-permute-start | bytes 442376 | tf_op jit(solution)/shard_map/ppermute | solution.py:930
  136.2 15.5 %collective-permute-start.38 = (bf16[576,128]{1,0:T(8,128)(2,1)S(1)}, bf16[576,128]{1,0:T(8,128)(2,1)S(1)}, u32[]{:S(2)}, u32[]{:S(2)}) collective-permute-start(bf16[576,128]{1,0:T(8,128)(2,1)S(1)} %get-tuple-element.286.refs_0_), channel_id=1, source_target_pairs={{0,16},{8,24},{16,0},{24,8},{1,17},{9,25},{17,1},{25,9},{2,18},{10... | collective-permute-start | bytes 442376 | tf_op jit(solution)/shard_map/ppermute | solution.py:930
  139.0 12.7 %collective-permute-start.37 = (bf16[576,128]{1,0:T(8,128)(2,1)S(1)}, bf16[576,128]{1,0:T(8,128)(2,1)S(1)}, u32[]{:S(2)}, u32[]{:S(2)}) collective-permute-start(bf16[576,128]{1,0:T(8,128)(2,1)S(1)} %get-tuple-element.286.refs_0_), channel_id=1, source_target_pairs={{0,24},{8,16},{16,8},{24,0},{1,25},{9,17},{17,9},{25,1},{2,26},{10... | collective-permute-start | bytes 442376 | tf_op jit(solution)/shard_map/ppermute | solution.py:930
  (22 other events, 108.8 us)

commit v6 on v5

--- a/solution.py
+++ b/solution.py
@@ -521,6 +521,20 @@
     params[...] = total
 
 
+def block_order(sz, core):
+    held = [0]
+    for step in range(bits_of(sz)):
+        held += [dist ^ step_bit(sz, step, core) for dist in held]
+    return held[1:]
+
+
+def pile_kernel(sz, meta, *refs):
+    at = 0
+    for piece in refs[:-1]:
+        refs[-1][at : at + piece.shape[0]] = piece[...]
+        at += piece.shape[0]
+
+
 def place_maps(sz, meta, own_maps, mine, other, skip, out):
     own = sz.states // sz.blocks
     count = own_maps.shape[0] // 2
@@ -531,9 +545,12 @@
     for index in range(2 * count):
         put(index, meta[0], own_maps[index])
     for side, pieces in ((meta[2], mine), (1 - meta[2], other)):
-        for dist, piece in enumerate(pieces):
+        for place, (even, odd) in enumerate(zip(block_order(sz, 0), block_order(sz, 1)), 1):
+            message = place.bit_length() - 1
+            each = pieces[message].shape[0] >> message
+            owner = meta[0] ^ jnp.where(side == 0, even, odd)
             for index in range(count):
-                put(side * count + index, meta[0] ^ (dist + 1), piece[skip + index])
+                put(side * count + index, owner, pieces[message][(place - (1 << message)) * each + skip + index])
 
 
 def open_kernel(sz, meta, perm, params, *refs):
@@ -564,7 +581,7 @@
 
 def middle_kernel(sz, meta, live, ahead, behind, states, params, normed, hidden, own_out, own_in, *refs):
     skip, gain_b, decay_b = skip_of(params, 0), gain_of(params, 1), decay_of(sz, params, 1)
-    far = sz.blocks - 1
+    far = bits_of(sz)
     mine, other, refs = refs[:far], refs[far : 2 * far], refs[2 * far :]
     w_out, w_in_b, slope, hidden_b, normed_b, driven_b, ends_b, send_b, enter = refs
     place_maps(sz, meta, own_out, mine, other, 0, w_out)
@@ -582,7 +599,7 @@
 
 def leave_kernel(sz, meta, live, ahead, behind, recv, params, ends, driven, normed, hidden, own_out, *refs):
     decay, skip = decay_of(sz, params, 1), skip_of(params, 1)
-    far = sz.blocks - 1
+    far = bits_of(sz)
     mine, other, refs = refs[:far], refs[far : 2 * far], refs[2 * far :]
     w_out, states, slope, last, enter = refs
     place_maps(sz, meta, own_out, mine, other, 3, w_out)
@@ -973,9 +990,17 @@
     first_pieces = across_all(first_pieces)
     cot_cut = call("cut_cotangent", sz, cut_kernel, [], [pltpu.with_memory_space_constraint(cotangent, pltpu.HBM)],
                    [((part, toks), BF)] * blocks, [((blocks, part, toks), F32), pltpu.SemaphoreType.DMA((blocks,))], limit=4, in_spec=HBM)
-    half_b, first_pieces[1], perm, cot_cut = after(half_b, first_pieces[1], perm, cot_cut)
+    first_pieces[1], perm, cot_cut = after(first_pieces[1], perm, cot_cut)
+    second_mine, held = [], half_b
+    for step in range(bits_of(sz)):
+        pairs = [(c * blocks + b, c * blocks + (b ^ step_bit(sz, step, c))) for c in range(2) for b in range(blocks)]
+        second_mine.append(lax.ppermute(held, ("core", "block"), pairs))
+        if step == 0:
+            second_mine[0], first_pieces = after(second_mine[0], first_pieces)
+        if step + 1 < bits_of(sz):
+            (held,) = call("pile_%d" % step, sz, pile_kernel, [], [held, second_mine[-1]], [((2 * held.shape[0], own, width), BF)], [])
     maps_a, params = call("join", sz, join_kernel, [], first_pieces, [((states, width), BF), ((8, width), F32)], [])
-    second_mine = [swap(half_b, dist) for dist in range(1, blocks)]
+
 
     mask = ((toks, LANES), F32)
     enter = ((4, SEGS, states), F32)

time: 156 us -> 151 us (0.968)
  waiting for transfers between devices: 52.9 us -> 48.9 us
    ppermute x12, waiting for transfers between devices: 39.5 us -> 34.2 us  [across(): lax.ppermute(x, ('core', 'block'), [pair[::-1] for pair in pairs] if back...]
    ppermute x28 -> x24, starting transfers between devices: 24.7 us -> 21 us  [swap(): lax.ppermute(x, axis, [(i, i ^ dist) for i in range(lax.axis_size(axis))])]
    ppermute x0 -> x2, starting transfers between devices: none -> 3.35 us  [on_device(): second_mine.append(lax.ppermute(held, ('core', 'block'), pairs))]
    ppermute x0 -> x2, waiting for transfers between devices: none -> 1.85 us  [on_device(): second_mine.append(lax.ppermute(held, ('core', 'block'), pairs))]
    ppermute x12, starting transfers between devices: 12.7 us -> 10.9 us  [across(): lax.ppermute(x, ('core', 'block'), [pair[::-1] for pair in pairs] if back...]
    ppermute x4, starting transfers between devices: 2.61 us -> 4.35 us  [neighbour(): return lax.ppermute(x, ('core', 'block'), pairs)]
    ppermute x28 -> x24, waiting for transfers between devices: 11.5 us -> 11.2 us  [swap(): lax.ppermute(x, axis, [(i, i ^ dist) for i in range(lax.axis_size(axis))])]
    pallas_call x27 -> x28, Pallas kernels: 57.7 us -> 57.7 us  [call(): pl.pallas_call(kernel, out_shape=out_shape, in_specs=[SMEM] * len(items)...]
  transfers between devices with their start and end apart: 47 -> 45, of which waited for: 18 -> 18; matrix products, arithmetic and copies ran while one was open for 0% -> 0% of each run, Pallas kernels for 29% -> 30%
where the time goes in v6:
time: 151 us
  Pallas kernels  57.7 us (38%)
  waiting for transfers between devices  48.9 us (32%)
  starting transfers between devices  42.8 us (28%)
    pallas_call x28, Pallas kernels, call(): pl.pallas_call(kernel, out_shape=out_shape, in_specs=[SMEM] * len(items)...  57.7 us
    ppermute x12, waiting for transfers between devices, across(): lax.ppermute(x, ('core', 'block'), [pair[::-1] for pair in pairs] if back...  34.2 us
    ppermute x24, starting transfers between devices, swap(): lax.ppermute(x, axis, [(i, i ^ dist) for i in range(lax.axis_size(axis))])  21 us
    ppermute x24, waiting for transfers between devices, swap(): lax.ppermute(x, axis, [(i, i ^ dist) for i in range(lax.axis_size(axis))])  11.2 us
    ppermute x12, starting transfers between devices, across(): lax.ppermute(x, ('core', 'block'), [pair[::-1] for pair in pairs] if back...  10.9 us
    ppermute x4, starting transfers between devices, neighbour(): return lax.ppermute(x, ('core', 'block'), pairs)  4.35 us
    ppermute x2, starting transfers between devices, on_device(): second_mine.append(lax.ppermute(held, ('core', 'block'), pairs))  3.35 us
    ppermute x3, starting transfers between devices, send_step(): came[step] = lax.ppermute(message, ('core', 'block'), pairs)  3.2 us
  transfers between devices with their start and end apart: 45, of which 18 were waited for; matrix products, arithmetic and copies ran while one was open for 0% of the time, Pallas kernels for 30%

profile of v6, /device:TPU:0, one launch (start us, length us, event | category | flops | bytes accessed | tf_op | source)
XLA Modules:
  0.0 150.9 jit_solution(13288499615199615252)
XLA Ops:
  0.6 1.9 %prepare.1 = (bf16[192,1024]{1,0:T(8,128)(2,1)S(1)}, bf16[192,1024]{1,0:T(8,128)(2,1)S(1)}, bf16[192,1024]{1,0:T(8,128)(2,1)S(1)}, bf16[192,1024]{1,0:T(8,128)(2...) custom-call(bf16[2,128,2048]{2,1,0:T(8,128)(2,1)} %refs_0_.2, f32[2,128]{1,0:T(2,128)} %refs_1_.1, ...), custom_call_target="tpu_custom_call" | custom-call | bytes 1000 | tf_op jit(solution)/shard_map/prepare/pallas_call | solution.py:923
  2.5 3.0 %collective-permute-start.2 = (bf16[5,96,512]{2,1,0:T(8,128)(2,1)S(1)}, bf16[5,96,512]{2,1,0:T(8,128)(2,1)S(1)}, u32[]{:S(2)}, u32[]{:S(2)}) collective-permute-start(bf16[5,96,512]{2,1,0:T(8,128)(2,1)S(1)} %get-tuple-element.167.refs_0_), channel_id=1, source_target_pairs={{0,1},{1,0},{2,3},{3,2},{4,6},{5,7},{6,4},{7,5},{8,9},{9,8},{10,11... | collective-permute-start | bytes 1474568 | tf_op jit(solution)/shard_map/ppermute | solution.py:997
  5.5 1.5 %collective-permute-start.1 = (bf16[192,1024]{1,0:T(8,128)(2,1)S(1)}, bf16[192,1024]{1,0:T(8,128)(2,1)S(1)}, u32[]{:S(2)}, u32[]{:S(2)}) collective-permute-start(bf16[192,1024]{1,0:T(8,128)(2,1)S(1)} %get-tuple-element.161), channel_id=1, source_target_pairs={{0,2},{1,6},{2,0},{3,4},{4,3},{5,7},{6,1},{7,5},{8,10},{9,14},{10,... | collective-permute-start | bytes 1179656 | tf_op jit(solution)/shard_map/ppermute | solution.py:955
  8.2 1.6 %cut_cotangent.1 = (bf16[128,1024]{1,0:T(8,128)(2,1)S(1)}, bf16[128,1024]{1,0:T(8,128)(2,1)S(1)}, bf16[128,1024]{1,0:T(8,128)(2,1)S(1)}, bf16[128,1024]{1,0:T(8,128)(2,1)S(1)}) custom-call(f32[2,128,2048]{2,1,0:T(8,128)} %refs_0_.3), custom_call_target="tpu_custom_call" | custom-call | bytes 1000 | tf_op jit(solution)/shard_map/cut_cotangent/pallas_call | solution.py:923
  10.2 13.9 %collective-permute-done.1.refs_1_.refs_4_ = bf16[192,1024]{1,0:T(8,128)(2,1)S(1)} collective-permute-done((bf16[192,1024]{1,0:T(8,128)(2,1)S(1)}, bf16[192,1024]{1,0:T(8,128)(2,1)S(1)}, u32[]{:S(2)}, u32[]{:S(2)}) %collective-permute-start.1) | collective-permute-done | bytes 393248 | tf_op jit(solution)/shard_map/ppermute | solution.py:955
  24.2 3.5 %collective-permute-done.3.refs_0_.refs_3_ = bf16[192,1024]{1,0:T(8,128)(2,1)S(1)} collective-permute-done((bf16[192,1024]{1,0:T(8,128)(2,1)S(1)}, bf16[192,1024]{1,0:T(8,128)(2,1)S(1)}, u32[]{:S(2)}, u32[]{:S(2)}) %collective-permute-start.3) | collective-permute-done | bytes 393248 | tf_op jit(solution)/shard_map/ppermute | solution.py:955
  30.7 2.7 %open.1 = (bf16[1024,512]{1,0:T(8,128)(2,1)S(1)}, bf16[1024,512]{1,0:T(8,128)(2,1)S(1)}, f32[1024,128]{1,0:T(8,128)S(1)}, f32[1024,128]{1,0:T(8,128)S(1)}, f32[1024,128]{1,0:T(8,128)S(1)}) custom-call(s32[2,2,2,2]{3,2,1,0:T(2,128)S(1)} %pad_add_fusion.refs_0_, bf16[1024,1024]{1,0:T(8,128)(2,1)S(1)} %fusion.refs_1_.refs_7_.refs_6_, ...), custom_call_target="tpu_custom_call" | custom-call | flops 1200000000 | bytes 1000 | tf_op jit(solution)/shard_map/open/pallas_call | solution.py:923
  33.4 3.0 %enter.1 = (bf16[768,512]{1,0:T(8,128)(2,1)S(1)}, f32[1024,768]{1,0:T(8,128)S(1)}, f32[4,16,384]{2,1,0:T(8,128)S(1)}, f32[1,2,384]{2,1,0:T(2,128)S(1)}) custom-call(s32[2,2,2,2]{3,2,1,0:T(2,128)S(1)} %pad_add_fusion.refs_0_, f32[1024,128]{1,0:T(8,128)S(1)} %get-tuple-element.177.refs_1_.refs_2_, f32[1024,128]{1,0:T(8,128)S(1)} %get-tuple-element.178.refs_2_.refs_3_, ...), custom_call_target="tpu_custom_call" | custom-call | bytes 1000 | tf_op jit(solution)/shard_map/enter/pallas_call | solution.py:923
  37.6 2.4 %chain.1.refs_4_.refs_2_.refs_7_ = bf16[1024,1536]{1,0:T(8,128)(2,1)S(1)} custom-call(s32[2,2,2,2]{3,2,1,0:T(2,128)S(1)} %pad_add_fusion.refs_0_, f32[1024,128]{1,0:T(8,128)S(1)} %get-tuple-element.177.refs_1_.refs_2_, f32[1024,128]{1,0:T(8,128)S(1)} %get-tuple-element.178.refs_2_.refs_3_, f32[1,2,384]{2,1,0:T(2,128)S(1)} %bitcast.18, ...), custom_call_target="tpu_custom_call" | custom-call | bytes 1000 | tf_op jit(solution)/shard_map/chain/pallas_call | solution.py:923
  40.0 1.8 %collective-permute-done.6.refs_11_.refs_12_ = bf16[10,96,512]{2,1,0:T(8,128)(2,1)S(1)} collective-permute-done((bf16[10,96,512]{2,1,0:T(8,128)(2,1)S(1)}, bf16[10,96,512]{2,1,0:T(8,128)(2,1)S(1)}, u32[]{:S(2)}, u32[]{:S(2)}) %collective-permute-start.6) | collective-permute-done | bytes 983072 | tf_op jit(solution)/shard_map/ppermute | solution.py:997
  42.4 2.0 %collective-permute-start.12 = (bf16[128,1024]{1,0:T(8,128)(2,1)S(1)}, bf16[128,1024]{1,0:T(8,128)(2,1)S(1)}, u32[]{:S(2)}, u32[]{:S(2)}) collective-permute-start(bf16[128,1024]{1,0:T(8,128)(2,1)S(1)} %get-tuple-element.202), channel_id=1, source_target_pairs={{0,6},{1,2},{2,4},{3,0},{4,7},{5,3},{6,5},{7,1},{8,14},{9,10},{10,... | collective-permute-start | bytes 786440 | tf_op jit(solution)/shard_map/ppermute | solution.py:955
  44.4 2.2 %collective-permute-start.14 = (bf16[128,1024]{1,0:T(8,128)(2,1)S(1)}, bf16[128,1024]{1,0:T(8,128)(2,1)S(1)}, u32[]{:S(2)}, u32[]{:S(2)}) collective-permute-start(bf16[128,1024]{1,0:T(8,128)(2,1)S(1)} %get-tuple-element.204), channel_id=1, source_target_pairs={{0,4},{1,0},{2,6},{3,2},{4,5},{5,1},{6,7},{7,3},{8,12},{9,8},{10,1... | collective-permute-start | bytes 786440 | tf_op jit(solution)/shard_map/ppermute | solution.py:955
  47.4 6.7 %middle.1 = (bf16[1536,512]{1,0:T(8,128)(2,1)S(1)}, bf16[768,512]{1,0:T(8,128)(2,1)S(1)}, bf16[1024,512]{1,0:T(8,128)(2,1)S(1)}, f32[1024,512]{1,0:T(8,128)S(1)}...) custom-call(s32[2,2,2,2]{3,2,1,0:T(2,128)S(1)} %pad_add_fusion.refs_, ...), custom_call_target="tpu_custom_call" | custom-call | flops 4400000000 | bytes 1000 | tf_op jit(solution)/shard_map/middle/pallas_call | solution.py:923
  54.0 3.5 %collective-permute-start.11 = (f32[2,384]{1,0:T(2,128)S(1)}, f32[2,384]{1,0:T(2,128)S(1)}, u32[]{:S(2)}, u32[]{:S(2)}) collective-permute-start(f32[2,384]{1,0:T(2,128)S(1)} %bitcast.23), channel_id=1, source_target_pairs={{0,4},{1,5},{2,6},{3,7},{4,0},{5,1},{6,2},{7,3},{8,12},{9,13},{10,... | collective-permute-start | bytes 9224 | tf_op jit(solution)/shard_map/ppermute | solution.py:969
  58.3 5.5 %leave.1 = (bf16[1536,512]{1,0:T(8,128)(2,1)S(1)}, bf16[1024,1536]{1,0:T(8,128)(2,1)S(1)}, bf16[1024,512]{1,0:T(8,128)(2,1)S(1)}, bf16[1024,512]{1,0:T(8,128)(2,1)S(1)}) custom-call(s32[2,2,2,2]{3,2,1,0:T(2,128)S(1)} %pad_add_fusion.refs_0_, f32[1024,128]{1,0:T(8,128)S(1)} %get-tuple-element.179.refs_1_, f32[1024,128]{1,0:T(8,128)S(1)} %get-tuple-element.177.refs_1_.refs_2_, ...), custom_call_target="tpu_custom_call" | custom-call | bytes 1000 | tf_op jit(solution)/shard_map/leave/pallas_call | solution.py:923
  63.9 5.1 %turn.1 = (f32[1024,512]{1,0:T(8,128)S(1)}, bf16[1024,512]{1,0:T(8,128)(2,1)S(1)}, f32[1024,1536]{1,0:T(8,128)S(1)}, f32[1,512]{1,0:T(1,128)S(1)}, f32[4,16,384]{2,1,0:T(8,128)S(1)}, /*index=5*/f32[1,2,384]{2,1,0:T(2,128)S(1)}) custom-call(s32[2,2,2,2]{3,2,1,0:T(2,128)S(1)} %pad_add_fusion.refs_0_, f32[1024,128]{1,0:T(8,128)S(1)} %get-tuple-element.177.refs_1_.refs_2_, ...), custom_call_target="tpu_custom_call" | custom-call | flops 2400000000 | bytes 1000 | tf_op jit(solution)/shard_map/turn/pallas_call | solution.py:923
  73.4 9.4 %back_middle.1 = (bf16[1024,768]{1,0:T(8,128)(2,1)S(1)}, f32[2,384]{1,0:T(2,128)S(1)}, f32[1,512]{1,0:T(1,128)S(1)}, f32[1024,512]{1,0:T(8,128)S(1)}, bf16[1024,...) custom-call(s32[2,2,2,2]{3,2,1,0:T(2,128)S(1)} %pad_add_fusion.refs_, ...), custom_call_target="tpu_custom_call" | custom-call | flops 4400000000 | bytes 1000 | tf_op jit(solution)/shard_map/back_middle/pallas_call | solution.py:923
  88.6 3.7 %back_chain.1 = (bf16[1024,768]{1,0:T(8,128)(2,1)S(1)}, f32[2,384]{1,0:T(2,128)S(1)}) custom-call(s32[2,2,2,2]{3,2,1,0:T(2,128)S(1)} %pad_add_fusion.refs_0_, f32[1024,128]{1,0:T(8,128)S(1)} %get-tuple-element.177.refs_1_.refs_2_, f32[1024,128]{1,0:T(8,128)S(1)} %get-tuple-element.178.refs_2_.refs_3_, f32[1,2,384]{2,1,0:T(2,128)S(1)} %bitcast.21, ...), custom_call_target="tpu_custom_call" | custom-call | flops 3600000000 | bytes 1000 | tf_op jit(solution)/shard_map/back_chain/pallas_call | solution.py:923
  94.8 1.8 %collective-permute-start.23 = (bf16[112,512]{1,0:T(8,128)(2,1)S(1)}, bf16[112,512]{1,0:T(8,128)(2,1)S(1)}, u32[]{:S(2)}, u32[]{:S(2)}) collective-permute-start(bf16[112,512]{1,0:T(8,128)(2,1)S(1)} %get-tuple-element.252), channel_id=1, source_target_pairs={{0,3},{1,2},{2,1},{3,0},{4,7},{5,6},{6,5},{7,4},{8,11},{9,10},{10,... | collective-permute-start | bytes 344072 | tf_op jit(solution)/shard_map/ppermute | solution.py:947
  98.4 4.1 %back_leave.1 = (bf16[256,1024]{1,0:T(8,128)(2,1)S(1)}, bf16[256,1024]{1,0:T(8,128)(2,1)S(1)}, bf16[256,1024]{1,0:T(8,128)(2,1)S(1)}, bf16[256,1024]{1,0:T(8,128)(2,1)S(1)}) custom-call(f32[8,512]{1,0:T(8,128)S(1)} %get-tuple-element.176.refs_2_.refs_3_.refs_4_.refs_5_.refs_6_.refs_0_, bf16[1024,768]{1,0:T(8,128)(2,1)S(1)} %get-tuple-element.243.refs_0_.refs_1_, ...), custom_call_target="tpu_custom_call" | custom-call | flops 2400000000 | bytes 1000 | tf_op jit(solution)/shard_map/back_leave/pallas_call | solution.py:923
  102.5 2.1 %collective-permute-done.24.refs_4_ = bf16[112,512]{1,0:T(8,128)(2,1)S(1)} collective-permute-done((bf16[112,512]{1,0:T(8,128)(2,1)S(1)}, bf16[112,512]{1,0:T(8,128)(2,1)S(1)}, u32[]{:S(2)}, u32[]{:S(2)}) %collective-permute-start.24) | collective-permute-done | bytes 114720 | tf_op jit(solution)/shard_map/ppermute | solution.py:947
  106.1 3.6 %collective-permute-start.27 = (bf16[192,128]{1,0:T(8,128)(2,1)S(1)}, bf16[192,128]{1,0:T(8,128)(2,1)S(1)}, u32[]{:S(2)}, u32[]{:S(2)}) collective-permute-start(bf16[192,128]{1,0:T(8,128)(2,1)S(1)} %get-tuple-element.261), channel_id=1, source_target_pairs={{0,24},{8,16},{16,8},{24,0},{1,25},{9,17},{17,9},{25,1},{2,26},{10... | collective-permute-start | bytes 147464 | tf_op jit(solution)/shard_map/ppermute | solution.py:947
  110.5 2.1 %collective-permute-done.27.refs_1_ = bf16[192,128]{1,0:T(8,128)(2,1)S(1)} collective-permute-done((bf16[192,128]{1,0:T(8,128)(2,1)S(1)}, bf16[192,128]{1,0:T(8,128)(2,1)S(1)}, u32[]{:S(2)}, u32[]{:S(2)}) %collective-permute-start.27) | collective-permute-done | bytes 49184 | tf_op jit(solution)/shard_map/ppermute | solution.py:947
  112.6 2.1 %collective-permute-done.28.refs_2_ = bf16[192,128]{1,0:T(8,128)(2,1)S(1)} collective-permute-done((bf16[192,128]{1,0:T(8,128)(2,1)S(1)}, bf16[192,128]{1,0:T(8,128)(2,1)S(1)}, u32[]{:S(2)}, u32[]{:S(2)}) %collective-permute-start.28) | collective-permute-done | bytes 49184 | tf_op jit(solution)/shard_map/ppermute | solution.py:947
  114.9 1.7 %collective-permute-start.30 = (bf16[256,1024]{1,0:T(8,128)(2,1)S(1)}, bf16[256,1024]{1,0:T(8,128)(2,1)S(1)}, u32[]{:S(2)}, u32[]{:S(2)}) collective-permute-start(bf16[256,1024]{1,0:T(8,128)(2,1)S(1)} %get-tuple-element.280), channel_id=1, source_target_pairs={{6,0},{2,1},{4,2},{0,3},{7,4},{3,5},{5,6},{1,7},{14,8},{10,9},{12,... | collective-permute-start | bytes 1572872 | tf_op jit(solution)/shard_map/ppermute | solution.py:955
  116.7 1.6 %collective-permute-start.32 = (bf16[400,128]{1,0:T(8,128)(2,1)S(1)}, bf16[400,128]{1,0:T(8,128)(2,1)S(1)}, u32[]{:S(2)}, u32[]{:S(2)}) collective-permute-start(bf16[400,128]{1,0:T(8,128)(2,1)S(1)} %get-tuple-element.283), channel_id=1, source_target_pairs={{0,24},{8,16},{16,8},{24,0},{1,25},{9,17},{17,9},{25,1},{2,26},{10... | collective-permute-start | bytes 307208 | tf_op jit(solution)/shard_map/ppermute | solution.py:947
  118.7 2.4 %collective-permute-start.34 = (bf16[400,128]{1,0:T(8,128)(2,1)S(1)}, bf16[400,128]{1,0:T(8,128)(2,1)S(1)}, u32[]{:S(2)}, u32[]{:S(2)}) collective-permute-start(bf16[400,128]{1,0:T(8,128)(2,1)S(1)} %get-tuple-element.285), channel_id=1, source_target_pairs={{0,8},{8,0},{16,24},{24,16},{1,9},{9,1},{17,25},{25,17},{2,10},{10... | collective-permute-start | bytes 307208 | tf_op jit(solution)/shard_map/ppermute | solution.py:947
  121.1 6.9 %collective-permute-done.30.refs_0_ = bf16[256,1024]{1,0:T(8,128)(2,1)S(1)} collective-permute-done((bf16[256,1024]{1,0:T(8,128)(2,1)S(1)}, bf16[256,1024]{1,0:T(8,128)(2,1)S(1)}, u32[]{:S(2)}, u32[]{:S(2)}) %collective-permute-start.30) | collective-permute-done | bytes 524320 | tf_op jit(solution)/shard_map/ppermute | solution.py:955
  131.0 2.8 %collective-permute-start.36 = (bf16[576,128]{1,0:T(8,128)(2,1)S(1)}, bf16[576,128]{1,0:T(8,128)(2,1)S(1)}, u32[]{:S(2)}, u32[]{:S(2)}) collective-permute-start(bf16[576,128]{1,0:T(8,128)(2,1)S(1)} %get-tuple-element.292.refs_0_), channel_id=1, source_target_pairs={{0,16},{8,24},{16,0},{24,8},{1,17},{9,25},{17,1},{25,9},{2,18},{10... | collective-permute-start | bytes 442376 | tf_op jit(solution)/shard_map/ppermute | solution.py:947
  135.2 8.8 %collective-permute-done.38.refs_1_ = bf16[256,1024]{1,0:T(8,128)(2,1)S(1)} collective-permute-done((bf16[256,1024]{1,0:T(8,128)(2,1)S(1)}, bf16[256,1024]{1,0:T(8,128)(2,1)S(1)}, u32[]{:S(2)}, u32[]{:S(2)}) %collective-permute-start.38) | collective-permute-done | bytes 524320 | tf_op jit(solution)/shard_map/ppermute | solution.py:955
  144.6 2.1 %spread.1 = (f32[2,128,2048]{2,1,0:T(8,128)}, f32[2,128,2048]{2,1,0:T(8,128)}) custom-call(bf16[256,1024]{1,0:T(8,128)(2,1)S(1)} %collective-permute-done.30.refs_0_, bf16[256,1024]{1,0:T(8,128)(2,1)S(1)} %collective-permute-done.38.refs_1_, bf16[256,1024]{1,0:T(8,128)(2,1)S(1)} %collective-permute-done.31.refs_2_, ...), custom_call_target="tpu_custom_call" | custom-call | flops 3600000000 | bytes 1000 | tf_op jit(solution)/shard_map/spread/pallas_call | solution.py:923
  148.7 2.1 %finish.1 = (f32[2,128]{1,0:T(2,128)}, f32[2,128]{1,0:T(2,128)}, f32[2,96]{1,0:T(2,128)}, f32[2,96]{1,0:T(2,128)}, f32[2,96]{1,0:T(2,128)}, /*index=5*/f32[2,2,96,512]{3,2,1,0:T(8,128)}, f32[2,4,96,512]{3,2,1,0:T(8,128)}) custom-call(bf16[576,128]{1,0:T(8,128)(2,1)S(1)} %get-tuple-element.292.refs_0_, bf16[576,128]{1,0:T(8,128)(2,1)S(1)} %collective-permute-done.35.refs_1_, ...), custom_call_target="tpu_custom_call" | custom-call | bytes 1000 | tf_op jit(solution)/shard_map/finish/pallas_call | solution.py:923
  (105 shorter events, 32.3 us)
Async XLA Ops:
  2.5 25.1 %collective-permute-start.2 = (bf16[5,96,512]{2,1,0:T(8,128)(2,1)S(1)}, bf16[5,96,512]{2,1,0:T(8,128)(2,1)S(1)}, u32[]{:S(2)}, u32[]{:S(2)}) collective-permute-start(bf16[5,96,512]{2,1,0:T(8,128)(2,1)S(1)} %get-tuple-element.167.refs_0_), channel_id=1, source_target_pairs={{0,1},{1,0},{2,3},{3,2},{4,6},{5,7},{6,4},{7,5},{8,9},{9,8},{10,11... | collective-permute-start | bytes 1474568 | tf_op jit(solution)/shard_map/ppermute | solution.py:997
  5.5 18.6 %collective-permute-start.1 = (bf16[192,1024]{1,0:T(8,128)(2,1)S(1)}, bf16[192,1024]{1,0:T(8,128)(2,1)S(1)}, u32[]{:S(2)}, u32[]{:S(2)}) collective-permute-start(bf16[192,1024]{1,0:T(8,128)(2,1)S(1)} %get-tuple-element.161), channel_id=1, source_target_pairs={{0,2},{1,6},{2,0},{3,4},{4,3},{5,7},{6,1},{7,5},{8,10},{9,14},{10,... | collective-permute-start | bytes 1179656 | tf_op jit(solution)/shard_map/ppermute | solution.py:955
  7.0 20.6 %collective-permute-start.3 = (bf16[192,1024]{1,0:T(8,128)(2,1)S(1)}, bf16[192,1024]{1,0:T(8,128)(2,1)S(1)}, u32[]{:S(2)}, u32[]{:S(2)}) collective-permute-start(bf16[192,1024]{1,0:T(8,128)(2,1)S(1)} %get-tuple-element.168), channel_id=1, source_target_pairs={{0,6},{1,2},{2,4},{3,0},{4,7},{5,3},{6,5},{7,1},{8,14},{9,10},{10,... | collective-permute-start | bytes 1179656 | tf_op jit(solution)/shard_map/ppermute | solution.py:955
  7.0 20.6 %collective-permute-start.4 = (bf16[192,1024]{1,0:T(8,128)(2,1)S(1)}, bf16[192,1024]{1,0:T(8,128)(2,1)S(1)}, u32[]{:S(2)}, u32[]{:S(2)}) collective-permute-start(bf16[192,1024]{1,0:T(8,128)(2,1)S(1)} %get-tuple-element.170), channel_id=1, source_target_pairs={{0,4},{1,0},{2,6},{3,2},{4,5},{5,1},{6,7},{7,3},{8,12},{9,8},{10,1... | collective-permute-start | bytes 1179656 | tf_op jit(solution)/shard_map/ppermute | solution.py:955
  7.5 20.1 %collective-permute-start.5 = (bf16[192,1024]{1,0:T(8,128)(2,1)S(1)}, bf16[192,1024]{1,0:T(8,128)(2,1)S(1)}, u32[]{:S(2)}, u32[]{:S(2)}) collective-permute-start(bf16[192,1024]{1,0:T(8,128)(2,1)S(1)} %get-tuple-element.171), channel_id=1, source_target_pairs={{0,0},{1,4},{2,2},{3,6},{4,1},{5,5},{6,3},{7,7},{8,8},{9,12},{10,1... | collective-permute-start | bytes 1179656 | tf_op jit(solution)/shard_map/ppermute | solution.py:955
  27.7 14.2 %collective-permute-start.6 = (bf16[10,96,512]{2,1,0:T(8,128)(2,1)S(1)}, bf16[10,96,512]{2,1,0:T(8,128)(2,1)S(1)}, u32[]{:S(2)}, u32[]{:S(2)}) collective-permute-start(bf16[10,96,512]{2,1,0:T(8,128)(2,1)S(1)} %pile_0.1), channel_id=1, source_target_pairs={{0,2},{1,3},{2,0},{3,1},{4,5},{5,4},{6,7},{7,6},{8,10},{9,11},{10,... | collective-permute-start | bytes 2949128 | tf_op jit(solution)/shard_map/ppermute | solution.py:997
  28.2 5.2 %collective-permute-start.7 = (bf16[384,512]{1,0:T(8,128)(2,1)S(1)}, bf16[384,512]{1,0:T(8,128)(2,1)S(1)}, u32[]{:S(2)}, u32[]{:S(2)}) collective-permute-start(bf16[384,512]{1,0:T(8,128)(2,1)S(1)} %get-tuple-element.182.refs_5_), channel_id=1, source_target_pairs={{0,4},{4,0},{1,5},{5,1},{2,6},{6,2},{3,7},{7,3},{8,12},{12,8},{9,1... | collective-permute-start | bytes 1179656 | tf_op jit(solution)/shard_map/ppermute | solution.py:947
  41.9 5.5 %collective-permute-start.10 = (bf16[10,96,512]{2,1,0:T(8,128)(2,1)S(1)}, bf16[10,96,512]{2,1,0:T(8,128)(2,1)S(1)}, u32[]{:S(2)}, u32[]{:S(2)}) collective-permute-start(bf16[10,96,512]{2,1,0:T(8,128)(2,1)S(1)} %collective-permute-done.6.refs_11_.refs_12_), channel_id=1, source_target_pairs={{0,4},{4,0},{1,5},{5,1},{2,6},{6,2},{3,7},{7,3},{8,12},{12,8},{9,1... | collective-permute-start | bytes 2949128 | tf_op jit(solution)/shard_map/ppermute | solution.py:947
  42.1 4.5 %collective-permute-start.9 = (bf16[5,96,512]{2,1,0:T(8,128)(2,1)S(1)}, bf16[5,96,512]{2,1,0:T(8,128)(2,1)S(1)}, u32[]{:S(2)}, u32[]{:S(2)}) collective-permute-start(bf16[5,96,512]{2,1,0:T(8,128)(2,1)S(1)} %collective-permute-done.2.refs_1_.refs_10_.refs_11_), channel_id=1, source_target_pairs={{0,4},{4,0},{1,5},{5,1},{2,6},{6,2},{3,7},{7,3},{8,12},{12,8},{9,1... | collective-permute-start | bytes 1474568 | tf_op jit(solution)/shard_map/ppermute | solution.py:947
  42.4 21.4 %collective-permute-start.12 = (bf16[128,1024]{1,0:T(8,128)(2,1)S(1)}, bf16[128,1024]{1,0:T(8,128)(2,1)S(1)}, u32[]{:S(2)}, u32[]{:S(2)}) collective-permute-start(bf16[128,1024]{1,0:T(8,128)(2,1)S(1)} %get-tuple-element.202), channel_id=1, source_target_pairs={{0,6},{1,2},{2,4},{3,0},{4,7},{5,3},{6,5},{7,1},{8,14},{9,10},{10,... | collective-permute-start | bytes 786440 | tf_op jit(solution)/shard_map/ppermute | solution.py:955
  44.4 19.4 %collective-permute-start.13 = (bf16[128,1024]{1,0:T(8,128)(2,1)S(1)}, bf16[128,1024]{1,0:T(8,128)(2,1)S(1)}, u32[]{:S(2)}, u32[]{:S(2)}) collective-permute-start(bf16[128,1024]{1,0:T(8,128)(2,1)S(1)} %get-tuple-element.203), channel_id=1, source_target_pairs={{0,2},{1,6},{2,0},{3,4},{4,3},{5,7},{6,1},{7,5},{8,10},{9,14},{10,... | collective-permute-start | bytes 786440 | tf_op jit(solution)/shard_map/ppermute | solution.py:955
  44.4 19.4 %collective-permute-start.14 = (bf16[128,1024]{1,0:T(8,128)(2,1)S(1)}, bf16[128,1024]{1,0:T(8,128)(2,1)S(1)}, u32[]{:S(2)}, u32[]{:S(2)}) collective-permute-start(bf16[128,1024]{1,0:T(8,128)(2,1)S(1)} %get-tuple-element.204), channel_id=1, source_target_pairs={{0,4},{1,0},{2,6},{3,2},{4,5},{5,1},{6,7},{7,3},{8,12},{9,8},{10,1... | collective-permute-start | bytes 786440 | tf_op jit(solution)/shard_map/ppermute | solution.py:955
  46.7 17.2 %collective-permute-start.15 = (bf16[128,1024]{1,0:T(8,128)(2,1)S(1)}, bf16[128,1024]{1,0:T(8,128)(2,1)S(1)}, u32[]{:S(2)}, u32[]{:S(2)}) collective-permute-start(bf16[128,1024]{1,0:T(8,128)(2,1)S(1)} %get-tuple-element.205), channel_id=1, source_target_pairs={{0,0},{1,4},{2,2},{3,6},{4,1},{5,5},{6,3},{7,7},{8,8},{9,12},{10,1... | collective-permute-start | bytes 786440 | tf_op jit(solution)/shard_map/ppermute | solution.py:955
  72.6 10.3 %collective-permute-start.18 = (bf16[384,512]{1,0:T(8,128)(2,1)S(1)}, bf16[384,512]{1,0:T(8,128)(2,1)S(1)}, u32[]{:S(2)}, u32[]{:S(2)}) collective-permute-start(bf16[384,512]{1,0:T(8,128)(2,1)S(1)} %get-tuple-element.218), channel_id=1, source_target_pairs={{0,1},{1,0},{2,3},{3,2},{4,6},{5,7},{6,4},{7,5},{8,9},{9,8},{10,11... | collective-permute-start | bytes 1179656 | tf_op jit(solution)/shard_map/ppermute | solution.py:1072
  87.6 17.0 %collective-permute-start.22 = (bf16[768,512]{1,0:T(8,128)(2,1)S(1)}, bf16[768,512]{1,0:T(8,128)(2,1)S(1)}, u32[]{:S(2)}, u32[]{:S(2)}) collective-permute-start(bf16[768,512]{1,0:T(8,128)(2,1)S(1)} %get-tuple-element.250), channel_id=1, source_target_pairs={{0,2},{1,3},{2,0},{3,1},{4,5},{5,4},{6,7},{7,6},{8,10},{9,11},{10,... | collective-permute-start | bytes 2359304 | tf_op jit(solution)/shard_map/ppermute | solution.py:1072
  94.8 7.6 %collective-permute-start.23 = (bf16[112,512]{1,0:T(8,128)(2,1)S(1)}, bf16[112,512]{1,0:T(8,128)(2,1)S(1)}, u32[]{:S(2)}, u32[]{:S(2)}) collective-permute-start(bf16[112,512]{1,0:T(8,128)(2,1)S(1)} %get-tuple-element.252), channel_id=1, source_target_pairs={{0,3},{1,2},{2,1},{3,0},{4,7},{5,6},{6,5},{7,4},{8,11},{9,10},{10,... | collective-permute-start | bytes 344072 | tf_op jit(solution)/shard_map/ppermute | solution.py:947
  96.6 7.9 %collective-permute-start.24 = (bf16[112,512]{1,0:T(8,128)(2,1)S(1)}, bf16[112,512]{1,0:T(8,128)(2,1)S(1)}, u32[]{:S(2)}, u32[]{:S(2)}) collective-permute-start(bf16[112,512]{1,0:T(8,128)(2,1)S(1)} %get-tuple-element.253), channel_id=1, source_target_pairs={{0,2},{1,3},{2,0},{3,1},{4,6},{5,7},{6,4},{7,5},{8,10},{9,11},{10,... | collective-permute-start | bytes 344072 | tf_op jit(solution)/shard_map/ppermute | solution.py:947
  97.6 7.0 %collective-permute-start.25 = (bf16[112,512]{1,0:T(8,128)(2,1)S(1)}, bf16[112,512]{1,0:T(8,128)(2,1)S(1)}, u32[]{:S(2)}, u32[]{:S(2)}) collective-permute-start(bf16[112,512]{1,0:T(8,128)(2,1)S(1)} %get-tuple-element.254), channel_id=1, source_target_pairs={{0,1},{1,0},{2,3},{3,2},{4,5},{5,4},{6,7},{7,6},{8,9},{9,8},{10,11... | collective-permute-start | bytes 344072 | tf_op jit(solution)/shard_map/ppermute | solution.py:947
  104.7 10.0 %collective-permute-start.26 = (bf16[288,512]{1,0:T(8,128)(2,1)S(1)}, bf16[288,512]{1,0:T(8,128)(2,1)S(1)}, u32[]{:S(2)}, u32[]{:S(2)}) collective-permute-start(bf16[288,512]{1,0:T(8,128)(2,1)S(1)} %get-tuple-element.258), channel_id=1, source_target_pairs={{0,1},{1,0},{2,3},{3,2},{4,6},{5,7},{6,4},{7,5},{8,9},{9,8},{10,11... | collective-permute-start | bytes 884744 | tf_op jit(solution)/shard_map/ppermute | solution.py:1072
  106.1 6.5 %collective-permute-start.27 = (bf16[192,128]{1,0:T(8,128)(2,1)S(1)}, bf16[192,128]{1,0:T(8,128)(2,1)S(1)}, u32[]{:S(2)}, u32[]{:S(2)}) collective-permute-start(bf16[192,128]{1,0:T(8,128)(2,1)S(1)} %get-tuple-element.261), channel_id=1, source_target_pairs={{0,24},{8,16},{16,8},{24,0},{1,25},{9,17},{17,9},{25,1},{2,26},{10... | collective-permute-start | bytes 147464 | tf_op jit(solution)/shard_map/ppermute | solution.py:947
  109.7 5.0 %collective-permute-start.28 = (bf16[192,128]{1,0:T(8,128)(2,1)S(1)}, bf16[192,128]{1,0:T(8,128)(2,1)S(1)}, u32[]{:S(2)}, u32[]{:S(2)}) collective-permute-start(bf16[192,128]{1,0:T(8,128)(2,1)S(1)} %get-tuple-element.262), channel_id=1, source_target_pairs={{0,16},{8,24},{16,0},{24,8},{1,17},{9,25},{17,1},{25,9},{2,18},{10... | collective-permute-start | bytes 147464 | tf_op jit(solution)/shard_map/ppermute | solution.py:947
  109.7 5.0 %collective-permute-start.29 = (bf16[192,128]{1,0:T(8,128)(2,1)S(1)}, bf16[192,128]{1,0:T(8,128)(2,1)S(1)}, u32[]{:S(2)}, u32[]{:S(2)}) collective-permute-start(bf16[192,128]{1,0:T(8,128)(2,1)S(1)} %get-tuple-element.263), channel_id=1, source_target_pairs={{0,8},{8,0},{16,24},{24,16},{1,9},{9,1},{17,25},{25,17},{2,10},{10... | collective-permute-start | bytes 147464 | tf_op jit(solution)/shard_map/ppermute | solution.py:947
  114.9 13.0 %collective-permute-start.30 = (bf16[256,1024]{1,0:T(8,128)(2,1)S(1)}, bf16[256,1024]{1,0:T(8,128)(2,1)S(1)}, u32[]{:S(2)}, u32[]{:S(2)}) collective-permute-start(bf16[256,1024]{1,0:T(8,128)(2,1)S(1)} %get-tuple-element.280), channel_id=1, source_target_pairs={{6,0},{2,1},{4,2},{0,3},{7,4},{3,5},{5,6},{1,7},{14,8},{10,9},{12,... | collective-permute-start | bytes 1572872 | tf_op jit(solution)/shard_map/ppermute | solution.py:955
  116.7 12.4 %collective-permute-start.31 = (bf16[256,1024]{1,0:T(8,128)(2,1)S(1)}, bf16[256,1024]{1,0:T(8,128)(2,1)S(1)}, u32[]{:S(2)}, u32[]{:S(2)}) collective-permute-start(bf16[256,1024]{1,0:T(8,128)(2,1)S(1)} %get-tuple-element.281), channel_id=1, source_target_pairs={{4,0},{0,1},{6,2},{2,3},{5,4},{1,5},{7,6},{3,7},{12,8},{8,9},{14,1... | collective-permute-start | bytes 1572872 | tf_op jit(solution)/shard_map/ppermute | solution.py:955
  116.7 12.4 %collective-permute-start.32 = (bf16[400,128]{1,0:T(8,128)(2,1)S(1)}, bf16[400,128]{1,0:T(8,128)(2,1)S(1)}, u32[]{:S(2)}, u32[]{:S(2)}) collective-permute-start(bf16[400,128]{1,0:T(8,128)(2,1)S(1)} %get-tuple-element.283), channel_id=1, source_target_pairs={{0,24},{8,16},{16,8},{24,0},{1,25},{9,17},{17,9},{25,1},{2,26},{10... | collective-permute-start | bytes 307208 | tf_op jit(solution)/shard_map/ppermute | solution.py:947
  118.3 10.8 %collective-permute-start.33 = (bf16[400,128]{1,0:T(8,128)(2,1)S(1)}, bf16[400,128]{1,0:T(8,128)(2,1)S(1)}, u32[]{:S(2)}, u32[]{:S(2)}) collective-permute-start(bf16[400,128]{1,0:T(8,128)(2,1)S(1)} %get-tuple-element.284), channel_id=1, source_target_pairs={{0,16},{8,24},{16,0},{24,8},{1,17},{9,25},{17,1},{25,9},{2,18},{10... | collective-permute-start | bytes 307208 | tf_op jit(solution)/shard_map/ppermute | solution.py:947
  118.7 10.4 %collective-permute-start.34 = (bf16[400,128]{1,0:T(8,128)(2,1)S(1)}, bf16[400,128]{1,0:T(8,128)(2,1)S(1)}, u32[]{:S(2)}, u32[]{:S(2)}) collective-permute-start(bf16[400,128]{1,0:T(8,128)(2,1)S(1)} %get-tuple-element.285), channel_id=1, source_target_pairs={{0,8},{8,0},{16,24},{24,16},{1,9},{9,1},{17,25},{25,17},{2,10},{10... | collective-permute-start | bytes 307208 | tf_op jit(solution)/shard_map/ppermute | solution.py:947
  129.1 14.9 %collective-permute-start.38 = (bf16[256,1024]{1,0:T(8,128)(2,1)S(1)}, bf16[256,1024]{1,0:T(8,128)(2,1)S(1)}, u32[]{:S(2)}, u32[]{:S(2)}) collective-permute-start(bf16[256,1024]{1,0:T(8,128)(2,1)S(1)} %get-tuple-element.289), channel_id=1, source_target_pairs={{2,0},{6,1},{0,2},{4,3},{3,4},{7,5},{1,6},{5,7},{10,8},{14,9},{8,1... | collective-permute-start | bytes 1572872 | tf_op jit(solution)/shard_map/ppermute | solution.py:955
  130.1 13.9 %collective-permute-start.39 = (bf16[256,1024]{1,0:T(8,128)(2,1)S(1)}, bf16[256,1024]{1,0:T(8,128)(2,1)S(1)}, u32[]{:S(2)}, u32[]{:S(2)}) collective-permute-start(bf16[256,1024]{1,0:T(8,128)(2,1)S(1)} %get-tuple-element.290), channel_id=1, source_target_pairs={{0,0},{4,1},{2,2},{6,3},{1,4},{5,5},{3,6},{7,7},{8,8},{12,9},{10,1... | collective-permute-start | bytes 1572872 | tf_op jit(solution)/shard_map/ppermute | solution.py:955
  130.8 15.9 %collective-permute-start.37 = (bf16[576,128]{1,0:T(8,128)(2,1)S(1)}, bf16[576,128]{1,0:T(8,128)(2,1)S(1)}, u32[]{:S(2)}, u32[]{:S(2)}) collective-permute-start(bf16[576,128]{1,0:T(8,128)(2,1)S(1)} %get-tuple-element.292.refs_0_), channel_id=1, source_target_pairs={{0,8},{8,0},{16,24},{24,16},{1,9},{9,1},{17,25},{25,17},{2,10},{10... | collective-permute-start | bytes 442376 | tf_op jit(solution)/shard_map/ppermute | solution.py:947
  131.0 15.7 %collective-permute-start.36 = (bf16[576,128]{1,0:T(8,128)(2,1)S(1)}, bf16[576,128]{1,0:T(8,128)(2,1)S(1)}, u32[]{:S(2)}, u32[]{:S(2)}) collective-permute-start(bf16[576,128]{1,0:T(8,128)(2,1)S(1)} %get-tuple-element.292.refs_0_), channel_id=1, source_target_pairs={{0,16},{8,24},{16,0},{24,8},{1,17},{9,25},{17,1},{25,9},{2,18},{10... | collective-permute-start | bytes 442376 | tf_op jit(solution)/shard_map/ppermute | solution.py:947
  133.8 12.9 %collective-permute-start.35 = (bf16[576,128]{1,0:T(8,128)(2,1)S(1)}, bf16[576,128]{1,0:T(8,128)(2,1)S(1)}, u32[]{:S(2)}, u32[]{:S(2)}) collective-permute-start(bf16[576,128]{1,0:T(8,128)(2,1)S(1)} %get-tuple-element.292.refs_0_), channel_id=1, source_target_pairs={{0,24},{8,16},{16,8},{24,0},{1,25},{9,17},{17,9},{25,1},{2,26},{10... | collective-permute-start | bytes 442376 | tf_op jit(solution)/shard_map/ppermute | solution.py:947
  (20 other events, 90.2 us)

commit v7 on v6

--- a/solution.py
+++ b/solution.py
@@ -102,7 +102,7 @@
         behind[rows_of(step), :] = onward_next
         return carry
 
-    lax.fori_loop(0, sz.steps, body, 0, unroll=4)
+    lax.fori_loop(0, sz.steps, body, 0, unroll=8)
 
 
 def through(sz, meta, first, length):
@@ -152,7 +152,7 @@
                 new.append((re, im))
         return tuple(new)
 
-    held = lax.fori_loop(0, sz.steps, body, tuple((zero, zero) for _ in range(2 * nq)), unroll=4)
+    held = lax.fori_loop(0, sz.steps, body, tuple((zero, zero) for _ in range(2 * nq)), unroll=8)
     for q in range(nq):
         cols = slice(q * LANES, (q + 1) * LANES)
         for side in range(2):
@@ -245,7 +245,7 @@
                 new.append((re, im))
         return tuple(new)
 
-    lax.fori_loop(0, sz.steps, body, load_enter(sz, enter), unroll=4)
+    lax.fori_loop(0, sz.steps, body, load_enter(sz, enter), unroll=8)
 
 
 def adjoint_chains(sz, decay, ahead, behind, source, enter, states, half, grad_driven, grad_decay):
@@ -288,8 +288,8 @@
         return body
 
     carry = (load_enter(sz, enter), tuple((zero, zero) for _ in range(nq)))
-    carry = lax.fori_loop(0, sz.steps // 2, make(False), carry, unroll=2)
-    carry = lax.fori_loop(sz.steps // 2, sz.steps, make(True), carry, unroll=2)
+    carry = lax.fori_loop(0, sz.steps // 2, make(False), carry, unroll=4)
+    carry = lax.fori_loop(sz.steps // 2, sz.steps, make(True), carry, unroll=4)
     for q in range(nq):
         cols = slice(q * LANES, (q + 1) * LANES)
         grad_decay[0:1, cols] = jnp.sum(carry[1][q][0], axis=0, keepdims=True)
@@ -958,7 +958,7 @@
         return [across(piece, dist, back) for dist, piece in enumerate(pieces)]
 
     table = jnp.stack([item_lengths, item_offsets])
-    items = [jnp.stack([table, swap(table, 1, "core")])]
+    other_table = swap(table, 1, "core")
 
     def neighbour(x, dist):
         pairs = []
@@ -1000,6 +1000,8 @@
         if step + 1 < bits_of(sz):
             (held,) = call("pile_%d" % step, sz, pile_kernel, [], [held, second_mine[-1]], [((2 * held.shape[0], own, width), BF)], [])
     maps_a, params = call("join", sz, join_kernel, [], first_pieces, [((states, width), BF), ((8, width), F32)], [])
+    maps_a, other_table = after(maps_a, other_table)
+    items = [jnp.stack([table, other_table])]
 
 
     mask = ((toks, LANES), F32)
@@ -1020,9 +1022,11 @@
     w_in_a, driven_a, ends_a, send_a = call(
         "enter", sz, enter_kernel, items, [ahead, behind, params, normed_a, maps_a, other_a], [w_in, drv, enter, snd], [enter])
     recv = exchange(send_a)
+    early_maps = [swap(piece, 1, "core") for piece in second_mine[:-1]]
+    recv, early_maps = after(recv, early_maps)
     (states_a,) = call("chain", sz, chain_kernel, items, [ahead, behind, recv, params, ends_a, driven_a], [sts], [enter])
-    second_mine, states_a = after(second_mine, states_a)
-    second_maps = second_mine, [swap(piece, 1, "core") for piece in second_mine]
+    last_mine, states_a = after(second_mine[-1], states_a)
+    second_maps = [*second_mine[:-1], last_mine], [*early_maps, swap(last_mine, 1, "core")]
     cot_cut, _ = after(cot_cut, recv)
     cot_pieces = across_all(cot_cut)
     w_out_a, w_in_b, slope_a, hidden_b, normed_b, driven_b, ends_b, send_b = call(

time: 151 us -> 150 us (level)
  no operation moved by 1% of the time
where the time goes in v7:
time: 150 us
  Pallas kernels  56.7 us (38%)
  waiting for transfers between devices  48.8 us (33%)
  starting transfers between devices  42.7 us (28%)
    pallas_call x28, Pallas kernels, call(): pl.pallas_call(kernel, out_shape=out_shape, in_specs=[SMEM] * len(items)...  56.7 us
    ppermute x12, waiting for transfers between devices, across(): lax.ppermute(x, ('core', 'block'), [pair[::-1] for pair in pairs] if back...  34 us
    ppermute x24, starting transfers between devices, swap(): lax.ppermute(x, axis, [(i, i ^ dist) for i in range(lax.axis_size(axis))])  21.3 us
    ppermute x24, waiting for transfers between devices, swap(): lax.ppermute(x, axis, [(i, i ^ dist) for i in range(lax.axis_size(axis))])  11.3 us
    ppermute x12, starting transfers between devices, across(): lax.ppermute(x, ('core', 'block'), [pair[::-1] for pair in pairs] if back...  10.7 us
    ppermute x4, starting transfers between devices, neighbour(): return lax.ppermute(x, ('core', 'block'), pairs)  4.04 us
    ppermute x2, starting transfers between devices, on_device(): second_mine.append(lax.ppermute(held, ('core', 'block'), pairs))  3.35 us
    ppermute x3, starting transfers between devices, send_step(): came[step] = lax.ppermute(message, ('core', 'block'), pairs)  3.26 us
  transfers between devices with their start and end apart: 45, of which 18 were waited for; matrix products, arithmetic and copies ran while one was open for 0% of the time, Pallas kernels for 30%

profile of v7, /device:TPU:0, one launch (start us, length us, event | category | flops | bytes accessed | tf_op | source)
XLA Modules:
  0.0 149.8 jit_solution(12112358025916506125)
XLA Ops:
  0.6 1.9 %prepare.1 = (bf16[192,1024]{1,0:T(8,128)(2,1)S(1)}, bf16[192,1024]{1,0:T(8,128)(2,1)S(1)}, bf16[192,1024]{1,0:T(8,128)(2,1)S(1)}, bf16[192,1024]{1,0:T(8,128)(2...) custom-call(bf16[2,128,2048]{2,1,0:T(8,128)(2,1)} %refs_0_.2, f32[2,128]{1,0:T(2,128)} %refs_1_.1, ...), custom_call_target="tpu_custom_call" | custom-call | bytes 1000 | tf_op jit(solution)/shard_map/prepare/pallas_call | solution.py:923
  2.5 3.0 %collective-permute-start = (bf16[5,96,512]{2,1,0:T(8,128)(2,1)S(1)}, bf16[5,96,512]{2,1,0:T(8,128)(2,1)S(1)}, u32[]{:S(2)}, u32[]{:S(2)}) collective-permute-start(bf16[5,96,512]{2,1,0:T(8,128)(2,1)S(1)} %get-tuple-element.164.refs_0_), channel_id=1, source_target_pairs={{0,1},{1,0},{2,3},{3,2},{4,6},{5,7},{6,4},{7,5},{8,9},{9,8},{10,11... | collective-permute-start | bytes 1474568 | tf_op jit(solution)/shard_map/ppermute | solution.py:997
  5.5 1.5 %collective-permute-start.2 = (bf16[192,1024]{1,0:T(8,128)(2,1)S(1)}, bf16[192,1024]{1,0:T(8,128)(2,1)S(1)}, u32[]{:S(2)}, u32[]{:S(2)}) collective-permute-start(bf16[192,1024]{1,0:T(8,128)(2,1)S(1)} %get-tuple-element.166), channel_id=1, source_target_pairs={{0,2},{1,6},{2,0},{3,4},{4,3},{5,7},{6,1},{7,5},{8,10},{9,14},{10,... | collective-permute-start | bytes 1179656 | tf_op jit(solution)/shard_map/ppermute | solution.py:955
  8.2 1.6 %cut_cotangent.1 = (bf16[128,1024]{1,0:T(8,128)(2,1)S(1)}, bf16[128,1024]{1,0:T(8,128)(2,1)S(1)}, bf16[128,1024]{1,0:T(8,128)(2,1)S(1)}, bf16[128,1024]{1,0:T(8,128)(2,1)S(1)}) custom-call(f32[2,128,2048]{2,1,0:T(8,128)} %refs_0_.3), custom_call_target="tpu_custom_call" | custom-call | bytes 1000 | tf_op jit(solution)/shard_map/cut_cotangent/pallas_call | solution.py:923
  10.2 13.9 %collective-permute-done.2.refs_1_.refs_4_ = bf16[192,1024]{1,0:T(8,128)(2,1)S(1)} collective-permute-done((bf16[192,1024]{1,0:T(8,128)(2,1)S(1)}, bf16[192,1024]{1,0:T(8,128)(2,1)S(1)}, u32[]{:S(2)}, u32[]{:S(2)}) %collective-permute-start.2) | collective-permute-done | bytes 393248 | tf_op jit(solution)/shard_map/ppermute | solution.py:955
  24.2 3.5 %collective-permute-done.1.refs_0_.refs_3_ = bf16[192,1024]{1,0:T(8,128)(2,1)S(1)} collective-permute-done((bf16[192,1024]{1,0:T(8,128)(2,1)S(1)}, bf16[192,1024]{1,0:T(8,128)(2,1)S(1)}, u32[]{:S(2)}, u32[]{:S(2)}) %collective-permute-start.1) | collective-permute-done | bytes 393248 | tf_op jit(solution)/shard_map/ppermute | solution.py:955
  31.1 2.6 %open.1 = (bf16[1024,512]{1,0:T(8,128)(2,1)S(1)}, bf16[1024,512]{1,0:T(8,128)(2,1)S(1)}, f32[1024,128]{1,0:T(8,128)S(1)}, f32[1024,128]{1,0:T(8,128)S(1)}, f32[1024,128]{1,0:T(8,128)S(1)}) custom-call(s32[2,2,2,2]{3,2,1,0:T(2,128)S(1)} %pad_add_fusion.refs_0_, bf16[1024,1024]{1,0:T(8,128)(2,1)S(1)} %fusion.refs_1_.refs_7_.refs_6_, ...), custom_call_target="tpu_custom_call" | custom-call | flops 1200000000 | bytes 1000 | tf_op jit(solution)/shard_map/open/pallas_call | solution.py:923
  33.8 2.9 %enter.1 = (bf16[768,512]{1,0:T(8,128)(2,1)S(1)}, f32[1024,768]{1,0:T(8,128)S(1)}, f32[4,16,384]{2,1,0:T(8,128)S(1)}, f32[1,2,384]{2,1,0:T(2,128)S(1)}) custom-call(s32[2,2,2,2]{3,2,1,0:T(2,128)S(1)} %pad_add_fusion.refs_0_, f32[1024,128]{1,0:T(8,128)S(1)} %get-tuple-element.182.refs_1_.refs_2_, f32[1024,128]{1,0:T(8,128)S(1)} %get-tuple-element.183.refs_2_.refs_3_, ...), custom_call_target="tpu_custom_call" | custom-call | bytes 1000 | tf_op jit(solution)/shard_map/enter/pallas_call | solution.py:923
  37.9 2.4 %chain.1.refs_4_.refs_2_.refs_7_ = bf16[1024,1536]{1,0:T(8,128)(2,1)S(1)} custom-call(s32[2,2,2,2]{3,2,1,0:T(2,128)S(1)} %pad_add_fusion.refs_0_, f32[1024,128]{1,0:T(8,128)S(1)} %get-tuple-element.182.refs_1_.refs_2_, f32[1024,128]{1,0:T(8,128)S(1)} %get-tuple-element.183.refs_2_.refs_3_, f32[1,2,384]{2,1,0:T(2,128)S(1)} %bitcast.18, ...), custom_call_target="tpu_custom_call" | custom-call | bytes 1000 | tf_op jit(solution)/shard_map/chain/pallas_call | solution.py:923
  40.3 1.6 %collective-permute-done.6.refs_11_.refs_12_ = bf16[10,96,512]{2,1,0:T(8,128)(2,1)S(1)} collective-permute-done((bf16[10,96,512]{2,1,0:T(8,128)(2,1)S(1)}, bf16[10,96,512]{2,1,0:T(8,128)(2,1)S(1)}, u32[]{:S(2)}, u32[]{:S(2)}) %collective-permute-start.6) | collective-permute-done | bytes 983072 | tf_op jit(solution)/shard_map/ppermute | solution.py:997
  42.2 1.7 %collective-permute-start.12 = (bf16[128,1024]{1,0:T(8,128)(2,1)S(1)}, bf16[128,1024]{1,0:T(8,128)(2,1)S(1)}, u32[]{:S(2)}, u32[]{:S(2)}) collective-permute-start(bf16[128,1024]{1,0:T(8,128)(2,1)S(1)} %get-tuple-element.208), channel_id=1, source_target_pairs={{0,6},{1,2},{2,4},{3,0},{4,7},{5,3},{6,5},{7,1},{8,14},{9,10},{10,... | collective-permute-start | bytes 786440 | tf_op jit(solution)/shard_map/ppermute | solution.py:955
  44.4 1.8 %collective-permute-start.14 = (bf16[128,1024]{1,0:T(8,128)(2,1)S(1)}, bf16[128,1024]{1,0:T(8,128)(2,1)S(1)}, u32[]{:S(2)}, u32[]{:S(2)}) collective-permute-start(bf16[128,1024]{1,0:T(8,128)(2,1)S(1)} %get-tuple-element.210), channel_id=1, source_target_pairs={{0,4},{1,0},{2,6},{3,2},{4,5},{5,1},{6,7},{7,3},{8,12},{9,8},{10,1... | collective-permute-start | bytes 786440 | tf_op jit(solution)/shard_map/ppermute | solution.py:955
  46.9 6.6 %middle.1 = (bf16[1536,512]{1,0:T(8,128)(2,1)S(1)}, bf16[768,512]{1,0:T(8,128)(2,1)S(1)}, bf16[1024,512]{1,0:T(8,128)(2,1)S(1)}, f32[1024,512]{1,0:T(8,128)S(1)}...) custom-call(s32[2,2,2,2]{3,2,1,0:T(2,128)S(1)} %pad_add_fusion.refs_, ...), custom_call_target="tpu_custom_call" | custom-call | flops 4400000000 | bytes 1000 | tf_op jit(solution)/shard_map/middle/pallas_call | solution.py:923
  53.5 3.5 %collective-permute-start.11 = (f32[2,384]{1,0:T(2,128)S(1)}, f32[2,384]{1,0:T(2,128)S(1)}, u32[]{:S(2)}, u32[]{:S(2)}) collective-permute-start(f32[2,384]{1,0:T(2,128)S(1)} %bitcast.23), channel_id=1, source_target_pairs={{0,4},{1,5},{2,6},{3,7},{4,0},{5,1},{6,2},{7,3},{8,12},{9,13},{10,... | collective-permute-start | bytes 9224 | tf_op jit(solution)/shard_map/ppermute | solution.py:969
  57.8 5.5 %leave.1 = (bf16[1536,512]{1,0:T(8,128)(2,1)S(1)}, bf16[1024,1536]{1,0:T(8,128)(2,1)S(1)}, bf16[1024,512]{1,0:T(8,128)(2,1)S(1)}, bf16[1024,512]{1,0:T(8,128)(2,1)S(1)}) custom-call(s32[2,2,2,2]{3,2,1,0:T(2,128)S(1)} %pad_add_fusion.refs_0_, f32[1024,128]{1,0:T(8,128)S(1)} %get-tuple-element.184.refs_1_, f32[1024,128]{1,0:T(8,128)S(1)} %get-tuple-element.182.refs_1_.refs_2_, ...), custom_call_target="tpu_custom_call" | custom-call | bytes 1000 | tf_op jit(solution)/shard_map/leave/pallas_call | solution.py:923
  63.4 5.0 %turn.1 = (f32[1024,512]{1,0:T(8,128)S(1)}, bf16[1024,512]{1,0:T(8,128)(2,1)S(1)}, f32[1024,1536]{1,0:T(8,128)S(1)}, f32[1,512]{1,0:T(1,128)S(1)}, f32[4,16,384]{2,1,0:T(8,128)S(1)}, /*index=5*/f32[1,2,384]{2,1,0:T(2,128)S(1)}) custom-call(s32[2,2,2,2]{3,2,1,0:T(2,128)S(1)} %pad_add_fusion.refs_0_, f32[1024,128]{1,0:T(8,128)S(1)} %get-tuple-element.182.refs_1_.refs_2_, ...), custom_call_target="tpu_custom_call" | custom-call | flops 2400000000 | bytes 1000 | tf_op jit(solution)/shard_map/turn/pallas_call | solution.py:923
  72.7 9.1 %back_middle.1 = (bf16[1024,768]{1,0:T(8,128)(2,1)S(1)}, f32[2,384]{1,0:T(2,128)S(1)}, f32[1,512]{1,0:T(1,128)S(1)}, f32[1024,512]{1,0:T(8,128)S(1)}, bf16[1024,...) custom-call(s32[2,2,2,2]{3,2,1,0:T(2,128)S(1)} %pad_add_fusion.refs_, ...), custom_call_target="tpu_custom_call" | custom-call | flops 4400000000 | bytes 1000 | tf_op jit(solution)/shard_map/back_middle/pallas_call | solution.py:923
  87.6 3.5 %back_chain.1 = (bf16[1024,768]{1,0:T(8,128)(2,1)S(1)}, f32[2,384]{1,0:T(2,128)S(1)}) custom-call(s32[2,2,2,2]{3,2,1,0:T(2,128)S(1)} %pad_add_fusion.refs_0_, f32[1024,128]{1,0:T(8,128)S(1)} %get-tuple-element.182.refs_1_.refs_2_, f32[1024,128]{1,0:T(8,128)S(1)} %get-tuple-element.183.refs_2_.refs_3_, f32[1,2,384]{2,1,0:T(2,128)S(1)} %bitcast.21, ...), custom_call_target="tpu_custom_call" | custom-call | flops 3600000000 | bytes 1000 | tf_op jit(solution)/shard_map/back_chain/pallas_call | solution.py:923
  93.6 1.8 %collective-permute-start.23 = (bf16[112,512]{1,0:T(8,128)(2,1)S(1)}, bf16[112,512]{1,0:T(8,128)(2,1)S(1)}, u32[]{:S(2)}, u32[]{:S(2)}) collective-permute-start(bf16[112,512]{1,0:T(8,128)(2,1)S(1)} %get-tuple-element.258), channel_id=1, source_target_pairs={{0,3},{1,2},{2,1},{3,0},{4,7},{5,6},{6,5},{7,4},{8,11},{9,10},{10,... | collective-permute-start | bytes 344072 | tf_op jit(solution)/shard_map/ppermute | solution.py:947
  97.2 4.1 %back_leave.1 = (bf16[256,1024]{1,0:T(8,128)(2,1)S(1)}, bf16[256,1024]{1,0:T(8,128)(2,1)S(1)}, bf16[256,1024]{1,0:T(8,128)(2,1)S(1)}, bf16[256,1024]{1,0:T(8,128)(2,1)S(1)}) custom-call(f32[8,512]{1,0:T(8,128)S(1)} %get-tuple-element.181.refs_2_.refs_3_.refs_4_.refs_5_.refs_6_.refs_0_, bf16[1024,768]{1,0:T(8,128)(2,1)S(1)} %get-tuple-element.249.refs_0_.refs_1_, ...), custom_call_target="tpu_custom_call" | custom-call | flops 2400000000 | bytes 1000 | tf_op jit(solution)/shard_map/back_leave/pallas_call | solution.py:923
  101.3 2.2 %collective-permute-done.24.refs_4_ = bf16[112,512]{1,0:T(8,128)(2,1)S(1)} collective-permute-done((bf16[112,512]{1,0:T(8,128)(2,1)S(1)}, bf16[112,512]{1,0:T(8,128)(2,1)S(1)}, u32[]{:S(2)}, u32[]{:S(2)}) %collective-permute-start.24) | collective-permute-done | bytes 114720 | tf_op jit(solution)/shard_map/ppermute | solution.py:947
  105.1 3.7 %collective-permute-start.27 = (bf16[192,128]{1,0:T(8,128)(2,1)S(1)}, bf16[192,128]{1,0:T(8,128)(2,1)S(1)}, u32[]{:S(2)}, u32[]{:S(2)}) collective-permute-start(bf16[192,128]{1,0:T(8,128)(2,1)S(1)} %get-tuple-element.267), channel_id=1, source_target_pairs={{0,24},{8,16},{16,8},{24,0},{1,25},{9,17},{17,9},{25,1},{2,26},{10... | collective-permute-start | bytes 147464 | tf_op jit(solution)/shard_map/ppermute | solution.py:947
  109.6 1.9 %collective-permute-done.27.refs_1_ = bf16[192,128]{1,0:T(8,128)(2,1)S(1)} collective-permute-done((bf16[192,128]{1,0:T(8,128)(2,1)S(1)}, bf16[192,128]{1,0:T(8,128)(2,1)S(1)}, u32[]{:S(2)}, u32[]{:S(2)}) %collective-permute-start.27) | collective-permute-done | bytes 49184 | tf_op jit(solution)/shard_map/ppermute | solution.py:947
  111.5 2.3 %collective-permute-done.28.refs_2_ = bf16[192,128]{1,0:T(8,128)(2,1)S(1)} collective-permute-done((bf16[192,128]{1,0:T(8,128)(2,1)S(1)}, bf16[192,128]{1,0:T(8,128)(2,1)S(1)}, u32[]{:S(2)}, u32[]{:S(2)}) %collective-permute-start.28) | collective-permute-done | bytes 49184 | tf_op jit(solution)/shard_map/ppermute | solution.py:947
  114.0 1.6 %collective-permute-start.30 = (bf16[256,1024]{1,0:T(8,128)(2,1)S(1)}, bf16[256,1024]{1,0:T(8,128)(2,1)S(1)}, u32[]{:S(2)}, u32[]{:S(2)}) collective-permute-start(bf16[256,1024]{1,0:T(8,128)(2,1)S(1)} %get-tuple-element.286), channel_id=1, source_target_pairs={{6,0},{2,1},{4,2},{0,3},{7,4},{3,5},{5,6},{1,7},{14,8},{10,9},{12,... | collective-permute-start | bytes 1572872 | tf_op jit(solution)/shard_map/ppermute | solution.py:955
  115.6 1.6 %collective-permute-start.32 = (bf16[400,128]{1,0:T(8,128)(2,1)S(1)}, bf16[400,128]{1,0:T(8,128)(2,1)S(1)}, u32[]{:S(2)}, u32[]{:S(2)}) collective-permute-start(bf16[400,128]{1,0:T(8,128)(2,1)S(1)} %get-tuple-element.289), channel_id=1, source_target_pairs={{0,24},{8,16},{16,8},{24,0},{1,25},{9,17},{17,9},{25,1},{2,26},{10... | collective-permute-start | bytes 307208 | tf_op jit(solution)/shard_map/ppermute | solution.py:947
  117.6 2.4 %collective-permute-start.34 = (bf16[400,128]{1,0:T(8,128)(2,1)S(1)}, bf16[400,128]{1,0:T(8,128)(2,1)S(1)}, u32[]{:S(2)}, u32[]{:S(2)}) collective-permute-start(bf16[400,128]{1,0:T(8,128)(2,1)S(1)} %get-tuple-element.291), channel_id=1, source_target_pairs={{0,8},{8,0},{16,24},{24,16},{1,9},{9,1},{17,25},{25,17},{2,10},{10... | collective-permute-start | bytes 307208 | tf_op jit(solution)/shard_map/ppermute | solution.py:947
  120.0 6.9 %collective-permute-done.30.refs_0_ = bf16[256,1024]{1,0:T(8,128)(2,1)S(1)} collective-permute-done((bf16[256,1024]{1,0:T(8,128)(2,1)S(1)}, bf16[256,1024]{1,0:T(8,128)(2,1)S(1)}, u32[]{:S(2)}, u32[]{:S(2)}) %collective-permute-start.30) | collective-permute-done | bytes 524320 | tf_op jit(solution)/shard_map/ppermute | solution.py:955
  130.1 2.8 %collective-permute-start.36 = (bf16[576,128]{1,0:T(8,128)(2,1)S(1)}, bf16[576,128]{1,0:T(8,128)(2,1)S(1)}, u32[]{:S(2)}, u32[]{:S(2)}) collective-permute-start(bf16[576,128]{1,0:T(8,128)(2,1)S(1)} %get-tuple-element.298.refs_0_), channel_id=1, source_target_pairs={{0,16},{8,24},{16,0},{24,8},{1,17},{9,25},{17,1},{25,9},{2,18},{10... | collective-permute-start | bytes 442376 | tf_op jit(solution)/shard_map/ppermute | solution.py:947
  134.3 8.6 %collective-permute-done.38.refs_1_ = bf16[256,1024]{1,0:T(8,128)(2,1)S(1)} collective-permute-done((bf16[256,1024]{1,0:T(8,128)(2,1)S(1)}, bf16[256,1024]{1,0:T(8,128)(2,1)S(1)}, u32[]{:S(2)}, u32[]{:S(2)}) %collective-permute-start.38) | collective-permute-done | bytes 524320 | tf_op jit(solution)/shard_map/ppermute | solution.py:955
  143.5 2.1 %spread.1 = (f32[2,128,2048]{2,1,0:T(8,128)}, f32[2,128,2048]{2,1,0:T(8,128)}) custom-call(bf16[256,1024]{1,0:T(8,128)(2,1)S(1)} %collective-permute-done.30.refs_0_, bf16[256,1024]{1,0:T(8,128)(2,1)S(1)} %collective-permute-done.38.refs_1_, bf16[256,1024]{1,0:T(8,128)(2,1)S(1)} %collective-permute-done.31.refs_2_, ...), custom_call_target="tpu_custom_call" | custom-call | flops 3600000000 | bytes 1000 | tf_op jit(solution)/shard_map/spread/pallas_call | solution.py:923
  147.7 2.1 %finish.1 = (f32[2,128]{1,0:T(2,128)}, f32[2,128]{1,0:T(2,128)}, f32[2,96]{1,0:T(2,128)}, f32[2,96]{1,0:T(2,128)}, f32[2,96]{1,0:T(2,128)}, /*index=5*/f32[2,2,96,512]{3,2,1,0:T(8,128)}, f32[2,4,96,512]{3,2,1,0:T(8,128)}) custom-call(bf16[576,128]{1,0:T(8,128)(2,1)S(1)} %get-tuple-element.298.refs_0_, bf16[576,128]{1,0:T(8,128)(2,1)S(1)} %collective-permute-done.35.refs_1_, ...), custom_call_target="tpu_custom_call" | custom-call | bytes 1000 | tf_op jit(solution)/shard_map/finish/pallas_call | solution.py:923
  (105 shorter events, 33.1 us)
Async XLA Ops:
  2.5 25.1 %collective-permute-start = (bf16[5,96,512]{2,1,0:T(8,128)(2,1)S(1)}, bf16[5,96,512]{2,1,0:T(8,128)(2,1)S(1)}, u32[]{:S(2)}, u32[]{:S(2)}) collective-permute-start(bf16[5,96,512]{2,1,0:T(8,128)(2,1)S(1)} %get-tuple-element.164.refs_0_), channel_id=1, source_target_pairs={{0,1},{1,0},{2,3},{3,2},{4,6},{5,7},{6,4},{7,5},{8,9},{9,8},{10,11... | collective-permute-start | bytes 1474568 | tf_op jit(solution)/shard_map/ppermute | solution.py:997
  5.5 18.6 %collective-permute-start.2 = (bf16[192,1024]{1,0:T(8,128)(2,1)S(1)}, bf16[192,1024]{1,0:T(8,128)(2,1)S(1)}, u32[]{:S(2)}, u32[]{:S(2)}) collective-permute-start(bf16[192,1024]{1,0:T(8,128)(2,1)S(1)} %get-tuple-element.166), channel_id=1, source_target_pairs={{0,2},{1,6},{2,0},{3,4},{4,3},{5,7},{6,1},{7,5},{8,10},{9,14},{10,... | collective-permute-start | bytes 1179656 | tf_op jit(solution)/shard_map/ppermute | solution.py:955
  7.0 20.6 %collective-permute-start.1 = (bf16[192,1024]{1,0:T(8,128)(2,1)S(1)}, bf16[192,1024]{1,0:T(8,128)(2,1)S(1)}, u32[]{:S(2)}, u32[]{:S(2)}) collective-permute-start(bf16[192,1024]{1,0:T(8,128)(2,1)S(1)} %get-tuple-element.165), channel_id=1, source_target_pairs={{0,6},{1,2},{2,4},{3,0},{4,7},{5,3},{6,5},{7,1},{8,14},{9,10},{10,... | collective-permute-start | bytes 1179656 | tf_op jit(solution)/shard_map/ppermute | solution.py:955
  7.0 20.6 %collective-permute-start.3 = (bf16[192,1024]{1,0:T(8,128)(2,1)S(1)}, bf16[192,1024]{1,0:T(8,128)(2,1)S(1)}, u32[]{:S(2)}, u32[]{:S(2)}) collective-permute-start(bf16[192,1024]{1,0:T(8,128)(2,1)S(1)} %get-tuple-element.172), channel_id=1, source_target_pairs={{0,4},{1,0},{2,6},{3,2},{4,5},{5,1},{6,7},{7,3},{8,12},{9,8},{10,1... | collective-permute-start | bytes 1179656 | tf_op jit(solution)/shard_map/ppermute | solution.py:955
  7.5 20.1 %collective-permute-start.4 = (bf16[192,1024]{1,0:T(8,128)(2,1)S(1)}, bf16[192,1024]{1,0:T(8,128)(2,1)S(1)}, u32[]{:S(2)}, u32[]{:S(2)}) collective-permute-start(bf16[192,1024]{1,0:T(8,128)(2,1)S(1)} %get-tuple-element.173), channel_id=1, source_target_pairs={{0,0},{1,4},{2,2},{3,6},{4,1},{5,5},{6,3},{7,7},{8,8},{9,12},{10,1... | collective-permute-start | bytes 1179656 | tf_op jit(solution)/shard_map/ppermute | solution.py:955
  27.7 14.2 %collective-permute-start.6 = (bf16[10,96,512]{2,1,0:T(8,128)(2,1)S(1)}, bf16[10,96,512]{2,1,0:T(8,128)(2,1)S(1)}, u32[]{:S(2)}, u32[]{:S(2)}) collective-permute-start(bf16[10,96,512]{2,1,0:T(8,128)(2,1)S(1)} %pile_0.1), channel_id=1, source_target_pairs={{0,2},{1,3},{2,0},{3,1},{4,5},{5,4},{6,7},{7,6},{8,10},{9,11},{10,... | collective-permute-start | bytes 2949128 | tf_op jit(solution)/shard_map/ppermute | solution.py:997
  28.1 9.8 %collective-permute-start.9 = (bf16[5,96,512]{2,1,0:T(8,128)(2,1)S(1)}, bf16[5,96,512]{2,1,0:T(8,128)(2,1)S(1)}, u32[]{:S(2)}, u32[]{:S(2)}) collective-permute-start(bf16[5,96,512]{2,1,0:T(8,128)(2,1)S(1)} %collective-permute-done.refs_1_.refs_10_.refs_11_), channel_id=1, source_target_pairs={{0,4},{4,0},{1,5},{5,1},{2,6},{6,2},{3,7},{7,3},{8,12},{12,8},{9,1... | collective-permute-start | bytes 1474568 | tf_op jit(solution)/shard_map/ppermute | solution.py:947
  41.9 5.0 %collective-permute-start.10 = (bf16[10,96,512]{2,1,0:T(8,128)(2,1)S(1)}, bf16[10,96,512]{2,1,0:T(8,128)(2,1)S(1)}, u32[]{:S(2)}, u32[]{:S(2)}) collective-permute-start(bf16[10,96,512]{2,1,0:T(8,128)(2,1)S(1)} %collective-permute-done.6.refs_11_.refs_12_), channel_id=1, source_target_pairs={{0,4},{4,0},{1,5},{5,1},{2,6},{6,2},{3,7},{7,3},{8,12},{12,8},{9,1... | collective-permute-start | bytes 2949128 | tf_op jit(solution)/shard_map/ppermute | solution.py:947
  42.2 21.1 %collective-permute-start.12 = (bf16[128,1024]{1,0:T(8,128)(2,1)S(1)}, bf16[128,1024]{1,0:T(8,128)(2,1)S(1)}, u32[]{:S(2)}, u32[]{:S(2)}) collective-permute-start(bf16[128,1024]{1,0:T(8,128)(2,1)S(1)} %get-tuple-element.208), channel_id=1, source_target_pairs={{0,6},{1,2},{2,4},{3,0},{4,7},{5,3},{6,5},{7,1},{8,14},{9,10},{10,... | collective-permute-start | bytes 786440 | tf_op jit(solution)/shard_map/ppermute | solution.py:955
  43.9 19.4 %collective-permute-start.13 = (bf16[128,1024]{1,0:T(8,128)(2,1)S(1)}, bf16[128,1024]{1,0:T(8,128)(2,1)S(1)}, u32[]{:S(2)}, u32[]{:S(2)}) collective-permute-start(bf16[128,1024]{1,0:T(8,128)(2,1)S(1)} %get-tuple-element.209), channel_id=1, source_target_pairs={{0,2},{1,6},{2,0},{3,4},{4,3},{5,7},{6,1},{7,5},{8,10},{9,14},{10,... | collective-permute-start | bytes 786440 | tf_op jit(solution)/shard_map/ppermute | solution.py:955
  44.4 19.0 %collective-permute-start.14 = (bf16[128,1024]{1,0:T(8,128)(2,1)S(1)}, bf16[128,1024]{1,0:T(8,128)(2,1)S(1)}, u32[]{:S(2)}, u32[]{:S(2)}) collective-permute-start(bf16[128,1024]{1,0:T(8,128)(2,1)S(1)} %get-tuple-element.210), channel_id=1, source_target_pairs={{0,4},{1,0},{2,6},{3,2},{4,5},{5,1},{6,7},{7,3},{8,12},{9,8},{10,1... | collective-permute-start | bytes 786440 | tf_op jit(solution)/shard_map/ppermute | solution.py:955
  46.2 17.2 %collective-permute-start.15 = (bf16[128,1024]{1,0:T(8,128)(2,1)S(1)}, bf16[128,1024]{1,0:T(8,128)(2,1)S(1)}, u32[]{:S(2)}, u32[]{:S(2)}) collective-permute-start(bf16[128,1024]{1,0:T(8,128)(2,1)S(1)} %get-tuple-element.211), channel_id=1, source_target_pairs={{0,0},{1,4},{2,2},{3,6},{4,1},{5,5},{6,3},{7,7},{8,8},{9,12},{10,1... | collective-permute-start | bytes 786440 | tf_op jit(solution)/shard_map/ppermute | solution.py:955
  53.5 4.3 %collective-permute-start.11 = (f32[2,384]{1,0:T(2,128)S(1)}, f32[2,384]{1,0:T(2,128)S(1)}, u32[]{:S(2)}, u32[]{:S(2)}) collective-permute-start(f32[2,384]{1,0:T(2,128)S(1)} %bitcast.23), channel_id=1, source_target_pairs={{0,4},{1,5},{2,6},{3,7},{4,0},{5,1},{6,2},{7,3},{8,12},{9,13},{10,... | collective-permute-start | bytes 9224 | tf_op jit(solution)/shard_map/ppermute | solution.py:969
  72.0 9.8 %collective-permute-start.18 = (bf16[384,512]{1,0:T(8,128)(2,1)S(1)}, bf16[384,512]{1,0:T(8,128)(2,1)S(1)}, u32[]{:S(2)}, u32[]{:S(2)}) collective-permute-start(bf16[384,512]{1,0:T(8,128)(2,1)S(1)} %get-tuple-element.224), channel_id=1, source_target_pairs={{0,1},{1,0},{2,3},{3,2},{4,6},{5,7},{6,4},{7,5},{8,9},{9,8},{10,11... | collective-permute-start | bytes 1179656 | tf_op jit(solution)/shard_map/ppermute | solution.py:1076
  86.5 17.0 %collective-permute-start.22 = (bf16[768,512]{1,0:T(8,128)(2,1)S(1)}, bf16[768,512]{1,0:T(8,128)(2,1)S(1)}, u32[]{:S(2)}, u32[]{:S(2)}) collective-permute-start(bf16[768,512]{1,0:T(8,128)(2,1)S(1)} %get-tuple-element.256), channel_id=1, source_target_pairs={{0,2},{1,3},{2,0},{3,1},{4,5},{5,4},{6,7},{7,6},{8,10},{9,11},{10,... | collective-permute-start | bytes 2359304 | tf_op jit(solution)/shard_map/ppermute | solution.py:1076
  93.6 7.6 %collective-permute-start.23 = (bf16[112,512]{1,0:T(8,128)(2,1)S(1)}, bf16[112,512]{1,0:T(8,128)(2,1)S(1)}, u32[]{:S(2)}, u32[]{:S(2)}) collective-permute-start(bf16[112,512]{1,0:T(8,128)(2,1)S(1)} %get-tuple-element.258), channel_id=1, source_target_pairs={{0,3},{1,2},{2,1},{3,0},{4,7},{5,6},{6,5},{7,4},{8,11},{9,10},{10,... | collective-permute-start | bytes 344072 | tf_op jit(solution)/shard_map/ppermute | solution.py:947
  95.5 8.0 %collective-permute-start.24 = (bf16[112,512]{1,0:T(8,128)(2,1)S(1)}, bf16[112,512]{1,0:T(8,128)(2,1)S(1)}, u32[]{:S(2)}, u32[]{:S(2)}) collective-permute-start(bf16[112,512]{1,0:T(8,128)(2,1)S(1)} %get-tuple-element.259), channel_id=1, source_target_pairs={{0,2},{1,3},{2,0},{3,1},{4,6},{5,7},{6,4},{7,5},{8,10},{9,11},{10,... | collective-permute-start | bytes 344072 | tf_op jit(solution)/shard_map/ppermute | solution.py:947
  96.5 7.0 %collective-permute-start.25 = (bf16[112,512]{1,0:T(8,128)(2,1)S(1)}, bf16[112,512]{1,0:T(8,128)(2,1)S(1)}, u32[]{:S(2)}, u32[]{:S(2)}) collective-permute-start(bf16[112,512]{1,0:T(8,128)(2,1)S(1)} %get-tuple-element.260), channel_id=1, source_target_pairs={{0,1},{1,0},{2,3},{3,2},{4,5},{5,4},{6,7},{7,6},{8,9},{9,8},{10,11... | collective-permute-start | bytes 344072 | tf_op jit(solution)/shard_map/ppermute | solution.py:947
  103.6 10.2 %collective-permute-start.26 = (bf16[288,512]{1,0:T(8,128)(2,1)S(1)}, bf16[288,512]{1,0:T(8,128)(2,1)S(1)}, u32[]{:S(2)}, u32[]{:S(2)}) collective-permute-start(bf16[288,512]{1,0:T(8,128)(2,1)S(1)} %get-tuple-element.264), channel_id=1, source_target_pairs={{0,1},{1,0},{2,3},{3,2},{4,6},{5,7},{6,4},{7,5},{8,9},{9,8},{10,11... | collective-permute-start | bytes 884744 | tf_op jit(solution)/shard_map/ppermute | solution.py:1076
  105.1 6.4 %collective-permute-start.27 = (bf16[192,128]{1,0:T(8,128)(2,1)S(1)}, bf16[192,128]{1,0:T(8,128)(2,1)S(1)}, u32[]{:S(2)}, u32[]{:S(2)}) collective-permute-start(bf16[192,128]{1,0:T(8,128)(2,1)S(1)} %get-tuple-element.267), channel_id=1, source_target_pairs={{0,24},{8,16},{16,8},{24,0},{1,25},{9,17},{17,9},{25,1},{2,26},{10... | collective-permute-start | bytes 147464 | tf_op jit(solution)/shard_map/ppermute | solution.py:947
  108.8 5.0 %collective-permute-start.28 = (bf16[192,128]{1,0:T(8,128)(2,1)S(1)}, bf16[192,128]{1,0:T(8,128)(2,1)S(1)}, u32[]{:S(2)}, u32[]{:S(2)}) collective-permute-start(bf16[192,128]{1,0:T(8,128)(2,1)S(1)} %get-tuple-element.268), channel_id=1, source_target_pairs={{0,16},{8,24},{16,0},{24,8},{1,17},{9,25},{17,1},{25,9},{2,18},{10... | collective-permute-start | bytes 147464 | tf_op jit(solution)/shard_map/ppermute | solution.py:947
  108.8 5.0 %collective-permute-start.29 = (bf16[192,128]{1,0:T(8,128)(2,1)S(1)}, bf16[192,128]{1,0:T(8,128)(2,1)S(1)}, u32[]{:S(2)}, u32[]{:S(2)}) collective-permute-start(bf16[192,128]{1,0:T(8,128)(2,1)S(1)} %get-tuple-element.269), channel_id=1, source_target_pairs={{0,8},{8,0},{16,24},{24,16},{1,9},{9,1},{17,25},{25,17},{2,10},{10... | collective-permute-start | bytes 147464 | tf_op jit(solution)/shard_map/ppermute | solution.py:947
  114.0 12.9 %collective-permute-start.30 = (bf16[256,1024]{1,0:T(8,128)(2,1)S(1)}, bf16[256,1024]{1,0:T(8,128)(2,1)S(1)}, u32[]{:S(2)}, u32[]{:S(2)}) collective-permute-start(bf16[256,1024]{1,0:T(8,128)(2,1)S(1)} %get-tuple-element.286), channel_id=1, source_target_pairs={{6,0},{2,1},{4,2},{0,3},{7,4},{3,5},{5,6},{1,7},{14,8},{10,9},{12,... | collective-permute-start | bytes 1572872 | tf_op jit(solution)/shard_map/ppermute | solution.py:955
  115.6 12.4 %collective-permute-start.31 = (bf16[256,1024]{1,0:T(8,128)(2,1)S(1)}, bf16[256,1024]{1,0:T(8,128)(2,1)S(1)}, u32[]{:S(2)}, u32[]{:S(2)}) collective-permute-start(bf16[256,1024]{1,0:T(8,128)(2,1)S(1)} %get-tuple-element.287), channel_id=1, source_target_pairs={{4,0},{0,1},{6,2},{2,3},{5,4},{1,5},{7,6},{3,7},{12,8},{8,9},{14,1... | collective-permute-start | bytes 1572872 | tf_op jit(solution)/shard_map/ppermute | solution.py:955
  115.6 12.4 %collective-permute-start.32 = (bf16[400,128]{1,0:T(8,128)(2,1)S(1)}, bf16[400,128]{1,0:T(8,128)(2,1)S(1)}, u32[]{:S(2)}, u32[]{:S(2)}) collective-permute-start(bf16[400,128]{1,0:T(8,128)(2,1)S(1)} %get-tuple-element.289), channel_id=1, source_target_pairs={{0,24},{8,16},{16,8},{24,0},{1,25},{9,17},{17,9},{25,1},{2,26},{10... | collective-permute-start | bytes 307208 | tf_op jit(solution)/shard_map/ppermute | solution.py:947
  117.2 10.8 %collective-permute-start.33 = (bf16[400,128]{1,0:T(8,128)(2,1)S(1)}, bf16[400,128]{1,0:T(8,128)(2,1)S(1)}, u32[]{:S(2)}, u32[]{:S(2)}) collective-permute-start(bf16[400,128]{1,0:T(8,128)(2,1)S(1)} %get-tuple-element.290), channel_id=1, source_target_pairs={{0,16},{8,24},{16,0},{24,8},{1,17},{9,25},{17,1},{25,9},{2,18},{10... | collective-permute-start | bytes 307208 | tf_op jit(solution)/shard_map/ppermute | solution.py:947
  117.6 10.3 %collective-permute-start.34 = (bf16[400,128]{1,0:T(8,128)(2,1)S(1)}, bf16[400,128]{1,0:T(8,128)(2,1)S(1)}, u32[]{:S(2)}, u32[]{:S(2)}) collective-permute-start(bf16[400,128]{1,0:T(8,128)(2,1)S(1)} %get-tuple-element.291), channel_id=1, source_target_pairs={{0,8},{8,0},{16,24},{24,16},{1,9},{9,1},{17,25},{25,17},{2,10},{10... | collective-permute-start | bytes 307208 | tf_op jit(solution)/shard_map/ppermute | solution.py:947
  128.0 14.9 %collective-permute-start.38 = (bf16[256,1024]{1,0:T(8,128)(2,1)S(1)}, bf16[256,1024]{1,0:T(8,128)(2,1)S(1)}, u32[]{:S(2)}, u32[]{:S(2)}) collective-permute-start(bf16[256,1024]{1,0:T(8,128)(2,1)S(1)} %get-tuple-element.295), channel_id=1, source_target_pairs={{2,0},{6,1},{0,2},{4,3},{3,4},{7,5},{1,6},{5,7},{10,8},{14,9},{8,1... | collective-permute-start | bytes 1572872 | tf_op jit(solution)/shard_map/ppermute | solution.py:955
  129.1 13.8 %collective-permute-start.39 = (bf16[256,1024]{1,0:T(8,128)(2,1)S(1)}, bf16[256,1024]{1,0:T(8,128)(2,1)S(1)}, u32[]{:S(2)}, u32[]{:S(2)}) collective-permute-start(bf16[256,1024]{1,0:T(8,128)(2,1)S(1)} %get-tuple-element.296), channel_id=1, source_target_pairs={{0,0},{4,1},{2,2},{6,3},{1,4},{5,5},{3,6},{7,7},{8,8},{12,9},{10,1... | collective-permute-start | bytes 1572872 | tf_op jit(solution)/shard_map/ppermute | solution.py:955
  129.8 15.8 %collective-permute-start.37 = (bf16[576,128]{1,0:T(8,128)(2,1)S(1)}, bf16[576,128]{1,0:T(8,128)(2,1)S(1)}, u32[]{:S(2)}, u32[]{:S(2)}) collective-permute-start(bf16[576,128]{1,0:T(8,128)(2,1)S(1)} %get-tuple-element.298.refs_0_), channel_id=1, source_target_pairs={{0,8},{8,0},{16,24},{24,16},{1,9},{9,1},{17,25},{25,17},{2,10},{10... | collective-permute-start | bytes 442376 | tf_op jit(solution)/shard_map/ppermute | solution.py:947
  130.1 15.5 %collective-permute-start.36 = (bf16[576,128]{1,0:T(8,128)(2,1)S(1)}, bf16[576,128]{1,0:T(8,128)(2,1)S(1)}, u32[]{:S(2)}, u32[]{:S(2)}) collective-permute-start(bf16[576,128]{1,0:T(8,128)(2,1)S(1)} %get-tuple-element.298.refs_0_), channel_id=1, source_target_pairs={{0,16},{8,24},{16,0},{24,8},{1,17},{9,25},{17,1},{25,9},{2,18},{10... | collective-permute-start | bytes 442376 | tf_op jit(solution)/shard_map/ppermute | solution.py:947
  132.9 12.7 %collective-permute-start.35 = (bf16[576,128]{1,0:T(8,128)(2,1)S(1)}, bf16[576,128]{1,0:T(8,128)(2,1)S(1)}, u32[]{:S(2)}, u32[]{:S(2)}) collective-permute-start(bf16[576,128]{1,0:T(8,128)(2,1)S(1)} %get-tuple-element.298.refs_0_), channel_id=1, source_target_pairs={{0,24},{8,16},{16,8},{24,0},{1,25},{9,17},{17,9},{25,1},{2,26},{10... | collective-permute-start | bytes 442376 | tf_op jit(solution)/shard_map/ppermute | solution.py:947
  (20 other events, 89.1 us)

commit v8 on v7

--- a/solution.py
+++ b/solution.py
@@ -892,14 +892,14 @@
         grad_step[at, :] = (turn[0] * gd[0] + turn[1] * gd[1]) * h
 
 
-def spread_kernel(sz, meta, *refs):
-    pieces, outs, wide, sems = refs[: sz.blocks], refs[sz.blocks : -2], refs[-2], refs[-1]
+def spread_kernel(indices, count, sz, meta, *refs):
+    pieces, outs, wide, sems = refs[: len(indices)], refs[-2 - count : -2], refs[-2], refs[-1]
     part = sz.width // sz.blocks
     copies = []
-    for dist, piece in enumerate(pieces):
+    for piece, dist in zip(pieces, indices):
         owner = meta[0] ^ turned(sz, dist)
         for index, out in enumerate(outs):
-            slot = dist * len(outs) + index
+            slot = len(copies)
             wide[slot] = piece[index * part : (index + 1) * part, :].astype(F32)
             cols = pl.ds(pl.multiple_of(lax.rem(owner, sz.chunks) * sz.toks, LANES), sz.toks)
             copy = pltpu.make_async_copy(wide.at[slot], out.at[lax.div(owner, sz.chunks), :, cols], sems.at[slot])
@@ -914,7 +914,7 @@
 HBM = pl.BlockSpec(memory_space=pltpu.HBM)
 
 
-def call(name, sz, body, items, args, outs, scratch, limit=10, in_spec=VMEM, out_spec=VMEM, time=0.0):
+def call(name, sz, body, items, args, outs, scratch, limit=10, in_spec=VMEM, out_spec=VMEM, time=0.0, onto=()):
     out_shape = [jax.ShapeDtypeStruct(shape, dtype) for shape, dtype in outs]
 
     def kernel(*refs):
@@ -923,13 +923,14 @@
     return pl.pallas_call(
         kernel,
         out_shape=out_shape,
-        in_specs=[SMEM] * len(items) + [in_spec] * len(args),
+        in_specs=[SMEM] * len(items) + [in_spec] * len(args) + [HBM] * len(onto),
         out_specs=[out_spec] * len(outs),
         scratch_shapes=[pltpu.VMEM(*item) if isinstance(item, tuple) else item for item in scratch],
         compiler_params=pltpu.CompilerParams(vmem_limit_bytes=limit << 20),
+        input_output_aliases={len(items) + len(args) + index: index for index in range(len(onto))},
         cost_estimate=pl.CostEstimate(flops=int(COST * time), bytes_accessed=1000, transcendentals=0),
         name=name,
-    )(*items, *args)
+    )(*items, *args, *onto)
 
 
 def on_device(tokens, cotangent, item_lengths, item_offsets, norm_gain, lambda_log, lambda_imag, log_step, input_map, output_map, skip_weight):
@@ -1075,9 +1076,10 @@
         pairs = [(c * blocks + b, c * blocks + (b ^ step_bit(sz, step, c))) for c in range(2) for b in range(blocks)]
         came[step] = lax.ppermute(message, ("core", "block"), pairs)
 
-    def spread(pieces):
-        return call("spread", sz, spread_kernel, [], pieces, [((micro, part, run), F32)] * 2,
-                    [((2 * blocks, part, toks), F32), pltpu.SemaphoreType.DMA((2 * blocks,))], limit=6, out_spec=HBM, time=9)
+    def spread(name, pieces, first, onto=(), time=0.0):
+        indices = tuple(range(first, blocks, 2))
+        return call(name, sz, partial(spread_kernel, indices, 2), [], pieces, [((micro, part, run), F32)] * 2,
+                    [((blocks, part, toks), F32), pltpu.SemaphoreType.DMA((blocks,))], limit=6, out_spec=HBM, time=time, onto=onto)
 
     lanes = width // LANES
 
@@ -1085,13 +1087,14 @@
         step = max(SEGS * planes // lanes, SEGS)
         return ((lanes * (-(-rows // step) * step), LANES), BF)
 
-    def over_planes(name, which, direct=()):
+    def over_planes(name, which, direct=(), send=True):
         ends = [(groups[index], place[groups[index].first + steps - 1, index]) for index in which]
         talls = [tall_of(group.rows(sz)) for group, _ in ends] + [tall_of(own)] * bool(direct)
         cut = sum(t[0][0] for t in talls) // planes + (16 if direct else 0)
         args = [x for index in which for x in (kept[index], came[groups[index].first + steps - 1])]
-        return swap_all(call(name, sz, partial(fold_block_kernel, planes, ends, bool(direct)), [], [*args, *direct],
-                             [((cut, LANES), BF)] * planes, talls), "plane")
+        parts = call(name, sz, partial(fold_block_kernel, planes, ends, bool(direct)), [], [*args, *direct],
+                     [((cut, LANES), BF)] * planes, talls)
+        return swap_all(parts, "plane") if send else parts
 
     up_b, twice_b, gstates_b, gskip_b, ends, send = call(
         "turn", sz, turn_kernel, items, [ahead, behind, slope_b, normed_b, w_out_b, params, perm, *cot_pieces],
@@ -1129,16 +1132,17 @@
         [keep, got, params, terms, more, ggain_b, gskip_a, gskip_b, gdecay_a, gdecay_b], [((own + 16, width), BF)] * blocks, [((8, width), F32)]))
     gdriven_a, sums_c[0] = after(gdriven_a, sums_c[0])
     sums_c = swap_all(sums_c)
+    message = halve(2)
+    kept[0], message = after(kept[0], message)
+    first_parts = over_planes("planes_a", [0], send=False) if steps <= 2 else []
+    first_parts, sums_c = after(first_parts, sums_c)
+    first_parts = swap_all(first_parts, "plane")
+    send_step(2, message)
+    gdriven_a, message = after(gdriven_a, message)
     last_pieces = call(
         "back_leave", sz, back_leave_kernel, [], [params, gdriven_a, up_a, slope_a, hidden_a, w_in_a, perm, last_b],
         [((2 * part, toks), BF)] * blocks, [rows_b, stacked], limit=12, time=6)
-    last_pieces, came[1], sums_c = after(last_pieces, came[1], sums_c)
-    message = halve(2)
-    kept[0], message = after(kept[0], message)
-    first_parts = over_planes("planes_a", [0]) if steps <= 2 else []
-    send_step(2, message)
-    if first_parts:
-        came[2], first_parts = after(came[2], first_parts)
+    last_pieces, came[2], first_parts = after(last_pieces, came[2], first_parts)
     for step in range(3, steps + 1):
         send_step(step, halve(step))
     parts = over_planes("planes", [1] if first_parts else [0, 1], sums_c)
@@ -1154,7 +1158,9 @@
     whole = swap_all([sum_all] * planes, "plane")
     late, others = after(late, [sum_all, tiny, *whole[planes - 0 :]])
     others = [swap(x, 1, "core") for x in others]
-    output, input_grad = spread([piece for pair in zip(early, late) for piece in pair])
+    halves = spread("spread_early", early, 0)
+    late, halves = after(late, halves)
+    output, input_grad = spread("spread_late", late, 1, halves, time=9)
     far = whole[1 : planes - 0]
     far, others, output = after(far, others, output)
     far = [swap(x, 1, "core") for x in far]

time: 150 us -> 150 us (level)
  waiting for transfers between devices: 48.8 us -> 46.7 us
    ppermute x24, waiting for transfers between devices: 11.3 us -> 5.62 us  [swap(): lax.ppermute(x, axis, [(i, i ^ dist) for i in range(lax.axis_size(axis))])]
    ppermute x3, waiting for transfers between devices: 0.01 us -> 4.35 us  [send_step(): came[step] = lax.ppermute(message, ('core', 'block'), pairs)]
    pallas_call x28 -> x29, Pallas kernels: 56.7 us -> 57.4 us  [call(): pl.pallas_call(kernel, out_shape=out_shape, in_specs=[SMEM] * len(items)...]
  transfers between devices with their start and end apart: 45 -> 45, of which waited for: 18 -> 19; matrix products, arithmetic and copies ran while one was open for 0% -> 0% of each run, Pallas kernels for 30% -> 31%
where the time goes in v8:
time: 150 us; the launch traced here: 149 us
  Pallas kernels  57.4 us (38%)
  waiting for transfers between devices  46.7 us (31%)
  starting transfers between devices  43.6 us (29%)
    pallas_call x29, Pallas kernels, call(): pl.pallas_call(kernel, out_shape=out_shape, in_specs=[SMEM] * len(items)...  57.4 us
    ppermute x12, waiting for transfers between devices, across(): lax.ppermute(x, ('core', 'block'), [pair[::-1] for pair in pairs] if back...  33.3 us
    ppermute x24, starting transfers between devices, swap(): lax.ppermute(x, axis, [(i, i ^ dist) for i in range(lax.axis_size(axis))])  21.8 us
    ppermute x12, starting transfers between devices, across(): lax.ppermute(x, ('core', 'block'), [pair[::-1] for pair in pairs] if back...  10.5 us
    ppermute x24, waiting for transfers between devices, swap(): lax.ppermute(x, axis, [(i, i ^ dist) for i in range(lax.axis_size(axis))])  5.62 us
    ppermute x3, waiting for transfers between devices, send_step(): came[step] = lax.ppermute(message, ('core', 'block'), pairs)  4.35 us
    ppermute x4, starting transfers between devices, neighbour(): return lax.ppermute(x, ('core', 'block'), pairs)  4.04 us
    ppermute x3, starting transfers between devices, send_step(): came[step] = lax.ppermute(message, ('core', 'block'), pairs)  3.91 us
  transfers between devices with their start and end apart: 45, of which 19 were waited for; matrix products, arithmetic and copies ran while one was open for 0% of the time, Pallas kernels for 31%

profile of v8, /device:TPU:0, one launch (start us, length us, event | category | flops | bytes accessed | tf_op | source)
XLA Modules:
  0.0 149.3 jit_solution(14533686992290586921)
XLA Ops:
  0.6 1.9 %prepare.1 = (bf16[192,1024]{1,0:T(8,128)(2,1)S(1)}, bf16[192,1024]{1,0:T(8,128)(2,1)S(1)}, bf16[192,1024]{1,0:T(8,128)(2,1)S(1)}, bf16[192,1024]{1,0:T(8,128)(2...) custom-call(bf16[2,128,2048]{2,1,0:T(8,128)(2,1)} %refs_0_.2, f32[2,128]{1,0:T(2,128)} %refs_1_.1, ...), custom_call_target="tpu_custom_call" | custom-call | bytes 1000 | tf_op jit(solution)/shard_map/prepare/pallas_call | solution.py:923
  2.5 3.0 %collective-permute-start = (bf16[5,96,512]{2,1,0:T(8,128)(2,1)S(1)}, bf16[5,96,512]{2,1,0:T(8,128)(2,1)S(1)}, u32[]{:S(2)}, u32[]{:S(2)}) collective-permute-start(bf16[5,96,512]{2,1,0:T(8,128)(2,1)S(1)} %get-tuple-element.174.refs_0_), channel_id=1, source_target_pairs={{0,1},{1,0},{2,3},{3,2},{4,6},{5,7},{6,4},{7,5},{8,9},{9,8},{10,11... | collective-permute-start | bytes 1474568 | tf_op jit(solution)/shard_map/ppermute | solution.py:998
  5.5 1.5 %collective-permute-start.2 = (bf16[192,1024]{1,0:T(8,128)(2,1)S(1)}, bf16[192,1024]{1,0:T(8,128)(2,1)S(1)}, u32[]{:S(2)}, u32[]{:S(2)}) collective-permute-start(bf16[192,1024]{1,0:T(8,128)(2,1)S(1)} %get-tuple-element.176), channel_id=1, source_target_pairs={{0,2},{1,6},{2,0},{3,4},{4,3},{5,7},{6,1},{7,5},{8,10},{9,14},{10,... | collective-permute-start | bytes 1179656 | tf_op jit(solution)/shard_map/ppermute | solution.py:956
  8.2 1.6 %cut_cotangent.1 = (bf16[128,1024]{1,0:T(8,128)(2,1)S(1)}, bf16[128,1024]{1,0:T(8,128)(2,1)S(1)}, bf16[128,1024]{1,0:T(8,128)(2,1)S(1)}, bf16[128,1024]{1,0:T(8,128)(2,1)S(1)}) custom-call(f32[2,128,2048]{2,1,0:T(8,128)} %refs_0_.3), custom_call_target="tpu_custom_call" | custom-call | bytes 1000 | tf_op jit(solution)/shard_map/cut_cotangent/pallas_call | solution.py:923
  10.2 13.9 %collective-permute-done.2.refs_1_.refs_4_ = bf16[192,1024]{1,0:T(8,128)(2,1)S(1)} collective-permute-done((bf16[192,1024]{1,0:T(8,128)(2,1)S(1)}, bf16[192,1024]{1,0:T(8,128)(2,1)S(1)}, u32[]{:S(2)}, u32[]{:S(2)}) %collective-permute-start.2) | collective-permute-done | bytes 393248 | tf_op jit(solution)/shard_map/ppermute | solution.py:956
  24.2 3.5 %collective-permute-done.1.refs_0_.refs_3_ = bf16[192,1024]{1,0:T(8,128)(2,1)S(1)} collective-permute-done((bf16[192,1024]{1,0:T(8,128)(2,1)S(1)}, bf16[192,1024]{1,0:T(8,128)(2,1)S(1)}, u32[]{:S(2)}, u32[]{:S(2)}) %collective-permute-start.1) | collective-permute-done | bytes 393248 | tf_op jit(solution)/shard_map/ppermute | solution.py:956
  31.1 2.6 %open.1 = (bf16[1024,512]{1,0:T(8,128)(2,1)S(1)}, bf16[1024,512]{1,0:T(8,128)(2,1)S(1)}, f32[1024,128]{1,0:T(8,128)S(1)}, f32[1024,128]{1,0:T(8,128)S(1)}, f32[1024,128]{1,0:T(8,128)S(1)}) custom-call(s32[2,2,2,2]{3,2,1,0:T(2,128)S(1)} %pad_add_fusion.refs_0_, bf16[1024,1024]{1,0:T(8,128)(2,1)S(1)} %fusion.refs_1_.refs_7_.refs_6_, ...), custom_call_target="tpu_custom_call" | custom-call | flops 1200000000 | bytes 1000 | tf_op jit(solution)/shard_map/open/pallas_call | solution.py:923
  33.8 2.9 %enter.1 = (bf16[768,512]{1,0:T(8,128)(2,1)S(1)}, f32[1024,768]{1,0:T(8,128)S(1)}, f32[4,16,384]{2,1,0:T(8,128)S(1)}, f32[1,2,384]{2,1,0:T(2,128)S(1)}) custom-call(s32[2,2,2,2]{3,2,1,0:T(2,128)S(1)} %pad_add_fusion.refs_0_, f32[1024,128]{1,0:T(8,128)S(1)} %get-tuple-element.192.refs_1_.refs_2_, f32[1024,128]{1,0:T(8,128)S(1)} %get-tuple-element.193.refs_2_.refs_3_, ...), custom_call_target="tpu_custom_call" | custom-call | bytes 1000 | tf_op jit(solution)/shard_map/enter/pallas_call | solution.py:923
  37.9 2.4 %chain.1.refs_4_.refs_2_.refs_7_ = bf16[1024,1536]{1,0:T(8,128)(2,1)S(1)} custom-call(s32[2,2,2,2]{3,2,1,0:T(2,128)S(1)} %pad_add_fusion.refs_0_, f32[1024,128]{1,0:T(8,128)S(1)} %get-tuple-element.192.refs_1_.refs_2_, f32[1024,128]{1,0:T(8,128)S(1)} %get-tuple-element.193.refs_2_.refs_3_, f32[1,2,384]{2,1,0:T(2,128)S(1)} %bitcast.18, ...), custom_call_target="tpu_custom_call" | custom-call | bytes 1000 | tf_op jit(solution)/shard_map/chain/pallas_call | solution.py:923
  40.3 1.6 %collective-permute-done.6.refs_11_.refs_12_ = bf16[10,96,512]{2,1,0:T(8,128)(2,1)S(1)} collective-permute-done((bf16[10,96,512]{2,1,0:T(8,128)(2,1)S(1)}, bf16[10,96,512]{2,1,0:T(8,128)(2,1)S(1)}, u32[]{:S(2)}, u32[]{:S(2)}) %collective-permute-start.6) | collective-permute-done | bytes 983072 | tf_op jit(solution)/shard_map/ppermute | solution.py:998
  42.2 1.7 %collective-permute-start.12 = (bf16[128,1024]{1,0:T(8,128)(2,1)S(1)}, bf16[128,1024]{1,0:T(8,128)(2,1)S(1)}, u32[]{:S(2)}, u32[]{:S(2)}) collective-permute-start(bf16[128,1024]{1,0:T(8,128)(2,1)S(1)} %get-tuple-element.218), channel_id=1, source_target_pairs={{0,6},{1,2},{2,4},{3,0},{4,7},{5,3},{6,5},{7,1},{8,14},{9,10},{10,... | collective-permute-start | bytes 786440 | tf_op jit(solution)/shard_map/ppermute | solution.py:956
  44.4 1.8 %collective-permute-start.14 = (bf16[128,1024]{1,0:T(8,128)(2,1)S(1)}, bf16[128,1024]{1,0:T(8,128)(2,1)S(1)}, u32[]{:S(2)}, u32[]{:S(2)}) collective-permute-start(bf16[128,1024]{1,0:T(8,128)(2,1)S(1)} %get-tuple-element.220), channel_id=1, source_target_pairs={{0,4},{1,0},{2,6},{3,2},{4,5},{5,1},{6,7},{7,3},{8,12},{9,8},{10,1... | collective-permute-start | bytes 786440 | tf_op jit(solution)/shard_map/ppermute | solution.py:956
  46.9 6.6 %middle.1 = (bf16[1536,512]{1,0:T(8,128)(2,1)S(1)}, bf16[768,512]{1,0:T(8,128)(2,1)S(1)}, bf16[1024,512]{1,0:T(8,128)(2,1)S(1)}, f32[1024,512]{1,0:T(8,128)S(1)}...) custom-call(s32[2,2,2,2]{3,2,1,0:T(2,128)S(1)} %pad_add_fusion.refs_, ...), custom_call_target="tpu_custom_call" | custom-call | flops 4400000000 | bytes 1000 | tf_op jit(solution)/shard_map/middle/pallas_call | solution.py:923
  53.5 3.5 %collective-permute-start.11 = (f32[2,384]{1,0:T(2,128)S(1)}, f32[2,384]{1,0:T(2,128)S(1)}, u32[]{:S(2)}, u32[]{:S(2)}) collective-permute-start(f32[2,384]{1,0:T(2,128)S(1)} %bitcast.23), channel_id=1, source_target_pairs={{0,4},{1,5},{2,6},{3,7},{4,0},{5,1},{6,2},{7,3},{8,12},{9,13},{10,... | collective-permute-start | bytes 9224 | tf_op jit(solution)/shard_map/ppermute | solution.py:970
  57.8 5.5 %leave.1 = (bf16[1536,512]{1,0:T(8,128)(2,1)S(1)}, bf16[1024,1536]{1,0:T(8,128)(2,1)S(1)}, bf16[1024,512]{1,0:T(8,128)(2,1)S(1)}, bf16[1024,512]{1,0:T(8,128)(2,1)S(1)}) custom-call(s32[2,2,2,2]{3,2,1,0:T(2,128)S(1)} %pad_add_fusion.refs_0_, f32[1024,128]{1,0:T(8,128)S(1)} %get-tuple-element.194.refs_1_, f32[1024,128]{1,0:T(8,128)S(1)} %get-tuple-element.192.refs_1_.refs_2_, ...), custom_call_target="tpu_custom_call" | custom-call | bytes 1000 | tf_op jit(solution)/shard_map/leave/pallas_call | solution.py:923
  63.4 5.0 %turn.1 = (f32[1024,512]{1,0:T(8,128)S(1)}, bf16[1024,512]{1,0:T(8,128)(2,1)S(1)}, f32[1024,1536]{1,0:T(8,128)S(1)}, f32[1,512]{1,0:T(1,128)S(1)}, f32[4,16,384]{2,1,0:T(8,128)S(1)}, /*index=5*/f32[1,2,384]{2,1,0:T(2,128)S(1)}) custom-call(s32[2,2,2,2]{3,2,1,0:T(2,128)S(1)} %pad_add_fusion.refs_0_, f32[1024,128]{1,0:T(8,128)S(1)} %get-tuple-element.192.refs_1_.refs_2_, ...), custom_call_target="tpu_custom_call" | custom-call | flops 2400000000 | bytes 1000 | tf_op jit(solution)/shard_map/turn/pallas_call | solution.py:923
  72.7 9.1 %back_middle.1 = (bf16[1024,768]{1,0:T(8,128)(2,1)S(1)}, f32[2,384]{1,0:T(2,128)S(1)}, f32[1,512]{1,0:T(1,128)S(1)}, f32[1024,512]{1,0:T(8,128)S(1)}, bf16[1024,...) custom-call(s32[2,2,2,2]{3,2,1,0:T(2,128)S(1)} %pad_add_fusion.refs_, ...), custom_call_target="tpu_custom_call" | custom-call | flops 4400000000 | bytes 1000 | tf_op jit(solution)/shard_map/back_middle/pallas_call | solution.py:923
  81.8 1.4 grads_b_send.1
  83.8 1.4 grads_b_keep.1.refs_2_
  87.6 3.5 %back_chain.1 = (bf16[1024,768]{1,0:T(8,128)(2,1)S(1)}, f32[2,384]{1,0:T(2,128)S(1)}) custom-call(s32[2,2,2,2]{3,2,1,0:T(2,128)S(1)} %pad_add_fusion.refs_0_, f32[1024,128]{1,0:T(8,128)S(1)} %get-tuple-element.192.refs_1_.refs_2_, f32[1024,128]{1,0:T(8,128)S(1)} %get-tuple-element.193.refs_2_.refs_3_, f32[1,2,384]{2,1,0:T(2,128)S(1)} %bitcast.21, ...), custom_call_target="tpu_custom_call" | custom-call | flops 3600000000 | bytes 1000 | tf_op jit(solution)/shard_map/back_chain/pallas_call | solution.py:923
  93.7 1.8 %collective-permute-start.24 = (bf16[112,512]{1,0:T(8,128)(2,1)S(1)}, bf16[112,512]{1,0:T(8,128)(2,1)S(1)}, u32[]{:S(2)}, u32[]{:S(2)}) collective-permute-start(bf16[112,512]{1,0:T(8,128)(2,1)S(1)} %get-tuple-element.277), channel_id=1, source_target_pairs={{0,3},{1,2},{2,1},{3,0},{4,7},{5,6},{6,5},{7,4},{8,11},{9,10},{10,... | collective-permute-start | bytes 344072 | tf_op jit(solution)/shard_map/ppermute | solution.py:948
  97.2 4.3 %collective-permute-done.22.refs_0_.refs_1_ = bf16[768,512]{1,0:T(8,128)(2,1)S(1)} collective-permute-done((bf16[768,512]{1,0:T(8,128)(2,1)S(1)}, bf16[768,512]{1,0:T(8,128)(2,1)S(1)}, u32[]{:S(2)}, u32[]{:S(2)}) %collective-permute-start.22) | collective-permute-done | bytes 786464 | tf_op jit(solution)/shard_map/ppermute | solution.py:1077
  101.7 2.1 %collective-permute-start.23 = (bf16[288,512]{1,0:T(8,128)(2,1)S(1)}, bf16[288,512]{1,0:T(8,128)(2,1)S(1)}, u32[]{:S(2)}, u32[]{:S(2)}) collective-permute-start(bf16[288,512]{1,0:T(8,128)(2,1)S(1)} %get-tuple-element.263), channel_id=1, source_target_pairs={{0,1},{1,0},{2,3},{3,2},{4,6},{5,7},{6,4},{7,5},{8,9},{9,8},{10,11... | collective-permute-start | bytes 884744 | tf_op jit(solution)/shard_map/ppermute | solution.py:1077
  104.0 4.5 %collective-permute-start.27 = (bf16[192,128]{1,0:T(8,128)(2,1)S(1)}, bf16[192,128]{1,0:T(8,128)(2,1)S(1)}, u32[]{:S(2)}, u32[]{:S(2)}) collective-permute-start(bf16[192,128]{1,0:T(8,128)(2,1)S(1)} %get-tuple-element.281), channel_id=1, source_target_pairs={{0,24},{8,16},{16,8},{24,0},{1,25},{9,17},{17,9},{25,1},{2,26},{10... | collective-permute-start | bytes 147464 | tf_op jit(solution)/shard_map/ppermute | solution.py:948
  109.1 4.1 %back_leave.1 = (bf16[256,1024]{1,0:T(8,128)(2,1)S(1)}, bf16[256,1024]{1,0:T(8,128)(2,1)S(1)}, bf16[256,1024]{1,0:T(8,128)(2,1)S(1)}, bf16[256,1024]{1,0:T(8,128)(2,1)S(1)}) custom-call(f32[8,512]{1,0:T(8,128)S(1)} %get-tuple-element.188.refs_2_.refs_3_.refs_4_.refs_5_.refs_6_.refs_0_, bf16[1024,768]{1,0:T(8,128)(2,1)S(1)} %get-tuple-element.264.refs_0_.refs_1_, ...), custom_call_target="tpu_custom_call" | custom-call | flops 2400000000 | bytes 1000 | tf_op jit(solution)/shard_map/back_leave/pallas_call | solution.py:923
  113.7 2.1 %collective-permute-start.30 = (bf16[256,1024]{1,0:T(8,128)(2,1)S(1)}, bf16[256,1024]{1,0:T(8,128)(2,1)S(1)}, u32[]{:S(2)}, u32[]{:S(2)}) collective-permute-start(bf16[256,1024]{1,0:T(8,128)(2,1)S(1)} %get-tuple-element.300), channel_id=1, source_target_pairs={{6,0},{2,1},{4,2},{0,3},{7,4},{3,5},{5,6},{1,7},{14,8},{10,9},{12,... | collective-permute-start | bytes 1572872 | tf_op jit(solution)/shard_map/ppermute | solution.py:956
  115.8 3.5 %collective-permute-start.32 = (bf16[400,128]{1,0:T(8,128)(2,1)S(1)}, bf16[400,128]{1,0:T(8,128)(2,1)S(1)}, u32[]{:S(2)}, u32[]{:S(2)}) collective-permute-start(bf16[400,128]{1,0:T(8,128)(2,1)S(1)} %get-tuple-element.303), channel_id=1, source_target_pairs={{0,24},{8,16},{16,8},{24,0},{1,25},{9,17},{17,9},{25,1},{2,26},{10... | collective-permute-start | bytes 307208 | tf_op jit(solution)/shard_map/ppermute | solution.py:948
  120.2 6.0 %collective-permute-done.30.refs_0_ = bf16[256,1024]{1,0:T(8,128)(2,1)S(1)} collective-permute-done((bf16[256,1024]{1,0:T(8,128)(2,1)S(1)}, bf16[256,1024]{1,0:T(8,128)(2,1)S(1)}, u32[]{:S(2)}, u32[]{:S(2)}) %collective-permute-start.30) | collective-permute-done | bytes 524320 | tf_op jit(solution)/shard_map/ppermute | solution.py:956
  126.2 1.9 %collective-permute-done.31.refs_1_ = bf16[256,1024]{1,0:T(8,128)(2,1)S(1)} collective-permute-done((bf16[256,1024]{1,0:T(8,128)(2,1)S(1)}, bf16[256,1024]{1,0:T(8,128)(2,1)S(1)}, u32[]{:S(2)}, u32[]{:S(2)}) %collective-permute-start.31) | collective-permute-done | bytes 524320 | tf_op jit(solution)/shard_map/ppermute | solution.py:956
  130.3 2.9 %collective-permute-start.36 = (bf16[576,128]{1,0:T(8,128)(2,1)S(1)}, bf16[576,128]{1,0:T(8,128)(2,1)S(1)}, u32[]{:S(2)}, u32[]{:S(2)}) collective-permute-start(bf16[576,128]{1,0:T(8,128)(2,1)S(1)} %get-tuple-element.312.refs_0_), channel_id=1, source_target_pairs={{0,16},{8,24},{16,0},{24,8},{1,17},{9,25},{17,1},{25,9},{2,18},{10... | collective-permute-start | bytes 442376 | tf_op jit(solution)/shard_map/ppermute | solution.py:948
  135.3 7.9 %collective-permute-done.38.refs_0_ = bf16[256,1024]{1,0:T(8,128)(2,1)S(1)} collective-permute-done((bf16[256,1024]{1,0:T(8,128)(2,1)S(1)}, bf16[256,1024]{1,0:T(8,128)(2,1)S(1)}, u32[]{:S(2)}, u32[]{:S(2)}) %collective-permute-start.38) | collective-permute-done | bytes 524320 | tf_op jit(solution)/shard_map/ppermute | solution.py:956
  147.2 2.1 %finish.1 = (f32[2,128]{1,0:T(2,128)}, f32[2,128]{1,0:T(2,128)}, f32[2,96]{1,0:T(2,128)}, f32[2,96]{1,0:T(2,128)}, f32[2,96]{1,0:T(2,128)}, /*index=5*/f32[2,2,96,512]{3,2,1,0:T(8,128)}, f32[2,4,96,512]{3,2,1,0:T(8,128)}) custom-call(bf16[576,128]{1,0:T(8,128)(2,1)S(1)} %get-tuple-element.312.refs_0_, bf16[576,128]{1,0:T(8,128)(2,1)S(1)} %collective-permute-done.35.refs_1_, ...), custom_call_target="tpu_custom_call" | custom-call | bytes 1000 | tf_op jit(solution)/shard_map/finish/pallas_call | solution.py:923
  (106 shorter events, 30.5 us)
Async XLA Ops:
  2.5 25.1 %collective-permute-start = (bf16[5,96,512]{2,1,0:T(8,128)(2,1)S(1)}, bf16[5,96,512]{2,1,0:T(8,128)(2,1)S(1)}, u32[]{:S(2)}, u32[]{:S(2)}) collective-permute-start(bf16[5,96,512]{2,1,0:T(8,128)(2,1)S(1)} %get-tuple-element.174.refs_0_), channel_id=1, source_target_pairs={{0,1},{1,0},{2,3},{3,2},{4,6},{5,7},{6,4},{7,5},{8,9},{9,8},{10,11... | collective-permute-start | bytes 1474568 | tf_op jit(solution)/shard_map/ppermute | solution.py:998
  5.5 18.6 %collective-permute-start.2 = (bf16[192,1024]{1,0:T(8,128)(2,1)S(1)}, bf16[192,1024]{1,0:T(8,128)(2,1)S(1)}, u32[]{:S(2)}, u32[]{:S(2)}) collective-permute-start(bf16[192,1024]{1,0:T(8,128)(2,1)S(1)} %get-tuple-element.176), channel_id=1, source_target_pairs={{0,2},{1,6},{2,0},{3,4},{4,3},{5,7},{6,1},{7,5},{8,10},{9,14},{10,... | collective-permute-start | bytes 1179656 | tf_op jit(solution)/shard_map/ppermute | solution.py:956
  7.0 20.6 %collective-permute-start.1 = (bf16[192,1024]{1,0:T(8,128)(2,1)S(1)}, bf16[192,1024]{1,0:T(8,128)(2,1)S(1)}, u32[]{:S(2)}, u32[]{:S(2)}) collective-permute-start(bf16[192,1024]{1,0:T(8,128)(2,1)S(1)} %get-tuple-element.175), channel_id=1, source_target_pairs={{0,6},{1,2},{2,4},{3,0},{4,7},{5,3},{6,5},{7,1},{8,14},{9,10},{10,... | collective-permute-start | bytes 1179656 | tf_op jit(solution)/shard_map/ppermute | solution.py:956
  7.0 20.6 %collective-permute-start.3 = (bf16[192,1024]{1,0:T(8,128)(2,1)S(1)}, bf16[192,1024]{1,0:T(8,128)(2,1)S(1)}, u32[]{:S(2)}, u32[]{:S(2)}) collective-permute-start(bf16[192,1024]{1,0:T(8,128)(2,1)S(1)} %get-tuple-element.182), channel_id=1, source_target_pairs={{0,4},{1,0},{2,6},{3,2},{4,5},{5,1},{6,7},{7,3},{8,12},{9,8},{10,1... | collective-permute-start | bytes 1179656 | tf_op jit(solution)/shard_map/ppermute | solution.py:956
  7.5 20.1 %collective-permute-start.4 = (bf16[192,1024]{1,0:T(8,128)(2,1)S(1)}, bf16[192,1024]{1,0:T(8,128)(2,1)S(1)}, u32[]{:S(2)}, u32[]{:S(2)}) collective-permute-start(bf16[192,1024]{1,0:T(8,128)(2,1)S(1)} %get-tuple-element.183), channel_id=1, source_target_pairs={{0,0},{1,4},{2,2},{3,6},{4,1},{5,5},{6,3},{7,7},{8,8},{9,12},{10,1... | collective-permute-start | bytes 1179656 | tf_op jit(solution)/shard_map/ppermute | solution.py:956
  27.7 14.2 %collective-permute-start.6 = (bf16[10,96,512]{2,1,0:T(8,128)(2,1)S(1)}, bf16[10,96,512]{2,1,0:T(8,128)(2,1)S(1)}, u32[]{:S(2)}, u32[]{:S(2)}) collective-permute-start(bf16[10,96,512]{2,1,0:T(8,128)(2,1)S(1)} %pile_0.1), channel_id=1, source_target_pairs={{0,2},{1,3},{2,0},{3,1},{4,5},{5,4},{6,7},{7,6},{8,10},{9,11},{10,... | collective-permute-start | bytes 2949128 | tf_op jit(solution)/shard_map/ppermute | solution.py:998
  28.1 9.8 %collective-permute-start.9 = (bf16[5,96,512]{2,1,0:T(8,128)(2,1)S(1)}, bf16[5,96,512]{2,1,0:T(8,128)(2,1)S(1)}, u32[]{:S(2)}, u32[]{:S(2)}) collective-permute-start(bf16[5,96,512]{2,1,0:T(8,128)(2,1)S(1)} %collective-permute-done.refs_1_.refs_10_.refs_11_), channel_id=1, source_target_pairs={{0,4},{4,0},{1,5},{5,1},{2,6},{6,2},{3,7},{7,3},{8,12},{12,8},{9,1... | collective-permute-start | bytes 1474568 | tf_op jit(solution)/shard_map/ppermute | solution.py:948
  41.9 5.0 %collective-permute-start.10 = (bf16[10,96,512]{2,1,0:T(8,128)(2,1)S(1)}, bf16[10,96,512]{2,1,0:T(8,128)(2,1)S(1)}, u32[]{:S(2)}, u32[]{:S(2)}) collective-permute-start(bf16[10,96,512]{2,1,0:T(8,128)(2,1)S(1)} %collective-permute-done.6.refs_11_.refs_12_), channel_id=1, source_target_pairs={{0,4},{4,0},{1,5},{5,1},{2,6},{6,2},{3,7},{7,3},{8,12},{12,8},{9,1... | collective-permute-start | bytes 2949128 | tf_op jit(solution)/shard_map/ppermute | solution.py:948
  42.2 21.1 %collective-permute-start.12 = (bf16[128,1024]{1,0:T(8,128)(2,1)S(1)}, bf16[128,1024]{1,0:T(8,128)(2,1)S(1)}, u32[]{:S(2)}, u32[]{:S(2)}) collective-permute-start(bf16[128,1024]{1,0:T(8,128)(2,1)S(1)} %get-tuple-element.218), channel_id=1, source_target_pairs={{0,6},{1,2},{2,4},{3,0},{4,7},{5,3},{6,5},{7,1},{8,14},{9,10},{10,... | collective-permute-start | bytes 786440 | tf_op jit(solution)/shard_map/ppermute | solution.py:956
  43.9 19.4 %collective-permute-start.13 = (bf16[128,1024]{1,0:T(8,128)(2,1)S(1)}, bf16[128,1024]{1,0:T(8,128)(2,1)S(1)}, u32[]{:S(2)}, u32[]{:S(2)}) collective-permute-start(bf16[128,1024]{1,0:T(8,128)(2,1)S(1)} %get-tuple-element.219), channel_id=1, source_target_pairs={{0,2},{1,6},{2,0},{3,4},{4,3},{5,7},{6,1},{7,5},{8,10},{9,14},{10,... | collective-permute-start | bytes 786440 | tf_op jit(solution)/shard_map/ppermute | solution.py:956
  44.4 19.0 %collective-permute-start.14 = (bf16[128,1024]{1,0:T(8,128)(2,1)S(1)}, bf16[128,1024]{1,0:T(8,128)(2,1)S(1)}, u32[]{:S(2)}, u32[]{:S(2)}) collective-permute-start(bf16[128,1024]{1,0:T(8,128)(2,1)S(1)} %get-tuple-element.220), channel_id=1, source_target_pairs={{0,4},{1,0},{2,6},{3,2},{4,5},{5,1},{6,7},{7,3},{8,12},{9,8},{10,1... | collective-permute-start | bytes 786440 | tf_op jit(solution)/shard_map/ppermute | solution.py:956
  46.2 17.2 %collective-permute-start.15 = (bf16[128,1024]{1,0:T(8,128)(2,1)S(1)}, bf16[128,1024]{1,0:T(8,128)(2,1)S(1)}, u32[]{:S(2)}, u32[]{:S(2)}) collective-permute-start(bf16[128,1024]{1,0:T(8,128)(2,1)S(1)} %get-tuple-element.221), channel_id=1, source_target_pairs={{0,0},{1,4},{2,2},{3,6},{4,1},{5,5},{6,3},{7,7},{8,8},{9,12},{10,1... | collective-permute-start | bytes 786440 | tf_op jit(solution)/shard_map/ppermute | solution.py:956
  53.5 4.3 %collective-permute-start.11 = (f32[2,384]{1,0:T(2,128)S(1)}, f32[2,384]{1,0:T(2,128)S(1)}, u32[]{:S(2)}, u32[]{:S(2)}) collective-permute-start(f32[2,384]{1,0:T(2,128)S(1)} %bitcast.23), channel_id=1, source_target_pairs={{0,4},{1,5},{2,6},{3,7},{4,0},{5,1},{6,2},{7,3},{8,12},{9,13},{10,... | collective-permute-start | bytes 9224 | tf_op jit(solution)/shard_map/ppermute | solution.py:970
  72.0 9.8 %collective-permute-start.19 = (bf16[384,512]{1,0:T(8,128)(2,1)S(1)}, bf16[384,512]{1,0:T(8,128)(2,1)S(1)}, u32[]{:S(2)}, u32[]{:S(2)}) collective-permute-start(bf16[384,512]{1,0:T(8,128)(2,1)S(1)} %get-tuple-element.235), channel_id=1, source_target_pairs={{0,1},{1,0},{2,3},{3,2},{4,6},{5,7},{6,4},{7,5},{8,9},{9,8},{10,11... | collective-permute-start | bytes 1179656 | tf_op jit(solution)/shard_map/ppermute | solution.py:1077
  86.5 15.1 %collective-permute-start.22 = (bf16[768,512]{1,0:T(8,128)(2,1)S(1)}, bf16[768,512]{1,0:T(8,128)(2,1)S(1)}, u32[]{:S(2)}, u32[]{:S(2)}) collective-permute-start(bf16[768,512]{1,0:T(8,128)(2,1)S(1)} %get-tuple-element.260), channel_id=1, source_target_pairs={{0,2},{1,3},{2,0},{3,1},{4,5},{5,4},{6,7},{7,6},{8,10},{9,11},{10,... | collective-permute-start | bytes 2359304 | tf_op jit(solution)/shard_map/ppermute | solution.py:1077
  93.7 10.2 %collective-permute-start.24 = (bf16[112,512]{1,0:T(8,128)(2,1)S(1)}, bf16[112,512]{1,0:T(8,128)(2,1)S(1)}, u32[]{:S(2)}, u32[]{:S(2)}) collective-permute-start(bf16[112,512]{1,0:T(8,128)(2,1)S(1)} %get-tuple-element.277), channel_id=1, source_target_pairs={{0,3},{1,2},{2,1},{3,0},{4,7},{5,6},{6,5},{7,4},{8,11},{9,10},{10,... | collective-permute-start | bytes 344072 | tf_op jit(solution)/shard_map/ppermute | solution.py:948
  95.5 8.5 %collective-permute-start.25 = (bf16[112,512]{1,0:T(8,128)(2,1)S(1)}, bf16[112,512]{1,0:T(8,128)(2,1)S(1)}, u32[]{:S(2)}, u32[]{:S(2)}) collective-permute-start(bf16[112,512]{1,0:T(8,128)(2,1)S(1)} %get-tuple-element.278), channel_id=1, source_target_pairs={{0,2},{1,3},{2,0},{3,1},{4,6},{5,7},{6,4},{7,5},{8,10},{9,11},{10,... | collective-permute-start | bytes 344072 | tf_op jit(solution)/shard_map/ppermute | solution.py:948
  96.5 7.5 %collective-permute-start.26 = (bf16[112,512]{1,0:T(8,128)(2,1)S(1)}, bf16[112,512]{1,0:T(8,128)(2,1)S(1)}, u32[]{:S(2)}, u32[]{:S(2)}) collective-permute-start(bf16[112,512]{1,0:T(8,128)(2,1)S(1)} %get-tuple-element.279), channel_id=1, source_target_pairs={{0,1},{1,0},{2,3},{3,2},{4,5},{5,4},{6,7},{7,6},{8,9},{9,8},{10,11... | collective-permute-start | bytes 344072 | tf_op jit(solution)/shard_map/ppermute | solution.py:948
  101.7 11.8 %collective-permute-start.23 = (bf16[288,512]{1,0:T(8,128)(2,1)S(1)}, bf16[288,512]{1,0:T(8,128)(2,1)S(1)}, u32[]{:S(2)}, u32[]{:S(2)}) collective-permute-start(bf16[288,512]{1,0:T(8,128)(2,1)S(1)} %get-tuple-element.263), channel_id=1, source_target_pairs={{0,1},{1,0},{2,3},{3,2},{4,6},{5,7},{6,4},{7,5},{8,9},{9,8},{10,11... | collective-permute-start | bytes 884744 | tf_op jit(solution)/shard_map/ppermute | solution.py:1077
  104.0 9.1 %collective-permute-start.27 = (bf16[192,128]{1,0:T(8,128)(2,1)S(1)}, bf16[192,128]{1,0:T(8,128)(2,1)S(1)}, u32[]{:S(2)}, u32[]{:S(2)}) collective-permute-start(bf16[192,128]{1,0:T(8,128)(2,1)S(1)} %get-tuple-element.281), channel_id=1, source_target_pairs={{0,24},{8,16},{16,8},{24,0},{1,25},{9,17},{17,9},{25,1},{2,26},{10... | collective-permute-start | bytes 147464 | tf_op jit(solution)/shard_map/ppermute | solution.py:948
  108.5 5.0 %collective-permute-start.28 = (bf16[192,128]{1,0:T(8,128)(2,1)S(1)}, bf16[192,128]{1,0:T(8,128)(2,1)S(1)}, u32[]{:S(2)}, u32[]{:S(2)}) collective-permute-start(bf16[192,128]{1,0:T(8,128)(2,1)S(1)} %get-tuple-element.282), channel_id=1, source_target_pairs={{0,16},{8,24},{16,0},{24,8},{1,17},{9,25},{17,1},{25,9},{2,18},{10... | collective-permute-start | bytes 147464 | tf_op jit(solution)/shard_map/ppermute | solution.py:948
  108.5 5.0 %collective-permute-start.29 = (bf16[192,128]{1,0:T(8,128)(2,1)S(1)}, bf16[192,128]{1,0:T(8,128)(2,1)S(1)}, u32[]{:S(2)}, u32[]{:S(2)}) collective-permute-start(bf16[192,128]{1,0:T(8,128)(2,1)S(1)} %get-tuple-element.283), channel_id=1, source_target_pairs={{0,8},{8,0},{16,24},{24,16},{1,9},{9,1},{17,25},{25,17},{2,10},{10... | collective-permute-start | bytes 147464 | tf_op jit(solution)/shard_map/ppermute | solution.py:948
  113.7 12.5 %collective-permute-start.30 = (bf16[256,1024]{1,0:T(8,128)(2,1)S(1)}, bf16[256,1024]{1,0:T(8,128)(2,1)S(1)}, u32[]{:S(2)}, u32[]{:S(2)}) collective-permute-start(bf16[256,1024]{1,0:T(8,128)(2,1)S(1)} %get-tuple-element.300), channel_id=1, source_target_pairs={{6,0},{2,1},{4,2},{0,3},{7,4},{3,5},{5,6},{1,7},{14,8},{10,9},{12,... | collective-permute-start | bytes 1572872 | tf_op jit(solution)/shard_map/ppermute | solution.py:956
  115.8 12.4 %collective-permute-start.31 = (bf16[256,1024]{1,0:T(8,128)(2,1)S(1)}, bf16[256,1024]{1,0:T(8,128)(2,1)S(1)}, u32[]{:S(2)}, u32[]{:S(2)}) collective-permute-start(bf16[256,1024]{1,0:T(8,128)(2,1)S(1)} %get-tuple-element.301), channel_id=1, source_target_pairs={{4,0},{0,1},{6,2},{2,3},{5,4},{1,5},{7,6},{3,7},{12,8},{8,9},{14,1... | collective-permute-start | bytes 1572872 | tf_op jit(solution)/shard_map/ppermute | solution.py:956
  115.8 12.4 %collective-permute-start.32 = (bf16[400,128]{1,0:T(8,128)(2,1)S(1)}, bf16[400,128]{1,0:T(8,128)(2,1)S(1)}, u32[]{:S(2)}, u32[]{:S(2)}) collective-permute-start(bf16[400,128]{1,0:T(8,128)(2,1)S(1)} %get-tuple-element.303), channel_id=1, source_target_pairs={{0,24},{8,16},{16,8},{24,0},{1,25},{9,17},{17,9},{25,1},{2,26},{10... | collective-permute-start | bytes 307208 | tf_op jit(solution)/shard_map/ppermute | solution.py:948
  119.3 8.9 %collective-permute-start.33 = (bf16[400,128]{1,0:T(8,128)(2,1)S(1)}, bf16[400,128]{1,0:T(8,128)(2,1)S(1)}, u32[]{:S(2)}, u32[]{:S(2)}) collective-permute-start(bf16[400,128]{1,0:T(8,128)(2,1)S(1)} %get-tuple-element.304), channel_id=1, source_target_pairs={{0,16},{8,24},{16,0},{24,8},{1,17},{9,25},{17,1},{25,9},{2,18},{10... | collective-permute-start | bytes 307208 | tf_op jit(solution)/shard_map/ppermute | solution.py:948
  119.3 8.9 %collective-permute-start.34 = (bf16[400,128]{1,0:T(8,128)(2,1)S(1)}, bf16[400,128]{1,0:T(8,128)(2,1)S(1)}, u32[]{:S(2)}, u32[]{:S(2)}) collective-permute-start(bf16[400,128]{1,0:T(8,128)(2,1)S(1)} %get-tuple-element.305), channel_id=1, source_target_pairs={{0,8},{8,0},{16,24},{24,16},{1,9},{9,1},{17,25},{25,17},{2,10},{10... | collective-permute-start | bytes 307208 | tf_op jit(solution)/shard_map/ppermute | solution.py:948
  128.4 14.9 %collective-permute-start.38 = (bf16[256,1024]{1,0:T(8,128)(2,1)S(1)}, bf16[256,1024]{1,0:T(8,128)(2,1)S(1)}, u32[]{:S(2)}, u32[]{:S(2)}) collective-permute-start(bf16[256,1024]{1,0:T(8,128)(2,1)S(1)} %get-tuple-element.309), channel_id=1, source_target_pairs={{2,0},{6,1},{0,2},{4,3},{3,4},{7,5},{1,6},{5,7},{10,8},{14,9},{8,1... | collective-permute-start | bytes 1572872 | tf_op jit(solution)/shard_map/ppermute | solution.py:956
  128.8 14.4 %collective-permute-start.39 = (bf16[256,1024]{1,0:T(8,128)(2,1)S(1)}, bf16[256,1024]{1,0:T(8,128)(2,1)S(1)}, u32[]{:S(2)}, u32[]{:S(2)}) collective-permute-start(bf16[256,1024]{1,0:T(8,128)(2,1)S(1)} %get-tuple-element.310), channel_id=1, source_target_pairs={{0,0},{4,1},{2,2},{6,3},{1,4},{5,5},{3,6},{7,7},{8,8},{12,9},{10,1... | collective-permute-start | bytes 1572872 | tf_op jit(solution)/shard_map/ppermute | solution.py:956
  129.5 15.7 %collective-permute-start.37 = (bf16[576,128]{1,0:T(8,128)(2,1)S(1)}, bf16[576,128]{1,0:T(8,128)(2,1)S(1)}, u32[]{:S(2)}, u32[]{:S(2)}) collective-permute-start(bf16[576,128]{1,0:T(8,128)(2,1)S(1)} %get-tuple-element.312.refs_0_), channel_id=1, source_target_pairs={{0,8},{8,0},{16,24},{24,16},{1,9},{9,1},{17,25},{25,17},{2,10},{10... | collective-permute-start | bytes 442376 | tf_op jit(solution)/shard_map/ppermute | solution.py:948
  130.3 14.8 %collective-permute-start.36 = (bf16[576,128]{1,0:T(8,128)(2,1)S(1)}, bf16[576,128]{1,0:T(8,128)(2,1)S(1)}, u32[]{:S(2)}, u32[]{:S(2)}) collective-permute-start(bf16[576,128]{1,0:T(8,128)(2,1)S(1)} %get-tuple-element.312.refs_0_), channel_id=1, source_target_pairs={{0,16},{8,24},{16,0},{24,8},{1,17},{9,25},{17,1},{25,9},{2,18},{10... | collective-permute-start | bytes 442376 | tf_op jit(solution)/shard_map/ppermute | solution.py:948
  133.3 11.9 %collective-permute-start.35 = (bf16[576,128]{1,0:T(8,128)(2,1)S(1)}, bf16[576,128]{1,0:T(8,128)(2,1)S(1)}, u32[]{:S(2)}, u32[]{:S(2)}) collective-permute-start(bf16[576,128]{1,0:T(8,128)(2,1)S(1)} %get-tuple-element.312.refs_0_), channel_id=1, source_target_pairs={{0,24},{8,16},{16,8},{24,0},{1,25},{9,17},{17,9},{25,1},{2,26},{10... | collective-permute-start | bytes 442376 | tf_op jit(solution)/shard_map/ppermute | solution.py:948
  (20 other events, 82.4 us)

commit v9 on v8

--- a/solution.py
+++ b/solution.py
@@ -1087,14 +1087,13 @@
         step = max(SEGS * planes // lanes, SEGS)
         return ((lanes * (-(-rows // step) * step), LANES), BF)
 
-    def over_planes(name, which, direct=(), send=True):
+    def over_planes(name, which, direct=()):
         ends = [(groups[index], place[groups[index].first + steps - 1, index]) for index in which]
         talls = [tall_of(group.rows(sz)) for group, _ in ends] + [tall_of(own)] * bool(direct)
         cut = sum(t[0][0] for t in talls) // planes + (16 if direct else 0)
         args = [x for index in which for x in (kept[index], came[groups[index].first + steps - 1])]
-        parts = call(name, sz, partial(fold_block_kernel, planes, ends, bool(direct)), [], [*args, *direct],
-                     [((cut, LANES), BF)] * planes, talls)
-        return swap_all(parts, "plane") if send else parts
+        return swap_all(call(name, sz, partial(fold_block_kernel, planes, ends, bool(direct)), [], [*args, *direct],
+                             [((cut, LANES), BF)] * planes, talls), "plane")
 
     up_b, twice_b, gstates_b, gskip_b, ends, send = call(
         "turn", sz, turn_kernel, items, [ahead, behind, slope_b, normed_b, w_out_b, params, perm, *cot_pieces],
@@ -1132,17 +1131,16 @@
         [keep, got, params, terms, more, ggain_b, gskip_a, gskip_b, gdecay_a, gdecay_b], [((own + 16, width), BF)] * blocks, [((8, width), F32)]))
     gdriven_a, sums_c[0] = after(gdriven_a, sums_c[0])
     sums_c = swap_all(sums_c)
-    message = halve(2)
-    kept[0], message = after(kept[0], message)
-    first_parts = over_planes("planes_a", [0], send=False) if steps <= 2 else []
-    first_parts, sums_c = after(first_parts, sums_c)
-    first_parts = swap_all(first_parts, "plane")
-    send_step(2, message)
-    gdriven_a, message = after(gdriven_a, message)
     last_pieces = call(
         "back_leave", sz, back_leave_kernel, [], [params, gdriven_a, up_a, slope_a, hidden_a, w_in_a, perm, last_b],
         [((2 * part, toks), BF)] * blocks, [rows_b, stacked], limit=12, time=6)
-    last_pieces, came[2], first_parts = after(last_pieces, came[2], first_parts)
+    last_pieces, came[1], sums_c = after(last_pieces, came[1], sums_c)
+    message = halve(2)
+    kept[0], message = after(kept[0], message)
+    first_parts = over_planes("planes_a", [0]) if steps <= 2 else []
+    send_step(2, message)
+    if first_parts:
+        came[2], first_parts = after(came[2], first_parts)
     for step in range(3, steps + 1):
         send_step(step, halve(step))
     parts = over_planes("planes", [1] if first_parts else [0, 1], sums_c)

time: 150 us -> 150 us (level)
    ppermute x24, waiting for transfers between devices: 5.62 us -> 11.3 us  [swap(): lax.ppermute(x, axis, [(i, i ^ dist) for i in range(lax.axis_size(axis))])]
    ppermute x3, waiting for transfers between devices: 4.35 us -> 0.01 us  [send_step(): came[step] = lax.ppermute(message, ('core', 'block'), pairs)]
  transfers between devices with their start and end apart: 45 -> 45, of which waited for: 19 -> 18; matrix products, arithmetic and copies ran while one was open for 0% -> 0% of each run, Pallas kernels for 31% -> 30%
where the time goes in v9:
time: 150 us
  Pallas kernels  57.4 us (38%)
  waiting for transfers between devices  47.4 us (32%)
  starting transfers between devices  43.3 us (29%)
    pallas_call x29, Pallas kernels, call(): pl.pallas_call(kernel, out_shape=out_shape, in_specs=[SMEM] * len(items)...  57.4 us
    ppermute x12, waiting for transfers between devices, across(): lax.ppermute(x, ('core', 'block'), [pair[::-1] for pair in pairs] if back...  32.6 us
    ppermute x24, starting transfers between devices, swap(): lax.ppermute(x, axis, [(i, i ^ dist) for i in range(lax.axis_size(axis))])  21.9 us
    ppermute x24, waiting for transfers between devices, swap(): lax.ppermute(x, axis, [(i, i ^ dist) for i in range(lax.axis_size(axis))])  11.3 us
    ppermute x12, starting transfers between devices, across(): lax.ppermute(x, ('core', 'block'), [pair[::-1] for pair in pairs] if back...  10.7 us
    ppermute x4, starting transfers between devices, neighbour(): return lax.ppermute(x, ('core', 'block'), pairs)  4.04 us
    ppermute x2, starting transfers between devices, on_device(): second_mine.append(lax.ppermute(held, ('core', 'block'), pairs))  3.35 us
    ppermute x3, starting transfers between devices, send_step(): came[step] = lax.ppermute(message, ('core', 'block'), pairs)  3.26 us
  transfers between devices with their start and end apart: 45, of which 18 were waited for; matrix products, arithmetic and copies ran while one was open for 0% of the time, Pallas kernels for 30%

profile of v9, /device:TPU:0, one launch (start us, length us, event | category | flops | bytes accessed | tf_op | source)
XLA Modules:
  0.0 149.6 jit_solution(8447942328585455073)
XLA Ops:
  0.6 1.9 %prepare.1 = (bf16[192,1024]{1,0:T(8,128)(2,1)S(1)}, bf16[192,1024]{1,0:T(8,128)(2,1)S(1)}, bf16[192,1024]{1,0:T(8,128)(2,1)S(1)}, bf16[192,1024]{1,0:T(8,128)(2...) custom-call(bf16[2,128,2048]{2,1,0:T(8,128)(2,1)} %refs_0_.2, f32[2,128]{1,0:T(2,128)} %refs_1_.1, ...), custom_call_target="tpu_custom_call" | custom-call | bytes 1000 | tf_op jit(solution)/shard_map/prepare/pallas_call | solution.py:923
  2.5 3.0 %collective-permute-start = (bf16[5,96,512]{2,1,0:T(8,128)(2,1)S(1)}, bf16[5,96,512]{2,1,0:T(8,128)(2,1)S(1)}, u32[]{:S(2)}, u32[]{:S(2)}) collective-permute-start(bf16[5,96,512]{2,1,0:T(8,128)(2,1)S(1)} %get-tuple-element.170.refs_0_), channel_id=1, source_target_pairs={{0,1},{1,0},{2,3},{3,2},{4,6},{5,7},{6,4},{7,5},{8,9},{9,8},{10,11... | collective-permute-start | bytes 1474568 | tf_op jit(solution)/shard_map/ppermute | solution.py:998
  5.5 1.5 %collective-permute-start.2 = (bf16[192,1024]{1,0:T(8,128)(2,1)S(1)}, bf16[192,1024]{1,0:T(8,128)(2,1)S(1)}, u32[]{:S(2)}, u32[]{:S(2)}) collective-permute-start(bf16[192,1024]{1,0:T(8,128)(2,1)S(1)} %get-tuple-element.172), channel_id=1, source_target_pairs={{0,2},{1,6},{2,0},{3,4},{4,3},{5,7},{6,1},{7,5},{8,10},{9,14},{10,... | collective-permute-start | bytes 1179656 | tf_op jit(solution)/shard_map/ppermute | solution.py:956
  8.2 1.6 %cut_cotangent.1 = (bf16[128,1024]{1,0:T(8,128)(2,1)S(1)}, bf16[128,1024]{1,0:T(8,128)(2,1)S(1)}, bf16[128,1024]{1,0:T(8,128)(2,1)S(1)}, bf16[128,1024]{1,0:T(8,128)(2,1)S(1)}) custom-call(f32[2,128,2048]{2,1,0:T(8,128)} %refs_0_.3), custom_call_target="tpu_custom_call" | custom-call | bytes 1000 | tf_op jit(solution)/shard_map/cut_cotangent/pallas_call | solution.py:923
  10.2 13.9 %collective-permute-done.2.refs_1_.refs_4_ = bf16[192,1024]{1,0:T(8,128)(2,1)S(1)} collective-permute-done((bf16[192,1024]{1,0:T(8,128)(2,1)S(1)}, bf16[192,1024]{1,0:T(8,128)(2,1)S(1)}, u32[]{:S(2)}, u32[]{:S(2)}) %collective-permute-start.2) | collective-permute-done | bytes 393248 | tf_op jit(solution)/shard_map/ppermute | solution.py:956
  24.2 3.5 %collective-permute-done.1.refs_0_.refs_3_ = bf16[192,1024]{1,0:T(8,128)(2,1)S(1)} collective-permute-done((bf16[192,1024]{1,0:T(8,128)(2,1)S(1)}, bf16[192,1024]{1,0:T(8,128)(2,1)S(1)}, u32[]{:S(2)}, u32[]{:S(2)}) %collective-permute-start.1) | collective-permute-done | bytes 393248 | tf_op jit(solution)/shard_map/ppermute | solution.py:956
  31.1 2.6 %open.1 = (bf16[1024,512]{1,0:T(8,128)(2,1)S(1)}, bf16[1024,512]{1,0:T(8,128)(2,1)S(1)}, f32[1024,128]{1,0:T(8,128)S(1)}, f32[1024,128]{1,0:T(8,128)S(1)}, f32[1024,128]{1,0:T(8,128)S(1)}) custom-call(s32[2,2,2,2]{3,2,1,0:T(2,128)S(1)} %pad_add_fusion.refs_0_, bf16[1024,1024]{1,0:T(8,128)(2,1)S(1)} %fusion.refs_1_.refs_7_.refs_6_, ...), custom_call_target="tpu_custom_call" | custom-call | flops 1200000000 | bytes 1000 | tf_op jit(solution)/shard_map/open/pallas_call | solution.py:923
  33.8 2.9 %enter.1 = (bf16[768,512]{1,0:T(8,128)(2,1)S(1)}, f32[1024,768]{1,0:T(8,128)S(1)}, f32[4,16,384]{2,1,0:T(8,128)S(1)}, f32[1,2,384]{2,1,0:T(2,128)S(1)}) custom-call(s32[2,2,2,2]{3,2,1,0:T(2,128)S(1)} %pad_add_fusion.refs_0_, f32[1024,128]{1,0:T(8,128)S(1)} %get-tuple-element.188.refs_1_.refs_2_, f32[1024,128]{1,0:T(8,128)S(1)} %get-tuple-element.189.refs_2_.refs_3_, ...), custom_call_target="tpu_custom_call" | custom-call | bytes 1000 | tf_op jit(solution)/shard_map/enter/pallas_call | solution.py:923
  37.9 2.4 %chain.1.refs_4_.refs_2_.refs_7_ = bf16[1024,1536]{1,0:T(8,128)(2,1)S(1)} custom-call(s32[2,2,2,2]{3,2,1,0:T(2,128)S(1)} %pad_add_fusion.refs_0_, f32[1024,128]{1,0:T(8,128)S(1)} %get-tuple-element.188.refs_1_.refs_2_, f32[1024,128]{1,0:T(8,128)S(1)} %get-tuple-element.189.refs_2_.refs_3_, f32[1,2,384]{2,1,0:T(2,128)S(1)} %bitcast.18, ...), custom_call_target="tpu_custom_call" | custom-call | bytes 1000 | tf_op jit(solution)/shard_map/chain/pallas_call | solution.py:923
  40.3 1.6 %collective-permute-done.6.refs_11_.refs_12_ = bf16[10,96,512]{2,1,0:T(8,128)(2,1)S(1)} collective-permute-done((bf16[10,96,512]{2,1,0:T(8,128)(2,1)S(1)}, bf16[10,96,512]{2,1,0:T(8,128)(2,1)S(1)}, u32[]{:S(2)}, u32[]{:S(2)}) %collective-permute-start.6) | collective-permute-done | bytes 983072 | tf_op jit(solution)/shard_map/ppermute | solution.py:998
  42.2 1.7 %collective-permute-start.12 = (bf16[128,1024]{1,0:T(8,128)(2,1)S(1)}, bf16[128,1024]{1,0:T(8,128)(2,1)S(1)}, u32[]{:S(2)}, u32[]{:S(2)}) collective-permute-start(bf16[128,1024]{1,0:T(8,128)(2,1)S(1)} %get-tuple-element.214), channel_id=1, source_target_pairs={{0,6},{1,2},{2,4},{3,0},{4,7},{5,3},{6,5},{7,1},{8,14},{9,10},{10,... | collective-permute-start | bytes 786440 | tf_op jit(solution)/shard_map/ppermute | solution.py:956
  44.4 1.8 %collective-permute-start.14 = (bf16[128,1024]{1,0:T(8,128)(2,1)S(1)}, bf16[128,1024]{1,0:T(8,128)(2,1)S(1)}, u32[]{:S(2)}, u32[]{:S(2)}) collective-permute-start(bf16[128,1024]{1,0:T(8,128)(2,1)S(1)} %get-tuple-element.216), channel_id=1, source_target_pairs={{0,4},{1,0},{2,6},{3,2},{4,5},{5,1},{6,7},{7,3},{8,12},{9,8},{10,1... | collective-permute-start | bytes 786440 | tf_op jit(solution)/shard_map/ppermute | solution.py:956
  46.9 6.6 %middle.1 = (bf16[1536,512]{1,0:T(8,128)(2,1)S(1)}, bf16[768,512]{1,0:T(8,128)(2,1)S(1)}, bf16[1024,512]{1,0:T(8,128)(2,1)S(1)}, f32[1024,512]{1,0:T(8,128)S(1)}...) custom-call(s32[2,2,2,2]{3,2,1,0:T(2,128)S(1)} %pad_add_fusion.refs_, ...), custom_call_target="tpu_custom_call" | custom-call | flops 4400000000 | bytes 1000 | tf_op jit(solution)/shard_map/middle/pallas_call | solution.py:923
  53.5 3.5 %collective-permute-start.11 = (f32[2,384]{1,0:T(2,128)S(1)}, f32[2,384]{1,0:T(2,128)S(1)}, u32[]{:S(2)}, u32[]{:S(2)}) collective-permute-start(f32[2,384]{1,0:T(2,128)S(1)} %bitcast.23), channel_id=1, source_target_pairs={{0,4},{1,5},{2,6},{3,7},{4,0},{5,1},{6,2},{7,3},{8,12},{9,13},{10,... | collective-permute-start | bytes 9224 | tf_op jit(solution)/shard_map/ppermute | solution.py:970
  57.8 5.5 %leave.1 = (bf16[1536,512]{1,0:T(8,128)(2,1)S(1)}, bf16[1024,1536]{1,0:T(8,128)(2,1)S(1)}, bf16[1024,512]{1,0:T(8,128)(2,1)S(1)}, bf16[1024,512]{1,0:T(8,128)(2,1)S(1)}) custom-call(s32[2,2,2,2]{3,2,1,0:T(2,128)S(1)} %pad_add_fusion.refs_0_, f32[1024,128]{1,0:T(8,128)S(1)} %get-tuple-element.190.refs_1_, f32[1024,128]{1,0:T(8,128)S(1)} %get-tuple-element.188.refs_1_.refs_2_, ...), custom_call_target="tpu_custom_call" | custom-call | bytes 1000 | tf_op jit(solution)/shard_map/leave/pallas_call | solution.py:923
  63.4 5.0 %turn.1 = (f32[1024,512]{1,0:T(8,128)S(1)}, bf16[1024,512]{1,0:T(8,128)(2,1)S(1)}, f32[1024,1536]{1,0:T(8,128)S(1)}, f32[1,512]{1,0:T(1,128)S(1)}, f32[4,16,384]{2,1,0:T(8,128)S(1)}, /*index=5*/f32[1,2,384]{2,1,0:T(2,128)S(1)}) custom-call(s32[2,2,2,2]{3,2,1,0:T(2,128)S(1)} %pad_add_fusion.refs_0_, f32[1024,128]{1,0:T(8,128)S(1)} %get-tuple-element.188.refs_1_.refs_2_, ...), custom_call_target="tpu_custom_call" | custom-call | flops 2400000000 | bytes 1000 | tf_op jit(solution)/shard_map/turn/pallas_call | solution.py:923
  72.7 9.1 %back_middle.1 = (bf16[1024,768]{1,0:T(8,128)(2,1)S(1)}, f32[2,384]{1,0:T(2,128)S(1)}, f32[1,512]{1,0:T(1,128)S(1)}, f32[1024,512]{1,0:T(8,128)S(1)}, bf16[1024,...) custom-call(s32[2,2,2,2]{3,2,1,0:T(2,128)S(1)} %pad_add_fusion.refs_, ...), custom_call_target="tpu_custom_call" | custom-call | flops 4400000000 | bytes 1000 | tf_op jit(solution)/shard_map/back_middle/pallas_call | solution.py:923
  81.8 1.4 grads_b_send.1
  87.6 3.5 %back_chain.1 = (bf16[1024,768]{1,0:T(8,128)(2,1)S(1)}, f32[2,384]{1,0:T(2,128)S(1)}) custom-call(s32[2,2,2,2]{3,2,1,0:T(2,128)S(1)} %pad_add_fusion.refs_0_, f32[1024,128]{1,0:T(8,128)S(1)} %get-tuple-element.188.refs_1_.refs_2_, f32[1024,128]{1,0:T(8,128)S(1)} %get-tuple-element.189.refs_2_.refs_3_, f32[1,2,384]{2,1,0:T(2,128)S(1)} %bitcast.21, ...), custom_call_target="tpu_custom_call" | custom-call | flops 3600000000 | bytes 1000 | tf_op jit(solution)/shard_map/back_chain/pallas_call | solution.py:923
  93.6 1.8 %collective-permute-start.23 = (bf16[112,512]{1,0:T(8,128)(2,1)S(1)}, bf16[112,512]{1,0:T(8,128)(2,1)S(1)}, u32[]{:S(2)}, u32[]{:S(2)}) collective-permute-start(bf16[112,512]{1,0:T(8,128)(2,1)S(1)} %get-tuple-element.264), channel_id=1, source_target_pairs={{0,3},{1,2},{2,1},{3,0},{4,7},{5,6},{6,5},{7,4},{8,11},{9,10},{10,... | collective-permute-start | bytes 344072 | tf_op jit(solution)/shard_map/ppermute | solution.py:948
  97.2 4.1 %back_leave.1 = (bf16[256,1024]{1,0:T(8,128)(2,1)S(1)}, bf16[256,1024]{1,0:T(8,128)(2,1)S(1)}, bf16[256,1024]{1,0:T(8,128)(2,1)S(1)}, bf16[256,1024]{1,0:T(8,128)(2,1)S(1)}) custom-call(f32[8,512]{1,0:T(8,128)S(1)} %get-tuple-element.187.refs_2_.refs_3_.refs_4_.refs_5_.refs_6_.refs_0_, bf16[1024,768]{1,0:T(8,128)(2,1)S(1)} %get-tuple-element.255.refs_0_.refs_1_, ...), custom_call_target="tpu_custom_call" | custom-call | flops 2400000000 | bytes 1000 | tf_op jit(solution)/shard_map/back_leave/pallas_call | solution.py:923
  101.3 2.2 %collective-permute-done.24.refs_4_ = bf16[112,512]{1,0:T(8,128)(2,1)S(1)} collective-permute-done((bf16[112,512]{1,0:T(8,128)(2,1)S(1)}, bf16[112,512]{1,0:T(8,128)(2,1)S(1)}, u32[]{:S(2)}, u32[]{:S(2)}) %collective-permute-start.24) | collective-permute-done | bytes 114720 | tf_op jit(solution)/shard_map/ppermute | solution.py:948
  105.1 3.7 %collective-permute-start.27 = (bf16[192,128]{1,0:T(8,128)(2,1)S(1)}, bf16[192,128]{1,0:T(8,128)(2,1)S(1)}, u32[]{:S(2)}, u32[]{:S(2)}) collective-permute-start(bf16[192,128]{1,0:T(8,128)(2,1)S(1)} %get-tuple-element.273), channel_id=1, source_target_pairs={{0,24},{8,16},{16,8},{24,0},{1,25},{9,17},{17,9},{25,1},{2,26},{10... | collective-permute-start | bytes 147464 | tf_op jit(solution)/shard_map/ppermute | solution.py:948
  109.6 1.9 %collective-permute-done.27.refs_1_ = bf16[192,128]{1,0:T(8,128)(2,1)S(1)} collective-permute-done((bf16[192,128]{1,0:T(8,128)(2,1)S(1)}, bf16[192,128]{1,0:T(8,128)(2,1)S(1)}, u32[]{:S(2)}, u32[]{:S(2)}) %collective-permute-start.27) | collective-permute-done | bytes 49184 | tf_op jit(solution)/shard_map/ppermute | solution.py:948
  111.5 2.3 %collective-permute-done.28.refs_2_ = bf16[192,128]{1,0:T(8,128)(2,1)S(1)} collective-permute-done((bf16[192,128]{1,0:T(8,128)(2,1)S(1)}, bf16[192,128]{1,0:T(8,128)(2,1)S(1)}, u32[]{:S(2)}, u32[]{:S(2)}) %collective-permute-start.28) | collective-permute-done | bytes 49184 | tf_op jit(solution)/shard_map/ppermute | solution.py:948
  114.0 1.6 %collective-permute-start.30 = (bf16[256,1024]{1,0:T(8,128)(2,1)S(1)}, bf16[256,1024]{1,0:T(8,128)(2,1)S(1)}, u32[]{:S(2)}, u32[]{:S(2)}) collective-permute-start(bf16[256,1024]{1,0:T(8,128)(2,1)S(1)} %get-tuple-element.292), channel_id=1, source_target_pairs={{6,0},{2,1},{4,2},{0,3},{7,4},{3,5},{5,6},{1,7},{14,8},{10,9},{12,... | collective-permute-start | bytes 1572872 | tf_op jit(solution)/shard_map/ppermute | solution.py:956
  115.6 1.6 %collective-permute-start.32 = (bf16[400,128]{1,0:T(8,128)(2,1)S(1)}, bf16[400,128]{1,0:T(8,128)(2,1)S(1)}, u32[]{:S(2)}, u32[]{:S(2)}) collective-permute-start(bf16[400,128]{1,0:T(8,128)(2,1)S(1)} %get-tuple-element.295), channel_id=1, source_target_pairs={{0,24},{8,16},{16,8},{24,0},{1,25},{9,17},{17,9},{25,1},{2,26},{10... | collective-permute-start | bytes 307208 | tf_op jit(solution)/shard_map/ppermute | solution.py:948
  117.6 2.4 %collective-permute-start.34 = (bf16[400,128]{1,0:T(8,128)(2,1)S(1)}, bf16[400,128]{1,0:T(8,128)(2,1)S(1)}, u32[]{:S(2)}, u32[]{:S(2)}) collective-permute-start(bf16[400,128]{1,0:T(8,128)(2,1)S(1)} %get-tuple-element.297), channel_id=1, source_target_pairs={{0,8},{8,0},{16,24},{24,16},{1,9},{9,1},{17,25},{25,17},{2,10},{10... | collective-permute-start | bytes 307208 | tf_op jit(solution)/shard_map/ppermute | solution.py:948
  120.0 6.9 %collective-permute-done.30.refs_0_ = bf16[256,1024]{1,0:T(8,128)(2,1)S(1)} collective-permute-done((bf16[256,1024]{1,0:T(8,128)(2,1)S(1)}, bf16[256,1024]{1,0:T(8,128)(2,1)S(1)}, u32[]{:S(2)}, u32[]{:S(2)}) %collective-permute-start.30) | collective-permute-done | bytes 524320 | tf_op jit(solution)/shard_map/ppermute | solution.py:956
  130.1 2.8 %collective-permute-start.36 = (bf16[576,128]{1,0:T(8,128)(2,1)S(1)}, bf16[576,128]{1,0:T(8,128)(2,1)S(1)}, u32[]{:S(2)}, u32[]{:S(2)}) collective-permute-start(bf16[576,128]{1,0:T(8,128)(2,1)S(1)} %get-tuple-element.304.refs_0_), channel_id=1, source_target_pairs={{0,16},{8,24},{16,0},{24,8},{1,17},{9,25},{17,1},{25,9},{2,18},{10... | collective-permute-start | bytes 442376 | tf_op jit(solution)/shard_map/ppermute | solution.py:948
  135.7 7.2 %collective-permute-done.38.refs_0_ = bf16[256,1024]{1,0:T(8,128)(2,1)S(1)} collective-permute-done((bf16[256,1024]{1,0:T(8,128)(2,1)S(1)}, bf16[256,1024]{1,0:T(8,128)(2,1)S(1)}, u32[]{:S(2)}, u32[]{:S(2)}) %collective-permute-start.38) | collective-permute-done | bytes 524320 | tf_op jit(solution)/shard_map/ppermute | solution.py:956
  147.5 2.1 %finish.1 = (f32[2,128]{1,0:T(2,128)}, f32[2,128]{1,0:T(2,128)}, f32[2,96]{1,0:T(2,128)}, f32[2,96]{1,0:T(2,128)}, f32[2,96]{1,0:T(2,128)}, /*index=5*/f32[2,2,96,512]{3,2,1,0:T(8,128)}, f32[2,4,96,512]{3,2,1,0:T(8,128)}) custom-call(bf16[576,128]{1,0:T(8,128)(2,1)S(1)} %get-tuple-element.304.refs_0_, bf16[576,128]{1,0:T(8,128)(2,1)S(1)} %collective-permute-done.35.refs_1_, ...), custom_call_target="tpu_custom_call" | custom-call | bytes 1000 | tf_op jit(solution)/shard_map/finish/pallas_call | solution.py:923
  (106 shorter events, 35.0 us)
Async XLA Ops:
  2.5 25.1 %collective-permute-start = (bf16[5,96,512]{2,1,0:T(8,128)(2,1)S(1)}, bf16[5,96,512]{2,1,0:T(8,128)(2,1)S(1)}, u32[]{:S(2)}, u32[]{:S(2)}) collective-permute-start(bf16[5,96,512]{2,1,0:T(8,128)(2,1)S(1)} %get-tuple-element.170.refs_0_), channel_id=1, source_target_pairs={{0,1},{1,0},{2,3},{3,2},{4,6},{5,7},{6,4},{7,5},{8,9},{9,8},{10,11... | collective-permute-start | bytes 1474568 | tf_op jit(solution)/shard_map/ppermute | solution.py:998
  5.5 18.6 %collective-permute-start.2 = (bf16[192,1024]{1,0:T(8,128)(2,1)S(1)}, bf16[192,1024]{1,0:T(8,128)(2,1)S(1)}, u32[]{:S(2)}, u32[]{:S(2)}) collective-permute-start(bf16[192,1024]{1,0:T(8,128)(2,1)S(1)} %get-tuple-element.172), channel_id=1, source_target_pairs={{0,2},{1,6},{2,0},{3,4},{4,3},{5,7},{6,1},{7,5},{8,10},{9,14},{10,... | collective-permute-start | bytes 1179656 | tf_op jit(solution)/shard_map/ppermute | solution.py:956
  7.0 20.6 %collective-permute-start.1 = (bf16[192,1024]{1,0:T(8,128)(2,1)S(1)}, bf16[192,1024]{1,0:T(8,128)(2,1)S(1)}, u32[]{:S(2)}, u32[]{:S(2)}) collective-permute-start(bf16[192,1024]{1,0:T(8,128)(2,1)S(1)} %get-tuple-element.171), channel_id=1, source_target_pairs={{0,6},{1,2},{2,4},{3,0},{4,7},{5,3},{6,5},{7,1},{8,14},{9,10},{10,... | collective-permute-start | bytes 1179656 | tf_op jit(solution)/shard_map/ppermute | solution.py:956
  7.0 20.6 %collective-permute-start.3 = (bf16[192,1024]{1,0:T(8,128)(2,1)S(1)}, bf16[192,1024]{1,0:T(8,128)(2,1)S(1)}, u32[]{:S(2)}, u32[]{:S(2)}) collective-permute-start(bf16[192,1024]{1,0:T(8,128)(2,1)S(1)} %get-tuple-element.178), channel_id=1, source_target_pairs={{0,4},{1,0},{2,6},{3,2},{4,5},{5,1},{6,7},{7,3},{8,12},{9,8},{10,1... | collective-permute-start | bytes 1179656 | tf_op jit(solution)/shard_map/ppermute | solution.py:956
  7.5 20.1 %collective-permute-start.4 = (bf16[192,1024]{1,0:T(8,128)(2,1)S(1)}, bf16[192,1024]{1,0:T(8,128)(2,1)S(1)}, u32[]{:S(2)}, u32[]{:S(2)}) collective-permute-start(bf16[192,1024]{1,0:T(8,128)(2,1)S(1)} %get-tuple-element.179), channel_id=1, source_target_pairs={{0,0},{1,4},{2,2},{3,6},{4,1},{5,5},{6,3},{7,7},{8,8},{9,12},{10,1... | collective-permute-start | bytes 1179656 | tf_op jit(solution)/shard_map/ppermute | solution.py:956
  27.7 14.2 %collective-permute-start.6 = (bf16[10,96,512]{2,1,0:T(8,128)(2,1)S(1)}, bf16[10,96,512]{2,1,0:T(8,128)(2,1)S(1)}, u32[]{:S(2)}, u32[]{:S(2)}) collective-permute-start(bf16[10,96,512]{2,1,0:T(8,128)(2,1)S(1)} %pile_0.1), channel_id=1, source_target_pairs={{0,2},{1,3},{2,0},{3,1},{4,5},{5,4},{6,7},{7,6},{8,10},{9,11},{10,... | collective-permute-start | bytes 2949128 | tf_op jit(solution)/shard_map/ppermute | solution.py:998
  28.1 9.8 %collective-permute-start.9 = (bf16[5,96,512]{2,1,0:T(8,128)(2,1)S(1)}, bf16[5,96,512]{2,1,0:T(8,128)(2,1)S(1)}, u32[]{:S(2)}, u32[]{:S(2)}) collective-permute-start(bf16[5,96,512]{2,1,0:T(8,128)(2,1)S(1)} %collective-permute-done.refs_1_.refs_10_.refs_11_), channel_id=1, source_target_pairs={{0,4},{4,0},{1,5},{5,1},{2,6},{6,2},{3,7},{7,3},{8,12},{12,8},{9,1... | collective-permute-start | bytes 1474568 | tf_op jit(solution)/shard_map/ppermute | solution.py:948
  41.9 5.0 %collective-permute-start.10 = (bf16[10,96,512]{2,1,0:T(8,128)(2,1)S(1)}, bf16[10,96,512]{2,1,0:T(8,128)(2,1)S(1)}, u32[]{:S(2)}, u32[]{:S(2)}) collective-permute-start(bf16[10,96,512]{2,1,0:T(8,128)(2,1)S(1)} %collective-permute-done.6.refs_11_.refs_12_), channel_id=1, source_target_pairs={{0,4},{4,0},{1,5},{5,1},{2,6},{6,2},{3,7},{7,3},{8,12},{12,8},{9,1... | collective-permute-start | bytes 2949128 | tf_op jit(solution)/shard_map/ppermute | solution.py:948
  42.2 21.1 %collective-permute-start.12 = (bf16[128,1024]{1,0:T(8,128)(2,1)S(1)}, bf16[128,1024]{1,0:T(8,128)(2,1)S(1)}, u32[]{:S(2)}, u32[]{:S(2)}) collective-permute-start(bf16[128,1024]{1,0:T(8,128)(2,1)S(1)} %get-tuple-element.214), channel_id=1, source_target_pairs={{0,6},{1,2},{2,4},{3,0},{4,7},{5,3},{6,5},{7,1},{8,14},{9,10},{10,... | collective-permute-start | bytes 786440 | tf_op jit(solution)/shard_map/ppermute | solution.py:956
  43.9 19.4 %collective-permute-start.13 = (bf16[128,1024]{1,0:T(8,128)(2,1)S(1)}, bf16[128,1024]{1,0:T(8,128)(2,1)S(1)}, u32[]{:S(2)}, u32[]{:S(2)}) collective-permute-start(bf16[128,1024]{1,0:T(8,128)(2,1)S(1)} %get-tuple-element.215), channel_id=1, source_target_pairs={{0,2},{1,6},{2,0},{3,4},{4,3},{5,7},{6,1},{7,5},{8,10},{9,14},{10,... | collective-permute-start | bytes 786440 | tf_op jit(solution)/shard_map/ppermute | solution.py:956
  44.4 19.0 %collective-permute-start.14 = (bf16[128,1024]{1,0:T(8,128)(2,1)S(1)}, bf16[128,1024]{1,0:T(8,128)(2,1)S(1)}, u32[]{:S(2)}, u32[]{:S(2)}) collective-permute-start(bf16[128,1024]{1,0:T(8,128)(2,1)S(1)} %get-tuple-element.216), channel_id=1, source_target_pairs={{0,4},{1,0},{2,6},{3,2},{4,5},{5,1},{6,7},{7,3},{8,12},{9,8},{10,1... | collective-permute-start | bytes 786440 | tf_op jit(solution)/shard_map/ppermute | solution.py:956
  46.2 17.2 %collective-permute-start.15 = (bf16[128,1024]{1,0:T(8,128)(2,1)S(1)}, bf16[128,1024]{1,0:T(8,128)(2,1)S(1)}, u32[]{:S(2)}, u32[]{:S(2)}) collective-permute-start(bf16[128,1024]{1,0:T(8,128)(2,1)S(1)} %get-tuple-element.217), channel_id=1, source_target_pairs={{0,0},{1,4},{2,2},{3,6},{4,1},{5,5},{6,3},{7,7},{8,8},{9,12},{10,1... | collective-permute-start | bytes 786440 | tf_op jit(solution)/shard_map/ppermute | solution.py:956
  53.5 4.3 %collective-permute-start.11 = (f32[2,384]{1,0:T(2,128)S(1)}, f32[2,384]{1,0:T(2,128)S(1)}, u32[]{:S(2)}, u32[]{:S(2)}) collective-permute-start(f32[2,384]{1,0:T(2,128)S(1)} %bitcast.23), channel_id=1, source_target_pairs={{0,4},{1,5},{2,6},{3,7},{4,0},{5,1},{6,2},{7,3},{8,12},{9,13},{10,... | collective-permute-start | bytes 9224 | tf_op jit(solution)/shard_map/ppermute | solution.py:970
  72.0 9.8 %collective-permute-start.18 = (bf16[384,512]{1,0:T(8,128)(2,1)S(1)}, bf16[384,512]{1,0:T(8,128)(2,1)S(1)}, u32[]{:S(2)}, u32[]{:S(2)}) collective-permute-start(bf16[384,512]{1,0:T(8,128)(2,1)S(1)} %get-tuple-element.230), channel_id=1, source_target_pairs={{0,1},{1,0},{2,3},{3,2},{4,6},{5,7},{6,4},{7,5},{8,9},{9,8},{10,11... | collective-permute-start | bytes 1179656 | tf_op jit(solution)/shard_map/ppermute | solution.py:1077
  86.5 17.0 %collective-permute-start.22 = (bf16[768,512]{1,0:T(8,128)(2,1)S(1)}, bf16[768,512]{1,0:T(8,128)(2,1)S(1)}, u32[]{:S(2)}, u32[]{:S(2)}) collective-permute-start(bf16[768,512]{1,0:T(8,128)(2,1)S(1)} %get-tuple-element.262), channel_id=1, source_target_pairs={{0,2},{1,3},{2,0},{3,1},{4,5},{5,4},{6,7},{7,6},{8,10},{9,11},{10,... | collective-permute-start | bytes 2359304 | tf_op jit(solution)/shard_map/ppermute | solution.py:1077
  93.6 7.6 %collective-permute-start.23 = (bf16[112,512]{1,0:T(8,128)(2,1)S(1)}, bf16[112,512]{1,0:T(8,128)(2,1)S(1)}, u32[]{:S(2)}, u32[]{:S(2)}) collective-permute-start(bf16[112,512]{1,0:T(8,128)(2,1)S(1)} %get-tuple-element.264), channel_id=1, source_target_pairs={{0,3},{1,2},{2,1},{3,0},{4,7},{5,6},{6,5},{7,4},{8,11},{9,10},{10,... | collective-permute-start | bytes 344072 | tf_op jit(solution)/shard_map/ppermute | solution.py:948
  95.5 8.0 %collective-permute-start.24 = (bf16[112,512]{1,0:T(8,128)(2,1)S(1)}, bf16[112,512]{1,0:T(8,128)(2,1)S(1)}, u32[]{:S(2)}, u32[]{:S(2)}) collective-permute-start(bf16[112,512]{1,0:T(8,128)(2,1)S(1)} %get-tuple-element.265), channel_id=1, source_target_pairs={{0,2},{1,3},{2,0},{3,1},{4,6},{5,7},{6,4},{7,5},{8,10},{9,11},{10,... | collective-permute-start | bytes 344072 | tf_op jit(solution)/shard_map/ppermute | solution.py:948
  96.5 7.0 %collective-permute-start.25 = (bf16[112,512]{1,0:T(8,128)(2,1)S(1)}, bf16[112,512]{1,0:T(8,128)(2,1)S(1)}, u32[]{:S(2)}, u32[]{:S(2)}) collective-permute-start(bf16[112,512]{1,0:T(8,128)(2,1)S(1)} %get-tuple-element.266), channel_id=1, source_target_pairs={{0,1},{1,0},{2,3},{3,2},{4,5},{5,4},{6,7},{7,6},{8,9},{9,8},{10,11... | collective-permute-start | bytes 344072 | tf_op jit(solution)/shard_map/ppermute | solution.py:948
  103.6 10.2 %collective-permute-start.26 = (bf16[288,512]{1,0:T(8,128)(2,1)S(1)}, bf16[288,512]{1,0:T(8,128)(2,1)S(1)}, u32[]{:S(2)}, u32[]{:S(2)}) collective-permute-start(bf16[288,512]{1,0:T(8,128)(2,1)S(1)} %get-tuple-element.270), channel_id=1, source_target_pairs={{0,1},{1,0},{2,3},{3,2},{4,6},{5,7},{6,4},{7,5},{8,9},{9,8},{10,11... | collective-permute-start | bytes 884744 | tf_op jit(solution)/shard_map/ppermute | solution.py:1077
  105.1 6.4 %collective-permute-start.27 = (bf16[192,128]{1,0:T(8,128)(2,1)S(1)}, bf16[192,128]{1,0:T(8,128)(2,1)S(1)}, u32[]{:S(2)}, u32[]{:S(2)}) collective-permute-start(bf16[192,128]{1,0:T(8,128)(2,1)S(1)} %get-tuple-element.273), channel_id=1, source_target_pairs={{0,24},{8,16},{16,8},{24,0},{1,25},{9,17},{17,9},{25,1},{2,26},{10... | collective-permute-start | bytes 147464 | tf_op jit(solution)/shard_map/ppermute | solution.py:948
  108.8 5.0 %collective-permute-start.28 = (bf16[192,128]{1,0:T(8,128)(2,1)S(1)}, bf16[192,128]{1,0:T(8,128)(2,1)S(1)}, u32[]{:S(2)}, u32[]{:S(2)}) collective-permute-start(bf16[192,128]{1,0:T(8,128)(2,1)S(1)} %get-tuple-element.274), channel_id=1, source_target_pairs={{0,16},{8,24},{16,0},{24,8},{1,17},{9,25},{17,1},{25,9},{2,18},{10... | collective-permute-start | bytes 147464 | tf_op jit(solution)/shard_map/ppermute | solution.py:948
  108.8 5.0 %collective-permute-start.29 = (bf16[192,128]{1,0:T(8,128)(2,1)S(1)}, bf16[192,128]{1,0:T(8,128)(2,1)S(1)}, u32[]{:S(2)}, u32[]{:S(2)}) collective-permute-start(bf16[192,128]{1,0:T(8,128)(2,1)S(1)} %get-tuple-element.275), channel_id=1, source_target_pairs={{0,8},{8,0},{16,24},{24,16},{1,9},{9,1},{17,25},{25,17},{2,10},{10... | collective-permute-start | bytes 147464 | tf_op jit(solution)/shard_map/ppermute | solution.py:948
  114.0 12.9 %collective-permute-start.30 = (bf16[256,1024]{1,0:T(8,128)(2,1)S(1)}, bf16[256,1024]{1,0:T(8,128)(2,1)S(1)}, u32[]{:S(2)}, u32[]{:S(2)}) collective-permute-start(bf16[256,1024]{1,0:T(8,128)(2,1)S(1)} %get-tuple-element.292), channel_id=1, source_target_pairs={{6,0},{2,1},{4,2},{0,3},{7,4},{3,5},{5,6},{1,7},{14,8},{10,9},{12,... | collective-permute-start | bytes 1572872 | tf_op jit(solution)/shard_map/ppermute | solution.py:956
  115.6 12.4 %collective-permute-start.31 = (bf16[256,1024]{1,0:T(8,128)(2,1)S(1)}, bf16[256,1024]{1,0:T(8,128)(2,1)S(1)}, u32[]{:S(2)}, u32[]{:S(2)}) collective-permute-start(bf16[256,1024]{1,0:T(8,128)(2,1)S(1)} %get-tuple-element.293), channel_id=1, source_target_pairs={{4,0},{0,1},{6,2},{2,3},{5,4},{1,5},{7,6},{3,7},{12,8},{8,9},{14,1... | collective-permute-start | bytes 1572872 | tf_op jit(solution)/shard_map/ppermute | solution.py:956
  115.6 12.4 %collective-permute-start.32 = (bf16[400,128]{1,0:T(8,128)(2,1)S(1)}, bf16[400,128]{1,0:T(8,128)(2,1)S(1)}, u32[]{:S(2)}, u32[]{:S(2)}) collective-permute-start(bf16[400,128]{1,0:T(8,128)(2,1)S(1)} %get-tuple-element.295), channel_id=1, source_target_pairs={{0,24},{8,16},{16,8},{24,0},{1,25},{9,17},{17,9},{25,1},{2,26},{10... | collective-permute-start | bytes 307208 | tf_op jit(solution)/shard_map/ppermute | solution.py:948
  117.2 10.8 %collective-permute-start.33 = (bf16[400,128]{1,0:T(8,128)(2,1)S(1)}, bf16[400,128]{1,0:T(8,128)(2,1)S(1)}, u32[]{:S(2)}, u32[]{:S(2)}) collective-permute-start(bf16[400,128]{1,0:T(8,128)(2,1)S(1)} %get-tuple-element.296), channel_id=1, source_target_pairs={{0,16},{8,24},{16,0},{24,8},{1,17},{9,25},{17,1},{25,9},{2,18},{10... | collective-permute-start | bytes 307208 | tf_op jit(solution)/shard_map/ppermute | solution.py:948
  117.6 10.3 %collective-permute-start.34 = (bf16[400,128]{1,0:T(8,128)(2,1)S(1)}, bf16[400,128]{1,0:T(8,128)(2,1)S(1)}, u32[]{:S(2)}, u32[]{:S(2)}) collective-permute-start(bf16[400,128]{1,0:T(8,128)(2,1)S(1)} %get-tuple-element.297), channel_id=1, source_target_pairs={{0,8},{8,0},{16,24},{24,16},{1,9},{9,1},{17,25},{25,17},{2,10},{10... | collective-permute-start | bytes 307208 | tf_op jit(solution)/shard_map/ppermute | solution.py:948
  128.0 14.9 %collective-permute-start.38 = (bf16[256,1024]{1,0:T(8,128)(2,1)S(1)}, bf16[256,1024]{1,0:T(8,128)(2,1)S(1)}, u32[]{:S(2)}, u32[]{:S(2)}) collective-permute-start(bf16[256,1024]{1,0:T(8,128)(2,1)S(1)} %get-tuple-element.301), channel_id=1, source_target_pairs={{2,0},{6,1},{0,2},{4,3},{3,4},{7,5},{1,6},{5,7},{10,8},{14,9},{8,1... | collective-permute-start | bytes 1572872 | tf_op jit(solution)/shard_map/ppermute | solution.py:956
  129.1 13.8 %collective-permute-start.39 = (bf16[256,1024]{1,0:T(8,128)(2,1)S(1)}, bf16[256,1024]{1,0:T(8,128)(2,1)S(1)}, u32[]{:S(2)}, u32[]{:S(2)}) collective-permute-start(bf16[256,1024]{1,0:T(8,128)(2,1)S(1)} %get-tuple-element.302), channel_id=1, source_target_pairs={{0,0},{4,1},{2,2},{6,3},{1,4},{5,5},{3,6},{7,7},{8,8},{12,9},{10,1... | collective-permute-start | bytes 1572872 | tf_op jit(solution)/shard_map/ppermute | solution.py:956
  129.8 15.0 %collective-permute-start.37 = (bf16[576,128]{1,0:T(8,128)(2,1)S(1)}, bf16[576,128]{1,0:T(8,128)(2,1)S(1)}, u32[]{:S(2)}, u32[]{:S(2)}) collective-permute-start(bf16[576,128]{1,0:T(8,128)(2,1)S(1)} %get-tuple-element.304.refs_0_), channel_id=1, source_target_pairs={{0,8},{8,0},{16,24},{24,16},{1,9},{9,1},{17,25},{25,17},{2,10},{10... | collective-permute-start | bytes 442376 | tf_op jit(solution)/shard_map/ppermute | solution.py:948
  130.1 14.7 %collective-permute-start.36 = (bf16[576,128]{1,0:T(8,128)(2,1)S(1)}, bf16[576,128]{1,0:T(8,128)(2,1)S(1)}, u32[]{:S(2)}, u32[]{:S(2)}) collective-permute-start(bf16[576,128]{1,0:T(8,128)(2,1)S(1)} %get-tuple-element.304.refs_0_), channel_id=1, source_target_pairs={{0,16},{8,24},{16,0},{24,8},{1,17},{9,25},{17,1},{25,9},{2,18},{10... | collective-permute-start | bytes 442376 | tf_op jit(solution)/shard_map/ppermute | solution.py:948
  132.9 11.9 %collective-permute-start.35 = (bf16[576,128]{1,0:T(8,128)(2,1)S(1)}, bf16[576,128]{1,0:T(8,128)(2,1)S(1)}, u32[]{:S(2)}, u32[]{:S(2)}) collective-permute-start(bf16[576,128]{1,0:T(8,128)(2,1)S(1)} %get-tuple-element.304.refs_0_), channel_id=1, source_target_pairs={{0,24},{8,16},{16,8},{24,0},{1,25},{9,17},{17,9},{25,1},{2,26},{10... | collective-permute-start | bytes 442376 | tf_op jit(solution)/shard_map/ppermute | solution.py:948
  (20 other events, 85.5 us)
